TPU v7x, 256 devices: a whole 4x4x8 slice. The times are simulated.
256 devices in a mesh: section: 4 (over z_hi, core), tp: 64 (over x, y, z_lo).
Axes of the slice: x: 4, y: 4, z: 8 (z_hi: 2, z_lo: 4; z = z_hi * 4 + z_lo), core: 2. Of those that a mesh axis runs over, the one named last changes fastest.
Arguments:
- travelling_inputs: bfloat16 [4, 512, 3072], P('section', 'tp'), may hold values from -6 to 6
- travelling_region: int32 [4, 512], P('section', 'tp'), may hold values 0 or 1
- arriving_tiles: bfloat16 [4, 512, 3072], P('section', 'tp'), may hold values from -6 to 6
- arriving_region: int32 [4, 512], P('section', 'tp'), may hold values 0 or 1
- prompt_embeddings: bfloat16 [2048, 3584], P(('section', 'tp')), may hold values from -6 to 6
- prompt_tally: int32 [1], replicated, may hold values from 512 to 2048
- adaptive_norm_weights: bfloat16 [4, 9216, 3584], P('section', 'tp'), may hold values from -0.09375 to 0.09375
- expansion_weights: bfloat16 [4, 12288, 3072], P('section', 'tp'), may hold values from -0.109375 to 0.109375
- contraction_weights: bfloat16 [4, 12288, 3072], P('section', 'tp'), may hold values from -0.0546875 to 0.0546875
Outputs:
- finished: bfloat16 [4, 512, 3072], P('section', 'tp')
- state: bfloat16 [4, 512, 3072], P('section', 'tp')
All inputs are finite; a program needn't handle non-finite values. No bound on the sum of `travelling_region` or of `arriving_region` on one device may be relied on, other than what follows from the above.
Results may differ from a plain program's by a relative error of at most 0.01.
Values may be sent and summed in bfloat16 or wider, within the bound.
No kernel may reach another device: no remote copies, remote signals or barrier semaphores. Data moves between devices by JAX's collectives and lax.ppermute only.
A program may use at most 64 MiB of HBM per device.

v0:
```python
import functools

import jax
import jax.numpy as jnp
import numpy as np
from jax import lax
from jax.experimental import pallas as pl
from jax.experimental.pallas import tpu as pltpu
from jax.sharding import Mesh, PartitionSpec as P

f32 = jnp.float32
bf16 = jnp.bfloat16

SIZES = {"zh": 2, "core": 2, "xh": 2, "xl": 2, "yh": 2, "yl": 2, "zc": 2, "zf": 2}
SECTION = ("zh", "core")
TP = ("xh", "xl", "yh", "yl", "zc", "zf")
PLANE = ("xh", "xl", "yh", "yl")
LINE = ("zc", "zf")
GROUP = ("xh",) + LINE
GROUP_SIZE = 8
SECTIONS = 4
LANES = 128
STEP = 256
SPAN = 768
IN_FLIGHT = 10


def from_neighbour(block, axis, distance):
    route = [((i + distance) % 4, i) for i in range(4)]
    return lax.ppermute(block, (axis + "h", axis + "l"), route)


def between_sections(block, edges):
    route = [
        (2 * start + half, 2 * end + (half ^ flip)) for start, end, flip in edges for half in (0, 1)
    ]
    return lax.ppermute(block, SECTION + ("zc",), route)


def after(value, *earlier):
    return lax.optimization_barrier((value,) + earlier)[0]


def exchange(block, axes):
    count = int(np.prod([SIZES[a] for a in axes]))
    copies = jnp.broadcast_to(block[None], (count,) + block.shape)
    return lax.all_to_all(copies, axes, 0, 0)


def ffn_kernel(lifts, drops, x_ref, mod_ref, *refs):
    held = len({i for i, _, _ in lifts + drops})
    weights = refs[:held]
    out_ref, up, down, inputs, hidden, acc, sem = refs[held:]
    copies = []
    for place, parts in ((up, lifts), (down, drops)):
        at = 0
        for i, first, rows in parts:
            copies.append(
                pltpu.make_async_copy(
                    weights[i].at[pl.ds(first, rows)],
                    place.at[pl.ds(at, rows)],
                    sem.at[len(copies)],
                )
            )
            at += rows
    total = at
    for copy in copies[:IN_FLIGHT]:
        copy.start()
    values = x_ref[...].astype(f32)
    center = jnp.mean(values, axis=1, keepdims=True)
    moved = values - center
    spread = jnp.mean(moved * moved, axis=1, keepdims=True)
    inputs[...] = (
        moved * lax.rsqrt(spread + 1e-06) * (1.0 + mod_ref[1:2]) + mod_ref[0:1]
    ).astype(bf16)
    ready = 0

    def wait_for(rows, skip, parts):
        nonlocal ready
        while sum(part[2] for part in parts[: ready - skip]) < rows:
            copies[ready].wait()
            if ready + IN_FLIGHT < len(copies):
                copies[ready + IN_FLIGHT].start()
            ready += 1

    for span in range(0, total, SPAN):
        wait_for(span + SPAN, 0, lifts)
        for at in range(span, span + SPAN, STEP):
            raised = lax.dot_general(
                inputs[...],
                up[at : at + STEP],
                (((1,), (1,)), ((), ())),
                preferred_element_type=f32,
            )
            hidden[:, at : at + STEP] = jax.nn.gelu(raised, approximate=True).astype(bf16)
    for at in range(0, total, SPAN):
        wait_for(at + SPAN, len(lifts), drops)
        for column in range(0, out_ref.shape[1], STEP):
            columns = slice(column, column + STEP)
            term = jnp.dot(
                hidden[:, at : at + SPAN], down[at : at + SPAN, columns], preferred_element_type=f32
            )
            if at:
                term = acc[:, columns] + term
            if at + SPAN < total:
                acc[:, columns] = term
            else:
                out_ref[:, columns] = term.astype(bf16)


def ffn(tokens, mod, weights, lifts, drops):
    rows, breadth = tokens.shape
    total = sum(part[2] for part in lifts)
    whole = pl.BlockSpec(memory_space=pltpu.VMEM)
    return pl.pallas_call(
        functools.partial(ffn_kernel, lifts, drops),
        out_shape=jax.ShapeDtypeStruct((rows, breadth), bf16),
        in_specs=[whole, whole] + [pl.BlockSpec(memory_space=pltpu.HBM)] * len(weights),
        out_specs=whole,
        scratch_shapes=[
            pltpu.VMEM((total, breadth), bf16),
            pltpu.VMEM((total, breadth), bf16),
            pltpu.VMEM((rows, breadth), bf16),
            pltpu.VMEM((rows, total), bf16),
            pltpu.VMEM((rows, breadth), f32),
            pltpu.SemaphoreType.DMA((len(lifts) + len(drops),)),
        ],
        compiler_params=pltpu.CompilerParams(vmem_limit_bytes=40 * 1024 * 1024),
        cost_estimate=pl.CostEstimate(
            flops=4 * rows * total * breadth,
            bytes_accessed=4 * total * breadth + 4 * rows * breadth,
            transcendentals=rows * total,
        ),
    )(tokens, mod, *weights)


def close_kernel(parts_ref, waiting_ref, gate_ref, out_ref):
    breadth = parts_ref.shape[2]
    result = parts_ref[0].astype(f32)
    for i in range(1, parts_ref.shape[0]):
        result += parts_ref[i].astype(f32)
    mask = waiting_ref[:, breadth:]
    kept = mask[:, :1].astype(f32)
    values = waiting_ref[:, :breadth].astype(f32)
    out_ref[:, :breadth] = (values + kept * gate_ref[...] * result).astype(bf16)
    out_ref[:, breadth:] = mask


def close(parts, waiting, gate):
    whole = pl.BlockSpec(memory_space=pltpu.VMEM)
    return pl.pallas_call(
        close_kernel,
        out_shape=jax.ShapeDtypeStruct(waiting.shape, waiting.dtype),
        in_specs=[whole] * 3,
        out_specs=whole,
        cost_estimate=pl.CostEstimate(
            flops=parts.size, bytes_accessed=2 * parts.size, transcendentals=0
        ),
    )(parts, waiting, gate)


def set_out(up, down, prompt_embeddings, prompt_tally, adaptive_norm_weights, waiting, arriving):
    together = lax.optimization_barrier
    middle = up.shape[0] // 2
    first = jnp.concatenate([up[:middle], down[:middle]], axis=0)
    second = jnp.concatenate([up[middle:], down[middle:]], axis=0)
    count_rows, encoded = prompt_embeddings.shape
    first_row = lax.axis_index(SECTION + TP) * count_rows
    keep = (first_row + lax.iota(jnp.int32, count_rows) < prompt_tally[0]).astype(bf16)
    partial = jnp.dot(keep[None, :], prompt_embeddings, preferred_element_type=f32)
    partial = partial.reshape(encoded // LANES, LANES)

    first, second, partial = together((first, second, partial))
    yp_first = from_neighbour(first, "y", 1)
    ym_second = from_neighbour(second, "y", -1)
    xa = from_neighbour(first, "x", 1)
    xb = from_neighbour(second, "x", -1)
    partial = jnp.sum(exchange(partial, SECTION + LINE), axis=0)
    entering = exchange(after(arriving, partial), SECTION)

    first, second, yp_first, ym_second, xa, xb, partial, entering = together(
        (first, second, yp_first, ym_second, xa, xb, partial, entering)
    )
    pooled = jnp.sum(exchange(partial, PLANE), axis=0)

    first, second, yp_first, ym_second, pooled = together(
        (first, second, yp_first, ym_second, pooled)
    )
    yp_second = from_neighbour(second, "y", 1)
    ym_first = from_neighbour(first, "y", -1)
    xa_yp = from_neighbour(yp_first, "x", 1)
    xb_ym = from_neighbour(ym_second, "x", -1)
    pooled = pooled / prompt_tally[0].astype(f32)
    normed = pooled * lax.rsqrt(jnp.mean(pooled * pooled) + 1e-06)
    cond = jax.nn.silu(normed).astype(bf16).reshape(encoded)
    local = jnp.dot(adaptive_norm_weights, cond, preferred_element_type=f32)
    columns = local.shape[0]
    rows = -(-columns // LANES)
    local = jnp.pad(local, (0, rows * LANES - columns)).reshape(rows, LANES)
    line = exchange(local, LINE)
    mine = exchange(after(waiting, line), LINE)
    halves = [block[part] for block in (yp_first, ym_second) for part in (slice(middle), slice(middle, None))]

    line, mine, halves, yp_second, ym_first, xa_yp, xb_ym = together(
        (line, mine, halves, yp_second, ym_first, xa_yp, xb_ym)
    )
    theirs = lax.ppermute(mine, "xh", [(0, 1), (1, 0)])
    modes = exchange(line, PLANE)
    modes, theirs, halves, yp_second, ym_first = together(
        (modes, theirs, halves, yp_second, ym_first)
    )
    y2 = [from_neighbour(half, "y", 1 if i < 2 else -1) for i, half in enumerate(halves)]
    xa_ym = from_neighbour(ym_first, "x", 1)
    xb_yp = from_neighbour(yp_second, "x", -1)
    modes = modes.reshape(-1, rows * LANES)[:, :columns].reshape(3, -1)
    upper = lax.axis_index("xh") == 1
    gathered = jnp.stack([jnp.where(upper, theirs, mine), jnp.where(upper, mine, theirs)])
    xa_yp_down = xa_yp[middle:]
    xb_ym_down = xb_ym[middle:]

    y2, xa_ym, xb_yp, modes, gathered, xa_yp_down, xb_ym_down = together(
        (y2, xa_ym, xb_yp, modes, gathered, xa_yp_down, xb_ym_down)
    )
    xa_y2_up = from_neighbour(y2[0], "x", 1)
    xb_y2_up = from_neighbour(y2[2], "x", -1)
    xa_y2_down = from_neighbour(xa_yp_down, "y", 1)
    xb_y2_down = from_neighbour(xb_ym_down, "y", -1)

    whole = [
        first, second, xa, xb, yp_first, ym_second, yp_second, ym_first, xa_yp, xb_ym, xa_ym, xb_yp
    ]
    count = len(whole)
    lifts = [(i, 0, middle) for i in range(count)]
    drops = [(i, middle, middle) for i in range(count)]
    lifts += [(count + i, 0, middle) for i in (0, 2, 4, 5)]
    drops += [(count + i, 0, middle) for i in (1, 3, 6, 7)]
    weights = whole + y2 + [xa_y2_up, xb_y2_up, xa_y2_down, xb_y2_down]
    layer = functools.partial(ffn, weights=weights, lifts=lifts, drops=drops)
    return modes, gathered, entering, layer


def per_device(
    travelling_inputs,
    travelling_region,
    arriving_tiles,
    arriving_region,
    prompt_embeddings,
    prompt_tally,
    adaptive_norm_weights,
    expansion_weights,
    contraction_weights,
):
    section_id = lax.axis_index(SECTION)
    is_first = section_id == 0
    tokens, breadth = travelling_inputs.shape[1:]

    def with_mask(values, region):
        column = jnp.broadcast_to(region.astype(bf16)[:, None], (tokens, LANES))
        return jnp.concatenate([values, column], axis=1)

    arriving = with_mask(arriving_tiles[0], arriving_region[0])
    waiting = with_mask(travelling_inputs[0], travelling_region[0])
    last = SECTIONS - 1
    mod, gathered, entering, layer = set_out(
        expansion_weights[0],
        contraction_weights[0],
        prompt_embeddings,
        prompt_tally,
        adaptive_norm_weights[0],
        travelling_inputs[0],
        arriving,
    )
    gathered, waiting, gate = lax.optimization_barrier((gathered, waiting, mod[2:]))
    finished = []
    for tick in range(SECTIONS):
        if tick:
            gathered = exchange(waiting[:, :breadth], GROUP)
        partial = layer(gathered.reshape(GROUP_SIZE * tokens, breadth), mod)
        parts = lax.all_to_all(partial.reshape(GROUP_SIZE, tokens, breadth), GROUP, 0, 0)
        produced = close(parts, waiting, gate)
        if tick < last:
            moved = between_sections(produced, [(0, 1, 0), (1, 2, 1), (2, 3, 0)])
            flip = int(tick >= 2)
            finished.append(between_sections(produced, [(last, tick, flip)]))
        else:
            moved = between_sections(produced, [(0, 1, 0), (1, 2, 0), (2, 3, 1)])
            finished.append(between_sections(produced, [(last, last, 1)]))
        waiting = jnp.where(is_first, entering[tick], moved)
    done = finished[last]
    for tick in range(last):
        done = jnp.where(section_id == tick, finished[tick], done)
    return done[None, :, :breadth], waiting[None, :, :breadth]


def solution(mesh):
    fine = Mesh(mesh.devices.reshape(tuple(SIZES.values())), tuple(SIZES))
    placed = (
        P(SECTION, TP, None),
        P(SECTION, TP),
        P(SECTION, TP, None),
        P(SECTION, TP),
        P(SECTION + TP, None),
        P(),
        P(SECTION, TP, None),
        P(SECTION, TP, None),
        P(SECTION, TP, None),
    )
    return jax.shard_map(
        per_device,
        mesh=fine,
        in_specs=placed,
        out_specs=(P(SECTION, TP, None), P(SECTION, TP, None)),
        check_vma=False,
    )
```

profile of v0, /device:TPU:1, one launch (start us, length us, event | category | flops | bytes accessed | tf_op | source)
XLA Modules:
  0.0 350.4 jit_solution(543865651535851024)
XLA Ops:
  4.3 3.6 %collective-permute-start = (bf16[192,3072]{1,0:T(8,128)(2,1)S(1)}, bf16[192,3072]{1,0:T(8,128)(2,1)}, u32[]{:S(2)}, u32[]{:S(2)}) collective-permute-start(bf16[192,3072]{1,0:T(8,128)(2,1)S(1)} %get-tuple-element.66.refs_0_), channel_id=1, source_target_pairs={{4,0},{8,4},{12,8},{0,12},{5,1},{9,5},{13,9},{1,13},{6,2},{10,6},{... | collective-permute-start | bytes 3538952 | tf_op jit(solution)/shard_map/ppermute | solution.py:30
  7.9 2.5 collective-permute-start.2
  11.1 9.7 %all-to-all-start = ((f32[16,28,128]{2,1,0:T(8,128)}), f32[16,28,128]{2,1,0:T(8,128)}, u32[]{:S(2)}, u32[]{:S(2)}) async-start(f32[16,28,128]{2,1,0:T(8,128)} %broadcast_in_dim.28), calls=%async_computation | async-start | bytes 524288 | tf_op jit(solution)/shard_map/all_to_all | solution.py:47
  20.9 9.6 %all-to-all-done = f32[16,28,128]{2,1,0:T(8,128)} async-done(((f32[16,28,128]{2,1,0:T(8,128)}), f32[16,28,128]{2,1,0:T(8,128)}, u32[]{:S(2)}, u32[]{:S(2)}) %all-to-all-start) | async-done | bytes 229408 | tf_op jit(solution)/shard_map/all_to_all | solution.py:47
  31.5 13.4 %all_to_all.65 = bf16[4,8,3200]{2,1,0:T(8,128)(2,1)} all-to-all(bf16[4,8,3200]{2,1,0:T(8,128)(2,1)S(1)} %broadcast_in_dim.30), channel_id=1, replica_groups=mesh['zh'=2,'core'=2,'xh'=2,'xl'=2,'yh'=2,'yl'=2,'zc'=2,'zf'=2] {'zh','c..., dimensions={0} | all-to-all | bytes 409600 | tf_op jit(solution)/shard_map/all_to_all | solution.py:47
  45.7 7.1 %all-to-all-start.2 = ((f32[16,28,128]{2,1,0:T(8,128)}), f32[16,28,128]{2,1,0:T(8,128)}, u32[]{:S(2)}, u32[]{:S(2)}) async-start(f32[16,28,128]{2,1,0:T(8,128)} %broadcast_in_dim.31), calls=%async_computation.2 | async-start | bytes 524288 | tf_op jit(solution)/shard_map/all_to_all | solution.py:47
  52.7 7.4 %all-to-all-done.2 = f32[16,28,128]{2,1,0:T(8,128)} async-done(((f32[16,28,128]{2,1,0:T(8,128)}), f32[16,28,128]{2,1,0:T(8,128)}, u32[]{:S(2)}, u32[]{:S(2)}) %all-to-all-start.2) | async-done | bytes 229408 | tf_op jit(solution)/shard_map/all_to_all | solution.py:47
  66.5 5.9 %all-to-all-start.3 = ((f32[4,2,128]{2,1,0:T(2,128)}), f32[4,2,128]{2,1,0:T(2,128)S(1)}, u32[]{:S(2)}, u32[]{:S(2)}) async-start(f32[4,2,128]{2,1,0:T(2,128)} %broadcast_in_dim.33), calls=%async_computation.3 | async-start | bytes 8192 | tf_op jit(solution)/shard_map/all_to_all | solution.py:47
  72.3 2.4 fusion.13
  74.7 2.2 all-to-all-done.3
  77.6 4.0 %all-to-all-start.4 = ((bf16[4,8,3072]{2,1,0:T(8,128)(2,1)}), bf16[4,8,3072]{2,1,0:T(8,128)(2,1)}, u32[]{:S(2)}, u32[]{:S(2)}) async-start(bf16[4,8,3072]{2,1,0:T(8,128)(2,1)} %broadcast_in_dim.34), calls=%async_computation.4 | async-start | bytes 393216 | tf_op jit(solution)/shard_map/all_to_all | solution.py:47
  81.5 2.4 fusion.14
  84.0 3.0 all-to-all-done.4
  88.2 11.4 %all_to_all.66 = f32[16,4,2,128]{3,2,1,0:T(2,128)} all-to-all(f32[16,4,2,128]{3,2,1,0:T(2,128)S(1)} %broadcast_in_dim.35), channel_id=1, replica_groups=mesh['zh'=2,'core'=2,'xh'=2,'xl'=2,'yh'=2,'yl'=2,'zc'=2,'zf'=2] {'xh','x..., dimensions={0} | all-to-all | bytes 131072 | tf_op jit(solution)/shard_map/all_to_all | solution.py:47
  102.0 1.9 slice.90
  104.0 2.0 slice.91
  106.7 2.5 collective-permute-done.10.refs_13_
  109.2 2.0 collective-permute-start.9
  111.2 1.8 select_bitcast_fusion.1
  114.2 2.0 collective-permute-done.11.refs_14_
  116.2 7.8 %collective-permute-done.12.refs_15_ = bf16[96,3072]{1,0:T(8,128)(2,1)} collective-permute-done((bf16[96,3072]{1,0:T(8,128)(2,1)}, bf16[96,3072]{1,0:T(8,128)(2,1)}, u32[]{:S(2)}, u32[]{:S(2)}) %collective-permute-start.12) | collective-permute-done | bytes 589856 | tf_op jit(solution)/shard_map/ppermute | solution.py:30
  126.2 3.3 collective-permute-start.17
  131.4 4.1 %collective-permute-done.15.refs_16_ = bf16[96,3072]{1,0:T(8,128)(2,1)S(1)} collective-permute-done((bf16[96,3072]{1,0:T(8,128)(2,1)}, bf16[96,3072]{1,0:T(8,128)(2,1)S(1)}, u32[]{:S(2)}, u32[]{:S(2)}) %collective-permute-start.15) | collective-permute-done | bytes 589856 | tf_op jit(solution)/shard_map/ppermute | solution.py:30
  137.2 5.1 %collective-permute-done.17.refs_18_ = bf16[96,3072]{1,0:T(8,128)(2,1)S(1)} collective-permute-done((bf16[96,3072]{1,0:T(8,128)(2,1)}, bf16[96,3072]{1,0:T(8,128)(2,1)S(1)}, u32[]{:S(2)}, u32[]{:S(2)}) %collective-permute-start.17) | collective-permute-done | bytes 589856 | tf_op jit(solution)/shard_map/ppermute | solution.py:30
  142.2 9.2 %shard_map.104 = bf16[64,3072]{1,0:T(8,128)(2,1)S(1)} custom-call(bf16[64,3072]{1,0:T(8,128)(2,1)S(1)} %bitcast.67, f32[3,3072]{1,0:T(4,128)S(1)} %reshape.70.mod_ref, bf16[192,3072]{1,0:T(8,128)(2,1)S(1)} %get-tuple-element.66.refs_0_, bf16[192,3072]{1,0:T(8,128)(2,1)S(1)} %get-tuple-element.65.refs_1_, bf16[192,3072]{1,0:T(8,128)(2,1)} %collective-permute-done.2.refs_2_, ...), custom_call_target="tpu_custom_call" | custom-call | flops 1207959552 | bytes 19660800 | tf_op jit(solution)/shard_map/pallas_call | solution.py:115
  151.5 18.2 %all_to_all.67.parts_ref = bf16[8,8,3072]{2,1,0:T(8,128)(2,1)} all-to-all(bf16[8,8,3072]{2,1,0:T(8,128)(2,1)S(1)} %bitcast.70), channel_id=1, replica_groups=mesh['zh'=2,'core'=2,'xh'=2,'xl'=2,'yh'=2,'yl'=2,'zc'=2,'zf'=2] {'xh','z..., dimensions={0} | all-to-all | bytes 786432 | tf_op jit(solution)/shard_map/all_to_all | solution.py:279
  169.7 1.7 shard_map.105
  171.5 9.9 %collective-permute-start.19 = (bf16[8,3200]{1,0:T(8,128)(2,1)}, bf16[8,3200]{1,0:T(8,128)(2,1)S(1)}, u32[]{:S(2)}, u32[]{:S(2)}) collective-permute-start(bf16[8,3200]{1,0:T(8,128)(2,1)} %shard_map.105), channel_id=1, source_target_pairs={{0,64},{2,66},{64,130},{66,128},{128,192},{130,194},{1,65},{3,67},... | collective-permute-start | bytes 153608 | tf_op jit(solution)/shard_map/ppermute | solution.py:37
  181.4 5.1 %collective-permute-done.19 = bf16[8,3200]{1,0:T(8,128)(2,1)S(1)} collective-permute-done((bf16[8,3200]{1,0:T(8,128)(2,1)}, bf16[8,3200]{1,0:T(8,128)(2,1)S(1)}, u32[]{:S(2)}, u32[]{:S(2)}) %collective-permute-start.19) | collective-permute-done | bytes 51232 | tf_op jit(solution)/shard_map/ppermute | solution.py:37
  187.3 16.2 %all_to_all.68 = bf16[8,8,3072]{2,1,0:T(8,128)(2,1)S(1)} all-to-all(bf16[8,8,3072]{2,1,0:T(8,128)(2,1)S(1)} %broadcast_in_dim.37), channel_id=1, replica_groups=mesh['zh'=2,'core'=2,'xh'=2,'xl'=2,'yh'=2,'yl'=2,'zc'=2,'zf'=2] {'xh','z..., dimensions={0} | all-to-all | bytes 786432 | tf_op jit(solution)/shard_map/all_to_all | solution.py:47
  205.7 9.2 %shard_map.106 = bf16[64,3072]{1,0:T(8,128)(2,1)S(1)} custom-call(bf16[64,3072]{1,0:T(8,128)(2,1)S(1)} %bitcast.71, f32[3,3072]{1,0:T(4,128)S(1)} %reshape.70.mod_ref, bf16[192,3072]{1,0:T(8,128)(2,1)S(1)} %get-tuple-element.66.refs_0_, bf16[192,3072]{1,0:T(8,128)(2,1)S(1)} %get-tuple-element.65.refs_1_, bf16[192,3072]{1,0:T(8,128)(2,1)} %collective-permute-done.2.refs_2_, ...), custom_call_target="tpu_custom_call" | custom-call | flops 1207959552 | bytes 19660800 | tf_op jit(solution)/shard_map/pallas_call | solution.py:115
  214.8 14.6 %all_to_all.69.parts_ref = bf16[8,8,3072]{2,1,0:T(8,128)(2,1)} all-to-all(bf16[8,8,3072]{2,1,0:T(8,128)(2,1)S(1)} %bitcast.72), channel_id=1, replica_groups=mesh['zh'=2,'core'=2,'xh'=2,'xl'=2,'yh'=2,'yl'=2,'zc'=2,'zf'=2] {'xh','z..., dimensions={0} | all-to-all | bytes 786432 | tf_op jit(solution)/shard_map/all_to_all | solution.py:279
  229.5 1.7 shard_map.107
  231.2 2.0 collective-permute-start.20
  233.3 3.8 %collective-permute-done.20 = bf16[8,3200]{1,0:T(8,128)(2,1)S(1)} collective-permute-done((bf16[8,3200]{1,0:T(8,128)(2,1)}, bf16[8,3200]{1,0:T(8,128)(2,1)S(1)}, u32[]{:S(2)}, u32[]{:S(2)}) %collective-permute-start.20) | collective-permute-done | bytes 51232 | tf_op jit(solution)/shard_map/ppermute | solution.py:37
  237.9 16.2 %all_to_all.70 = bf16[8,8,3072]{2,1,0:T(8,128)(2,1)S(1)} all-to-all(bf16[8,8,3072]{2,1,0:T(8,128)(2,1)S(1)} %broadcast_in_dim.38), channel_id=1, replica_groups=mesh['zh'=2,'core'=2,'xh'=2,'xl'=2,'yh'=2,'yl'=2,'zc'=2,'zf'=2] {'xh','z..., dimensions={0} | all-to-all | bytes 786432 | tf_op jit(solution)/shard_map/all_to_all | solution.py:47
  256.2 9.2 %shard_map.108 = bf16[64,3072]{1,0:T(8,128)(2,1)S(1)} custom-call(bf16[64,3072]{1,0:T(8,128)(2,1)S(1)} %bitcast.73, f32[3,3072]{1,0:T(4,128)S(1)} %reshape.70.mod_ref, bf16[192,3072]{1,0:T(8,128)(2,1)S(1)} %get-tuple-element.66.refs_0_, bf16[192,3072]{1,0:T(8,128)(2,1)S(1)} %get-tuple-element.65.refs_1_, bf16[192,3072]{1,0:T(8,128)(2,1)} %collective-permute-done.2.refs_2_, ...), custom_call_target="tpu_custom_call" | custom-call | flops 1207959552 | bytes 19660800 | tf_op jit(solution)/shard_map/pallas_call | solution.py:115
  265.4 14.6 %all_to_all.71.parts_ref = bf16[8,8,3072]{2,1,0:T(8,128)(2,1)} all-to-all(bf16[8,8,3072]{2,1,0:T(8,128)(2,1)S(1)} %bitcast.74), channel_id=1, replica_groups=mesh['zh'=2,'core'=2,'xh'=2,'xl'=2,'yh'=2,'yl'=2,'zc'=2,'zf'=2] {'xh','z..., dimensions={0} | all-to-all | bytes 786432 | tf_op jit(solution)/shard_map/all_to_all | solution.py:279
  280.0 1.7 shard_map.109
  281.8 2.0 collective-permute-start.24
  283.8 3.8 %collective-permute-done.24 = bf16[8,3200]{1,0:T(8,128)(2,1)S(1)} collective-permute-done((bf16[8,3200]{1,0:T(8,128)(2,1)}, bf16[8,3200]{1,0:T(8,128)(2,1)S(1)}, u32[]{:S(2)}, u32[]{:S(2)}) %collective-permute-start.24) | collective-permute-done | bytes 51232 | tf_op jit(solution)/shard_map/ppermute | solution.py:37
  288.4 16.2 %all_to_all.72 = bf16[8,8,3072]{2,1,0:T(8,128)(2,1)S(1)} all-to-all(bf16[8,8,3072]{2,1,0:T(8,128)(2,1)S(1)} %broadcast_in_dim.39), channel_id=1, replica_groups=mesh['zh'=2,'core'=2,'xh'=2,'xl'=2,'yh'=2,'yl'=2,'zc'=2,'zf'=2] {'xh','z..., dimensions={0} | all-to-all | bytes 786432 | tf_op jit(solution)/shard_map/all_to_all | solution.py:47
  306.8 9.2 %shard_map.110 = bf16[64,3072]{1,0:T(8,128)(2,1)S(1)} custom-call(bf16[64,3072]{1,0:T(8,128)(2,1)S(1)} %bitcast.69, f32[3,3072]{1,0:T(4,128)S(1)} %reshape.70.mod_ref, bf16[192,3072]{1,0:T(8,128)(2,1)S(1)} %get-tuple-element.66.refs_0_, bf16[192,3072]{1,0:T(8,128)(2,1)S(1)} %get-tuple-element.65.refs_1_, bf16[192,3072]{1,0:T(8,128)(2,1)} %collective-permute-done.2.refs_2_, ...), custom_call_target="tpu_custom_call" | custom-call | flops 1207959552 | bytes 19660800 | tf_op jit(solution)/shard_map/pallas_call | solution.py:115
  316.7 3.6 %all-to-all-start.12 = ((bf16[8,8,3072]{2,1,0:T(8,128)(2,1)}), bf16[8,8,3072]{2,1,0:T(8,128)(2,1)S(1)}, u32[]{:S(2)}, u32[]{:S(2)}) async-start(bf16[8,8,3072]{2,1,0:T(8,128)(2,1)} %bitcast.68), calls=%async_computation.12 | async-start | bytes 786432 | tf_op jit(solution)/shard_map/all_to_all | solution.py:279
  320.3 11.3 %all-to-all-done.12.parts_ref = bf16[8,8,3072]{2,1,0:T(8,128)(2,1)S(1)} async-done(((bf16[8,8,3072]{2,1,0:T(8,128)(2,1)}), bf16[8,8,3072]{2,1,0:T(8,128)(2,1)S(1)}, u32[]{:S(2)}, u32[]{:S(2)}) %all-to-all-start.12) | async-done | bytes 393248 | tf_op jit(solution)/shard_map/all_to_all | solution.py:279
  332.4 1.7 shard_map.111
  334.1 3.6 %collective-permute-start.26 = (bf16[8,3200]{1,0:T(8,128)(2,1)}, bf16[8,3200]{1,0:T(8,128)(2,1)S(1)}, u32[]{:S(2)}, u32[]{:S(2)}) collective-permute-start(bf16[8,3200]{1,0:T(8,128)(2,1)} %shard_map.111), channel_id=1, source_target_pairs={{0,64},{2,66},{64,128},{66,130},{128,194},{130,192},{1,65},{3,67},... | collective-permute-start | bytes 153608 | tf_op jit(solution)/shard_map/ppermute | solution.py:37
  342.5 7.3 %collective-permute-done.22 = bf16[8,3200]{1,0:T(8,128)(2,1)S(1)} collective-permute-done((bf16[8,3200]{1,0:T(8,128)(2,1)S(1)}, bf16[8,3200]{1,0:T(8,128)(2,1)S(1)}, u32[]{:S(2)}, u32[]{:S(2)}) %collective-permute-start.22) | collective-permute-done | bytes 51232 | tf_op jit(solution)/shard_map/ppermute | solution.py:37
  (137 shorter events, 39.0 us)
Async XLA Ops:
  0.6 64.8 %copy-start = (bf16[1,144,3584]{2,1,0:T(8,128)(2,1)S(1)}, bf16[1,144,3584]{2,1,0:T(8,128)(2,1)}, u32[]{:S(2)}) copy-start(bf16[1,144,3584]{2,1,0:T(8,128)(2,1)} %param.15) | copy-start | bytes 3096580
  4.1 16.8 %copy-start.29 = (s32[1,8]{1,0:T(1,128)S(1)}, s32[1,8]{1,0:T(1,128)}, u32[]{:S(2)}) copy-start(s32[1,8]{1,0:T(1,128)} %param.12) | copy-start | bytes 100
  4.1 16.9 %copy-start.28 = (bf16[1,8,3072]{2,1,0:T(8,128)(2,1)S(1)}, bf16[1,8,3072]{2,1,0:T(8,128)(2,1)}, u32[]{:S(2)}) copy-start(bf16[1,8,3072]{2,1,0:T(8,128)(2,1)} %param.11) | copy-start | bytes 147460
  4.3 40.7 %collective-permute-start = (bf16[192,3072]{1,0:T(8,128)(2,1)S(1)}, bf16[192,3072]{1,0:T(8,128)(2,1)}, u32[]{:S(2)}, u32[]{:S(2)}) collective-permute-start(bf16[192,3072]{1,0:T(8,128)(2,1)S(1)} %get-tuple-element.66.refs_0_), channel_id=1, source_target_pairs={{4,0},{8,4},{12,8},{0,12},{5,1},{9,5},{13,9},{1,13},{6,2},{10,6},{... | collective-permute-start | bytes 3538952 | tf_op jit(solution)/shard_map/ppermute | solution.py:30
  7.9 37.0 %collective-permute-start.1 = (bf16[192,3072]{1,0:T(8,128)(2,1)S(1)}, bf16[192,3072]{1,0:T(8,128)(2,1)}, u32[]{:S(2)}, u32[]{:S(2)}) collective-permute-start(bf16[192,3072]{1,0:T(8,128)(2,1)S(1)} %get-tuple-element.65.refs_1_), channel_id=1, source_target_pairs={{12,0},{0,4},{4,8},{8,12},{13,1},{1,5},{5,9},{9,13},{14,2},{2,6},{... | collective-permute-start | bytes 3538952 | tf_op jit(solution)/shard_map/ppermute | solution.py:30
  7.9 37.0 %collective-permute-start.2 = (bf16[192,3072]{1,0:T(8,128)(2,1)S(1)}, bf16[192,3072]{1,0:T(8,128)(2,1)}, u32[]{:S(2)}, u32[]{:S(2)}) collective-permute-start(bf16[192,3072]{1,0:T(8,128)(2,1)S(1)} %get-tuple-element.66.refs_0_), channel_id=1, source_target_pairs={{16,0},{32,16},{48,32},{0,48},{17,1},{33,17},{49,33},{1,49},{18,2}... | collective-permute-start | bytes 3538952 | tf_op jit(solution)/shard_map/ppermute | solution.py:30
  10.4 34.5 %collective-permute-start.3 = (bf16[192,3072]{1,0:T(8,128)(2,1)S(1)}, bf16[192,3072]{1,0:T(8,128)(2,1)}, u32[]{:S(2)}, u32[]{:S(2)}) collective-permute-start(bf16[192,3072]{1,0:T(8,128)(2,1)S(1)} %get-tuple-element.65.refs_1_), channel_id=1, source_target_pairs={{48,0},{0,16},{16,32},{32,48},{49,1},{1,17},{17,33},{33,49},{50,2}... | collective-permute-start | bytes 3538952 | tf_op jit(solution)/shard_map/ppermute | solution.py:30
  11.1 19.4 %all-to-all-start = ((f32[16,28,128]{2,1,0:T(8,128)}), f32[16,28,128]{2,1,0:T(8,128)}, u32[]{:S(2)}, u32[]{:S(2)}) async-start(f32[16,28,128]{2,1,0:T(8,128)} %broadcast_in_dim.28), calls=%async_computation | async-start | bytes 524288 | tf_op jit(solution)/shard_map/all_to_all | solution.py:47
  45.7 14.4 %all-to-all-start.2 = ((f32[16,28,128]{2,1,0:T(8,128)}), f32[16,28,128]{2,1,0:T(8,128)}, u32[]{:S(2)}, u32[]{:S(2)}) async-start(f32[16,28,128]{2,1,0:T(8,128)} %broadcast_in_dim.31), calls=%async_computation.2 | async-start | bytes 524288 | tf_op jit(solution)/shard_map/all_to_all | solution.py:47
  61.1 25.9 %collective-permute-start.4 = (bf16[192,3072]{1,0:T(8,128)(2,1)S(1)}, bf16[192,3072]{1,0:T(8,128)(2,1)}, u32[]{:S(2)}, u32[]{:S(2)}) collective-permute-start(bf16[192,3072]{1,0:T(8,128)(2,1)S(1)} %get-tuple-element.65.refs_1_), channel_id=1, source_target_pairs={{4,0},{8,4},{12,8},{0,12},{5,1},{9,5},{13,9},{1,13},{6,2},{10,6},{... | collective-permute-start | bytes 3538952 | tf_op jit(solution)/shard_map/ppermute | solution.py:30
  61.9 25.1 %collective-permute-start.5 = (bf16[192,3072]{1,0:T(8,128)(2,1)S(1)}, bf16[192,3072]{1,0:T(8,128)(2,1)}, u32[]{:S(2)}, u32[]{:S(2)}) collective-permute-start(bf16[192,3072]{1,0:T(8,128)(2,1)S(1)} %get-tuple-element.66.refs_0_), channel_id=1, source_target_pairs={{12,0},{0,4},{4,8},{8,12},{13,1},{1,5},{5,9},{9,13},{14,2},{2,6},{... | collective-permute-start | bytes 3538952 | tf_op jit(solution)/shard_map/ppermute | solution.py:30
  62.6 24.4 %collective-permute-start.6 = (bf16[192,3072]{1,0:T(8,128)(2,1)}, bf16[192,3072]{1,0:T(8,128)(2,1)}, u32[]{:S(2)}, u32[]{:S(2)}) collective-permute-start(bf16[192,3072]{1,0:T(8,128)(2,1)} %collective-permute-done.refs_4_), channel_id=1, source_target_pairs={{16,0},{32,16},{48,32},{0,48},{17,1},{33,17},{49,33},{1,49},{18,2}... | collective-permute-start | bytes 3538952 | tf_op jit(solution)/shard_map/ppermute | solution.py:30
  63.4 23.8 %collective-permute-start.7 = (bf16[192,3072]{1,0:T(8,128)(2,1)}, bf16[192,3072]{1,0:T(8,128)(2,1)}, u32[]{:S(2)}, u32[]{:S(2)}) collective-permute-start(bf16[192,3072]{1,0:T(8,128)(2,1)} %collective-permute-done.1.refs_5_), channel_id=1, source_target_pairs={{48,0},{0,16},{16,32},{32,48},{49,1},{1,17},{17,33},{33,49},{50,2}... | collective-permute-start | bytes 3538952 | tf_op jit(solution)/shard_map/ppermute | solution.py:30
  66.5 10.4 %all-to-all-start.3 = ((f32[4,2,128]{2,1,0:T(2,128)}), f32[4,2,128]{2,1,0:T(2,128)S(1)}, u32[]{:S(2)}, u32[]{:S(2)}) async-start(f32[4,2,128]{2,1,0:T(2,128)} %broadcast_in_dim.33), calls=%async_computation.3 | async-start | bytes 8192 | tf_op jit(solution)/shard_map/all_to_all | solution.py:47
  77.6 9.5 %all-to-all-start.4 = ((bf16[4,8,3072]{2,1,0:T(8,128)(2,1)}), bf16[4,8,3072]{2,1,0:T(8,128)(2,1)}, u32[]{:S(2)}, u32[]{:S(2)}) async-start(bf16[4,8,3072]{2,1,0:T(8,128)(2,1)} %broadcast_in_dim.34), calls=%async_computation.4 | async-start | bytes 393216 | tf_op jit(solution)/shard_map/all_to_all | solution.py:47
  87.3 12.3 %collective-permute-start.8 = (bf16[4,8,3072]{2,1,0:T(8,128)(2,1)}, bf16[4,8,3072]{2,1,0:T(8,128)(2,1)}, u32[]{:S(2)}, u32[]{:S(2)}) collective-permute-start(bf16[4,8,3072]{2,1,0:T(8,128)(2,1)} %all-to-all-done.4), channel_id=1, source_target_pairs={{0,32},{32,0},{1,33},{33,1},{2,34},{34,2},{3,35},{35,3},{4,36},{36... | collective-permute-start | bytes 589832 | tf_op jit(solution)/shard_map/ppermute | solution.py:207
  99.6 9.6 %collective-permute-start.10 = (bf16[96,3072]{1,0:T(8,128)(2,1)}, bf16[96,3072]{1,0:T(8,128)(2,1)}, u32[]{:S(2)}, u32[]{:S(2)}) collective-permute-start(bf16[96,3072]{1,0:T(8,128)(2,1)} %get-tuple-element.76), channel_id=1, source_target_pairs={{4,0},{8,4},{12,8},{0,12},{5,1},{9,5},{13,9},{1,13},{6,2},{10,6},{... | collective-permute-start | bytes 1769480 | tf_op jit(solution)/shard_map/ppermute | solution.py:30
  100.6 24.0 %collective-permute-start.13 = (bf16[192,3072]{1,0:T(8,128)(2,1)}, bf16[192,3072]{1,0:T(8,128)(2,1)}, u32[]{:S(2)}, u32[]{:S(2)}) collective-permute-start(bf16[192,3072]{1,0:T(8,128)(2,1)} %collective-permute-done.5.refs_7_), channel_id=1, source_target_pairs={{16,0},{32,16},{48,32},{0,48},{17,1},{33,17},{49,33},{1,49},{18,2}... | collective-permute-start | bytes 3538952 | tf_op jit(solution)/shard_map/ppermute | solution.py:30
  101.4 23.2 %collective-permute-start.14 = (bf16[192,3072]{1,0:T(8,128)(2,1)}, bf16[192,3072]{1,0:T(8,128)(2,1)}, u32[]{:S(2)}, u32[]{:S(2)}) collective-permute-start(bf16[192,3072]{1,0:T(8,128)(2,1)} %collective-permute-done.4.refs_6_), channel_id=1, source_target_pairs={{48,0},{0,16},{16,32},{32,48},{49,1},{1,17},{17,33},{33,49},{50,2}... | collective-permute-start | bytes 3538952 | tf_op jit(solution)/shard_map/ppermute | solution.py:30
  105.9 10.3 %collective-permute-start.11 = (bf16[96,3072]{1,0:T(8,128)(2,1)}, bf16[96,3072]{1,0:T(8,128)(2,1)}, u32[]{:S(2)}, u32[]{:S(2)}) collective-permute-start(bf16[96,3072]{1,0:T(8,128)(2,1)} %get-tuple-element.77), channel_id=1, source_target_pairs={{12,0},{0,4},{4,8},{8,12},{13,1},{1,5},{5,9},{9,13},{14,2},{2,6},{... | collective-permute-start | bytes 1769480 | tf_op jit(solution)/shard_map/ppermute | solution.py:30
  106.4 17.6 %collective-permute-start.12 = (bf16[96,3072]{1,0:T(8,128)(2,1)}, bf16[96,3072]{1,0:T(8,128)(2,1)}, u32[]{:S(2)}, u32[]{:S(2)}) collective-permute-start(bf16[96,3072]{1,0:T(8,128)(2,1)} %get-tuple-element.78), channel_id=1, source_target_pairs={{12,0},{0,4},{4,8},{8,12},{13,1},{1,5},{5,9},{9,13},{14,2},{2,6},{... | collective-permute-start | bytes 1769480 | tf_op jit(solution)/shard_map/ppermute | solution.py:30
  109.2 15.4 %collective-permute-start.9 = (bf16[96,3072]{1,0:T(8,128)(2,1)}, bf16[96,3072]{1,0:T(8,128)(2,1)}, u32[]{:S(2)}, u32[]{:S(2)}) collective-permute-start(bf16[96,3072]{1,0:T(8,128)(2,1)} %get-tuple-element.75), channel_id=1, source_target_pairs={{4,0},{8,4},{12,8},{0,12},{5,1},{9,5},{13,9},{1,13},{6,2},{10,6},{... | collective-permute-start | bytes 1769480 | tf_op jit(solution)/shard_map/ppermute | solution.py:30
  124.6 10.9 %collective-permute-start.15 = (bf16[96,3072]{1,0:T(8,128)(2,1)}, bf16[96,3072]{1,0:T(8,128)(2,1)S(1)}, u32[]{:S(2)}, u32[]{:S(2)}) collective-permute-start(bf16[96,3072]{1,0:T(8,128)(2,1)} %collective-permute-done.9.refs_12_), channel_id=1, source_target_pairs={{16,0},{32,16},{48,32},{0,48},{17,1},{33,17},{49,33},{1,49},{18,2}... | collective-permute-start | bytes 1769480 | tf_op jit(solution)/shard_map/ppermute | solution.py:30
  126.2 11.0 %collective-permute-start.16 = (bf16[96,3072]{1,0:T(8,128)(2,1)}, bf16[96,3072]{1,0:T(8,128)(2,1)S(1)}, u32[]{:S(2)}, u32[]{:S(2)}) collective-permute-start(bf16[96,3072]{1,0:T(8,128)(2,1)} %collective-permute-done.11.refs_14_), channel_id=1, source_target_pairs={{48,0},{0,16},{16,32},{32,48},{49,1},{1,17},{17,33},{33,49},{50,2}... | collective-permute-start | bytes 1769480 | tf_op jit(solution)/shard_map/ppermute | solution.py:30
  126.2 16.0 %collective-permute-start.17 = (bf16[96,3072]{1,0:T(8,128)(2,1)}, bf16[96,3072]{1,0:T(8,128)(2,1)S(1)}, u32[]{:S(2)}, u32[]{:S(2)}) collective-permute-start(bf16[96,3072]{1,0:T(8,128)(2,1)} %slice.90), channel_id=1, source_target_pairs={{4,0},{8,4},{12,8},{0,12},{5,1},{9,5},{13,9},{1,13},{6,2},{10,6},{... | collective-permute-start | bytes 1769480 | tf_op jit(solution)/shard_map/ppermute | solution.py:30
  129.5 12.8 %collective-permute-start.18 = (bf16[96,3072]{1,0:T(8,128)(2,1)}, bf16[96,3072]{1,0:T(8,128)(2,1)S(1)}, u32[]{:S(2)}, u32[]{:S(2)}) collective-permute-start(bf16[96,3072]{1,0:T(8,128)(2,1)} %slice.91), channel_id=1, source_target_pairs={{12,0},{0,4},{4,8},{8,12},{13,1},{1,5},{5,9},{9,13},{14,2},{2,6},{... | collective-permute-start | bytes 1769480 | tf_op jit(solution)/shard_map/ppermute | solution.py:30
  135.6 15.9 %copy-start.1 = (bf16[96,3072]{1,0:T(8,128)(2,1)}, bf16[96,3072]{1,0:T(8,128)(2,1)S(1)}, u32[]{:S(2)}) copy-start(bf16[96,3072]{1,0:T(8,128)(2,1)S(1)} %collective-permute-done.15.refs_16_) | copy-start | bytes 1769476
  171.5 15.0 %collective-permute-start.19 = (bf16[8,3200]{1,0:T(8,128)(2,1)}, bf16[8,3200]{1,0:T(8,128)(2,1)S(1)}, u32[]{:S(2)}, u32[]{:S(2)}) collective-permute-start(bf16[8,3200]{1,0:T(8,128)(2,1)} %shard_map.105), channel_id=1, source_target_pairs={{0,64},{2,66},{64,130},{66,128},{128,192},{130,194},{1,65},{3,67},... | collective-permute-start | bytes 153608 | tf_op jit(solution)/shard_map/ppermute | solution.py:37
  181.4 22.1 %copy-start.2 = (bf16[96,3072]{1,0:T(8,128)(2,1)S(1)}, bf16[96,3072]{1,0:T(8,128)(2,1)}, u32[]{:S(2)}) copy-start(bf16[96,3072]{1,0:T(8,128)(2,1)} %copy-done.1) | copy-start | bytes 1769476
  181.4 22.1 %copy-start.6 = (bf16[96,3072]{1,0:T(8,128)(2,1)S(1)}, bf16[96,3072]{1,0:T(8,128)(2,1)}, u32[]{:S(2)}) copy-start(bf16[96,3072]{1,0:T(8,128)(2,1)} %copy-done.5) | copy-start | bytes 1769476
  187.3 27.5 %copy-start.21 = (bf16[8,3200]{1,0:T(8,128)(2,1)}, bf16[8,3200]{1,0:T(8,128)(2,1)S(1)}, u32[]{:S(2)}) copy-start(bf16[8,3200]{1,0:T(8,128)(2,1)S(1)} %bitcast_select_fusion.1.waiting_ref) | copy-start | bytes 153604
  231.2 22.9 %copy-start.3 = (bf16[96,3072]{1,0:T(8,128)(2,1)S(1)}, bf16[96,3072]{1,0:T(8,128)(2,1)}, u32[]{:S(2)}) copy-start(bf16[96,3072]{1,0:T(8,128)(2,1)} %copy-done.1) | copy-start | bytes 1769476
  231.2 22.9 %copy-start.7 = (bf16[96,3072]{1,0:T(8,128)(2,1)S(1)}, bf16[96,3072]{1,0:T(8,128)(2,1)}, u32[]{:S(2)}) copy-start(bf16[96,3072]{1,0:T(8,128)(2,1)} %copy-done.5) | copy-start | bytes 1769476
  231.2 5.8 %collective-permute-start.20 = (bf16[8,3200]{1,0:T(8,128)(2,1)}, bf16[8,3200]{1,0:T(8,128)(2,1)S(1)}, u32[]{:S(2)}, u32[]{:S(2)}) collective-permute-start(bf16[8,3200]{1,0:T(8,128)(2,1)} %shard_map.107), channel_id=1, source_target_pairs={{0,64},{2,66},{64,130},{66,128},{128,192},{130,194},{1,65},{3,67},... | collective-permute-start | bytes 153608 | tf_op jit(solution)/shard_map/ppermute | solution.py:37
  237.8 27.5 %copy-start.22 = (bf16[8,3200]{1,0:T(8,128)(2,1)}, bf16[8,3200]{1,0:T(8,128)(2,1)S(1)}, u32[]{:S(2)}) copy-start(bf16[8,3200]{1,0:T(8,128)(2,1)S(1)} %bitcast_select_fusion.2.waiting_ref) | copy-start | bytes 153604
  281.8 22.9 %copy-start.4 = (bf16[96,3072]{1,0:T(8,128)(2,1)S(1)}, bf16[96,3072]{1,0:T(8,128)(2,1)}, u32[]{:S(2)}) copy-start(bf16[96,3072]{1,0:T(8,128)(2,1)} %copy-done.1) | copy-start | bytes 1769476
  281.8 22.9 %copy-start.8 = (bf16[96,3072]{1,0:T(8,128)(2,1)S(1)}, bf16[96,3072]{1,0:T(8,128)(2,1)}, u32[]{:S(2)}) copy-start(bf16[96,3072]{1,0:T(8,128)(2,1)} %copy-done.5) | copy-start | bytes 1769476
  281.8 5.8 %collective-permute-start.24 = (bf16[8,3200]{1,0:T(8,128)(2,1)}, bf16[8,3200]{1,0:T(8,128)(2,1)S(1)}, u32[]{:S(2)}, u32[]{:S(2)}) collective-permute-start(bf16[8,3200]{1,0:T(8,128)(2,1)} %shard_map.109), channel_id=1, source_target_pairs={{0,64},{2,66},{64,130},{66,128},{128,192},{130,194},{1,65},{3,67},... | collective-permute-start | bytes 153608 | tf_op jit(solution)/shard_map/ppermute | solution.py:37
  288.4 27.5 %copy-start.20 = (bf16[8,3200]{1,0:T(8,128)(2,1)}, bf16[8,3200]{1,0:T(8,128)(2,1)S(1)}, u32[]{:S(2)}) copy-start(bf16[8,3200]{1,0:T(8,128)(2,1)S(1)} %bitcast_select_fusion.waiting_ref) | copy-start | bytes 153604
  316.7 21.8 %copy-start.25 = (bf16[8,3200]{1,0:T(8,128)(2,1)S(1)}, bf16[8,3200]{1,0:T(8,128)(2,1)}, u32[]{:S(2)}) copy-start(bf16[8,3200]{1,0:T(8,128)(2,1)} %shard_map.105) | copy-start | bytes 153604
  316.7 22.5 %copy-start.26 = (bf16[8,3200]{1,0:T(8,128)(2,1)S(1)}, bf16[8,3200]{1,0:T(8,128)(2,1)}, u32[]{:S(2)}) copy-start(bf16[8,3200]{1,0:T(8,128)(2,1)} %shard_map.107) | copy-start | bytes 153604
  316.7 23.8 %copy-start.27 = (bf16[8,3200]{1,0:T(8,128)(2,1)S(1)}, bf16[8,3200]{1,0:T(8,128)(2,1)}, u32[]{:S(2)}) copy-start(bf16[8,3200]{1,0:T(8,128)(2,1)} %shard_map.109) | copy-start | bytes 153604
  316.7 14.9 %all-to-all-start.12 = ((bf16[8,8,3072]{2,1,0:T(8,128)(2,1)}), bf16[8,8,3072]{2,1,0:T(8,128)(2,1)S(1)}, u32[]{:S(2)}, u32[]{:S(2)}) async-start(bf16[8,8,3072]{2,1,0:T(8,128)(2,1)} %bitcast.68), calls=%async_computation.12 | async-start | bytes 786432 | tf_op jit(solution)/shard_map/all_to_all | solution.py:279
  334.1 7.7 %collective-permute-start.26 = (bf16[8,3200]{1,0:T(8,128)(2,1)}, bf16[8,3200]{1,0:T(8,128)(2,1)S(1)}, u32[]{:S(2)}, u32[]{:S(2)}) collective-permute-start(bf16[8,3200]{1,0:T(8,128)(2,1)} %shard_map.111), channel_id=1, source_target_pairs={{0,64},{2,66},{64,128},{66,130},{128,194},{130,192},{1,65},{3,67},... | collective-permute-start | bytes 153608 | tf_op jit(solution)/shard_map/ppermute | solution.py:37
  338.5 4.0 %collective-permute-start.23 = (bf16[8,3200]{1,0:T(8,128)(2,1)S(1)}, bf16[8,3200]{1,0:T(8,128)(2,1)S(1)}, u32[]{:S(2)}, u32[]{:S(2)}) collective-permute-start(bf16[8,3200]{1,0:T(8,128)(2,1)S(1)} %copy-done.25), channel_id=1, source_target_pairs={{192,0},{194,2},{193,1},{195,3},{196,4},{198,6},{197,5},{199,7},{2... | collective-permute-start | bytes 153608 | tf_op jit(solution)/shard_map/ppermute | solution.py:37
  339.2 10.6 %collective-permute-start.22 = (bf16[8,3200]{1,0:T(8,128)(2,1)S(1)}, bf16[8,3200]{1,0:T(8,128)(2,1)S(1)}, u32[]{:S(2)}, u32[]{:S(2)}) collective-permute-start(bf16[8,3200]{1,0:T(8,128)(2,1)S(1)} %copy-done.26), channel_id=1, source_target_pairs={{192,64},{194,66},{193,65},{195,67},{196,68},{198,70},{197,69},{19... | collective-permute-start | bytes 153608 | tf_op jit(solution)/shard_map/ppermute | solution.py:37
  340.5 9.3 %collective-permute-start.21 = (bf16[8,3200]{1,0:T(8,128)(2,1)S(1)}, bf16[8,3200]{1,0:T(8,128)(2,1)S(1)}, u32[]{:S(2)}, u32[]{:S(2)}) collective-permute-start(bf16[8,3200]{1,0:T(8,128)(2,1)S(1)} %copy-done.27), channel_id=1, source_target_pairs={{192,130},{194,128},{193,131},{195,129},{196,134},{198,132},{197,1... | collective-permute-start | bytes 153608 | tf_op jit(solution)/shard_map/ppermute | solution.py:37
  341.1 8.7 %collective-permute-start.25 = (bf16[8,3200]{1,0:T(8,128)(2,1)}, bf16[8,3200]{1,0:T(8,128)(2,1)S(1)}, u32[]{:S(2)}, u32[]{:S(2)}) collective-permute-start(bf16[8,3200]{1,0:T(8,128)(2,1)} %shard_map.111), channel_id=1, source_target_pairs={{192,194},{194,192},{193,195},{195,193},{196,198},{198,196},{197,1... | collective-permute-start | bytes 153608 | tf_op jit(solution)/shard_map/ppermute | solution.py:37
  (14 other events, 56.0 us)
where the time goes:
time: 352 us; the launch traced here: 350 us
  blocking collectives  121 us (34%)
  waiting for transfers between devices  77.4 us (22%)
  starting transfers between devices  71.1 us (20%)
  Pallas kernels  43.6 us (12%)
  local copies, waits for them, and re-layouts  23 us (7%)
  other arithmetic  10.6 us (3%)
    all_to_all x5, blocking collectives, exchange(): return lax.all_to_all(copies, axes, 0, 0)  73.3 us
    all_to_all x3, blocking collectives, per_device(): lax.all_to_all(partial.reshape(GROUP_SIZE, tokens, breadth), GROUP, 0, 0)  47.5 us
    pallas_call x4, Pallas kernels, ffn(): pl.pallas_call(functools.partial(ffn_kernel, lifts, drops), out_shape=jax...  36.7 us
    all_to_all x4, starting transfers between devices, exchange(): return lax.all_to_all(copies, axes, 0, 0)  26.6 us
    ppermute x18, waiting for transfers between devices, from_neighbour(): return lax.ppermute(block, (axis + 'h', axis + 'l'), route)  24 us
    all_to_all x4, waiting for transfers between devices, exchange(): return lax.all_to_all(copies, axes, 0, 0)  22.2 us
    ppermute x8, starting transfers between devices, between_sections(): return lax.ppermute(block, SECTION + ('zc',), route)  20.8 us
    ppermute x8, waiting for transfers between devices, between_sections(): return lax.ppermute(block, SECTION + ('zc',), route)  20 us
  transfers between devices with their start and end apart: 32, of which 17 were waited for; matrix products, arithmetic and copies ran while one was open for 5% of the time, Pallas kernels for 0%

commit v1 on v0

--- a/solution.py
+++ b/solution.py
@@ -21,7 +21,6 @@
 SECTIONS = 4
 LANES = 128
 STEP = 256
-SPAN = 768
 IN_FLIGHT = 10
 
 
@@ -47,10 +46,38 @@
     return lax.all_to_all(copies, axes, 0, 0)
 
 
-def ffn_kernel(lifts, drops, x_ref, mod_ref, *refs):
+def modulate(x_ref, mod_ref, inputs):
+    values = x_ref[...].astype(f32)
+    center = jnp.mean(values, axis=1, keepdims=True)
+    moved = values - center
+    spread = jnp.mean(moved * moved, axis=1, keepdims=True)
+    inputs[...] = (
+        moved * lax.rsqrt(spread + 1e-06) * (1.0 + mod_ref[1:2]) + mod_ref[0:1]
+    ).astype(bf16)
+
+
+def raise_rows(inputs, up, hidden, start, stop):
+    for at in range(start, stop, STEP):
+        raised = lax.dot_general(
+            inputs[...],
+            up[at : at + STEP],
+            (((1,), (1,)), ((), ())),
+            preferred_element_type=f32,
+        )
+        hidden[:, at : at + STEP] = jax.nn.gelu(raised, approximate=True).astype(bf16)
+
+
+def lower_rows(hidden, down, out_ref):
+    for at in range(0, out_ref.shape[1], STEP):
+        out_ref[:, at : at + STEP] = jnp.dot(
+            hidden[...], down[:, at : at + STEP], preferred_element_type=f32
+        ).astype(bf16)
+
+
+def first_kernel(lifts, drops, x_ref, mod_ref, *refs):
     held = len({i for i, _, _ in lifts + drops})
     weights = refs[:held]
-    out_ref, up, down, inputs, hidden, acc, sem = refs[held:]
+    out_ref, up, down, inputs, hidden, sem = refs[held:]
     copies = []
     for place, parts in ((up, lifts), (down, drops)):
         at = 0
@@ -66,72 +93,63 @@
     total = at
     for copy in copies[:IN_FLIGHT]:
         copy.start()
-    values = x_ref[...].astype(f32)
-    center = jnp.mean(values, axis=1, keepdims=True)
-    moved = values - center
-    spread = jnp.mean(moved * moved, axis=1, keepdims=True)
-    inputs[...] = (
-        moved * lax.rsqrt(spread + 1e-06) * (1.0 + mod_ref[1:2]) + mod_ref[0:1]
-    ).astype(bf16)
+    modulate(x_ref, mod_ref, inputs)
     ready = 0
-
-    def wait_for(rows, skip, parts):
-        nonlocal ready
-        while sum(part[2] for part in parts[: ready - skip]) < rows:
+    half = len(lifts) // 2
+    for stop in (half, len(lifts), len(copies)):
+        while ready < stop:
             copies[ready].wait()
             if ready + IN_FLIGHT < len(copies):
                 copies[ready + IN_FLIGHT].start()
             ready += 1
-
-    for span in range(0, total, SPAN):
-        wait_for(span + SPAN, 0, lifts)
-        for at in range(span, span + SPAN, STEP):
-            raised = lax.dot_general(
-                inputs[...],
-                up[at : at + STEP],
-                (((1,), (1,)), ((), ())),
-                preferred_element_type=f32,
-            )
-            hidden[:, at : at + STEP] = jax.nn.gelu(raised, approximate=True).astype(bf16)
-    for at in range(0, total, SPAN):
-        wait_for(at + SPAN, len(lifts), drops)
-        for column in range(0, out_ref.shape[1], STEP):
-            columns = slice(column, column + STEP)
-            term = jnp.dot(
-                hidden[:, at : at + SPAN], down[at : at + SPAN, columns], preferred_element_type=f32
-            )
-            if at:
-                term = acc[:, columns] + term
-            if at + SPAN < total:
-                acc[:, columns] = term
-            else:
-                out_ref[:, columns] = term.astype(bf16)
-
-
-def ffn(tokens, mod, weights, lifts, drops):
+        if stop == half:
+            raise_rows(inputs, up, hidden, 0, total // 2)
+        elif stop == len(lifts):
+            raise_rows(inputs, up, hidden, total // 2, total)
+    lower_rows(hidden, down, out_ref)
+
+
+def later_kernel(x_ref, mod_ref, up, down, out_ref, inputs, hidden):
+    modulate(x_ref, mod_ref, inputs)
+    raise_rows(inputs, up, hidden, 0, up.shape[0])
+    lower_rows(hidden, down, out_ref)
+
+
+def layer_call(kernel, tokens, mod, weights, pieces, total, semaphores):
     rows, breadth = tokens.shape
-    total = sum(part[2] for part in lifts)
     whole = pl.BlockSpec(memory_space=pltpu.VMEM)
+    outs = [jax.ShapeDtypeStruct((rows, breadth), bf16)]
+    if pieces:
+        outs += [jax.ShapeDtypeStruct((total, breadth), bf16)] * 2
+    space = pl.BlockSpec(memory_space=pltpu.HBM) if pieces else whole
     return pl.pallas_call(
-        functools.partial(ffn_kernel, lifts, drops),
-        out_shape=jax.ShapeDtypeStruct((rows, breadth), bf16),
-        in_specs=[whole, whole] + [pl.BlockSpec(memory_space=pltpu.HBM)] * len(weights),
-        out_specs=whole,
+        kernel,
+        out_shape=outs,
+        in_specs=[whole, whole] + [space] * len(weights),
+        out_specs=[whole] * len(outs),
         scratch_shapes=[
-            pltpu.VMEM((total, breadth), bf16),
-            pltpu.VMEM((total, breadth), bf16),
             pltpu.VMEM((rows, breadth), bf16),
             pltpu.VMEM((rows, total), bf16),
-            pltpu.VMEM((rows, breadth), f32),
-            pltpu.SemaphoreType.DMA((len(lifts) + len(drops),)),
-        ],
-        compiler_params=pltpu.CompilerParams(vmem_limit_bytes=40 * 1024 * 1024),
+        ]
+        + semaphores,
+        compiler_params=pltpu.CompilerParams(vmem_limit_bytes=24 * 1024 * 1024),
         cost_estimate=pl.CostEstimate(
             flops=4 * rows * total * breadth,
             bytes_accessed=4 * total * breadth + 4 * rows * breadth,
             transcendentals=rows * total,
         ),
     )(tokens, mod, *weights)
+
+
+def first_layer(tokens, mod, weights, lifts, drops):
+    total = sum(part[2] for part in lifts)
+    kernel = functools.partial(first_kernel, lifts, drops)
+    semaphores = [pltpu.SemaphoreType.DMA((len(lifts) + len(drops),))]
+    return layer_call(kernel, tokens, mod, weights, True, total, semaphores)
+
+
+def later_layer(tokens, mod, up, down):
+    return layer_call(later_kernel, tokens, mod, (up, down), False, up.shape[0], [])[0]
 
 
 def close_kernel(parts_ref, waiting_ref, gate_ref, out_ref):
@@ -206,9 +224,6 @@
     )
     theirs = lax.ppermute(mine, "xh", [(0, 1), (1, 0)])
     modes = exchange(line, PLANE)
-    modes, theirs, halves, yp_second, ym_first = together(
-        (modes, theirs, halves, yp_second, ym_first)
-    )
     y2 = [from_neighbour(half, "y", 1 if i < 2 else -1) for i, half in enumerate(halves)]
     xa_ym = from_neighbour(ym_first, "x", 1)
     xb_yp = from_neighbour(yp_second, "x", -1)
@@ -218,8 +233,8 @@
     xa_yp_down = xa_yp[middle:]
     xb_ym_down = xb_ym[middle:]
 
-    y2, xa_ym, xb_yp, modes, gathered, xa_yp_down, xb_ym_down = together(
-        (y2, xa_ym, xb_yp, modes, gathered, xa_yp_down, xb_ym_down)
+    y2, xa_ym, xb_yp, xa_yp_down, xb_ym_down = together(
+        (y2, xa_ym, xb_yp, xa_yp_down, xb_ym_down)
     )
     xa_y2_up = from_neighbour(y2[0], "x", 1)
     xb_y2_up = from_neighbour(y2[2], "x", -1)
@@ -235,7 +250,7 @@
     lifts += [(count + i, 0, middle) for i in (0, 2, 4, 5)]
     drops += [(count + i, 0, middle) for i in (1, 3, 6, 7)]
     weights = whole + y2 + [xa_y2_up, xb_y2_up, xa_y2_down, xb_y2_down]
-    layer = functools.partial(ffn, weights=weights, lifts=lifts, drops=drops)
+    layer = functools.partial(first_layer, weights=weights, lifts=lifts, drops=drops)
     return modes, gathered, entering, layer
 
 
@@ -275,7 +290,12 @@
     for tick in range(SECTIONS):
         if tick:
             gathered = exchange(waiting[:, :breadth], GROUP)
-        partial = layer(gathered.reshape(GROUP_SIZE * tokens, breadth), mod)
+            gathered, finished[-1] = lax.optimization_barrier((gathered, finished[-1]))
+        gathered = gathered.reshape(GROUP_SIZE * tokens, breadth)
+        if tick:
+            partial = later_layer(gathered, mod, up, down)
+        else:
+            partial, up, down = layer(gathered, mod)
         parts = lax.all_to_all(partial.reshape(GROUP_SIZE, tokens, breadth), GROUP, 0, 0)
         produced = close(parts, waiting, gate)
         if tick < last:

time: 352 us -> 347 us (0.986)
  blocking collectives: 121 us -> 62 us
  waiting for transfers between devices: 77.4 us -> 102 us
  starting transfers between devices: 71.1 us -> 92.6 us
  local copies, waits for them, and re-layouts: 23 us -> 43.2 us
  Pallas kernels: 43.6 us -> 33.7 us
    all_to_all x5 -> x1, blocking collectives: 73.3 us -> 13.4 us  [exchange(): return lax.all_to_all(copies, axes, 0, 0)]
    all_to_all x4 -> x8, waiting for transfers between devices: 22.2 us -> 59.1 us  [exchange(): return lax.all_to_all(copies, axes, 0, 0)]
    unnamed x61 -> x49, local copies, waits for them, and re-layouts: 8.19 us -> 29 us
    all_to_all x4 -> x8, starting transfers between devices: 26.6 us -> 41.4 us  [exchange(): return lax.all_to_all(copies, axes, 0, 0)]
    pallas_call x4, Pallas kernels: 36.7 us -> 26.8 us  [layer_call(): pl.pallas_call(kernel, out_shape=outs, in_specs=[whole, whole] + [space]...]
    ppermute x18, waiting for transfers between devices: 24 us -> 14.2 us  [from_neighbour(): return lax.ppermute(block, (axis + 'h', axis + 'l'), route)]
    ppermute x8, starting transfers between devices: 20.8 us -> 25.1 us  [between_sections(): return lax.ppermute(block, SECTION + ('zc',), route)]
  transfers between devices with their start and end apart: 32 -> 36, of which waited for: 17 -> 18; matrix products, arithmetic and copies ran while one was open for 5% -> 4% of each run, Pallas kernels for 0% -> 0%
where the time goes in v1:
time: 347 us; the launch traced here: 345 us
  waiting for transfers between devices  102 us (29%)
  starting transfers between devices  92.6 us (27%)
  blocking collectives  62 us (18%)
  local copies, waits for them, and re-layouts  43.2 us (12%)
  Pallas kernels  33.7 us (10%)
  other arithmetic  7.17 us (2%)
    all_to_all x8, waiting for transfers between devices, exchange(): return lax.all_to_all(copies, axes, 0, 0)  59.1 us
    all_to_all x3, blocking collectives, per_device(): lax.all_to_all(partial.reshape(GROUP_SIZE, tokens, breadth), GROUP, 0, 0)  48.6 us
    all_to_all x8, starting transfers between devices, exchange(): return lax.all_to_all(copies, axes, 0, 0)  41.4 us
    unnamed x49, local copies, waits for them, and re-layouts  29 us
    pallas_call x4, Pallas kernels, layer_call(): pl.pallas_call(kernel, out_shape=outs, in_specs=[whole, whole] + [space]...  26.8 us
    ppermute x8, starting transfers between devices, between_sections(): return lax.ppermute(block, SECTION + ('zc',), route)  25.1 us
    ppermute x18, starting transfers between devices, from_neighbour(): return lax.ppermute(block, (axis + 'h', axis + 'l'), route)  19.7 us
    ppermute x8, waiting for transfers between devices, between_sections(): return lax.ppermute(block, SECTION + ('zc',), route)  17.7 us
  transfers between devices with their start and end apart: 36, of which 18 were waited for; matrix products, arithmetic and copies ran while one was open for 4% of the time, Pallas kernels for 0%

profile of v1, /device:TPU:1, one launch (start us, length us, event | category | flops | bytes accessed | tf_op | source)
XLA Modules:
  0.0 344.8 jit_solution(8574552379631566128)
XLA Ops:
  5.7 3.6 %collective-permute-start = (bf16[192,3072]{1,0:T(8,128)(2,1)}, bf16[192,3072]{1,0:T(8,128)(2,1)S(1)}, u32[]{:S(2)}, u32[]{:S(2)}) collective-permute-start(bf16[192,3072]{1,0:T(8,128)(2,1)} %get-tuple-element.65.refs_0_), channel_id=1, source_target_pairs={{4,0},{8,4},{12,8},{0,12},{5,1},{9,5},{13,9},{1,13},{6,2},{10,6},{... | collective-permute-start | bytes 3538952 | tf_op jit(solution)/shard_map/ppermute | solution.py:29
  9.2 2.5 collective-permute-start.2
  12.5 9.7 %all-to-all-start = ((f32[16,28,128]{2,1,0:T(8,128)}), f32[16,28,128]{2,1,0:T(8,128)}, u32[]{:S(2)}, u32[]{:S(2)}) async-start(f32[16,28,128]{2,1,0:T(8,128)} %broadcast_in_dim.28), calls=%async_computation | async-start | bytes 524288 | tf_op jit(solution)/shard_map/all_to_all | solution.py:46
  22.3 9.6 %all-to-all-done = f32[16,28,128]{2,1,0:T(8,128)} async-done(((f32[16,28,128]{2,1,0:T(8,128)}), f32[16,28,128]{2,1,0:T(8,128)}, u32[]{:S(2)}, u32[]{:S(2)}) %all-to-all-start) | async-done | bytes 229408 | tf_op jit(solution)/shard_map/all_to_all | solution.py:46
  32.9 13.4 %all_to_all.65 = bf16[4,8,3200]{2,1,0:T(8,128)(2,1)} all-to-all(bf16[4,8,3200]{2,1,0:T(8,128)(2,1)S(1)} %broadcast_in_dim.30), channel_id=1, replica_groups=mesh['zh'=2,'core'=2,'xh'=2,'xl'=2,'yh'=2,'yl'=2,'zc'=2,'zf'=2] {'zh','c..., dimensions={0} | all-to-all | bytes 409600 | tf_op jit(solution)/shard_map/all_to_all | solution.py:46
  47.0 7.1 %all-to-all-start.2 = ((f32[16,28,128]{2,1,0:T(8,128)}), f32[16,28,128]{2,1,0:T(8,128)}, u32[]{:S(2)}, u32[]{:S(2)}) async-start(f32[16,28,128]{2,1,0:T(8,128)} %broadcast_in_dim.31), calls=%async_computation.2 | async-start | bytes 524288 | tf_op jit(solution)/shard_map/all_to_all | solution.py:46
  54.1 7.4 %all-to-all-done.2 = f32[16,28,128]{2,1,0:T(8,128)} async-done(((f32[16,28,128]{2,1,0:T(8,128)}), f32[16,28,128]{2,1,0:T(8,128)}, u32[]{:S(2)}, u32[]{:S(2)}) %all-to-all-start.2) | async-done | bytes 229408 | tf_op jit(solution)/shard_map/all_to_all | solution.py:46
  67.8 5.9 %all-to-all-start.3 = ((f32[4,2,128]{2,1,0:T(2,128)}), f32[4,2,128]{2,1,0:T(2,128)S(1)}, u32[]{:S(2)}, u32[]{:S(2)}) async-start(f32[4,2,128]{2,1,0:T(2,128)} %broadcast_in_dim.33), calls=%async_computation.3 | async-start | bytes 8192 | tf_op jit(solution)/shard_map/all_to_all | solution.py:46
  74.8 3.4 all-to-all-done.3
  78.9 4.0 %all-to-all-start.4 = ((bf16[4,8,3072]{2,1,0:T(8,128)(2,1)}), bf16[4,8,3072]{2,1,0:T(8,128)(2,1)}, u32[]{:S(2)}, u32[]{:S(2)}) async-start(bf16[4,8,3072]{2,1,0:T(8,128)(2,1)} %broadcast_in_dim.34), calls=%async_computation.4 | async-start | bytes 393216 | tf_op jit(solution)/shard_map/all_to_all | solution.py:46
  84.0 4.3 %all-to-all-done.4 = bf16[4,8,3072]{2,1,0:T(8,128)(2,1)} async-done(((bf16[4,8,3072]{2,1,0:T(8,128)(2,1)}), bf16[4,8,3072]{2,1,0:T(8,128)(2,1)}, u32[]{:S(2)}, u32[]{:S(2)}) %all-to-all-start.4) | async-done | bytes 196640 | tf_op jit(solution)/shard_map/all_to_all | solution.py:46
  92.5 5.0 %collective-permute-done.10.refs_13_ = bf16[96,3072]{1,0:T(8,128)(2,1)S(1)} collective-permute-done((bf16[96,3072]{1,0:T(8,128)(2,1)}, bf16[96,3072]{1,0:T(8,128)(2,1)S(1)}, u32[]{:S(2)}, u32[]{:S(2)}) %collective-permute-start.10) | collective-permute-done | bytes 589856 | tf_op jit(solution)/shard_map/ppermute | solution.py:29
  98.4 3.0 collective-permute-start.9
  102.0 4.4 %all-to-all-start.5 = ((f32[16,4,2,128]{3,2,1,0:T(2,128)}), f32[16,4,2,128]{3,2,1,0:T(2,128)S(1)}, u32[]{:S(2)}, u32[]{:S(2)}) async-start(f32[16,4,2,128]{3,2,1,0:T(2,128)} %broadcast_in_dim.36), calls=%async_computation.5 | async-start | bytes 131072 | tf_op jit(solution)/shard_map/all_to_all | solution.py:46
  106.4 3.0 collective-permute-start.8
  113.9 3.3 all-to-all-done.5
  124.1 5.6 %collective-permute-done.15.refs_16_ = bf16[96,3072]{1,0:T(8,128)(2,1)S(1)} collective-permute-done((bf16[96,3072]{1,0:T(8,128)(2,1)}, bf16[96,3072]{1,0:T(8,128)(2,1)S(1)}, u32[]{:S(2)}, u32[]{:S(2)}) %collective-permute-start.15) | collective-permute-done | bytes 589856 | tf_op jit(solution)/shard_map/ppermute | solution.py:29
  129.7 3.0 collective-permute-done.16.refs_17_
  133.2 11.6 %shard_map.104 = (bf16[64,3072]{1,0:T(8,128)(2,1)S(1)}, bf16[1536,3072]{1,0:T(8,128)(2,1)S(1)}, bf16[1536,3072]{1,0:T(8,128)(2,1)}) custom-call(bf16[64,3072]{1,0:T(8,128)(2,1)S(1)} %bitcast.67, f32[3,3072]{1,0:T(4,128)S(1)} %reshape.70.mod_ref, bf16[192,3072]{1,0:T(8,128)(2,1)} %get-tuple-element.65.refs_0_, bf16[192,3072]{1,0:T(8,128)(2,1)} %get-tuple-element.64.refs_1_, ...), custom_call_target="tpu_custom_call" | custom-call | flops 1207959552 | bytes 19660800 | tf_op jit(solution)/shard_map/pallas_call | solution.py:125
  144.7 3.6 %copy-done.1 = bf16[1536,3072]{1,0:T(8,128)(2,1)} copy-done((bf16[1536,3072]{1,0:T(8,128)(2,1)}, bf16[1536,3072]{1,0:T(8,128)(2,1)S(1)}, u32[]{:S(2)}) %copy-start.1) | copy-done | bytes 9437208
  148.3 19.4 %all_to_all.66.parts_ref = bf16[8,8,3072]{2,1,0:T(8,128)(2,1)} all-to-all(bf16[8,8,3072]{2,1,0:T(8,128)(2,1)S(1)} %bitcast.73), channel_id=1, replica_groups=mesh['zh'=2,'core'=2,'xh'=2,'xl'=2,'yh'=2,'yl'=2,'zc'=2,'zf'=2] {'xh','z..., dimensions={0} | all-to-all | bytes 786432 | tf_op jit(solution)/shard_map/all_to_all | solution.py:299
  169.4 11.2 %collective-permute-start.19 = (bf16[8,3200]{1,0:T(8,128)(2,1)}, bf16[8,3200]{1,0:T(8,128)(2,1)S(1)}, u32[]{:S(2)}, u32[]{:S(2)}) collective-permute-start(bf16[8,3200]{1,0:T(8,128)(2,1)} %shard_map.105), channel_id=1, source_target_pairs={{0,64},{2,66},{64,130},{66,128},{128,192},{130,194},{1,65},{3,67},... | collective-permute-start | bytes 153608 | tf_op jit(solution)/shard_map/ppermute | solution.py:36
  180.6 2.2 collective-permute-done.19
  183.6 3.5 %all-to-all-start.7 = ((bf16[8,8,3072]{2,1,0:T(8,128)(2,1)}), bf16[8,8,3072]{2,1,0:T(8,128)(2,1)S(1)}, u32[]{:S(2)}, u32[]{:S(2)}) async-start(bf16[8,8,3072]{2,1,0:T(8,128)(2,1)} %broadcast_in_dim.37), calls=%async_computation.7 | async-start | bytes 786432 | tf_op jit(solution)/shard_map/all_to_all | solution.py:46
  188.0 13.3 %all-to-all-done.7 = bf16[8,8,3072]{2,1,0:T(8,128)(2,1)S(1)} async-done(((bf16[8,8,3072]{2,1,0:T(8,128)(2,1)}), bf16[8,8,3072]{2,1,0:T(8,128)(2,1)S(1)}, u32[]{:S(2)}, u32[]{:S(2)}) %all-to-all-start.7) | async-done | bytes 393248 | tf_op jit(solution)/shard_map/all_to_all | solution.py:46
  201.3 3.7 %copy-done.2 = bf16[1536,3072]{1,0:T(8,128)(2,1)S(1)} copy-done((bf16[1536,3072]{1,0:T(8,128)(2,1)S(1)}, bf16[1536,3072]{1,0:T(8,128)(2,1)}, u32[]{:S(2)}) %copy-start.2) | copy-done | bytes 9437208
  205.0 3.7 %copy-done.5 = bf16[1536,3072]{1,0:T(8,128)(2,1)S(1)} copy-done((bf16[1536,3072]{1,0:T(8,128)(2,1)S(1)}, bf16[1536,3072]{1,0:T(8,128)(2,1)}, u32[]{:S(2)}) %copy-start.5) | copy-done | bytes 9437208
  208.7 4.8 %shard_map.106 = bf16[64,3072]{1,0:T(8,128)(2,1)S(1)} custom-call(bf16[64,3072]{1,0:T(8,128)(2,1)S(1)} %bitcast.69, f32[3,3072]{1,0:T(4,128)S(1)} %reshape.70.mod_ref, bf16[1536,3072]{1,0:T(8,128)(2,1)S(1)} %copy-done.2, bf16[1536,3072]{1,0:T(8,128)(2,1)S(1)} %copy-done.5), custom_call_target="tpu_custom_call" | custom-call | flops 1207959552 | bytes 19660800 | tf_op jit(solution)/shard_map/pallas_call | solution.py:125
  213.5 14.6 %all_to_all.67.parts_ref = bf16[8,8,3072]{2,1,0:T(8,128)(2,1)} all-to-all(bf16[8,8,3072]{2,1,0:T(8,128)(2,1)S(1)} %bitcast.71), channel_id=1, replica_groups=mesh['zh'=2,'core'=2,'xh'=2,'xl'=2,'yh'=2,'yl'=2,'zc'=2,'zf'=2] {'xh','z..., dimensions={0} | all-to-all | bytes 786432 | tf_op jit(solution)/shard_map/all_to_all | solution.py:299
  229.9 2.9 collective-permute-start.21
  232.8 2.9 collective-permute-done.21
  236.5 3.5 %all-to-all-start.9 = ((bf16[8,8,3072]{2,1,0:T(8,128)(2,1)}), bf16[8,8,3072]{2,1,0:T(8,128)(2,1)S(1)}, u32[]{:S(2)}, u32[]{:S(2)}) async-start(bf16[8,8,3072]{2,1,0:T(8,128)(2,1)} %broadcast_in_dim.38), calls=%async_computation.9 | async-start | bytes 786432 | tf_op jit(solution)/shard_map/all_to_all | solution.py:46
  241.3 8.2 %collective-permute-done.22 = bf16[8,3200]{1,0:T(8,128)(2,1)S(1)} collective-permute-done((bf16[8,3200]{1,0:T(8,128)(2,1)S(1)}, bf16[8,3200]{1,0:T(8,128)(2,1)S(1)}, u32[]{:S(2)}, u32[]{:S(2)}) %collective-permute-start.22) | collective-permute-done | bytes 51232 | tf_op jit(solution)/shard_map/ppermute | solution.py:36
  249.5 4.7 %all-to-all-done.9 = bf16[8,8,3072]{2,1,0:T(8,128)(2,1)S(1)} async-done(((bf16[8,8,3072]{2,1,0:T(8,128)(2,1)}), bf16[8,8,3072]{2,1,0:T(8,128)(2,1)S(1)}, u32[]{:S(2)}, u32[]{:S(2)}) %all-to-all-start.9) | async-done | bytes 393248 | tf_op jit(solution)/shard_map/all_to_all | solution.py:46
  254.2 3.7 %copy-done.3 = bf16[1536,3072]{1,0:T(8,128)(2,1)S(1)} copy-done((bf16[1536,3072]{1,0:T(8,128)(2,1)S(1)}, bf16[1536,3072]{1,0:T(8,128)(2,1)}, u32[]{:S(2)}) %copy-start.3) | copy-done | bytes 9437208
  257.9 3.7 %copy-done.6 = bf16[1536,3072]{1,0:T(8,128)(2,1)S(1)} copy-done((bf16[1536,3072]{1,0:T(8,128)(2,1)S(1)}, bf16[1536,3072]{1,0:T(8,128)(2,1)}, u32[]{:S(2)}) %copy-start.6) | copy-done | bytes 9437208
  261.6 4.8 %shard_map.108 = bf16[64,3072]{1,0:T(8,128)(2,1)S(1)} custom-call(bf16[64,3072]{1,0:T(8,128)(2,1)S(1)} %bitcast.70, f32[3,3072]{1,0:T(4,128)S(1)} %reshape.70.mod_ref, bf16[1536,3072]{1,0:T(8,128)(2,1)S(1)} %copy-done.3, bf16[1536,3072]{1,0:T(8,128)(2,1)S(1)} %copy-done.6), custom_call_target="tpu_custom_call" | custom-call | flops 1207959552 | bytes 19660800 | tf_op jit(solution)/shard_map/pallas_call | solution.py:125
  266.4 14.6 %all_to_all.68.parts_ref = bf16[8,8,3072]{2,1,0:T(8,128)(2,1)} all-to-all(bf16[8,8,3072]{2,1,0:T(8,128)(2,1)S(1)} %bitcast.72), channel_id=1, replica_groups=mesh['zh'=2,'core'=2,'xh'=2,'xl'=2,'yh'=2,'yl'=2,'zc'=2,'zf'=2] {'xh','z..., dimensions={0} | all-to-all | bytes 786432 | tf_op jit(solution)/shard_map/all_to_all | solution.py:299
  282.8 2.3 collective-permute-start.23
  285.1 3.6 %collective-permute-done.23 = bf16[8,3200]{1,0:T(8,128)(2,1)S(1)} collective-permute-done((bf16[8,3200]{1,0:T(8,128)(2,1)}, bf16[8,3200]{1,0:T(8,128)(2,1)S(1)}, u32[]{:S(2)}, u32[]{:S(2)}) %collective-permute-start.23) | collective-permute-done | bytes 51232 | tf_op jit(solution)/shard_map/ppermute | solution.py:36
  289.4 3.5 %all-to-all-start.11 = ((bf16[8,8,3072]{2,1,0:T(8,128)(2,1)}), bf16[8,8,3072]{2,1,0:T(8,128)(2,1)S(1)}, u32[]{:S(2)}, u32[]{:S(2)}) async-start(bf16[8,8,3072]{2,1,0:T(8,128)(2,1)} %broadcast_in_dim.39), calls=%async_computation.11 | async-start | bytes 786432 | tf_op jit(solution)/shard_map/all_to_all | solution.py:46
  293.6 13.0 %all-to-all-done.11 = bf16[8,8,3072]{2,1,0:T(8,128)(2,1)S(1)} async-done(((bf16[8,8,3072]{2,1,0:T(8,128)(2,1)}), bf16[8,8,3072]{2,1,0:T(8,128)(2,1)S(1)}, u32[]{:S(2)}, u32[]{:S(2)}) %all-to-all-start.11) | async-done | bytes 393248 | tf_op jit(solution)/shard_map/all_to_all | solution.py:46
  306.6 3.7 %copy-done.4 = bf16[1536,3072]{1,0:T(8,128)(2,1)S(1)} copy-done((bf16[1536,3072]{1,0:T(8,128)(2,1)S(1)}, bf16[1536,3072]{1,0:T(8,128)(2,1)}, u32[]{:S(2)}) %copy-start.4) | copy-done | bytes 9437208
  310.3 3.7 %copy-done.7 = bf16[1536,3072]{1,0:T(8,128)(2,1)S(1)} copy-done((bf16[1536,3072]{1,0:T(8,128)(2,1)S(1)}, bf16[1536,3072]{1,0:T(8,128)(2,1)}, u32[]{:S(2)}) %copy-start.7) | copy-done | bytes 9437208
  314.0 5.6 %shard_map.110 = bf16[64,3072]{1,0:T(8,128)(2,1)} custom-call(bf16[64,3072]{1,0:T(8,128)(2,1)S(1)} %bitcast.68, f32[3,3072]{1,0:T(4,128)S(1)} %reshape.70.mod_ref, bf16[1536,3072]{1,0:T(8,128)(2,1)S(1)} %copy-done.4, bf16[1536,3072]{1,0:T(8,128)(2,1)S(1)} %copy-done.7), custom_call_target="tpu_custom_call" | custom-call | flops 1207959552 | bytes 19660800 | tf_op jit(solution)/shard_map/pallas_call | solution.py:125
  319.6 3.5 %all-to-all-start.12 = ((bf16[8,8,3072]{2,1,0:T(8,128)(2,1)}), bf16[8,8,3072]{2,1,0:T(8,128)(2,1)S(1)}, u32[]{:S(2)}, u32[]{:S(2)}) async-start(bf16[8,8,3072]{2,1,0:T(8,128)(2,1)} %bitcast.29), calls=%async_computation.12 | async-start | bytes 786432 | tf_op jit(solution)/shard_map/all_to_all | solution.py:299
  323.0 11.3 %all-to-all-done.12.parts_ref = bf16[8,8,3072]{2,1,0:T(8,128)(2,1)S(1)} async-done(((bf16[8,8,3072]{2,1,0:T(8,128)(2,1)}), bf16[8,8,3072]{2,1,0:T(8,128)(2,1)S(1)}, u32[]{:S(2)}, u32[]{:S(2)}) %all-to-all-start.12) | async-done | bytes 393248 | tf_op jit(solution)/shard_map/all_to_all | solution.py:299
  336.8 5.3 %collective-permute-start.26 = (bf16[8,3200]{1,0:T(8,128)(2,1)}, bf16[8,3200]{1,0:T(8,128)(2,1)S(1)}, u32[]{:S(2)}, u32[]{:S(2)}) collective-permute-start(bf16[8,3200]{1,0:T(8,128)(2,1)} %shard_map.111), channel_id=1, source_target_pairs={{0,64},{2,66},{64,128},{66,130},{128,194},{130,192},{1,65},{3,67},... | collective-permute-start | bytes 153608 | tf_op jit(solution)/shard_map/ppermute | solution.py:36
  (129 shorter events, 48.5 us)
Async XLA Ops:
  0.6 66.2 %copy-start = (bf16[1,144,3584]{2,1,0:T(8,128)(2,1)S(1)}, bf16[1,144,3584]{2,1,0:T(8,128)(2,1)}, u32[]{:S(2)}) copy-start(bf16[1,144,3584]{2,1,0:T(8,128)(2,1)} %param.15) | copy-start | bytes 3096580
  4.1 18.1 %copy-start.22 = (s32[1,8]{1,0:T(1,128)S(1)}, s32[1,8]{1,0:T(1,128)}, u32[]{:S(2)}) copy-start(s32[1,8]{1,0:T(1,128)} %param.12) | copy-start | bytes 100
  4.1 18.2 %copy-start.21 = (bf16[1,8,3072]{2,1,0:T(8,128)(2,1)S(1)}, bf16[1,8,3072]{2,1,0:T(8,128)(2,1)}, u32[]{:S(2)}) copy-start(bf16[1,8,3072]{2,1,0:T(8,128)(2,1)} %param.11) | copy-start | bytes 147460
  5.7 40.6 %collective-permute-start = (bf16[192,3072]{1,0:T(8,128)(2,1)}, bf16[192,3072]{1,0:T(8,128)(2,1)S(1)}, u32[]{:S(2)}, u32[]{:S(2)}) collective-permute-start(bf16[192,3072]{1,0:T(8,128)(2,1)} %get-tuple-element.65.refs_0_), channel_id=1, source_target_pairs={{4,0},{8,4},{12,8},{0,12},{5,1},{9,5},{13,9},{1,13},{6,2},{10,6},{... | collective-permute-start | bytes 3538952 | tf_op jit(solution)/shard_map/ppermute | solution.py:29
  9.2 37.0 %collective-permute-start.1 = (bf16[192,3072]{1,0:T(8,128)(2,1)}, bf16[192,3072]{1,0:T(8,128)(2,1)S(1)}, u32[]{:S(2)}, u32[]{:S(2)}) collective-permute-start(bf16[192,3072]{1,0:T(8,128)(2,1)} %get-tuple-element.64.refs_1_), channel_id=1, source_target_pairs={{12,0},{0,4},{4,8},{8,12},{13,1},{1,5},{5,9},{9,13},{14,2},{2,6},{... | collective-permute-start | bytes 3538952 | tf_op jit(solution)/shard_map/ppermute | solution.py:29
  9.2 37.0 %collective-permute-start.2 = (bf16[192,3072]{1,0:T(8,128)(2,1)}, bf16[192,3072]{1,0:T(8,128)(2,1)}, u32[]{:S(2)}, u32[]{:S(2)}) collective-permute-start(bf16[192,3072]{1,0:T(8,128)(2,1)} %get-tuple-element.65.refs_0_), channel_id=1, source_target_pairs={{16,0},{32,16},{48,32},{0,48},{17,1},{33,17},{49,33},{1,49},{18,2}... | collective-permute-start | bytes 3538952 | tf_op jit(solution)/shard_map/ppermute | solution.py:29
  11.7 34.5 %collective-permute-start.3 = (bf16[192,3072]{1,0:T(8,128)(2,1)}, bf16[192,3072]{1,0:T(8,128)(2,1)}, u32[]{:S(2)}, u32[]{:S(2)}) collective-permute-start(bf16[192,3072]{1,0:T(8,128)(2,1)} %get-tuple-element.64.refs_1_), channel_id=1, source_target_pairs={{48,0},{0,16},{16,32},{32,48},{49,1},{1,17},{17,33},{33,49},{50,2}... | collective-permute-start | bytes 3538952 | tf_op jit(solution)/shard_map/ppermute | solution.py:29
  12.5 19.4 %all-to-all-start = ((f32[16,28,128]{2,1,0:T(8,128)}), f32[16,28,128]{2,1,0:T(8,128)}, u32[]{:S(2)}, u32[]{:S(2)}) async-start(f32[16,28,128]{2,1,0:T(8,128)} %broadcast_in_dim.28), calls=%async_computation | async-start | bytes 524288 | tf_op jit(solution)/shard_map/all_to_all | solution.py:46
  47.0 14.4 %all-to-all-start.2 = ((f32[16,28,128]{2,1,0:T(8,128)}), f32[16,28,128]{2,1,0:T(8,128)}, u32[]{:S(2)}, u32[]{:S(2)}) async-start(f32[16,28,128]{2,1,0:T(8,128)} %broadcast_in_dim.31), calls=%async_computation.2 | async-start | bytes 524288 | tf_op jit(solution)/shard_map/all_to_all | solution.py:46
  62.4 25.9 %collective-permute-start.4 = (bf16[192,3072]{1,0:T(8,128)(2,1)}, bf16[192,3072]{1,0:T(8,128)(2,1)}, u32[]{:S(2)}, u32[]{:S(2)}) collective-permute-start(bf16[192,3072]{1,0:T(8,128)(2,1)} %get-tuple-element.64.refs_1_), channel_id=1, source_target_pairs={{4,0},{8,4},{12,8},{0,12},{5,1},{9,5},{13,9},{1,13},{6,2},{10,6},{... | collective-permute-start | bytes 3538952 | tf_op jit(solution)/shard_map/ppermute | solution.py:29
  63.3 25.1 %collective-permute-start.5 = (bf16[192,3072]{1,0:T(8,128)(2,1)}, bf16[192,3072]{1,0:T(8,128)(2,1)}, u32[]{:S(2)}, u32[]{:S(2)}) collective-permute-start(bf16[192,3072]{1,0:T(8,128)(2,1)} %get-tuple-element.65.refs_0_), channel_id=1, source_target_pairs={{12,0},{0,4},{4,8},{8,12},{13,1},{1,5},{5,9},{9,13},{14,2},{2,6},{... | collective-permute-start | bytes 3538952 | tf_op jit(solution)/shard_map/ppermute | solution.py:29
  64.0 24.4 %collective-permute-start.6 = (bf16[192,3072]{1,0:T(8,128)(2,1)S(1)}, bf16[192,3072]{1,0:T(8,128)(2,1)}, u32[]{:S(2)}, u32[]{:S(2)}) collective-permute-start(bf16[192,3072]{1,0:T(8,128)(2,1)S(1)} %collective-permute-done.refs_4_), channel_id=1, source_target_pairs={{16,0},{32,16},{48,32},{0,48},{17,1},{33,17},{49,33},{1,49},{18,2}... | collective-permute-start | bytes 3538952 | tf_op jit(solution)/shard_map/ppermute | solution.py:29
  64.8 23.6 %collective-permute-start.7 = (bf16[192,3072]{1,0:T(8,128)(2,1)S(1)}, bf16[192,3072]{1,0:T(8,128)(2,1)}, u32[]{:S(2)}, u32[]{:S(2)}) collective-permute-start(bf16[192,3072]{1,0:T(8,128)(2,1)S(1)} %collective-permute-done.1.refs_5_), channel_id=1, source_target_pairs={{48,0},{0,16},{16,32},{32,48},{49,1},{1,17},{17,33},{33,49},{50,2}... | collective-permute-start | bytes 3538952 | tf_op jit(solution)/shard_map/ppermute | solution.py:29
  67.8 10.4 %all-to-all-start.3 = ((f32[4,2,128]{2,1,0:T(2,128)}), f32[4,2,128]{2,1,0:T(2,128)S(1)}, u32[]{:S(2)}, u32[]{:S(2)}) async-start(f32[4,2,128]{2,1,0:T(2,128)} %broadcast_in_dim.33), calls=%async_computation.3 | async-start | bytes 8192 | tf_op jit(solution)/shard_map/all_to_all | solution.py:46
  78.9 9.5 %all-to-all-start.4 = ((bf16[4,8,3072]{2,1,0:T(8,128)(2,1)}), bf16[4,8,3072]{2,1,0:T(8,128)(2,1)}, u32[]{:S(2)}, u32[]{:S(2)}) async-start(bf16[4,8,3072]{2,1,0:T(8,128)(2,1)} %broadcast_in_dim.34), calls=%async_computation.4 | async-start | bytes 393216 | tf_op jit(solution)/shard_map/all_to_all | solution.py:46
  82.9 18.5 %copy-start.23 = (s32[1,8]{1,0:T(1,128)S(1)}, s32[1,8]{1,0:T(1,128)}, u32[]{:S(2)}) copy-start(s32[1,8]{1,0:T(1,128)} %param.10) | copy-start | bytes 100
  88.4 9.2 %collective-permute-start.10 = (bf16[96,3072]{1,0:T(8,128)(2,1)}, bf16[96,3072]{1,0:T(8,128)(2,1)S(1)}, u32[]{:S(2)}, u32[]{:S(2)}) collective-permute-start(bf16[96,3072]{1,0:T(8,128)(2,1)} %get-tuple-element.76), channel_id=1, source_target_pairs={{4,0},{8,4},{12,8},{0,12},{5,1},{9,5},{13,9},{1,13},{6,2},{10,6},{... | collective-permute-start | bytes 1769480 | tf_op jit(solution)/shard_map/ppermute | solution.py:29
  90.4 29.0 %collective-permute-start.13 = (bf16[192,3072]{1,0:T(8,128)(2,1)}, bf16[192,3072]{1,0:T(8,128)(2,1)}, u32[]{:S(2)}, u32[]{:S(2)}) collective-permute-start(bf16[192,3072]{1,0:T(8,128)(2,1)} %collective-permute-done.5.refs_7_), channel_id=1, source_target_pairs={{16,0},{32,16},{48,32},{0,48},{17,1},{33,17},{49,33},{1,49},{18,2}... | collective-permute-start | bytes 3538952 | tf_op jit(solution)/shard_map/ppermute | solution.py:29
  92.3 27.1 %collective-permute-start.14 = (bf16[192,3072]{1,0:T(8,128)(2,1)}, bf16[192,3072]{1,0:T(8,128)(2,1)}, u32[]{:S(2)}, u32[]{:S(2)}) collective-permute-start(bf16[192,3072]{1,0:T(8,128)(2,1)} %collective-permute-done.4.refs_6_), channel_id=1, source_target_pairs={{48,0},{0,16},{16,32},{32,48},{49,1},{1,17},{17,33},{33,49},{50,2}... | collective-permute-start | bytes 3538952 | tf_op jit(solution)/shard_map/ppermute | solution.py:29
  92.3 14.1 %collective-permute-start.11 = (bf16[96,3072]{1,0:T(8,128)(2,1)}, bf16[96,3072]{1,0:T(8,128)(2,1)}, u32[]{:S(2)}, u32[]{:S(2)}) collective-permute-start(bf16[96,3072]{1,0:T(8,128)(2,1)} %get-tuple-element.77), channel_id=1, source_target_pairs={{12,0},{0,4},{4,8},{8,12},{13,1},{1,5},{5,9},{9,13},{14,2},{2,6},{... | collective-permute-start | bytes 1769480 | tf_op jit(solution)/shard_map/ppermute | solution.py:29
  92.3 27.1 %collective-permute-start.12 = (bf16[96,3072]{1,0:T(8,128)(2,1)}, bf16[96,3072]{1,0:T(8,128)(2,1)}, u32[]{:S(2)}, u32[]{:S(2)}) collective-permute-start(bf16[96,3072]{1,0:T(8,128)(2,1)} %get-tuple-element.78), channel_id=1, source_target_pairs={{12,0},{0,4},{4,8},{8,12},{13,1},{1,5},{5,9},{9,13},{14,2},{2,6},{... | collective-permute-start | bytes 1769480 | tf_op jit(solution)/shard_map/ppermute | solution.py:29
  98.4 21.0 %collective-permute-start.9 = (bf16[96,3072]{1,0:T(8,128)(2,1)}, bf16[96,3072]{1,0:T(8,128)(2,1)}, u32[]{:S(2)}, u32[]{:S(2)}) collective-permute-start(bf16[96,3072]{1,0:T(8,128)(2,1)} %get-tuple-element.75), channel_id=1, source_target_pairs={{4,0},{8,4},{12,8},{0,12},{5,1},{9,5},{13,9},{1,13},{6,2},{10,6},{... | collective-permute-start | bytes 1769480 | tf_op jit(solution)/shard_map/ppermute | solution.py:29
  102.0 15.2 %all-to-all-start.5 = ((f32[16,4,2,128]{3,2,1,0:T(2,128)}), f32[16,4,2,128]{3,2,1,0:T(2,128)S(1)}, u32[]{:S(2)}, u32[]{:S(2)}) async-start(f32[16,4,2,128]{3,2,1,0:T(2,128)} %broadcast_in_dim.36), calls=%async_computation.5 | async-start | bytes 131072 | tf_op jit(solution)/shard_map/all_to_all | solution.py:46
  106.4 16.5 %collective-permute-start.8 = (bf16[4,8,3072]{2,1,0:T(8,128)(2,1)}, bf16[4,8,3072]{2,1,0:T(8,128)(2,1)}, u32[]{:S(2)}, u32[]{:S(2)}) collective-permute-start(bf16[4,8,3072]{2,1,0:T(8,128)(2,1)} %all-to-all-done.4), channel_id=1, source_target_pairs={{0,32},{32,0},{1,33},{33,1},{2,34},{34,2},{3,35},{35,3},{4,36},{36... | collective-permute-start | bytes 589832 | tf_op jit(solution)/shard_map/ppermute | solution.py:225
  118.8 14.4 %copy-start.9 = (bf16[96,3072]{1,0:T(8,128)(2,1)S(1)}, bf16[96,3072]{1,0:T(8,128)(2,1)}, u32[]{:S(2)}) copy-start(bf16[96,3072]{1,0:T(8,128)(2,1)} %copy-done.8) | copy-start | bytes 1769476
  119.4 10.2 %collective-permute-start.15 = (bf16[96,3072]{1,0:T(8,128)(2,1)}, bf16[96,3072]{1,0:T(8,128)(2,1)S(1)}, u32[]{:S(2)}, u32[]{:S(2)}) collective-permute-start(bf16[96,3072]{1,0:T(8,128)(2,1)} %collective-permute-done.9.refs_12_), channel_id=1, source_target_pairs={{16,0},{32,16},{48,32},{0,48},{17,1},{33,17},{49,33},{1,49},{18,2}... | collective-permute-start | bytes 1769480 | tf_op jit(solution)/shard_map/ppermute | solution.py:29
  120.7 11.9 %collective-permute-start.16 = (bf16[96,3072]{1,0:T(8,128)(2,1)}, bf16[96,3072]{1,0:T(8,128)(2,1)S(1)}, u32[]{:S(2)}, u32[]{:S(2)}) collective-permute-start(bf16[96,3072]{1,0:T(8,128)(2,1)} %collective-permute-done.11.refs_14_), channel_id=1, source_target_pairs={{48,0},{0,16},{16,32},{32,48},{49,1},{1,17},{17,33},{33,49},{50,2}... | collective-permute-start | bytes 1769480 | tf_op jit(solution)/shard_map/ppermute | solution.py:29
  121.0 11.7 %collective-permute-start.17 = (bf16[96,3072]{1,0:T(8,128)(2,1)}, bf16[96,3072]{1,0:T(8,128)(2,1)S(1)}, u32[]{:S(2)}, u32[]{:S(2)}) collective-permute-start(bf16[96,3072]{1,0:T(8,128)(2,1)} %slice.92), channel_id=1, source_target_pairs={{4,0},{8,4},{12,8},{0,12},{5,1},{9,5},{13,9},{1,13},{6,2},{10,6},{... | collective-permute-start | bytes 1769480 | tf_op jit(solution)/shard_map/ppermute | solution.py:29
  123.0 10.2 %collective-permute-start.18 = (bf16[96,3072]{1,0:T(8,128)(2,1)}, bf16[96,3072]{1,0:T(8,128)(2,1)S(1)}, u32[]{:S(2)}, u32[]{:S(2)}) collective-permute-start(bf16[96,3072]{1,0:T(8,128)(2,1)} %slice.93), channel_id=1, source_target_pairs={{12,0},{0,4},{4,8},{8,12},{13,1},{1,5},{5,9},{9,13},{14,2},{2,6},{... | collective-permute-start | bytes 1769480 | tf_op jit(solution)/shard_map/ppermute | solution.py:29
  148.3 34.4 %copy-start.12 = (bf16[4,8,3200]{2,1,0:T(8,128)(2,1)S(1)}, bf16[4,8,3200]{2,1,0:T(8,128)(2,1)}, u32[]{:S(2)}) copy-start(bf16[4,8,3200]{2,1,0:T(8,128)(2,1)} %all_to_all.65) | copy-start | bytes 614404
  169.4 17.6 %copy-start.18 = (bf16[8,3200]{1,0:T(8,128)(2,1)S(1)}, bf16[8,3200]{1,0:T(8,128)(2,1)}, u32[]{:S(2)}) copy-start(bf16[8,3200]{1,0:T(8,128)(2,1)} %shard_map.105) | copy-start | bytes 153604
  169.4 13.3 %collective-permute-start.19 = (bf16[8,3200]{1,0:T(8,128)(2,1)}, bf16[8,3200]{1,0:T(8,128)(2,1)S(1)}, u32[]{:S(2)}, u32[]{:S(2)}) collective-permute-start(bf16[8,3200]{1,0:T(8,128)(2,1)} %shard_map.105), channel_id=1, source_target_pairs={{0,64},{2,66},{64,130},{66,128},{128,192},{130,194},{1,65},{3,67},... | collective-permute-start | bytes 153608 | tf_op jit(solution)/shard_map/ppermute | solution.py:36
  182.8 30.7 %copy-start.14 = (bf16[8,3200]{1,0:T(8,128)(2,1)}, bf16[8,3200]{1,0:T(8,128)(2,1)S(1)}, u32[]{:S(2)}) copy-start(bf16[8,3200]{1,0:T(8,128)(2,1)S(1)} %bitcast_select_fusion.waiting_ref) | copy-start | bytes 153604
  183.6 17.7 %all-to-all-start.7 = ((bf16[8,8,3072]{2,1,0:T(8,128)(2,1)}), bf16[8,8,3072]{2,1,0:T(8,128)(2,1)S(1)}, u32[]{:S(2)}, u32[]{:S(2)}) async-start(bf16[8,8,3072]{2,1,0:T(8,128)(2,1)} %broadcast_in_dim.37), calls=%async_computation.7 | async-start | bytes 786432 | tf_op jit(solution)/shard_map/all_to_all | solution.py:46
  187.1 0.9 collective-permute-start.20
  229.9 10.1 %copy-start.19 = (bf16[8,3200]{1,0:T(8,128)(2,1)S(1)}, bf16[8,3200]{1,0:T(8,128)(2,1)}, u32[]{:S(2)}) copy-start(bf16[8,3200]{1,0:T(8,128)(2,1)} %shard_map.107) | copy-start | bytes 153604
  229.9 5.8 %collective-permute-start.21 = (bf16[8,3200]{1,0:T(8,128)(2,1)}, bf16[8,3200]{1,0:T(8,128)(2,1)S(1)}, u32[]{:S(2)}, u32[]{:S(2)}) collective-permute-start(bf16[8,3200]{1,0:T(8,128)(2,1)} %shard_map.107), channel_id=1, source_target_pairs={{0,64},{2,66},{64,130},{66,128},{128,192},{130,194},{1,65},{3,67},... | collective-permute-start | bytes 153608 | tf_op jit(solution)/shard_map/ppermute | solution.py:36
  235.7 30.7 %copy-start.15 = (bf16[8,3200]{1,0:T(8,128)(2,1)}, bf16[8,3200]{1,0:T(8,128)(2,1)S(1)}, u32[]{:S(2)}) copy-start(bf16[8,3200]{1,0:T(8,128)(2,1)S(1)} %bitcast_select_fusion.1.waiting_ref) | copy-start | bytes 153604
  236.5 17.7 %all-to-all-start.9 = ((bf16[8,8,3072]{2,1,0:T(8,128)(2,1)}), bf16[8,8,3072]{2,1,0:T(8,128)(2,1)S(1)}, u32[]{:S(2)}, u32[]{:S(2)}) async-start(bf16[8,8,3072]{2,1,0:T(8,128)(2,1)} %broadcast_in_dim.38), calls=%async_computation.9 | async-start | bytes 786432 | tf_op jit(solution)/shard_map/all_to_all | solution.py:46
  240.0 9.5 %collective-permute-start.22 = (bf16[8,3200]{1,0:T(8,128)(2,1)S(1)}, bf16[8,3200]{1,0:T(8,128)(2,1)S(1)}, u32[]{:S(2)}, u32[]{:S(2)}) collective-permute-start(bf16[8,3200]{1,0:T(8,128)(2,1)S(1)} %copy-done.19), channel_id=1, source_target_pairs={{192,64},{194,66},{193,65},{195,67},{196,68},{198,70},{197,69},{19... | collective-permute-start | bytes 153608 | tf_op jit(solution)/shard_map/ppermute | solution.py:36
  282.8 10.1 %copy-start.20 = (bf16[8,3200]{1,0:T(8,128)(2,1)S(1)}, bf16[8,3200]{1,0:T(8,128)(2,1)}, u32[]{:S(2)}) copy-start(bf16[8,3200]{1,0:T(8,128)(2,1)} %shard_map.109) | copy-start | bytes 153604
  282.8 5.8 %collective-permute-start.23 = (bf16[8,3200]{1,0:T(8,128)(2,1)}, bf16[8,3200]{1,0:T(8,128)(2,1)S(1)}, u32[]{:S(2)}, u32[]{:S(2)}) collective-permute-start(bf16[8,3200]{1,0:T(8,128)(2,1)} %shard_map.109), channel_id=1, source_target_pairs={{0,64},{2,66},{64,130},{66,128},{128,192},{130,194},{1,65},{3,67},... | collective-permute-start | bytes 153608 | tf_op jit(solution)/shard_map/ppermute | solution.py:36
  288.6 30.9 %copy-start.13 = (bf16[8,3200]{1,0:T(8,128)(2,1)}, bf16[8,3200]{1,0:T(8,128)(2,1)S(1)}, u32[]{:S(2)}) copy-start(bf16[8,3200]{1,0:T(8,128)(2,1)S(1)} %bitcast_select_fusion.2.waiting_ref) | copy-start | bytes 153604
  289.4 17.2 %all-to-all-start.11 = ((bf16[8,8,3072]{2,1,0:T(8,128)(2,1)}), bf16[8,8,3072]{2,1,0:T(8,128)(2,1)S(1)}, u32[]{:S(2)}, u32[]{:S(2)}) async-start(bf16[8,8,3072]{2,1,0:T(8,128)(2,1)} %broadcast_in_dim.39), calls=%async_computation.11 | async-start | bytes 786432 | tf_op jit(solution)/shard_map/all_to_all | solution.py:46
  292.9 0.7 collective-permute-start.24
  319.6 14.8 %all-to-all-start.12 = ((bf16[8,8,3072]{2,1,0:T(8,128)(2,1)}), bf16[8,8,3072]{2,1,0:T(8,128)(2,1)S(1)}, u32[]{:S(2)}, u32[]{:S(2)}) async-start(bf16[8,8,3072]{2,1,0:T(8,128)(2,1)} %bitcast.29), calls=%async_computation.12 | async-start | bytes 786432 | tf_op jit(solution)/shard_map/all_to_all | solution.py:299
  336.8 6.8 %collective-permute-start.26 = (bf16[8,3200]{1,0:T(8,128)(2,1)}, bf16[8,3200]{1,0:T(8,128)(2,1)S(1)}, u32[]{:S(2)}, u32[]{:S(2)}) collective-permute-start(bf16[8,3200]{1,0:T(8,128)(2,1)} %shard_map.111), channel_id=1, source_target_pairs={{0,64},{2,66},{64,128},{66,130},{128,194},{130,192},{1,65},{3,67},... | collective-permute-start | bytes 153608 | tf_op jit(solution)/shard_map/ppermute | solution.py:36
  342.1 2.1 collective-permute-start.25
  (12 other events, 34.1 us)

commit v2 on v0

--- a/solution.py
+++ b/solution.py
@@ -21,8 +21,6 @@
 SECTIONS = 4
 LANES = 128
 STEP = 256
-SPAN = 768
-IN_FLIGHT = 10
 
 
 def from_neighbour(block, axis, distance):
@@ -47,25 +45,7 @@
     return lax.all_to_all(copies, axes, 0, 0)
 
 
-def ffn_kernel(lifts, drops, x_ref, mod_ref, *refs):
-    held = len({i for i, _, _ in lifts + drops})
-    weights = refs[:held]
-    out_ref, up, down, inputs, hidden, acc, sem = refs[held:]
-    copies = []
-    for place, parts in ((up, lifts), (down, drops)):
-        at = 0
-        for i, first, rows in parts:
-            copies.append(
-                pltpu.make_async_copy(
-                    weights[i].at[pl.ds(first, rows)],
-                    place.at[pl.ds(at, rows)],
-                    sem.at[len(copies)],
-                )
-            )
-            at += rows
-    total = at
-    for copy in copies[:IN_FLIGHT]:
-        copy.start()
+def modulate(x_ref, mod_ref, inputs):
     values = x_ref[...].astype(f32)
     center = jnp.mean(values, axis=1, keepdims=True)
     moved = values - center
@@ -73,65 +53,79 @@
     inputs[...] = (
         moved * lax.rsqrt(spread + 1e-06) * (1.0 + mod_ref[1:2]) + mod_ref[0:1]
     ).astype(bf16)
-    ready = 0
-
-    def wait_for(rows, skip, parts):
-        nonlocal ready
-        while sum(part[2] for part in parts[: ready - skip]) < rows:
-            copies[ready].wait()
-            if ready + IN_FLIGHT < len(copies):
-                copies[ready + IN_FLIGHT].start()
-            ready += 1
-
-    for span in range(0, total, SPAN):
-        wait_for(span + SPAN, 0, lifts)
-        for at in range(span, span + SPAN, STEP):
-            raised = lax.dot_general(
-                inputs[...],
-                up[at : at + STEP],
-                (((1,), (1,)), ((), ())),
-                preferred_element_type=f32,
-            )
-            hidden[:, at : at + STEP] = jax.nn.gelu(raised, approximate=True).astype(bf16)
-    for at in range(0, total, SPAN):
-        wait_for(at + SPAN, len(lifts), drops)
-        for column in range(0, out_ref.shape[1], STEP):
-            columns = slice(column, column + STEP)
-            term = jnp.dot(
-                hidden[:, at : at + SPAN], down[at : at + SPAN, columns], preferred_element_type=f32
-            )
-            if at:
-                term = acc[:, columns] + term
-            if at + SPAN < total:
-                acc[:, columns] = term
-            else:
-                out_ref[:, columns] = term.astype(bf16)
-
-
-def ffn(tokens, mod, weights, lifts, drops):
+
+
+def layer_kernel(x_ref, mod_ref, up, down, up_end, down_end, out_ref, inputs, hidden):
+    modulate(x_ref, mod_ref, inputs)
+    main = up.shape[0]
+    total = main + up_end.shape[0]
+    for at in range(0, total, STEP):
+        rows = up[at : at + STEP] if at < main else up_end[at - main : at - main + STEP]
+        raised = lax.dot_general(
+            inputs[...], rows, (((1,), (1,)), ((), ())), preferred_element_type=f32
+        )
+        hidden[:, at : at + STEP] = jax.nn.gelu(raised, approximate=True).astype(bf16)
+    for at in range(0, out_ref.shape[1], STEP):
+        columns = slice(at, at + STEP)
+        result = jnp.dot(hidden[:, :main], down[:, columns], preferred_element_type=f32)
+        result += jnp.dot(hidden[:, main:], down_end[:, columns], preferred_element_type=f32)
+        out_ref[:, columns] = result.astype(bf16)
+
+
+def layer(tokens, mod, up, down, up_end, down_end):
     rows, breadth = tokens.shape
-    total = sum(part[2] for part in lifts)
+    total = up.shape[0] + up_end.shape[0]
     whole = pl.BlockSpec(memory_space=pltpu.VMEM)
     return pl.pallas_call(
-        functools.partial(ffn_kernel, lifts, drops),
+        layer_kernel,
         out_shape=jax.ShapeDtypeStruct((rows, breadth), bf16),
-        in_specs=[whole, whole] + [pl.BlockSpec(memory_space=pltpu.HBM)] * len(weights),
+        in_specs=[whole] * 6,
         out_specs=whole,
         scratch_shapes=[
-            pltpu.VMEM((total, breadth), bf16),
-            pltpu.VMEM((total, breadth), bf16),
             pltpu.VMEM((rows, breadth), bf16),
             pltpu.VMEM((rows, total), bf16),
-            pltpu.VMEM((rows, breadth), f32),
-            pltpu.SemaphoreType.DMA((len(lifts) + len(drops),)),
         ],
-        compiler_params=pltpu.CompilerParams(vmem_limit_bytes=40 * 1024 * 1024),
+        compiler_params=pltpu.CompilerParams(vmem_limit_bytes=24 * 1024 * 1024),
         cost_estimate=pl.CostEstimate(
             flops=4 * rows * total * breadth,
             bytes_accessed=4 * total * breadth + 4 * rows * breadth,
             transcendentals=rows * total,
         ),
-    )(tokens, mod, *weights)
+    )(tokens, mod, up, down, up_end, down_end)
+
+
+def place_kernel(plan, *refs):
+    sem = refs[-1]
+    outs = refs[-3:-1]
+    copies = []
+    for piece, first, rows, which, at in plan:
+        copies.append(
+            pltpu.make_async_copy(
+                refs[piece].at[pl.ds(first, rows)],
+                outs[which].at[pl.ds(at, rows)],
+                sem.at[len(copies)],
+            )
+        )
+    for copy in copies:
+        copy.start()
+    for copy in copies:
+        copy.wait()
+
+
+def place(plan, pieces, total):
+    breadth = pieces[0].shape[1]
+    whole = pl.BlockSpec(memory_space=pltpu.VMEM)
+    return pl.pallas_call(
+        functools.partial(place_kernel, plan),
+        out_shape=[jax.ShapeDtypeStruct((total, breadth), bf16)] * 2,
+        in_specs=[pl.BlockSpec(memory_space=pl.ANY)] * len(pieces),
+        out_specs=[whole] * 2,
+        scratch_shapes=[pltpu.SemaphoreType.DMA((len(plan),))],
+        compiler_params=pltpu.CompilerParams(vmem_limit_bytes=20 * 1024 * 1024),
+        cost_estimate=pl.CostEstimate(
+            flops=0, bytes_accessed=8 * total * breadth, transcendentals=0
+        ),
+    )(*pieces)
 
 
 def close_kernel(parts_ref, waiting_ref, gate_ref, out_ref):
@@ -176,10 +170,9 @@
     xa = from_neighbour(first, "x", 1)
     xb = from_neighbour(second, "x", -1)
     partial = jnp.sum(exchange(partial, SECTION + LINE), axis=0)
-    entering = exchange(after(arriving, partial), SECTION)
-
-    first, second, yp_first, ym_second, xa, xb, partial, entering = together(
-        (first, second, yp_first, ym_second, xa, xb, partial, entering)
+
+    first, second, yp_first, ym_second, xa, xb, partial = together(
+        (first, second, yp_first, ym_second, xa, xb, partial)
     )
     pooled = jnp.sum(exchange(partial, PLANE), axis=0)
 
@@ -204,22 +197,16 @@
     line, mine, halves, yp_second, ym_first, xa_yp, xb_ym = together(
         (line, mine, halves, yp_second, ym_first, xa_yp, xb_ym)
     )
-    theirs = lax.ppermute(mine, "xh", [(0, 1), (1, 0)])
-    modes = exchange(line, PLANE)
-    modes, theirs, halves, yp_second, ym_first = together(
-        (modes, theirs, halves, yp_second, ym_first)
-    )
     y2 = [from_neighbour(half, "y", 1 if i < 2 else -1) for i, half in enumerate(halves)]
     xa_ym = from_neighbour(ym_first, "x", 1)
     xb_yp = from_neighbour(yp_second, "x", -1)
-    modes = modes.reshape(-1, rows * LANES)[:, :columns].reshape(3, -1)
-    upper = lax.axis_index("xh") == 1
-    gathered = jnp.stack([jnp.where(upper, theirs, mine), jnp.where(upper, mine, theirs)])
+    theirs = lax.ppermute(mine, "xh", [(0, 1), (1, 0)])
+    entering = exchange(after(arriving, mine), SECTION)
     xa_yp_down = xa_yp[middle:]
     xb_ym_down = xb_ym[middle:]
 
-    y2, xa_ym, xb_yp, modes, gathered, xa_yp_down, xb_ym_down = together(
-        (y2, xa_ym, xb_yp, modes, gathered, xa_yp_down, xb_ym_down)
+    y2, xa_ym, xb_yp, xa_yp_down, xb_ym_down, entering, line = together(
+        (y2, xa_ym, xb_yp, xa_yp_down, xb_ym_down, entering, line)
     )
     xa_y2_up = from_neighbour(y2[0], "x", 1)
     xb_y2_up = from_neighbour(y2[2], "x", -1)
@@ -230,13 +217,28 @@
         first, second, xa, xb, yp_first, ym_second, yp_second, ym_first, xa_yp, xb_ym, xa_ym, xb_yp
     ]
     count = len(whole)
-    lifts = [(i, 0, middle) for i in range(count)]
-    drops = [(i, middle, middle) for i in range(count)]
-    lifts += [(count + i, 0, middle) for i in (0, 2, 4, 5)]
-    drops += [(count + i, 0, middle) for i in (1, 3, 6, 7)]
-    weights = whole + y2 + [xa_y2_up, xb_y2_up, xa_y2_down, xb_y2_down]
-    layer = functools.partial(ffn, weights=weights, lifts=lifts, drops=drops)
-    return modes, gathered, entering, layer
+    total = (count + 4) * middle
+    main = (total - 1) // STEP * STEP
+    cut = main - (count + 1) * middle
+    plan = [
+        (i, which * middle, middle, which, i * middle) for i in range(count) for which in (0, 1)
+    ]
+    plan += [(count + which, 0, middle, which, count * middle) for which in (0, 1)]
+    plan += [(count + 2 + which, 0, cut, which, main - cut) for which in (0, 1)]
+    up_rows, down_rows = place(plan, whole + y2, main)
+    modes = exchange(after(line, up_rows), PLANE)
+    modes = modes.reshape(-1, rows * LANES)[:, :columns].reshape(3, -1)
+    upper = lax.axis_index("xh") == 1
+    gathered = jnp.stack([jnp.where(upper, theirs, mine), jnp.where(upper, mine, theirs)])
+    plan = [(which, cut, middle - cut, which, 0) for which in (0, 1)]
+    plan += [
+        (2 + 2 * which + i, 0, middle, which, (1 + i) * middle - cut)
+        for which in (0, 1)
+        for i in (0, 1)
+    ]
+    ends = [y2[2], y2[3], xa_y2_up, xb_y2_up, xa_y2_down, xb_y2_down]
+    up_end, down_end = place(plan, ends, total - main)
+    return modes, gathered, entering, (up_rows, down_rows, up_end, down_end)
 
 
 def per_device(
@@ -261,7 +263,7 @@
     arriving = with_mask(arriving_tiles[0], arriving_region[0])
     waiting = with_mask(travelling_inputs[0], travelling_region[0])
     last = SECTIONS - 1
-    mod, gathered, entering, layer = set_out(
+    mod, gathered, entering, weights = set_out(
         expansion_weights[0],
         contraction_weights[0],
         prompt_embeddings,
@@ -271,24 +273,26 @@
         arriving,
     )
     gathered, waiting, gate = lax.optimization_barrier((gathered, waiting, mod[2:]))
-    finished = []
+    moves = []
     for tick in range(SECTIONS):
         if tick:
             gathered = exchange(waiting[:, :breadth], GROUP)
-        partial = layer(gathered.reshape(GROUP_SIZE * tokens, breadth), mod)
+        partial = layer(gathered.reshape(GROUP_SIZE * tokens, breadth), mod, *weights)
         parts = lax.all_to_all(partial.reshape(GROUP_SIZE, tokens, breadth), GROUP, 0, 0)
+        if tick == last:
+            third = between_sections(after(produced, parts), [(last, 2, 1)])
         produced = close(parts, waiting, gate)
         if tick < last:
-            moved = between_sections(produced, [(0, 1, 0), (1, 2, 1), (2, 3, 0)])
-            flip = int(tick >= 2)
-            finished.append(between_sections(produced, [(last, tick, flip)]))
+            edges = [(0, 1, 0), (1, 2, 1), (2, 3, 0)]
+            if tick < 2:
+                edges.append((last, 0, 0))
         else:
-            moved = between_sections(produced, [(0, 1, 0), (1, 2, 0), (2, 3, 1)])
-            finished.append(between_sections(produced, [(last, last, 1)]))
-        waiting = jnp.where(is_first, entering[tick], moved)
-    done = finished[last]
-    for tick in range(last):
-        done = jnp.where(section_id == tick, finished[tick], done)
+            edges = [(0, 1, 0), (1, 2, 0), (2, 3, 1)]
+        moves.append(between_sections(produced, edges))
+        waiting = jnp.where(is_first, entering[tick], moves[tick])
+    sent = jnp.where(is_first, moves[1], produced)
+    second = between_sections(sent, [(0, 1, 0), (last, last, 1)])
+    done = jnp.where(is_first, moves[0], jnp.where(section_id == 2, third, second))
     return done[None, :, :breadth], waiting[None, :, :breadth]
 
 

time: 352 us -> 360 us (1.023)
  blocking collectives: 121 us -> 91.1 us
  local copies, waits for them, and re-layouts: 23 us -> 51.5 us
  starting transfers between devices: 71.1 us -> 88.8 us
  Pallas kernels: 43.6 us -> 34.4 us
    unnamed x61 -> x53, local copies, waits for them, and re-layouts: 8.19 us -> 37.9 us
    all_to_all x5 -> x3, blocking collectives: 73.3 us -> 46.4 us  [exchange(): return lax.all_to_all(copies, axes, 0, 0)]
    all_to_all x4 -> x6, starting transfers between devices: 26.6 us -> 41.9 us  [exchange(): return lax.all_to_all(copies, axes, 0, 0)]
    ppermute x8 -> x6, waiting for transfers between devices: 20 us -> 5.03 us  [between_sections(): return lax.ppermute(block, SECTION + ('zc',), route)]
    all_to_all x4 -> x6, waiting for transfers between devices: 22.2 us -> 36.3 us  [exchange(): return lax.all_to_all(copies, axes, 0, 0)]
    pallas_call x4 -> x6, Pallas kernels: 36.7 us -> 27.5 us  [the longest x4 20.5 us: layer(): pl.pallas_call(layer_kernel, out_shape=jax.ShapeDtypeStruct((rows, breadt...]
    ppermute x8 -> x6, starting transfers between devices: 20.8 us -> 25.2 us  [between_sections(): return lax.ppermute(block, SECTION + ('zc',), route)]
  transfers between devices with their start and end apart: 32 -> 32, of which waited for: 17 -> 18; matrix products, arithmetic and copies ran while one was open for 5% -> 4% of each run, Pallas kernels for 0% -> 1%
where the time goes in v2:
time: 360 us; the launch traced here: 358 us
  blocking collectives  91.1 us (25%)
  starting transfers between devices  88.8 us (25%)
  waiting for transfers between devices  77.5 us (22%)
  local copies, waits for them, and re-layouts  51.5 us (14%)
  Pallas kernels  34.4 us (10%)
  other arithmetic  12.2 us (3%)
    all_to_all x3, blocking collectives, exchange(): return lax.all_to_all(copies, axes, 0, 0)  46.4 us
    all_to_all x3, blocking collectives, per_device(): lax.all_to_all(partial.reshape(GROUP_SIZE, tokens, breadth), GROUP, 0, 0)  44.6 us
    all_to_all x6, starting transfers between devices, exchange(): return lax.all_to_all(copies, axes, 0, 0)  41.9 us
    unnamed x53, local copies, waits for them, and re-layouts  37.9 us
    all_to_all x6, waiting for transfers between devices, exchange(): return lax.all_to_all(copies, axes, 0, 0)  36.3 us
    ppermute x6, starting transfers between devices, between_sections(): return lax.ppermute(block, SECTION + ('zc',), route)  25.2 us
    ppermute x18, waiting for transfers between devices, from_neighbour(): return lax.ppermute(block, (axis + 'h', axis + 'l'), route)  23.6 us
    pallas_call x4, Pallas kernels, layer(): pl.pallas_call(layer_kernel, out_shape=jax.ShapeDtypeStruct((rows, breadt...  20.5 us
  transfers between devices with their start and end apart: 32, of which 18 were waited for; matrix products, arithmetic and copies ran while one was open for 4% of the time, Pallas kernels for 1%

profile of v2, /device:TPU:1, one launch (start us, length us, event | category | flops | bytes accessed | tf_op | source)
XLA Modules:
  0.0 358.3 jit_solution(14936293912454721720)
XLA Ops:
  4.9 3.6 collective-permute-start
  8.5 2.5 collective-permute-start.2
  11.0 19.2 %all_to_all.65 = f32[16,28,128]{2,1,0:T(8,128)} all-to-all(f32[16,28,128]{2,1,0:T(8,128)S(1)} %broadcast_in_dim.28), channel_id=1, replica_groups=mesh['zh'=2,'core'=2,'xh'=2,'xl'=2,'yh'=2,'yl'=2,'zc'=2,'zf'=2] {'zh','c..., dimensions={0} | all-to-all | bytes 458752 | tf_op jit(solution)/shard_map/all_to_all | solution.py:45
  31.1 2.3 collective-permute-done.refs_4_
  33.4 3.1 collective-permute-done.1.refs_5_
  36.5 2.2 collective-permute-done.3.refs_3_
  39.4 4.2 %all-to-all-start.1 = ((f32[16,28,128]{2,1,0:T(8,128)}), f32[16,28,128]{2,1,0:T(8,128)}, u32[]{:S(2)}, u32[]{:S(2)}) async-start(f32[16,28,128]{2,1,0:T(8,128)} %broadcast_in_dim.29), calls=%async_computation.1 | async-start | bytes 524288 | tf_op jit(solution)/shard_map/all_to_all | solution.py:45
  43.6 7.5 %all-to-all-done.1 = f32[16,28,128]{2,1,0:T(8,128)} async-done(((f32[16,28,128]{2,1,0:T(8,128)}), f32[16,28,128]{2,1,0:T(8,128)}, u32[]{:S(2)}, u32[]{:S(2)}) %all-to-all-start.1) | async-done | bytes 229408 | tf_op jit(solution)/shard_map/all_to_all | solution.py:45
  54.4 5.6 %all-to-all-start.2 = ((f32[4,2,128]{2,1,0:T(2,128)}), f32[4,2,128]{2,1,0:T(2,128)S(1)}, u32[]{:S(2)}, u32[]{:S(2)}) async-start(f32[4,2,128]{2,1,0:T(2,128)} %broadcast_in_dim.31), calls=%async_computation.2 | async-start | bytes 8192 | tf_op jit(solution)/shard_map/all_to_all | solution.py:45
  65.2 4.2 %all-to-all-start.3 = ((bf16[4,8,3072]{2,1,0:T(8,128)(2,1)}), bf16[4,8,3072]{2,1,0:T(8,128)(2,1)}, u32[]{:S(2)}, u32[]{:S(2)}) async-start(bf16[4,8,3072]{2,1,0:T(8,128)(2,1)} %broadcast_in_dim.32), calls=%async_computation.3 | async-start | bytes 393216 | tf_op jit(solution)/shard_map/all_to_all | solution.py:45
  70.5 4.4 %all-to-all-done.3 = bf16[4,8,3072]{2,1,0:T(8,128)(2,1)} async-done(((bf16[4,8,3072]{2,1,0:T(8,128)(2,1)}), bf16[4,8,3072]{2,1,0:T(8,128)(2,1)}, u32[]{:S(2)}, u32[]{:S(2)}) %all-to-all-start.3) | async-done | bytes 196640 | tf_op jit(solution)/shard_map/all_to_all | solution.py:45
  74.8 9.3 %collective-permute-done.4.refs_6_ = bf16[192,3072]{1,0:T(8,128)(2,1)} collective-permute-done((bf16[192,3072]{1,0:T(8,128)(2,1)}, bf16[192,3072]{1,0:T(8,128)(2,1)}, u32[]{:S(2)}, u32[]{:S(2)}) %collective-permute-start.4) | collective-permute-done | bytes 1179680 | tf_op jit(solution)/shard_map/ppermute | solution.py:28
  91.1 4.7 %collective-permute-done.9.refs_12_ = bf16[96,3072]{1,0:T(8,128)(2,1)} collective-permute-done((bf16[96,3072]{1,0:T(8,128)(2,1)}, bf16[96,3072]{1,0:T(8,128)(2,1)}, u32[]{:S(2)}, u32[]{:S(2)}) %collective-permute-start.9) | collective-permute-done | bytes 589856 | tf_op jit(solution)/shard_map/ppermute | solution.py:28
  96.8 19.1 %all-to-all-start.4 = ((bf16[4,8,3200]{2,1,0:T(8,128)(2,1)}), bf16[4,8,3200]{2,1,0:T(8,128)(2,1)}, u32[]{:S(2)}, u32[]{:S(2)}) async-start(bf16[4,8,3200]{2,1,0:T(8,128)(2,1)} %broadcast_in_dim.35), calls=%async_computation.4 | async-start | bytes 409600 | tf_op jit(solution)/shard_map/all_to_all | solution.py:45
  116.6 1.9 slice.87
  118.5 1.9 slice.88
  120.5 4.2 %all-to-all-done.4 = bf16[4,8,3200]{2,1,0:T(8,128)(2,1)} async-done(((bf16[4,8,3200]{2,1,0:T(8,128)(2,1)}), bf16[4,8,3200]{2,1,0:T(8,128)(2,1)}, u32[]{:S(2)}, u32[]{:S(2)}) %all-to-all-start.4) | async-done | bytes 204832 | tf_op jit(solution)/shard_map/all_to_all | solution.py:45
  126.2 2.5 collective-permute-start.17
  130.5 5.1 %shard_map.104 = (bf16[1280,3072]{1,0:T(8,128)(2,1)S(1)}, bf16[1280,3072]{1,0:T(8,128)(2,1)S(1)}) custom-call(bf16[192,3072]{1,0:T(8,128)(2,1)} %get-tuple-element.61.refs_0_, bf16[192,3072]{1,0:T(8,128)(2,1)} %get-tuple-element.60.refs_1_, bf16[192,3072]{1,0:T(8,128)(2,1)} %collective-permute-done.2.refs_2_, ...), custom_call_target="tpu_custom_call" | custom-call | bytes 31457280 | tf_op jit(solution)/shard_map/pallas_call | solution.py:118
  135.7 3.1 copy-done.1
  138.8 3.1 copy-done.6
  142.5 5.3 %all-to-all-start.5 = ((f32[16,4,2,128]{3,2,1,0:T(2,128)}), f32[16,4,2,128]{3,2,1,0:T(2,128)S(1)}, u32[]{:S(2)}, u32[]{:S(2)}) async-start(f32[16,4,2,128]{3,2,1,0:T(2,128)} %broadcast_in_dim.36), calls=%async_computation.5 | async-start | bytes 131072 | tf_op jit(solution)/shard_map/all_to_all | solution.py:45
  148.9 5.5 %all-to-all-done.5 = f32[16,4,2,128]{3,2,1,0:T(2,128)S(1)} async-done(((f32[16,4,2,128]{3,2,1,0:T(2,128)}), f32[16,4,2,128]{3,2,1,0:T(2,128)S(1)}, u32[]{:S(2)}, u32[]{:S(2)}) %all-to-all-start.5) | async-done | bytes 65568 | tf_op jit(solution)/shard_map/all_to_all | solution.py:45
  157.0 3.8 %copy-done.2 = bf16[1280,3072]{1,0:T(8,128)(2,1)S(1)} copy-done((bf16[1280,3072]{1,0:T(8,128)(2,1)S(1)}, bf16[1280,3072]{1,0:T(8,128)(2,1)}, u32[]{:S(2)}) %copy-start.2) | copy-done | bytes 7864344
  160.8 3.2 copy-done.7
  164.0 4.9 %shard_map.106 = bf16[64,3072]{1,0:T(8,128)(2,1)S(1)} custom-call(bf16[64,3072]{1,0:T(8,128)(2,1)S(1)} %bitcast.67, f32[3,3072]{1,0:T(4,128)S(1)} %reshape.70.mod_ref, bf16[1280,3072]{1,0:T(8,128)(2,1)S(1)} %copy-done.2, bf16[1280,3072]{1,0:T(8,128)(2,1)S(1)} %copy-done.7, bf16[256,3072]{1,0:T(8,128)(2,1)S(1)} %get-tuple-element.88.up_end, ...), custom_call_target="tpu_custom_call" | custom-call | flops 1207959552 | bytes 19660800 | tf_op jit(solution)/shard_map/pallas_call | solution.py:79
  168.9 16.5 %all_to_all.66.parts_ref = bf16[8,8,3072]{2,1,0:T(8,128)(2,1)} all-to-all(bf16[8,8,3072]{2,1,0:T(8,128)(2,1)S(1)} %bitcast.69), channel_id=1, replica_groups=mesh['zh'=2,'core'=2,'xh'=2,'xl'=2,'yh'=2,'yl'=2,'zc'=2,'zf'=2] {'xh','z..., dimensions={0} | all-to-all | bytes 786432 | tf_op jit(solution)/shard_map/all_to_all | solution.py:281
  187.2 4.8 %collective-permute-start.19 = (bf16[8,3200]{1,0:T(8,128)(2,1)}, bf16[8,3200]{1,0:T(8,128)(2,1)S(1)}, u32[]{:S(2)}, u32[]{:S(2)}) collective-permute-start(bf16[8,3200]{1,0:T(8,128)(2,1)} %shard_map.107), channel_id=1, source_target_pairs={{0,64},{2,66},{64,130},{66,128},{128,192},{130,194},{192,0},{194,2... | collective-permute-start | bytes 153608 | tf_op jit(solution)/shard_map/ppermute | solution.py:35
  194.3 13.6 %all_to_all.67 = bf16[8,8,3072]{2,1,0:T(8,128)(2,1)S(1)} all-to-all(bf16[8,8,3072]{2,1,0:T(8,128)(2,1)S(1)} %broadcast_in_dim.37), channel_id=1, replica_groups=mesh['zh'=2,'core'=2,'xh'=2,'xl'=2,'yh'=2,'yl'=2,'zc'=2,'zf'=2] {'xh','z..., dimensions={0} | all-to-all | bytes 786432 | tf_op jit(solution)/shard_map/all_to_all | solution.py:45
  207.9 3.2 copy-done.3
  211.1 3.2 copy-done.8
  215.8 4.9 %shard_map.108 = bf16[64,3072]{1,0:T(8,128)(2,1)S(1)} custom-call(bf16[64,3072]{1,0:T(8,128)(2,1)S(1)} %bitcast.70, f32[3,3072]{1,0:T(4,128)S(1)} %reshape.70.mod_ref, bf16[1280,3072]{1,0:T(8,128)(2,1)S(1)} %copy-done.3, bf16[1280,3072]{1,0:T(8,128)(2,1)S(1)} %copy-done.8, bf16[256,3072]{1,0:T(8,128)(2,1)S(1)} %get-tuple-element.88.up_end, ...), custom_call_target="tpu_custom_call" | custom-call | flops 1207959552 | bytes 19660800 | tf_op jit(solution)/shard_map/pallas_call | solution.py:79
  220.7 13.2 %all_to_all.68.parts_ref = bf16[8,8,3072]{2,1,0:T(8,128)(2,1)} all-to-all(bf16[8,8,3072]{2,1,0:T(8,128)(2,1)S(1)} %bitcast.71), channel_id=1, replica_groups=mesh['zh'=2,'core'=2,'xh'=2,'xl'=2,'yh'=2,'yl'=2,'zc'=2,'zf'=2] {'xh','z..., dimensions={0} | all-to-all | bytes 786432 | tf_op jit(solution)/shard_map/all_to_all | solution.py:281
  235.7 9.9 %collective-permute-start.20 = (bf16[8,3200]{1,0:T(8,128)(2,1)}, bf16[8,3200]{1,0:T(8,128)(2,1)S(1)}, u32[]{:S(2)}, u32[]{:S(2)}) collective-permute-start(bf16[8,3200]{1,0:T(8,128)(2,1)} %shard_map.109), channel_id=1, source_target_pairs={{0,64},{2,66},{64,130},{66,128},{128,192},{130,194},{192,0},{194,2... | collective-permute-start | bytes 153608 | tf_op jit(solution)/shard_map/ppermute | solution.py:35
  247.9 13.7 %all_to_all.69 = bf16[8,8,3072]{2,1,0:T(8,128)(2,1)S(1)} all-to-all(bf16[8,8,3072]{2,1,0:T(8,128)(2,1)S(1)} %broadcast_in_dim.38), channel_id=1, replica_groups=mesh['zh'=2,'core'=2,'xh'=2,'xl'=2,'yh'=2,'yl'=2,'zc'=2,'zf'=2] {'xh','z..., dimensions={0} | all-to-all | bytes 786432 | tf_op jit(solution)/shard_map/all_to_all | solution.py:45
  261.6 3.2 copy-done.4
  264.8 3.2 copy-done.9
  269.5 4.9 %shard_map.110 = bf16[64,3072]{1,0:T(8,128)(2,1)S(1)} custom-call(bf16[64,3072]{1,0:T(8,128)(2,1)S(1)} %bitcast.72, f32[3,3072]{1,0:T(4,128)S(1)} %reshape.70.mod_ref, bf16[1280,3072]{1,0:T(8,128)(2,1)S(1)} %copy-done.4, bf16[1280,3072]{1,0:T(8,128)(2,1)S(1)} %copy-done.9, bf16[256,3072]{1,0:T(8,128)(2,1)S(1)} %get-tuple-element.88.up_end, ...), custom_call_target="tpu_custom_call" | custom-call | flops 1207959552 | bytes 19660800 | tf_op jit(solution)/shard_map/pallas_call | solution.py:79
  274.4 14.9 %all_to_all.70.parts_ref = bf16[8,8,3072]{2,1,0:T(8,128)(2,1)} all-to-all(bf16[8,8,3072]{2,1,0:T(8,128)(2,1)S(1)} %bitcast.73), channel_id=1, replica_groups=mesh['zh'=2,'core'=2,'xh'=2,'xl'=2,'yh'=2,'yl'=2,'zc'=2,'zf'=2] {'xh','z..., dimensions={0} | all-to-all | bytes 786432 | tf_op jit(solution)/shard_map/all_to_all | solution.py:281
  291.1 5.8 %collective-permute-start.21 = (bf16[8,3200]{1,0:T(8,128)(2,1)}, bf16[8,3200]{1,0:T(8,128)(2,1)S(1)}, u32[]{:S(2)}, u32[]{:S(2)}) collective-permute-start(bf16[8,3200]{1,0:T(8,128)(2,1)} %shard_map.111), channel_id=1, source_target_pairs={{0,64},{2,66},{64,130},{66,128},{128,192},{130,194},{1,65},{3,67},... | collective-permute-start | bytes 153608 | tf_op jit(solution)/shard_map/ppermute | solution.py:35
  300.0 3.5 all-to-all-start.11
  303.5 14.4 %all-to-all-done.11 = bf16[8,8,3072]{2,1,0:T(8,128)(2,1)S(1)} async-done(((bf16[8,8,3072]{2,1,0:T(8,128)(2,1)}), bf16[8,8,3072]{2,1,0:T(8,128)(2,1)S(1)}, u32[]{:S(2)}, u32[]{:S(2)}) %all-to-all-start.11) | async-done | bytes 393248 | tf_op jit(solution)/shard_map/all_to_all | solution.py:45
  318.0 3.2 copy-done.5
  321.2 3.2 copy-done.10
  325.8 5.7 %shard_map.112 = bf16[64,3072]{1,0:T(8,128)(2,1)} custom-call(bf16[64,3072]{1,0:T(8,128)(2,1)S(1)} %bitcast.68, f32[3,3072]{1,0:T(4,128)S(1)} %reshape.70.mod_ref, bf16[1280,3072]{1,0:T(8,128)(2,1)S(1)} %copy-done.5, bf16[1280,3072]{1,0:T(8,128)(2,1)S(1)} %copy-done.10, bf16[256,3072]{1,0:T(8,128)(2,1)S(1)} %get-tuple-element.88.up_end, ...), custom_call_target="tpu_custom_call" | custom-call | flops 1207959552 | bytes 19660800 | tf_op jit(solution)/shard_map/pallas_call | solution.py:79
  331.5 3.6 %all-to-all-start.12 = ((bf16[8,8,3072]{2,1,0:T(8,128)(2,1)}), bf16[8,8,3072]{2,1,0:T(8,128)(2,1)S(1)}, u32[]{:S(2)}, u32[]{:S(2)}) async-start(bf16[8,8,3072]{2,1,0:T(8,128)(2,1)} %bitcast.29), calls=%async_computation.12 | async-start | bytes 786432 | tf_op jit(solution)/shard_map/all_to_all | solution.py:281
  335.9 12.6 %all-to-all-done.12.parts_ref = bf16[8,8,3072]{2,1,0:T(8,128)(2,1)S(1)} async-done(((bf16[8,8,3072]{2,1,0:T(8,128)(2,1)}), bf16[8,8,3072]{2,1,0:T(8,128)(2,1)S(1)}, u32[]{:S(2)}, u32[]{:S(2)}) %all-to-all-start.12) | async-done | bytes 393248 | tf_op jit(solution)/shard_map/all_to_all | solution.py:281
  351.0 2.8 collective-permute-start.24
  (130 shorter events, 55.6 us)
Async XLA Ops:
  0.6 52.8 %copy-start = (bf16[1,144,3584]{2,1,0:T(8,128)(2,1)S(1)}, bf16[1,144,3584]{2,1,0:T(8,128)(2,1)}, u32[]{:S(2)}) copy-start(bf16[1,144,3584]{2,1,0:T(8,128)(2,1)} %param.15) | copy-start | bytes 3096580
  4.9 28.5 %collective-permute-start = (bf16[192,3072]{1,0:T(8,128)(2,1)}, bf16[192,3072]{1,0:T(8,128)(2,1)S(1)}, u32[]{:S(2)}, u32[]{:S(2)}) collective-permute-start(bf16[192,3072]{1,0:T(8,128)(2,1)} %get-tuple-element.61.refs_0_), channel_id=1, source_target_pairs={{4,0},{8,4},{12,8},{0,12},{5,1},{9,5},{13,9},{1,13},{6,2},{10,6},{... | collective-permute-start | bytes 3538952 | tf_op jit(solution)/shard_map/ppermute | solution.py:28
  8.5 28.0 %collective-permute-start.1 = (bf16[192,3072]{1,0:T(8,128)(2,1)}, bf16[192,3072]{1,0:T(8,128)(2,1)S(1)}, u32[]{:S(2)}, u32[]{:S(2)}) collective-permute-start(bf16[192,3072]{1,0:T(8,128)(2,1)} %get-tuple-element.60.refs_1_), channel_id=1, source_target_pairs={{12,0},{0,4},{4,8},{8,12},{13,1},{1,5},{5,9},{9,13},{14,2},{2,6},{... | collective-permute-start | bytes 3538952 | tf_op jit(solution)/shard_map/ppermute | solution.py:28
  8.5 28.0 %collective-permute-start.2 = (bf16[192,3072]{1,0:T(8,128)(2,1)}, bf16[192,3072]{1,0:T(8,128)(2,1)}, u32[]{:S(2)}, u32[]{:S(2)}) collective-permute-start(bf16[192,3072]{1,0:T(8,128)(2,1)} %get-tuple-element.61.refs_0_), channel_id=1, source_target_pairs={{16,0},{32,16},{48,32},{0,48},{17,1},{33,17},{49,33},{1,49},{18,2}... | collective-permute-start | bytes 3538952 | tf_op jit(solution)/shard_map/ppermute | solution.py:28
  10.9 27.7 %collective-permute-start.3 = (bf16[192,3072]{1,0:T(8,128)(2,1)}, bf16[192,3072]{1,0:T(8,128)(2,1)}, u32[]{:S(2)}, u32[]{:S(2)}) collective-permute-start(bf16[192,3072]{1,0:T(8,128)(2,1)} %get-tuple-element.60.refs_1_), channel_id=1, source_target_pairs={{48,0},{0,16},{16,32},{32,48},{49,1},{1,17},{17,33},{33,49},{50,2}... | collective-permute-start | bytes 3538952 | tf_op jit(solution)/shard_map/ppermute | solution.py:28
  39.4 11.7 %all-to-all-start.1 = ((f32[16,28,128]{2,1,0:T(8,128)}), f32[16,28,128]{2,1,0:T(8,128)}, u32[]{:S(2)}, u32[]{:S(2)}) async-start(f32[16,28,128]{2,1,0:T(8,128)} %broadcast_in_dim.29), calls=%async_computation.1 | async-start | bytes 524288 | tf_op jit(solution)/shard_map/all_to_all | solution.py:45
  54.4 10.0 %all-to-all-start.2 = ((f32[4,2,128]{2,1,0:T(2,128)}), f32[4,2,128]{2,1,0:T(2,128)S(1)}, u32[]{:S(2)}, u32[]{:S(2)}) async-start(f32[4,2,128]{2,1,0:T(2,128)} %broadcast_in_dim.31), calls=%async_computation.2 | async-start | bytes 8192 | tf_op jit(solution)/shard_map/all_to_all | solution.py:45
  60.1 4.4 %copy-start.20 = (bf16[1,8,3072]{2,1,0:T(8,128)(2,1)S(1)}, bf16[1,8,3072]{2,1,0:T(8,128)(2,1)}, u32[]{:S(2)}) copy-start(bf16[1,8,3072]{2,1,0:T(8,128)(2,1)} %param.9) | copy-start | bytes 147460
  60.1 24.1 %collective-permute-start.4 = (bf16[192,3072]{1,0:T(8,128)(2,1)}, bf16[192,3072]{1,0:T(8,128)(2,1)}, u32[]{:S(2)}, u32[]{:S(2)}) collective-permute-start(bf16[192,3072]{1,0:T(8,128)(2,1)} %get-tuple-element.60.refs_1_), channel_id=1, source_target_pairs={{4,0},{8,4},{12,8},{0,12},{5,1},{9,5},{13,9},{1,13},{6,2},{10,6},{... | collective-permute-start | bytes 3538952 | tf_op jit(solution)/shard_map/ppermute | solution.py:28
  60.8 25.0 %collective-permute-start.5 = (bf16[192,3072]{1,0:T(8,128)(2,1)}, bf16[192,3072]{1,0:T(8,128)(2,1)}, u32[]{:S(2)}, u32[]{:S(2)}) collective-permute-start(bf16[192,3072]{1,0:T(8,128)(2,1)} %get-tuple-element.61.refs_0_), channel_id=1, source_target_pairs={{12,0},{0,4},{4,8},{8,12},{13,1},{1,5},{5,9},{9,13},{14,2},{2,6},{... | collective-permute-start | bytes 3538952 | tf_op jit(solution)/shard_map/ppermute | solution.py:28
  61.5 24.2 %collective-permute-start.6 = (bf16[192,3072]{1,0:T(8,128)(2,1)S(1)}, bf16[192,3072]{1,0:T(8,128)(2,1)}, u32[]{:S(2)}, u32[]{:S(2)}) collective-permute-start(bf16[192,3072]{1,0:T(8,128)(2,1)S(1)} %collective-permute-done.refs_4_), channel_id=1, source_target_pairs={{16,0},{32,16},{48,32},{0,48},{17,1},{33,17},{49,33},{1,49},{18,2}... | collective-permute-start | bytes 3538952 | tf_op jit(solution)/shard_map/ppermute | solution.py:28
  62.2 24.1 %collective-permute-start.7 = (bf16[192,3072]{1,0:T(8,128)(2,1)S(1)}, bf16[192,3072]{1,0:T(8,128)(2,1)}, u32[]{:S(2)}, u32[]{:S(2)}) collective-permute-start(bf16[192,3072]{1,0:T(8,128)(2,1)S(1)} %collective-permute-done.1.refs_5_), channel_id=1, source_target_pairs={{48,0},{0,16},{16,32},{32,48},{49,1},{1,17},{17,33},{33,49},{50,2}... | collective-permute-start | bytes 3538952 | tf_op jit(solution)/shard_map/ppermute | solution.py:28
  65.2 9.7 %all-to-all-start.3 = ((bf16[4,8,3072]{2,1,0:T(8,128)(2,1)}), bf16[4,8,3072]{2,1,0:T(8,128)(2,1)}, u32[]{:S(2)}, u32[]{:S(2)}) async-start(bf16[4,8,3072]{2,1,0:T(8,128)(2,1)} %broadcast_in_dim.32), calls=%async_computation.3 | async-start | bytes 393216 | tf_op jit(solution)/shard_map/all_to_all | solution.py:45
  69.3 20.1 %copy-start.24 = (s32[1,8]{1,0:T(1,128)S(1)}, s32[1,8]{1,0:T(1,128)}, u32[]{:S(2)}) copy-start(s32[1,8]{1,0:T(1,128)} %param.12) | copy-start | bytes 100
  69.4 20.4 %copy-start.23 = (bf16[1,8,3072]{2,1,0:T(8,128)(2,1)S(1)}, bf16[1,8,3072]{2,1,0:T(8,128)(2,1)}, u32[]{:S(2)}) copy-start(bf16[1,8,3072]{2,1,0:T(8,128)(2,1)} %param.11) | copy-start | bytes 147460
  69.4 26.7 %copy-start.25 = (s32[1,8]{1,0:T(1,128)S(1)}, s32[1,8]{1,0:T(1,128)}, u32[]{:S(2)}) copy-start(s32[1,8]{1,0:T(1,128)} %param.10) | copy-start | bytes 100
  86.2 9.5 %collective-permute-start.9 = (bf16[96,3072]{1,0:T(8,128)(2,1)}, bf16[96,3072]{1,0:T(8,128)(2,1)}, u32[]{:S(2)}, u32[]{:S(2)}) collective-permute-start(bf16[96,3072]{1,0:T(8,128)(2,1)} %get-tuple-element.63), channel_id=1, source_target_pairs={{4,0},{8,4},{12,8},{0,12},{5,1},{9,5},{13,9},{1,13},{6,2},{10,6},{... | collective-permute-start | bytes 1769480 | tf_op jit(solution)/shard_map/ppermute | solution.py:28
  88.0 36.7 %collective-permute-start.13 = (bf16[192,3072]{1,0:T(8,128)(2,1)}, bf16[192,3072]{1,0:T(8,128)(2,1)}, u32[]{:S(2)}, u32[]{:S(2)}) collective-permute-start(bf16[192,3072]{1,0:T(8,128)(2,1)} %collective-permute-done.5.refs_7_), channel_id=1, source_target_pairs={{16,0},{32,16},{48,32},{0,48},{17,1},{33,17},{49,33},{1,49},{18,2}... | collective-permute-start | bytes 3538952 | tf_op jit(solution)/shard_map/ppermute | solution.py:28
  88.2 36.4 %collective-permute-start.14 = (bf16[192,3072]{1,0:T(8,128)(2,1)}, bf16[192,3072]{1,0:T(8,128)(2,1)}, u32[]{:S(2)}, u32[]{:S(2)}) collective-permute-start(bf16[192,3072]{1,0:T(8,128)(2,1)} %collective-permute-done.4.refs_6_), channel_id=1, source_target_pairs={{48,0},{0,16},{16,32},{32,48},{49,1},{1,17},{17,33},{33,49},{50,2}... | collective-permute-start | bytes 3538952 | tf_op jit(solution)/shard_map/ppermute | solution.py:28
  89.4 26.5 %collective-permute-start.10 = (bf16[96,3072]{1,0:T(8,128)(2,1)}, bf16[96,3072]{1,0:T(8,128)(2,1)}, u32[]{:S(2)}, u32[]{:S(2)}) collective-permute-start(bf16[96,3072]{1,0:T(8,128)(2,1)} %get-tuple-element.64), channel_id=1, source_target_pairs={{4,0},{8,4},{12,8},{0,12},{5,1},{9,5},{13,9},{1,13},{6,2},{10,6},{... | collective-permute-start | bytes 1769480 | tf_op jit(solution)/shard_map/ppermute | solution.py:28
  89.8 34.9 %collective-permute-start.11 = (bf16[96,3072]{1,0:T(8,128)(2,1)}, bf16[96,3072]{1,0:T(8,128)(2,1)}, u32[]{:S(2)}, u32[]{:S(2)}) collective-permute-start(bf16[96,3072]{1,0:T(8,128)(2,1)} %get-tuple-element.65), channel_id=1, source_target_pairs={{12,0},{0,4},{4,8},{8,12},{13,1},{1,5},{5,9},{9,13},{14,2},{2,6},{... | collective-permute-start | bytes 1769480 | tf_op jit(solution)/shard_map/ppermute | solution.py:28
  95.7 28.9 %collective-permute-start.12 = (bf16[96,3072]{1,0:T(8,128)(2,1)}, bf16[96,3072]{1,0:T(8,128)(2,1)}, u32[]{:S(2)}, u32[]{:S(2)}) collective-permute-start(bf16[96,3072]{1,0:T(8,128)(2,1)} %get-tuple-element.66), channel_id=1, source_target_pairs={{12,0},{0,4},{4,8},{8,12},{13,1},{1,5},{5,9},{9,13},{14,2},{2,6},{... | collective-permute-start | bytes 1769480 | tf_op jit(solution)/shard_map/ppermute | solution.py:28
  96.8 27.9 %all-to-all-start.4 = ((bf16[4,8,3200]{2,1,0:T(8,128)(2,1)}), bf16[4,8,3200]{2,1,0:T(8,128)(2,1)}, u32[]{:S(2)}, u32[]{:S(2)}) async-start(bf16[4,8,3200]{2,1,0:T(8,128)(2,1)} %broadcast_in_dim.35), calls=%async_computation.4 | async-start | bytes 409600 | tf_op jit(solution)/shard_map/all_to_all | solution.py:45
  115.9 12.8 %collective-permute-start.8 = (bf16[4,8,3072]{2,1,0:T(8,128)(2,1)}, bf16[4,8,3072]{2,1,0:T(8,128)(2,1)}, u32[]{:S(2)}, u32[]{:S(2)}) collective-permute-start(bf16[4,8,3072]{2,1,0:T(8,128)(2,1)} %all-to-all-done.3), channel_id=1, source_target_pairs={{0,32},{32,0},{1,33},{33,1},{2,34},{34,2},{3,35},{35,3},{4,36},{36... | collective-permute-start | bytes 589832 | tf_op jit(solution)/shard_map/ppermute | solution.py:203
  124.6 30.4 %collective-permute-start.15 = (bf16[96,3072]{1,0:T(8,128)(2,1)}, bf16[96,3072]{1,0:T(8,128)(2,1)}, u32[]{:S(2)}, u32[]{:S(2)}) collective-permute-start(bf16[96,3072]{1,0:T(8,128)(2,1)} %collective-permute-done.9.refs_12_), channel_id=1, source_target_pairs={{16,0},{32,16},{48,32},{0,48},{17,1},{33,17},{49,33},{1,49},{18,2}... | collective-permute-start | bytes 1769480 | tf_op jit(solution)/shard_map/ppermute | solution.py:28
  124.7 30.3 %collective-permute-start.16 = (bf16[96,3072]{1,0:T(8,128)(2,1)}, bf16[96,3072]{1,0:T(8,128)(2,1)}, u32[]{:S(2)}, u32[]{:S(2)}) collective-permute-start(bf16[96,3072]{1,0:T(8,128)(2,1)} %collective-permute-done.11.refs_14_.refs_0_), channel_id=1, source_target_pairs={{48,0},{0,16},{16,32},{32,48},{49,1},{1,17},{17,33},{33,49},{50,2}... | collective-permute-start | bytes 1769480 | tf_op jit(solution)/shard_map/ppermute | solution.py:28
  126.2 28.9 %collective-permute-start.17 = (bf16[96,3072]{1,0:T(8,128)(2,1)}, bf16[96,3072]{1,0:T(8,128)(2,1)}, u32[]{:S(2)}, u32[]{:S(2)}) collective-permute-start(bf16[96,3072]{1,0:T(8,128)(2,1)} %slice.87), channel_id=1, source_target_pairs={{4,0},{8,4},{12,8},{0,12},{5,1},{9,5},{13,9},{1,13},{6,2},{10,6},{... | collective-permute-start | bytes 1769480 | tf_op jit(solution)/shard_map/ppermute | solution.py:28
  128.7 26.4 %collective-permute-start.18 = (bf16[96,3072]{1,0:T(8,128)(2,1)}, bf16[96,3072]{1,0:T(8,128)(2,1)}, u32[]{:S(2)}, u32[]{:S(2)}) collective-permute-start(bf16[96,3072]{1,0:T(8,128)(2,1)} %slice.88), channel_id=1, source_target_pairs={{12,0},{0,4},{4,8},{8,12},{13,1},{1,5},{5,9},{9,13},{14,2},{2,6},{... | collective-permute-start | bytes 1769480 | tf_op jit(solution)/shard_map/ppermute | solution.py:28
  142.5 11.8 %all-to-all-start.5 = ((f32[16,4,2,128]{3,2,1,0:T(2,128)}), f32[16,4,2,128]{3,2,1,0:T(2,128)S(1)}, u32[]{:S(2)}, u32[]{:S(2)}) async-start(f32[16,4,2,128]{3,2,1,0:T(2,128)} %broadcast_in_dim.36), calls=%async_computation.5 | async-start | bytes 131072 | tf_op jit(solution)/shard_map/all_to_all | solution.py:45
  157.0 12.0 %copy-start.11 = (bf16[256,3072]{1,0:T(8,128)(2,1)}, bf16[256,3072]{1,0:T(8,128)(2,1)S(1)}, u32[]{:S(2)}) copy-start(bf16[256,3072]{1,0:T(8,128)(2,1)S(1)} %get-tuple-element.89.down_end) | copy-start | bytes 4718596
  157.0 3.8 %copy-start.2 = (bf16[1280,3072]{1,0:T(8,128)(2,1)S(1)}, bf16[1280,3072]{1,0:T(8,128)(2,1)}, u32[]{:S(2)}) copy-start(bf16[1280,3072]{1,0:T(8,128)(2,1)} %copy-done.1) | copy-start | bytes 23592964
  160.8 3.2 copy-start.7
  187.2 6.3 %collective-permute-start.19 = (bf16[8,3200]{1,0:T(8,128)(2,1)}, bf16[8,3200]{1,0:T(8,128)(2,1)S(1)}, u32[]{:S(2)}, u32[]{:S(2)}) collective-permute-start(bf16[8,3200]{1,0:T(8,128)(2,1)} %shard_map.107), channel_id=1, source_target_pairs={{0,64},{2,66},{64,130},{66,128},{128,192},{130,194},{192,0},{194,2... | collective-permute-start | bytes 153608 | tf_op jit(solution)/shard_map/ppermute | solution.py:35
  194.3 26.4 %copy-start.18 = (bf16[8,3200]{1,0:T(8,128)(2,1)}, bf16[8,3200]{1,0:T(8,128)(2,1)S(1)}, u32[]{:S(2)}) copy-start(bf16[8,3200]{1,0:T(8,128)(2,1)S(1)} %bitcast_select_fusion.1.waiting_ref) | copy-start | bytes 153604
  207.9 3.2 copy-start.3
  235.7 11.4 %collective-permute-start.20 = (bf16[8,3200]{1,0:T(8,128)(2,1)}, bf16[8,3200]{1,0:T(8,128)(2,1)S(1)}, u32[]{:S(2)}, u32[]{:S(2)}) collective-permute-start(bf16[8,3200]{1,0:T(8,128)(2,1)} %shard_map.109), channel_id=1, source_target_pairs={{0,64},{2,66},{64,130},{66,128},{128,192},{130,194},{192,0},{194,2... | collective-permute-start | bytes 153608 | tf_op jit(solution)/shard_map/ppermute | solution.py:35
  247.9 26.5 %copy-start.19 = (bf16[8,3200]{1,0:T(8,128)(2,1)}, bf16[8,3200]{1,0:T(8,128)(2,1)S(1)}, u32[]{:S(2)}) copy-start(bf16[8,3200]{1,0:T(8,128)(2,1)S(1)} %bitcast_select_fusion.2.waiting_ref) | copy-start | bytes 153604
  261.6 3.2 copy-start.4
  264.8 3.2 copy-start.9
  291.1 7.3 %collective-permute-start.21 = (bf16[8,3200]{1,0:T(8,128)(2,1)}, bf16[8,3200]{1,0:T(8,128)(2,1)S(1)}, u32[]{:S(2)}, u32[]{:S(2)}) collective-permute-start(bf16[8,3200]{1,0:T(8,128)(2,1)} %shard_map.111), channel_id=1, source_target_pairs={{0,64},{2,66},{64,130},{66,128},{128,192},{130,194},{1,65},{3,67},... | collective-permute-start | bytes 153608 | tf_op jit(solution)/shard_map/ppermute | solution.py:35
  299.2 32.3 %copy-start.17 = (bf16[8,3200]{1,0:T(8,128)(2,1)}, bf16[8,3200]{1,0:T(8,128)(2,1)S(1)}, u32[]{:S(2)}) copy-start(bf16[8,3200]{1,0:T(8,128)(2,1)S(1)} %bitcast_select_fusion.waiting_ref) | copy-start | bytes 153604
  300.0 18.0 %all-to-all-start.11 = ((bf16[8,8,3072]{2,1,0:T(8,128)(2,1)}), bf16[8,8,3072]{2,1,0:T(8,128)(2,1)S(1)}, u32[]{:S(2)}, u32[]{:S(2)}) async-start(bf16[8,8,3072]{2,1,0:T(8,128)(2,1)} %broadcast_in_dim.39), calls=%async_computation.11 | async-start | bytes 786432 | tf_op jit(solution)/shard_map/all_to_all | solution.py:45
  317.9 3.2 copy-start.5
  331.5 24.3 %copy-start.22 = (bf16[8,3200]{1,0:T(8,128)(2,1)S(1)}, bf16[8,3200]{1,0:T(8,128)(2,1)}, u32[]{:S(2)}) copy-start(bf16[8,3200]{1,0:T(8,128)(2,1)} %shard_map.111) | copy-start | bytes 153604
  331.5 17.0 %all-to-all-start.12 = ((bf16[8,8,3072]{2,1,0:T(8,128)(2,1)}), bf16[8,8,3072]{2,1,0:T(8,128)(2,1)S(1)}, u32[]{:S(2)}, u32[]{:S(2)}) async-start(bf16[8,8,3072]{2,1,0:T(8,128)(2,1)} %bitcast.29), calls=%async_computation.12 | async-start | bytes 786432 | tf_op jit(solution)/shard_map/all_to_all | solution.py:281
  351.0 5.6 %collective-permute-start.24 = (bf16[8,3200]{1,0:T(8,128)(2,1)}, bf16[8,3200]{1,0:T(8,128)(2,1)S(1)}, u32[]{:S(2)}, u32[]{:S(2)}) collective-permute-start(bf16[8,3200]{1,0:T(8,128)(2,1)} %shard_map.113), channel_id=1, source_target_pairs={{0,64},{2,66},{64,128},{66,130},{128,194},{130,192},{1,65},{3,67},... | collective-permute-start | bytes 153608 | tf_op jit(solution)/shard_map/ppermute | solution.py:35
  354.6 3.1 collective-permute-start.23
  355.9 1.8 collective-permute-start.22
  (10 other events, 20.1 us)

commit v3 on v2

--- a/solution.py
+++ b/solution.py
@@ -147,6 +147,7 @@
         out_shape=jax.ShapeDtypeStruct(waiting.shape, waiting.dtype),
         in_specs=[whole] * 3,
         out_specs=whole,
+        compiler_params=pltpu.CompilerParams(vmem_limit_bytes=4 * 1024 * 1024),
         cost_estimate=pl.CostEstimate(
             flops=parts.size, bytes_accessed=2 * parts.size, transcendentals=0
         ),
@@ -170,9 +171,11 @@
     xa = from_neighbour(first, "x", 1)
     xb = from_neighbour(second, "x", -1)
     partial = jnp.sum(exchange(partial, SECTION + LINE), axis=0)
-
-    first, second, yp_first, ym_second, xa, xb, partial = together(
-        (first, second, yp_first, ym_second, xa, xb, partial)
+    entering = exchange(after(arriving, partial), SECTION)
+    entering = [entering[section] for section in range(SECTIONS)]
+
+    first, second, yp_first, ym_second, xa, xb, partial, entering = together(
+        (first, second, yp_first, ym_second, xa, xb, partial, entering)
     )
     pooled = jnp.sum(exchange(partial, PLANE), axis=0)
 
@@ -201,12 +204,13 @@
     xa_ym = from_neighbour(ym_first, "x", 1)
     xb_yp = from_neighbour(yp_second, "x", -1)
     theirs = lax.ppermute(mine, "xh", [(0, 1), (1, 0)])
-    entering = exchange(after(arriving, mine), SECTION)
+    modes = exchange(line, PLANE)
+    modes = modes.reshape(-1, rows * LANES)[:, :columns].reshape(3, -1)
     xa_yp_down = xa_yp[middle:]
     xb_ym_down = xb_ym[middle:]
 
-    y2, xa_ym, xb_yp, xa_yp_down, xb_ym_down, entering, line = together(
-        (y2, xa_ym, xb_yp, xa_yp_down, xb_ym_down, entering, line)
+    y2, xa_ym, xb_yp, xa_yp_down, xb_ym_down, modes = together(
+        (y2, xa_ym, xb_yp, xa_yp_down, xb_ym_down, modes)
     )
     xa_y2_up = from_neighbour(y2[0], "x", 1)
     xb_y2_up = from_neighbour(y2[2], "x", -1)
@@ -226,8 +230,6 @@
     plan += [(count + which, 0, middle, which, count * middle) for which in (0, 1)]
     plan += [(count + 2 + which, 0, cut, which, main - cut) for which in (0, 1)]
     up_rows, down_rows = place(plan, whole + y2, main)
-    modes = exchange(after(line, up_rows), PLANE)
-    modes = modes.reshape(-1, rows * LANES)[:, :columns].reshape(3, -1)
     upper = lax.axis_index("xh") == 1
     gathered = jnp.stack([jnp.where(upper, theirs, mine), jnp.where(upper, mine, theirs)])
     plan = [(which, cut, middle - cut, which, 0) for which in (0, 1)]
@@ -272,7 +274,10 @@
         travelling_inputs[0],
         arriving,
     )
-    gathered, waiting, gate = lax.optimization_barrier((gathered, waiting, mod[2:]))
+    is_third = section_id == 2
+    gathered, waiting, gate, entering, is_first, is_third = lax.optimization_barrier(
+        (gathered, waiting, mod[2:], entering, is_first, is_third)
+    )
     moves = []
     for tick in range(SECTIONS):
         if tick:
@@ -292,7 +297,7 @@
         waiting = jnp.where(is_first, entering[tick], moves[tick])
     sent = jnp.where(is_first, moves[1], produced)
     second = between_sections(sent, [(0, 1, 0), (last, last, 1)])
-    done = jnp.where(is_first, moves[0], jnp.where(section_id == 2, third, second))
+    done = jnp.where(is_first, moves[0], jnp.where(is_third, third, second))
     return done[None, :, :breadth], waiting[None, :, :breadth]
 
 

time: 360 us -> 327 us (0.908)
  local copies, waits for them, and re-layouts: 51.5 us -> 16.4 us
  Pallas kernels: 34.4 us -> 26.2 us
  other arithmetic: 12.2 us -> 5.63 us
  blocking collectives: 91.1 us -> 97.2 us
  waiting for transfers between devices: 77.5 us -> 83.3 us
  starting transfers between devices: 88.8 us -> 93.6 us
    unnamed x53 -> x23, local copies, waits for them, and re-layouts: 37.9 us -> 1.81 us
    ppermute x18, waiting for transfers between devices: 23.6 us -> 52.5 us  [from_neighbour(): return lax.ppermute(block, (axis + 'h', axis + 'l'), route)]
    ppermute x6, starting transfers between devices: 25.2 us -> 43.2 us  [between_sections(): return lax.ppermute(block, SECTION + ('zc',), route)]
    all_to_all x1 -> x0, waiting for transfers between devices: 12.6 us -> none  [per_device(): lax.all_to_all(partial.reshape(GROUP_SIZE, tokens, breadth), GROUP, 0, 0)]
    all_to_all x3 -> x4, blocking collectives: 44.6 us -> 56.4 us  [per_device(): lax.all_to_all(partial.reshape(GROUP_SIZE, tokens, breadth), GROUP, 0, 0)]
    all_to_all x6, waiting for transfers between devices: 36.3 us -> 25.1 us  [exchange(): return lax.all_to_all(copies, axes, 0, 0)]
    all_to_all x6, starting transfers between devices: 41.9 us -> 31.9 us  [exchange(): return lax.all_to_all(copies, axes, 0, 0)]
    pallas_call x4, Pallas kernels: 6.92 us -> 0.35 us  [close(): pl.pallas_call(close_kernel, out_shape=jax.ShapeDtypeStruct(waiting.shape...]
  transfers between devices with their start and end apart: 32 -> 31, of which waited for: 18 -> 20; matrix products, arithmetic and copies ran while one was open for 4% -> 4% of each run, Pallas kernels for 1% -> 1%
where the time goes in v3:
time: 327 us; the launch traced here: 325 us
  blocking collectives  97.2 us (30%)
  starting transfers between devices  93.6 us (29%)
  waiting for transfers between devices  83.3 us (25%)
  Pallas kernels  26.2 us (8%)
  local copies, waits for them, and re-layouts  16.4 us (5%)
  other arithmetic  5.63 us (2%)
    all_to_all x4, blocking collectives, per_device(): lax.all_to_all(partial.reshape(GROUP_SIZE, tokens, breadth), GROUP, 0, 0)  56.4 us
    ppermute x18, waiting for transfers between devices, from_neighbour(): return lax.ppermute(block, (axis + 'h', axis + 'l'), route)  52.5 us
    ppermute x6, starting transfers between devices, between_sections(): return lax.ppermute(block, SECTION + ('zc',), route)  43.2 us
    all_to_all x3, blocking collectives, exchange(): return lax.all_to_all(copies, axes, 0, 0)  40.8 us
    all_to_all x6, starting transfers between devices, exchange(): return lax.all_to_all(copies, axes, 0, 0)  31.9 us
    all_to_all x6, waiting for transfers between devices, exchange(): return lax.all_to_all(copies, axes, 0, 0)  25.1 us
    pallas_call x4, Pallas kernels, layer(): pl.pallas_call(layer_kernel, out_shape=jax.ShapeDtypeStruct((rows, breadt...  19.8 us
    ppermute x18, starting transfers between devices, from_neighbour(): return lax.ppermute(block, (axis + 'h', axis + 'l'), route)  17.2 us
  transfers between devices with their start and end apart: 31, of which 20 were waited for; matrix products, arithmetic and copies ran while one was open for 4% of the time, Pallas kernels for 1%

profile of v3, /device:TPU:1, one launch (start us, length us, event | category | flops | bytes accessed | tf_op | source)
XLA Modules:
  0.0 325.1 jit_solution(17478383742737100099)
XLA Ops:
  0.7 1.5 slice_bitcast_fusion
  3.3 1.6 pad_maximum_fusion
  5.7 10.0 %all-to-all-start = ((f32[16,28,128]{2,1,0:T(8,128)}), f32[16,28,128]{2,1,0:T(8,128)S(1)}, u32[]{:S(2)}, u32[]{:S(2)}) async-start(f32[16,28,128]{2,1,0:T(8,128)} %broadcast_in_dim.28), calls=%async_computation | async-start | bytes 524288 | tf_op jit(solution)/shard_map/all_to_all | solution.py:45
  15.8 9.5 %all-to-all-done = f32[16,28,128]{2,1,0:T(8,128)S(1)} async-done(((f32[16,28,128]{2,1,0:T(8,128)}), f32[16,28,128]{2,1,0:T(8,128)S(1)}, u32[]{:S(2)}, u32[]{:S(2)}) %all-to-all-start) | async-done | bytes 229408 | tf_op jit(solution)/shard_map/all_to_all | solution.py:45
  26.0 4.8 %all-to-all-start.1 = ((bf16[4,8,3200]{2,1,0:T(8,128)(2,1)}), bf16[4,8,3200]{2,1,0:T(8,128)(2,1)}, u32[]{:S(2)}, u32[]{:S(2)}) async-start(bf16[4,8,3200]{2,1,0:T(8,128)(2,1)} %broadcast_in_dim.30), calls=%async_computation.1 | async-start | bytes 409600 | tf_op jit(solution)/shard_map/all_to_all | solution.py:45
  30.8 2.7 collective-permute-start
  33.5 2.5 collective-permute-start.2
  36.0 3.5 %all-to-all-done.1 = bf16[4,8,3200]{2,1,0:T(8,128)(2,1)} async-done(((bf16[4,8,3200]{2,1,0:T(8,128)(2,1)}), bf16[4,8,3200]{2,1,0:T(8,128)(2,1)}, u32[]{:S(2)}, u32[]{:S(2)}) %all-to-all-start.1) | async-done | bytes 204832 | tf_op jit(solution)/shard_map/all_to_all | solution.py:45
  39.5 1.5 slice_bitcast_fusion.4
  41.1 18.2 %collective-permute-done.refs_4_ = bf16[192,3072]{1,0:T(8,128)(2,1)S(1)} collective-permute-done((bf16[192,3072]{1,0:T(8,128)(2,1)}, bf16[192,3072]{1,0:T(8,128)(2,1)S(1)}, u32[]{:S(2)}, u32[]{:S(2)}) %collective-permute-start) | collective-permute-done | bytes 1179680 | tf_op jit(solution)/shard_map/ppermute | solution.py:28
  59.2 3.1 collective-permute-done.1.refs_5_
  62.3 2.2 collective-permute-done.3.refs_3_
  65.3 4.2 %all-to-all-start.2 = ((f32[16,28,128]{2,1,0:T(8,128)}), f32[16,28,128]{2,1,0:T(8,128)}, u32[]{:S(2)}, u32[]{:S(2)}) async-start(f32[16,28,128]{2,1,0:T(8,128)} %broadcast_in_dim.31), calls=%async_computation.2 | async-start | bytes 524288 | tf_op jit(solution)/shard_map/all_to_all | solution.py:45
  69.5 7.3 %all-to-all-done.2 = f32[16,28,128]{2,1,0:T(8,128)} async-done(((f32[16,28,128]{2,1,0:T(8,128)}), f32[16,28,128]{2,1,0:T(8,128)}, u32[]{:S(2)}, u32[]{:S(2)}) %all-to-all-start.2) | async-done | bytes 229408 | tf_op jit(solution)/shard_map/all_to_all | solution.py:45
  80.1 3.7 %all-to-all-start.3 = ((f32[4,2,128]{2,1,0:T(2,128)}), f32[4,2,128]{2,1,0:T(2,128)S(1)}, u32[]{:S(2)}, u32[]{:S(2)}) async-start(f32[4,2,128]{2,1,0:T(2,128)} %broadcast_in_dim.33), calls=%async_computation.3 | async-start | bytes 8192 | tf_op jit(solution)/shard_map/all_to_all | solution.py:45
  88.9 4.1 %all-to-all-start.4 = ((bf16[4,8,3072]{2,1,0:T(8,128)(2,1)}), bf16[4,8,3072]{2,1,0:T(8,128)(2,1)}, u32[]{:S(2)}, u32[]{:S(2)}) async-start(bf16[4,8,3072]{2,1,0:T(8,128)(2,1)} %broadcast_in_dim.34), calls=%async_computation.4 | async-start | bytes 393216 | tf_op jit(solution)/shard_map/all_to_all | solution.py:45
  94.2 4.4 %all-to-all-done.4 = bf16[4,8,3072]{2,1,0:T(8,128)(2,1)} async-done(((bf16[4,8,3072]{2,1,0:T(8,128)(2,1)}), bf16[4,8,3072]{2,1,0:T(8,128)(2,1)}, u32[]{:S(2)}, u32[]{:S(2)}) %all-to-all-start.4) | async-done | bytes 196640 | tf_op jit(solution)/shard_map/all_to_all | solution.py:45
  98.6 9.9 %collective-permute-done.4.refs_6_ = bf16[192,3072]{1,0:T(8,128)(2,1)} collective-permute-done((bf16[192,3072]{1,0:T(8,128)(2,1)}, bf16[192,3072]{1,0:T(8,128)(2,1)}, u32[]{:S(2)}, u32[]{:S(2)}) %collective-permute-start.4) | collective-permute-done | bytes 1179680 | tf_op jit(solution)/shard_map/ppermute | solution.py:28
  108.5 1.6 collective-permute-done.5.refs_7_
  111.2 1.7 collective-permute-start.9
  114.3 1.5 collective-permute-start.11
  115.8 5.8 %collective-permute-done.9.refs_12_ = bf16[96,3072]{1,0:T(8,128)(2,1)} collective-permute-done((bf16[96,3072]{1,0:T(8,128)(2,1)}, bf16[96,3072]{1,0:T(8,128)(2,1)}, u32[]{:S(2)}, u32[]{:S(2)}) %collective-permute-start.9) | collective-permute-done | bytes 589856 | tf_op jit(solution)/shard_map/ppermute | solution.py:28
  123.0 5.1 %all-to-all-start.5 = ((f32[16,4,2,128]{3,2,1,0:T(2,128)}), f32[16,4,2,128]{3,2,1,0:T(2,128)}, u32[]{:S(2)}, u32[]{:S(2)}) async-start(f32[16,4,2,128]{3,2,1,0:T(2,128)} %broadcast_in_dim.36), calls=%async_computation.5 | async-start | bytes 131072 | tf_op jit(solution)/shard_map/all_to_all | solution.py:45
  128.0 6.2 %collective-permute-done.10.refs_13_ = bf16[96,3072]{1,0:T(8,128)(2,1)} collective-permute-done((bf16[96,3072]{1,0:T(8,128)(2,1)}, bf16[96,3072]{1,0:T(8,128)(2,1)}, u32[]{:S(2)}, u32[]{:S(2)}) %collective-permute-start.10) | collective-permute-done | bytes 589856 | tf_op jit(solution)/shard_map/ppermute | solution.py:28
  135.5 1.9 slice.91
  137.5 1.9 slice.92
  139.4 1.5 copy.19
  143.4 2.2 collective-permute-start.17
  146.8 4.9 %shard_map.104 = (bf16[1280,3072]{1,0:T(8,128)(2,1)S(1)}, bf16[1280,3072]{1,0:T(8,128)(2,1)S(1)}) custom-call(bf16[192,3072]{1,0:T(8,128)(2,1)} %get-tuple-element.70.refs_0_, bf16[192,3072]{1,0:T(8,128)(2,1)S(1)} %copy-done.1, bf16[192,3072]{1,0:T(8,128)(2,1)} %collective-permute-done.2.refs_2_, bf16[192,3072]{1,0:T(8,128)(2,1)} %collective-permute-done.3.refs_3_, ...), custom_call_target="tpu_custom_call" | custom-call | bytes 31457280 | tf_op jit(solution)/shard_map/pallas_call | solution.py:118
  153.5 2.5 collective-permute-done.18.refs_5_
  157.2 4.9 %shard_map.106 = bf16[64,3072]{1,0:T(8,128)(2,1)S(1)} custom-call(bf16[64,3072]{1,0:T(8,128)(2,1)S(1)} %bitcast.67, f32[3,3072]{1,0:T(4,128)S(1)} %reshape.70.mod_ref, bf16[1280,3072]{1,0:T(8,128)(2,1)S(1)} %get-tuple-element.96.up, bf16[1280,3072]{1,0:T(8,128)(2,1)S(1)} %get-tuple-element.97.down, bf16[256,3072]{1,0:T(8,128)(2,1)S(1)} %get-tuple-element.100.up_end, ...), custom_call_target="tpu_custom_call" | custom-call | flops 1207959552 | bytes 19660800 | tf_op jit(solution)/shard_map/pallas_call | solution.py:79
  162.2 16.0 %all_to_all.65.parts_ref = bf16[8,8,3072]{2,1,0:T(8,128)(2,1)S(1)} all-to-all(bf16[8,8,3072]{2,1,0:T(8,128)(2,1)S(1)} %bitcast.70), channel_id=1, replica_groups=mesh['zh'=2,'core'=2,'xh'=2,'xl'=2,'yh'=2,'yl'=2,'zc'=2,'zf'=2] {'xh','z..., dimensions={0} | all-to-all | bytes 786432 | tf_op jit(solution)/shard_map/all_to_all | solution.py:286
  178.2 12.7 %collective-permute-start.19 = (bf16[8,3200]{1,0:T(8,128)(2,1)S(1)}, bf16[8,3200]{1,0:T(8,128)(2,1)S(1)}, u32[]{:S(2)}, u32[]{:S(2)}) collective-permute-start(bf16[8,3200]{1,0:T(8,128)(2,1)S(1)} %shard_map.107), channel_id=1, source_target_pairs={{0,64},{2,66},{64,130},{66,128},{128,192},{130,194},{192,0},{194,2... | collective-permute-start | bytes 153608 | tf_op jit(solution)/shard_map/ppermute | solution.py:35
  192.3 13.8 %all_to_all.66 = bf16[8,8,3072]{2,1,0:T(8,128)(2,1)S(1)} all-to-all(bf16[8,8,3072]{2,1,0:T(8,128)(2,1)S(1)} %broadcast_in_dim.37), channel_id=1, replica_groups=mesh['zh'=2,'core'=2,'xh'=2,'xl'=2,'yh'=2,'yl'=2,'zc'=2,'zf'=2] {'xh','z..., dimensions={0} | all-to-all | bytes 786432 | tf_op jit(solution)/shard_map/all_to_all | solution.py:45
  206.1 4.9 %shard_map.108 = bf16[64,3072]{1,0:T(8,128)(2,1)S(1)} custom-call(bf16[64,3072]{1,0:T(8,128)(2,1)S(1)} %bitcast.71, f32[3,3072]{1,0:T(4,128)S(1)} %reshape.70.mod_ref, bf16[1280,3072]{1,0:T(8,128)(2,1)S(1)} %get-tuple-element.96.up, bf16[1280,3072]{1,0:T(8,128)(2,1)S(1)} %get-tuple-element.97.down, bf16[256,3072]{1,0:T(8,128)(2,1)S(1)} %get-tuple-element.100.up_end, ...), custom_call_target="tpu_custom_call" | custom-call | flops 1207959552 | bytes 19660800 | tf_op jit(solution)/shard_map/pallas_call | solution.py:79
  211.0 15.2 %all_to_all.67.parts_ref = bf16[8,8,3072]{2,1,0:T(8,128)(2,1)S(1)} all-to-all(bf16[8,8,3072]{2,1,0:T(8,128)(2,1)S(1)} %bitcast.72), channel_id=1, replica_groups=mesh['zh'=2,'core'=2,'xh'=2,'xl'=2,'yh'=2,'yl'=2,'zc'=2,'zf'=2] {'xh','z..., dimensions={0} | all-to-all | bytes 786432 | tf_op jit(solution)/shard_map/all_to_all | solution.py:286
  226.3 3.0 collective-permute-start.20
  229.3 2.4 collective-permute-done.20
  231.8 12.5 %all_to_all.68 = bf16[8,8,3072]{2,1,0:T(8,128)(2,1)S(1)} all-to-all(bf16[8,8,3072]{2,1,0:T(8,128)(2,1)S(1)} %broadcast_in_dim.38), channel_id=1, replica_groups=mesh['zh'=2,'core'=2,'xh'=2,'xl'=2,'yh'=2,'yl'=2,'zc'=2,'zf'=2] {'xh','z..., dimensions={0} | all-to-all | bytes 786432 | tf_op jit(solution)/shard_map/all_to_all | solution.py:45
  244.3 4.9 %shard_map.110 = bf16[64,3072]{1,0:T(8,128)(2,1)S(1)} custom-call(bf16[64,3072]{1,0:T(8,128)(2,1)S(1)} %bitcast.73, f32[3,3072]{1,0:T(4,128)S(1)} %reshape.70.mod_ref, bf16[1280,3072]{1,0:T(8,128)(2,1)S(1)} %get-tuple-element.96.up, bf16[1280,3072]{1,0:T(8,128)(2,1)S(1)} %get-tuple-element.97.down, bf16[256,3072]{1,0:T(8,128)(2,1)S(1)} %get-tuple-element.100.up_end, ...), custom_call_target="tpu_custom_call" | custom-call | flops 1207959552 | bytes 19660800 | tf_op jit(solution)/shard_map/pallas_call | solution.py:79
  249.2 12.5 %all_to_all.69.parts_ref = bf16[8,8,3072]{2,1,0:T(8,128)(2,1)S(1)} all-to-all(bf16[8,8,3072]{2,1,0:T(8,128)(2,1)S(1)} %bitcast.74), channel_id=1, replica_groups=mesh['zh'=2,'core'=2,'xh'=2,'xl'=2,'yh'=2,'yl'=2,'zc'=2,'zf'=2] {'xh','z..., dimensions={0} | all-to-all | bytes 786432 | tf_op jit(solution)/shard_map/all_to_all | solution.py:286
  261.9 14.8 %collective-permute-start.21 = (bf16[8,3200]{1,0:T(8,128)(2,1)S(1)}, bf16[8,3200]{1,0:T(8,128)(2,1)S(1)}, u32[]{:S(2)}, u32[]{:S(2)}) collective-permute-start(bf16[8,3200]{1,0:T(8,128)(2,1)S(1)} %shard_map.111), channel_id=1, source_target_pairs={{0,64},{2,66},{64,130},{66,128},{128,192},{130,194},{1,65},{3,67},... | collective-permute-start | bytes 153608 | tf_op jit(solution)/shard_map/ppermute | solution.py:35
  276.6 1.6 collective-permute-done.21
  278.3 14.5 %all_to_all.70 = bf16[8,8,3072]{2,1,0:T(8,128)(2,1)S(1)} all-to-all(bf16[8,8,3072]{2,1,0:T(8,128)(2,1)S(1)} %broadcast_in_dim.39), channel_id=1, replica_groups=mesh['zh'=2,'core'=2,'xh'=2,'xl'=2,'yh'=2,'yl'=2,'zc'=2,'zf'=2] {'xh','z..., dimensions={0} | all-to-all | bytes 786432 | tf_op jit(solution)/shard_map/all_to_all | solution.py:45
  292.8 4.9 %shard_map.112 = bf16[64,3072]{1,0:T(8,128)(2,1)S(1)} custom-call(bf16[64,3072]{1,0:T(8,128)(2,1)S(1)} %bitcast.68, f32[3,3072]{1,0:T(4,128)S(1)} %reshape.70.mod_ref, bf16[1280,3072]{1,0:T(8,128)(2,1)S(1)} %get-tuple-element.96.up, bf16[1280,3072]{1,0:T(8,128)(2,1)S(1)} %get-tuple-element.97.down, bf16[256,3072]{1,0:T(8,128)(2,1)S(1)} %get-tuple-element.100.up_end, ...), custom_call_target="tpu_custom_call" | custom-call | flops 1207959552 | bytes 19660800 | tf_op jit(solution)/shard_map/pallas_call | solution.py:79
  297.7 12.7 %all_to_all.71.parts_ref = bf16[8,8,3072]{2,1,0:T(8,128)(2,1)S(1)} all-to-all(bf16[8,8,3072]{2,1,0:T(8,128)(2,1)S(1)} %bitcast.69), channel_id=1, replica_groups=mesh['zh'=2,'core'=2,'xh'=2,'xl'=2,'yh'=2,'yl'=2,'zc'=2,'zf'=2] {'xh','z..., dimensions={0} | all-to-all | bytes 786432 | tf_op jit(solution)/shard_map/all_to_all | solution.py:286
  310.5 10.8 %collective-permute-start.24 = (bf16[8,3200]{1,0:T(8,128)(2,1)S(1)}, bf16[8,3200]{1,0:T(8,128)(2,1)S(1)}, u32[]{:S(2)}, u32[]{:S(2)}) collective-permute-start(bf16[8,3200]{1,0:T(8,128)(2,1)S(1)} %shard_map.113), channel_id=1, source_target_pairs={{0,64},{2,66},{64,128},{66,130},{128,194},{130,192},{1,65},{3,67},... | collective-permute-start | bytes 153608 | tf_op jit(solution)/shard_map/ppermute | solution.py:35
  321.3 1.3 collective-permute-start.23
  (99 shorter events, 27.6 us)
Async XLA Ops:
  0.6 78.5 %copy-start = (bf16[1,144,3584]{2,1,0:T(8,128)(2,1)S(1)}, bf16[1,144,3584]{2,1,0:T(8,128)(2,1)}, u32[]{:S(2)}) copy-start(bf16[1,144,3584]{2,1,0:T(8,128)(2,1)} %param.15) | copy-start | bytes 3096580
  0.6 1.7 copy-start.2
  2.4 0.8 copy-start.7
  3.3 12.3 %copy-start.9 = (s32[1,8]{1,0:T(1,128)S(1)}, s32[1,8]{1,0:T(1,128)}, u32[]{:S(2)}) copy-start(s32[1,8]{1,0:T(1,128)} %param.12) | copy-start | bytes 100
  3.3 12.4 %copy-start.8 = (bf16[1,8,3072]{2,1,0:T(8,128)(2,1)S(1)}, bf16[1,8,3072]{2,1,0:T(8,128)(2,1)}, u32[]{:S(2)}) copy-start(bf16[1,8,3072]{2,1,0:T(8,128)(2,1)} %param.11) | copy-start | bytes 147460
  5.7 19.6 %all-to-all-start = ((f32[16,28,128]{2,1,0:T(8,128)}), f32[16,28,128]{2,1,0:T(8,128)S(1)}, u32[]{:S(2)}, u32[]{:S(2)}) async-start(f32[16,28,128]{2,1,0:T(8,128)} %broadcast_in_dim.28), calls=%async_computation | async-start | bytes 524288 | tf_op jit(solution)/shard_map/all_to_all | solution.py:45
  26.0 13.6 %all-to-all-start.1 = ((bf16[4,8,3200]{2,1,0:T(8,128)(2,1)}), bf16[4,8,3200]{2,1,0:T(8,128)(2,1)}, u32[]{:S(2)}, u32[]{:S(2)}) async-start(bf16[4,8,3200]{2,1,0:T(8,128)(2,1)} %broadcast_in_dim.30), calls=%async_computation.1 | async-start | bytes 409600 | tf_op jit(solution)/shard_map/all_to_all | solution.py:45
  30.8 28.4 %collective-permute-start = (bf16[192,3072]{1,0:T(8,128)(2,1)}, bf16[192,3072]{1,0:T(8,128)(2,1)S(1)}, u32[]{:S(2)}, u32[]{:S(2)}) collective-permute-start(bf16[192,3072]{1,0:T(8,128)(2,1)} %get-tuple-element.70.refs_0_), channel_id=1, source_target_pairs={{4,0},{8,4},{12,8},{0,12},{5,1},{9,5},{13,9},{1,13},{6,2},{10,6},{... | collective-permute-start | bytes 3538952 | tf_op jit(solution)/shard_map/ppermute | solution.py:28
  33.5 28.8 %collective-permute-start.1 = (bf16[192,3072]{1,0:T(8,128)(2,1)}, bf16[192,3072]{1,0:T(8,128)(2,1)S(1)}, u32[]{:S(2)}, u32[]{:S(2)}) collective-permute-start(bf16[192,3072]{1,0:T(8,128)(2,1)} %get-tuple-element.69.refs_1_), channel_id=1, source_target_pairs={{12,0},{0,4},{4,8},{8,12},{13,1},{1,5},{5,9},{9,13},{14,2},{2,6},{... | collective-permute-start | bytes 3538952 | tf_op jit(solution)/shard_map/ppermute | solution.py:28
  33.5 28.8 %collective-permute-start.2 = (bf16[192,3072]{1,0:T(8,128)(2,1)}, bf16[192,3072]{1,0:T(8,128)(2,1)}, u32[]{:S(2)}, u32[]{:S(2)}) collective-permute-start(bf16[192,3072]{1,0:T(8,128)(2,1)} %get-tuple-element.70.refs_0_), channel_id=1, source_target_pairs={{16,0},{32,16},{48,32},{0,48},{17,1},{33,17},{49,33},{1,49},{18,2}... | collective-permute-start | bytes 3538952 | tf_op jit(solution)/shard_map/ppermute | solution.py:28
  36.0 28.5 %collective-permute-start.3 = (bf16[192,3072]{1,0:T(8,128)(2,1)}, bf16[192,3072]{1,0:T(8,128)(2,1)}, u32[]{:S(2)}, u32[]{:S(2)}) collective-permute-start(bf16[192,3072]{1,0:T(8,128)(2,1)} %get-tuple-element.69.refs_1_), channel_id=1, source_target_pairs={{48,0},{0,16},{16,32},{32,48},{49,1},{1,17},{17,33},{33,49},{50,2}... | collective-permute-start | bytes 3538952 | tf_op jit(solution)/shard_map/ppermute | solution.py:28
  65.3 11.5 %all-to-all-start.2 = ((f32[16,28,128]{2,1,0:T(8,128)}), f32[16,28,128]{2,1,0:T(8,128)}, u32[]{:S(2)}, u32[]{:S(2)}) async-start(f32[16,28,128]{2,1,0:T(8,128)} %broadcast_in_dim.31), calls=%async_computation.2 | async-start | bytes 524288 | tf_op jit(solution)/shard_map/all_to_all | solution.py:45
  80.1 8.1 %all-to-all-start.3 = ((f32[4,2,128]{2,1,0:T(2,128)}), f32[4,2,128]{2,1,0:T(2,128)S(1)}, u32[]{:S(2)}, u32[]{:S(2)}) async-start(f32[4,2,128]{2,1,0:T(2,128)} %broadcast_in_dim.33), calls=%async_computation.3 | async-start | bytes 8192 | tf_op jit(solution)/shard_map/all_to_all | solution.py:45
  83.8 4.4 %copy-start.6 = (bf16[1,8,3072]{2,1,0:T(8,128)(2,1)S(1)}, bf16[1,8,3072]{2,1,0:T(8,128)(2,1)}, u32[]{:S(2)}) copy-start(bf16[1,8,3072]{2,1,0:T(8,128)(2,1)} %param.9) | copy-start | bytes 147460
  83.8 24.7 %collective-permute-start.4 = (bf16[192,3072]{1,0:T(8,128)(2,1)}, bf16[192,3072]{1,0:T(8,128)(2,1)}, u32[]{:S(2)}, u32[]{:S(2)}) collective-permute-start(bf16[192,3072]{1,0:T(8,128)(2,1)} %get-tuple-element.69.refs_1_), channel_id=1, source_target_pairs={{4,0},{8,4},{12,8},{0,12},{5,1},{9,5},{13,9},{1,13},{6,2},{10,6},{... | collective-permute-start | bytes 3538952 | tf_op jit(solution)/shard_map/ppermute | solution.py:28
  84.5 25.6 %collective-permute-start.5 = (bf16[192,3072]{1,0:T(8,128)(2,1)}, bf16[192,3072]{1,0:T(8,128)(2,1)}, u32[]{:S(2)}, u32[]{:S(2)}) collective-permute-start(bf16[192,3072]{1,0:T(8,128)(2,1)} %get-tuple-element.70.refs_0_), channel_id=1, source_target_pairs={{12,0},{0,4},{4,8},{8,12},{13,1},{1,5},{5,9},{9,13},{14,2},{2,6},{... | collective-permute-start | bytes 3538952 | tf_op jit(solution)/shard_map/ppermute | solution.py:28
  85.3 24.9 %collective-permute-start.6 = (bf16[192,3072]{1,0:T(8,128)(2,1)S(1)}, bf16[192,3072]{1,0:T(8,128)(2,1)}, u32[]{:S(2)}, u32[]{:S(2)}) collective-permute-start(bf16[192,3072]{1,0:T(8,128)(2,1)S(1)} %collective-permute-done.refs_4_), channel_id=1, source_target_pairs={{16,0},{32,16},{48,32},{0,48},{17,1},{33,17},{49,33},{1,49},{18,2}... | collective-permute-start | bytes 3538952 | tf_op jit(solution)/shard_map/ppermute | solution.py:28
  86.2 25.0 %collective-permute-start.7 = (bf16[192,3072]{1,0:T(8,128)(2,1)S(1)}, bf16[192,3072]{1,0:T(8,128)(2,1)}, u32[]{:S(2)}, u32[]{:S(2)}) collective-permute-start(bf16[192,3072]{1,0:T(8,128)(2,1)S(1)} %collective-permute-done.1.refs_5_), channel_id=1, source_target_pairs={{48,0},{0,16},{16,32},{32,48},{49,1},{1,17},{17,33},{33,49},{50,2}... | collective-permute-start | bytes 3538952 | tf_op jit(solution)/shard_map/ppermute | solution.py:28
  88.9 9.6 %all-to-all-start.4 = ((bf16[4,8,3072]{2,1,0:T(8,128)(2,1)}), bf16[4,8,3072]{2,1,0:T(8,128)(2,1)}, u32[]{:S(2)}, u32[]{:S(2)}) async-start(bf16[4,8,3072]{2,1,0:T(8,128)(2,1)} %broadcast_in_dim.34), calls=%async_computation.4 | async-start | bytes 393216 | tf_op jit(solution)/shard_map/all_to_all | solution.py:45
  93.1 29.2 %copy-start.10 = (s32[1,8]{1,0:T(1,128)S(1)}, s32[1,8]{1,0:T(1,128)}, u32[]{:S(2)}) copy-start(s32[1,8]{1,0:T(1,128)} %param.10) | copy-start | bytes 100
  111.2 10.4 %collective-permute-start.9 = (bf16[96,3072]{1,0:T(8,128)(2,1)}, bf16[96,3072]{1,0:T(8,128)(2,1)}, u32[]{:S(2)}, u32[]{:S(2)}) collective-permute-start(bf16[96,3072]{1,0:T(8,128)(2,1)} %get-tuple-element.72), channel_id=1, source_target_pairs={{4,0},{8,4},{12,8},{0,12},{5,1},{9,5},{13,9},{1,13},{6,2},{10,6},{... | collective-permute-start | bytes 1769480 | tf_op jit(solution)/shard_map/ppermute | solution.py:28
  112.9 29.0 %collective-permute-start.13 = (bf16[192,3072]{1,0:T(8,128)(2,1)}, bf16[192,3072]{1,0:T(8,128)(2,1)}, u32[]{:S(2)}, u32[]{:S(2)}) collective-permute-start(bf16[192,3072]{1,0:T(8,128)(2,1)} %collective-permute-done.5.refs_7_), channel_id=1, source_target_pairs={{16,0},{32,16},{48,32},{0,48},{17,1},{33,17},{49,33},{1,49},{18,2}... | collective-permute-start | bytes 3538952 | tf_op jit(solution)/shard_map/ppermute | solution.py:28
  113.2 28.7 %collective-permute-start.14 = (bf16[192,3072]{1,0:T(8,128)(2,1)}, bf16[192,3072]{1,0:T(8,128)(2,1)}, u32[]{:S(2)}, u32[]{:S(2)}) collective-permute-start(bf16[192,3072]{1,0:T(8,128)(2,1)} %collective-permute-done.4.refs_6_), channel_id=1, source_target_pairs={{48,0},{0,16},{16,32},{32,48},{49,1},{1,17},{17,33},{33,49},{50,2}... | collective-permute-start | bytes 3538952 | tf_op jit(solution)/shard_map/ppermute | solution.py:28
  114.3 19.9 %collective-permute-start.10 = (bf16[96,3072]{1,0:T(8,128)(2,1)}, bf16[96,3072]{1,0:T(8,128)(2,1)}, u32[]{:S(2)}, u32[]{:S(2)}) collective-permute-start(bf16[96,3072]{1,0:T(8,128)(2,1)} %get-tuple-element.73), channel_id=1, source_target_pairs={{4,0},{8,4},{12,8},{0,12},{5,1},{9,5},{13,9},{1,13},{6,2},{10,6},{... | collective-permute-start | bytes 1769480 | tf_op jit(solution)/shard_map/ppermute | solution.py:28
  114.3 27.5 %collective-permute-start.11 = (bf16[96,3072]{1,0:T(8,128)(2,1)}, bf16[96,3072]{1,0:T(8,128)(2,1)}, u32[]{:S(2)}, u32[]{:S(2)}) collective-permute-start(bf16[96,3072]{1,0:T(8,128)(2,1)} %get-tuple-element.74), channel_id=1, source_target_pairs={{12,0},{0,4},{4,8},{8,12},{13,1},{1,5},{5,9},{9,13},{14,2},{2,6},{... | collective-permute-start | bytes 1769480 | tf_op jit(solution)/shard_map/ppermute | solution.py:28
  121.6 20.3 %collective-permute-start.12 = (bf16[96,3072]{1,0:T(8,128)(2,1)}, bf16[96,3072]{1,0:T(8,128)(2,1)}, u32[]{:S(2)}, u32[]{:S(2)}) collective-permute-start(bf16[96,3072]{1,0:T(8,128)(2,1)} %get-tuple-element.75), channel_id=1, source_target_pairs={{12,0},{0,4},{4,8},{8,12},{13,1},{1,5},{5,9},{9,13},{14,2},{2,6},{... | collective-permute-start | bytes 1769480 | tf_op jit(solution)/shard_map/ppermute | solution.py:28
  123.0 16.5 %all-to-all-start.5 = ((f32[16,4,2,128]{3,2,1,0:T(2,128)}), f32[16,4,2,128]{3,2,1,0:T(2,128)}, u32[]{:S(2)}, u32[]{:S(2)}) async-start(f32[16,4,2,128]{3,2,1,0:T(2,128)} %broadcast_in_dim.36), calls=%async_computation.5 | async-start | bytes 131072 | tf_op jit(solution)/shard_map/all_to_all | solution.py:45
  134.2 11.4 %collective-permute-start.8 = (bf16[4,8,3072]{2,1,0:T(8,128)(2,1)}, bf16[4,8,3072]{2,1,0:T(8,128)(2,1)}, u32[]{:S(2)}, u32[]{:S(2)}) collective-permute-start(bf16[4,8,3072]{2,1,0:T(8,128)(2,1)} %all-to-all-done.4), channel_id=1, source_target_pairs={{0,32},{32,0},{1,33},{33,1},{2,34},{34,2},{3,35},{35,3},{4,36},{36... | collective-permute-start | bytes 589832 | tf_op jit(solution)/shard_map/ppermute | solution.py:206
  141.8 4.9 %copy-start.1 = (bf16[192,3072]{1,0:T(8,128)(2,1)S(1)}, bf16[192,3072]{1,0:T(8,128)(2,1)}, u32[]{:S(2)}) copy-start(bf16[192,3072]{1,0:T(8,128)(2,1)} %get-tuple-element.69.refs_1_) | copy-start | bytes 3538948
  141.9 10.9 %collective-permute-start.15 = (bf16[96,3072]{1,0:T(8,128)(2,1)}, bf16[96,3072]{1,0:T(8,128)(2,1)S(1)}, u32[]{:S(2)}, u32[]{:S(2)}) collective-permute-start(bf16[96,3072]{1,0:T(8,128)(2,1)} %collective-permute-done.9.refs_12_), channel_id=1, source_target_pairs={{16,0},{32,16},{48,32},{0,48},{17,1},{33,17},{49,33},{1,49},{18,2}... | collective-permute-start | bytes 1769480 | tf_op jit(solution)/shard_map/ppermute | solution.py:28
  142.9 10.6 %collective-permute-start.16 = (bf16[96,3072]{1,0:T(8,128)(2,1)}, bf16[96,3072]{1,0:T(8,128)(2,1)S(1)}, u32[]{:S(2)}, u32[]{:S(2)}) collective-permute-start(bf16[96,3072]{1,0:T(8,128)(2,1)} %collective-permute-done.11.refs_14_.refs_0_), channel_id=1, source_target_pairs={{48,0},{0,16},{16,32},{32,48},{49,1},{1,17},{17,33},{33,49},{50,2}... | collective-permute-start | bytes 1769480 | tf_op jit(solution)/shard_map/ppermute | solution.py:28
  143.4 10.1 %collective-permute-start.17 = (bf16[96,3072]{1,0:T(8,128)(2,1)}, bf16[96,3072]{1,0:T(8,128)(2,1)S(1)}, u32[]{:S(2)}, u32[]{:S(2)}) collective-permute-start(bf16[96,3072]{1,0:T(8,128)(2,1)} %slice.91), channel_id=1, source_target_pairs={{4,0},{8,4},{12,8},{0,12},{5,1},{9,5},{13,9},{1,13},{6,2},{10,6},{... | collective-permute-start | bytes 1769480 | tf_op jit(solution)/shard_map/ppermute | solution.py:28
  145.6 10.4 %collective-permute-start.18 = (bf16[96,3072]{1,0:T(8,128)(2,1)}, bf16[96,3072]{1,0:T(8,128)(2,1)S(1)}, u32[]{:S(2)}, u32[]{:S(2)}) collective-permute-start(bf16[96,3072]{1,0:T(8,128)(2,1)} %slice.92), channel_id=1, source_target_pairs={{12,0},{0,4},{4,8},{8,12},{13,1},{1,5},{5,9},{9,13},{14,2},{2,6},{... | collective-permute-start | bytes 1769480 | tf_op jit(solution)/shard_map/ppermute | solution.py:28
  162.2 30.0 %copy-start.4 = (bf16[8,3200]{1,0:T(8,128)(2,1)S(1)}, bf16[8,3200]{1,0:T(8,128)(2,1)}, u32[]{:S(2)}) copy-start(bf16[8,3200]{1,0:T(8,128)(2,1)} %get-tuple-element.106) | copy-start | bytes 153604
  178.2 13.9 %collective-permute-start.19 = (bf16[8,3200]{1,0:T(8,128)(2,1)S(1)}, bf16[8,3200]{1,0:T(8,128)(2,1)S(1)}, u32[]{:S(2)}, u32[]{:S(2)}) collective-permute-start(bf16[8,3200]{1,0:T(8,128)(2,1)S(1)} %shard_map.107), channel_id=1, source_target_pairs={{0,64},{2,66},{64,130},{66,128},{128,192},{130,194},{192,0},{194,2... | collective-permute-start | bytes 153608 | tf_op jit(solution)/shard_map/ppermute | solution.py:35
  211.0 20.7 %copy-start.3 = (bf16[8,3200]{1,0:T(8,128)(2,1)S(1)}, bf16[8,3200]{1,0:T(8,128)(2,1)}, u32[]{:S(2)}) copy-start(bf16[8,3200]{1,0:T(8,128)(2,1)} %get-tuple-element.105) | copy-start | bytes 153604
  226.3 5.4 %collective-permute-start.20 = (bf16[8,3200]{1,0:T(8,128)(2,1)S(1)}, bf16[8,3200]{1,0:T(8,128)(2,1)S(1)}, u32[]{:S(2)}, u32[]{:S(2)}) collective-permute-start(bf16[8,3200]{1,0:T(8,128)(2,1)S(1)} %shard_map.109), channel_id=1, source_target_pairs={{0,64},{2,66},{64,130},{66,128},{128,192},{130,194},{192,0},{194,2... | collective-permute-start | bytes 153608 | tf_op jit(solution)/shard_map/ppermute | solution.py:35
  261.9 16.4 %collective-permute-start.21 = (bf16[8,3200]{1,0:T(8,128)(2,1)S(1)}, bf16[8,3200]{1,0:T(8,128)(2,1)S(1)}, u32[]{:S(2)}, u32[]{:S(2)}) collective-permute-start(bf16[8,3200]{1,0:T(8,128)(2,1)S(1)} %shard_map.111), channel_id=1, source_target_pairs={{0,64},{2,66},{64,130},{66,128},{128,192},{130,194},{1,65},{3,67},... | collective-permute-start | bytes 153608 | tf_op jit(solution)/shard_map/ppermute | solution.py:35
  297.7 25.6 %copy-start.5 = (bf16[8,3200]{1,0:T(8,128)(2,1)S(1)}, bf16[8,3200]{1,0:T(8,128)(2,1)}, u32[]{:S(2)}) copy-start(bf16[8,3200]{1,0:T(8,128)(2,1)} %get-tuple-element.109) | copy-start | bytes 153604
  310.5 12.8 %collective-permute-start.24 = (bf16[8,3200]{1,0:T(8,128)(2,1)S(1)}, bf16[8,3200]{1,0:T(8,128)(2,1)S(1)}, u32[]{:S(2)}, u32[]{:S(2)}) collective-permute-start(bf16[8,3200]{1,0:T(8,128)(2,1)S(1)} %shard_map.113), channel_id=1, source_target_pairs={{0,64},{2,66},{64,128},{66,130},{128,194},{130,192},{1,65},{3,67},... | collective-permute-start | bytes 153608 | tf_op jit(solution)/shard_map/ppermute | solution.py:35
  321.3 3.1 collective-permute-start.23
  322.6 1.8 collective-permute-start.22

commit v4 on v3

--- a/solution.py
+++ b/solution.py
@@ -172,16 +172,11 @@
     xb = from_neighbour(second, "x", -1)
     partial = jnp.sum(exchange(partial, SECTION + LINE), axis=0)
     entering = exchange(after(arriving, partial), SECTION)
-    entering = [entering[section] for section in range(SECTIONS)]
 
     first, second, yp_first, ym_second, xa, xb, partial, entering = together(
         (first, second, yp_first, ym_second, xa, xb, partial, entering)
     )
     pooled = jnp.sum(exchange(partial, PLANE), axis=0)
-
-    first, second, yp_first, ym_second, pooled = together(
-        (first, second, yp_first, ym_second, pooled)
-    )
     yp_second = from_neighbour(second, "y", 1)
     ym_first = from_neighbour(first, "y", -1)
     xa_yp = from_neighbour(yp_first, "x", 1)
@@ -275,6 +270,7 @@
         arriving,
     )
     is_third = section_id == 2
+    entering = [entering[section] for section in range(SECTIONS)]
     gathered, waiting, gate, entering, is_first, is_third = lax.optimization_barrier(
         (gathered, waiting, mod[2:], entering, is_first, is_third)
     )

time: 327 us -> 304 us (0.930)
  waiting for transfers between devices: 83.3 us -> 53.6 us
  blocking collectives: 97.2 us -> 120 us
  starting transfers between devices: 93.6 us -> 77.4 us
    ppermute x18, waiting for transfers between devices: 52.5 us -> 24 us  [from_neighbour(): return lax.ppermute(block, (axis + 'h', axis + 'l'), route)]
    ppermute x6, starting transfers between devices: 43.2 us -> 27.2 us  [between_sections(): return lax.ppermute(block, SECTION + ('zc',), route)]
    all_to_all x3 -> x4, blocking collectives: 40.8 us -> 56.6 us  [exchange(): return lax.all_to_all(copies, axes, 0, 0)]
    all_to_all x4, blocking collectives: 56.4 us -> 63.8 us  [per_device(): lax.all_to_all(partial.reshape(GROUP_SIZE, tokens, breadth), GROUP, 0, 0)]
    all_to_all x6 -> x5, waiting for transfers between devices: 25.1 us -> 22.4 us  [exchange(): return lax.all_to_all(copies, axes, 0, 0)]
    all_to_all x6 -> x5, starting transfers between devices: 31.9 us -> 31.5 us  [exchange(): return lax.all_to_all(copies, axes, 0, 0)]
  transfers between devices with their start and end apart: 31 -> 30, of which waited for: 20 -> 15; matrix products, arithmetic and copies ran while one was open for 4% -> 6% of each run, Pallas kernels for 1% -> 2%
where the time goes in v4:
time: 304 us; the launch traced here: 303 us
  blocking collectives  120 us (39%)
  starting transfers between devices  77.4 us (25%)
  waiting for transfers between devices  53.6 us (18%)
  Pallas kernels  26.4 us (9%)
  local copies, waits for them, and re-layouts  15.7 us (5%)
  other arithmetic  6.59 us (2%)
    all_to_all x4, blocking collectives, per_device(): lax.all_to_all(partial.reshape(GROUP_SIZE, tokens, breadth), GROUP, 0, 0)  63.8 us
    all_to_all x4, blocking collectives, exchange(): return lax.all_to_all(copies, axes, 0, 0)  56.6 us
    all_to_all x5, starting transfers between devices, exchange(): return lax.all_to_all(copies, axes, 0, 0)  31.5 us
    ppermute x6, starting transfers between devices, between_sections(): return lax.ppermute(block, SECTION + ('zc',), route)  27.2 us
    ppermute x18, waiting for transfers between devices, from_neighbour(): return lax.ppermute(block, (axis + 'h', axis + 'l'), route)  24 us
    all_to_all x5, waiting for transfers between devices, exchange(): return lax.all_to_all(copies, axes, 0, 0)  22.4 us
    pallas_call x4, Pallas kernels, layer(): pl.pallas_call(layer_kernel, out_shape=jax.ShapeDtypeStruct((rows, breadt...  19.8 us
    ppermute x18, starting transfers between devices, from_neighbour(): return lax.ppermute(block, (axis + 'h', axis + 'l'), route)  18 us
  transfers between devices with their start and end apart: 30, of which 15 were waited for; matrix products, arithmetic and copies ran while one was open for 6% of the time, Pallas kernels for 2%

profile of v4, /device:TPU:1, one launch (start us, length us, event | category | flops | bytes accessed | tf_op | source)
XLA Modules:
  0.0 303.0 jit_solution(13522351310914058220)
XLA Ops:
  0.7 1.5 slice_bitcast_fusion
  3.3 1.6 pad_maximum_fusion
  4.9 3.6 %collective-permute-start = (bf16[192,3072]{1,0:T(8,128)(2,1)}, bf16[192,3072]{1,0:T(8,128)(2,1)S(1)}, u32[]{:S(2)}, u32[]{:S(2)}) collective-permute-start(bf16[192,3072]{1,0:T(8,128)(2,1)} %get-tuple-element.57.refs_0_), channel_id=1, source_target_pairs={{4,0},{8,4},{12,8},{0,12},{5,1},{9,5},{13,9},{1,13},{6,2},{10,6},{... | collective-permute-start | bytes 3538952 | tf_op jit(solution)/shard_map/ppermute | solution.py:28
  8.5 2.5 collective-permute-start.2
  11.7 9.7 %all-to-all-start = ((f32[16,28,128]{2,1,0:T(8,128)}), f32[16,28,128]{2,1,0:T(8,128)}, u32[]{:S(2)}, u32[]{:S(2)}) async-start(f32[16,28,128]{2,1,0:T(8,128)} %broadcast_in_dim.28), calls=%async_computation | async-start | bytes 524288 | tf_op jit(solution)/shard_map/all_to_all | solution.py:45
  21.5 9.6 %all-to-all-done = f32[16,28,128]{2,1,0:T(8,128)} async-done(((f32[16,28,128]{2,1,0:T(8,128)}), f32[16,28,128]{2,1,0:T(8,128)}, u32[]{:S(2)}, u32[]{:S(2)}) %all-to-all-start) | async-done | bytes 229408 | tf_op jit(solution)/shard_map/all_to_all | solution.py:45
  32.1 13.4 %all_to_all.65 = bf16[4,8,3200]{2,1,0:T(8,128)(2,1)} all-to-all(bf16[4,8,3200]{2,1,0:T(8,128)(2,1)S(1)} %broadcast_in_dim.30), channel_id=1, replica_groups=mesh['zh'=2,'core'=2,'xh'=2,'xl'=2,'yh'=2,'yl'=2,'zc'=2,'zf'=2] {'zh','c..., dimensions={0} | all-to-all | bytes 409600 | tf_op jit(solution)/shard_map/all_to_all | solution.py:45
  46.3 7.1 %all-to-all-start.2 = ((f32[16,28,128]{2,1,0:T(8,128)}), f32[16,28,128]{2,1,0:T(8,128)}, u32[]{:S(2)}, u32[]{:S(2)}) async-start(f32[16,28,128]{2,1,0:T(8,128)} %broadcast_in_dim.31), calls=%async_computation.2 | async-start | bytes 524288 | tf_op jit(solution)/shard_map/all_to_all | solution.py:45
  53.4 2.5 collective-permute-start.4
  55.9 2.4 collective-permute-start.6
  58.3 2.5 all-to-all-done.2
  64.1 6.0 %all-to-all-start.3 = ((f32[4,2,128]{2,1,0:T(2,128)}), f32[4,2,128]{2,1,0:T(2,128)S(1)}, u32[]{:S(2)}, u32[]{:S(2)}) async-start(f32[4,2,128]{2,1,0:T(2,128)} %broadcast_in_dim.33), calls=%async_computation.3 | async-start | bytes 8192 | tf_op jit(solution)/shard_map/all_to_all | solution.py:45
  71.2 3.4 %all-to-all-done.3 = f32[4,2,128]{2,1,0:T(2,128)S(1)} async-done(((f32[4,2,128]{2,1,0:T(2,128)}), f32[4,2,128]{2,1,0:T(2,128)S(1)}, u32[]{:S(2)}, u32[]{:S(2)}) %all-to-all-start.3) | async-done | bytes 4128 | tf_op jit(solution)/shard_map/all_to_all | solution.py:45
  75.3 4.0 %all-to-all-start.4 = ((bf16[4,8,3072]{2,1,0:T(8,128)(2,1)}), bf16[4,8,3072]{2,1,0:T(8,128)(2,1)}, u32[]{:S(2)}, u32[]{:S(2)}) async-start(bf16[4,8,3072]{2,1,0:T(8,128)(2,1)} %broadcast_in_dim.34), calls=%async_computation.4 | async-start | bytes 393216 | tf_op jit(solution)/shard_map/all_to_all | solution.py:45
  80.5 4.3 %all-to-all-done.4 = bf16[4,8,3072]{2,1,0:T(8,128)(2,1)} async-done(((bf16[4,8,3072]{2,1,0:T(8,128)(2,1)}), bf16[4,8,3072]{2,1,0:T(8,128)(2,1)}, u32[]{:S(2)}, u32[]{:S(2)}) %all-to-all-start.4) | async-done | bytes 196640 | tf_op jit(solution)/shard_map/all_to_all | solution.py:45
  84.8 1.3 collective-permute-start.9
  89.9 4.7 %all-to-all-start.5 = ((f32[16,4,2,128]{3,2,1,0:T(2,128)}), f32[16,4,2,128]{3,2,1,0:T(2,128)}, u32[]{:S(2)}, u32[]{:S(2)}) async-start(f32[16,4,2,128]{3,2,1,0:T(2,128)} %broadcast_in_dim.36), calls=%async_computation.5 | async-start | bytes 131072 | tf_op jit(solution)/shard_map/all_to_all | solution.py:45
  94.6 1.4 collective-permute-done.9.refs_12_
  96.2 12.4 %collective-permute-done.10.refs_13_ = bf16[96,3072]{1,0:T(8,128)(2,1)} collective-permute-done((bf16[96,3072]{1,0:T(8,128)(2,1)}, bf16[96,3072]{1,0:T(8,128)(2,1)}, u32[]{:S(2)}, u32[]{:S(2)}) %collective-permute-start.10) | collective-permute-done | bytes 589856 | tf_op jit(solution)/shard_map/ppermute | solution.py:28
  108.9 1.5 slice_bitcast_fusion.4
  110.4 1.9 slice.87
  112.3 1.9 slice.88
  114.3 2.6 all-to-all-done.5
  116.9 1.5 copy.19
  119.3 6.8 %collective-permute-done.12.refs_15_.refs_1_ = bf16[96,3072]{1,0:T(8,128)(2,1)} collective-permute-done((bf16[96,3072]{1,0:T(8,128)(2,1)}, bf16[96,3072]{1,0:T(8,128)(2,1)}, u32[]{:S(2)}, u32[]{:S(2)}) %collective-permute-start.12) | collective-permute-done | bytes 589856 | tf_op jit(solution)/shard_map/ppermute | solution.py:28
  130.2 5.1 %shard_map.104 = (bf16[1280,3072]{1,0:T(8,128)(2,1)S(1)}, bf16[1280,3072]{1,0:T(8,128)(2,1)S(1)}) custom-call(bf16[192,3072]{1,0:T(8,128)(2,1)} %get-tuple-element.57.refs_0_, bf16[192,3072]{1,0:T(8,128)(2,1)} %get-tuple-element.56.refs_1_, bf16[192,3072]{1,0:T(8,128)(2,1)} %collective-permute-done.2.refs_2_, ...), custom_call_target="tpu_custom_call" | custom-call | bytes 31457280 | tf_op jit(solution)/shard_map/pallas_call | solution.py:118
  135.4 1.5 collective-permute-done.15.refs_2_
  136.9 1.4 collective-permute-done.16.refs_3_
  138.7 1.2 shard_map.105
  139.9 4.9 %shard_map.106 = bf16[64,3072]{1,0:T(8,128)(2,1)S(1)} custom-call(bf16[64,3072]{1,0:T(8,128)(2,1)S(1)} %bitcast.67, f32[3,3072]{1,0:T(4,128)S(1)} %reshape.75.mod_ref, bf16[1280,3072]{1,0:T(8,128)(2,1)S(1)} %get-tuple-element.80.up, bf16[1280,3072]{1,0:T(8,128)(2,1)S(1)} %get-tuple-element.81.down, bf16[256,3072]{1,0:T(8,128)(2,1)S(1)} %get-tuple-element.84.up_end, ...), custom_call_target="tpu_custom_call" | custom-call | flops 1207959552 | bytes 19660800 | tf_op jit(solution)/shard_map/pallas_call | solution.py:79
  144.9 21.5 %all_to_all.66.parts_ref = bf16[8,8,3072]{2,1,0:T(8,128)(2,1)S(1)} all-to-all(bf16[8,8,3072]{2,1,0:T(8,128)(2,1)S(1)} %bitcast.70), channel_id=1, replica_groups=mesh['zh'=2,'core'=2,'xh'=2,'xl'=2,'yh'=2,'yl'=2,'zc'=2,'zf'=2] {'xh','z..., dimensions={0} | all-to-all | bytes 786432 | tf_op jit(solution)/shard_map/all_to_all | solution.py:282
  166.4 4.2 %collective-permute-start.19 = (bf16[8,3200]{1,0:T(8,128)(2,1)S(1)}, bf16[8,3200]{1,0:T(8,128)(2,1)S(1)}, u32[]{:S(2)}, u32[]{:S(2)}) collective-permute-start(bf16[8,3200]{1,0:T(8,128)(2,1)S(1)} %shard_map.107), channel_id=1, source_target_pairs={{0,64},{2,66},{64,130},{66,128},{128,192},{130,194},{192,0},{194,2... | collective-permute-start | bytes 153608 | tf_op jit(solution)/shard_map/ppermute | solution.py:35
  170.7 2.5 collective-permute-done.19
  173.2 12.5 %all_to_all.67 = bf16[8,8,3072]{2,1,0:T(8,128)(2,1)S(1)} all-to-all(bf16[8,8,3072]{2,1,0:T(8,128)(2,1)S(1)} %broadcast_in_dim.37), channel_id=1, replica_groups=mesh['zh'=2,'core'=2,'xh'=2,'xl'=2,'yh'=2,'yl'=2,'zc'=2,'zf'=2] {'xh','z..., dimensions={0} | all-to-all | bytes 786432 | tf_op jit(solution)/shard_map/all_to_all | solution.py:45
  185.7 4.9 %shard_map.108 = bf16[64,3072]{1,0:T(8,128)(2,1)S(1)} custom-call(bf16[64,3072]{1,0:T(8,128)(2,1)S(1)} %bitcast.71, f32[3,3072]{1,0:T(4,128)S(1)} %reshape.75.mod_ref, bf16[1280,3072]{1,0:T(8,128)(2,1)S(1)} %get-tuple-element.80.up, bf16[1280,3072]{1,0:T(8,128)(2,1)S(1)} %get-tuple-element.81.down, bf16[256,3072]{1,0:T(8,128)(2,1)S(1)} %get-tuple-element.84.up_end, ...), custom_call_target="tpu_custom_call" | custom-call | flops 1207959552 | bytes 19660800 | tf_op jit(solution)/shard_map/pallas_call | solution.py:79
  190.7 12.7 %all_to_all.68.parts_ref = bf16[8,8,3072]{2,1,0:T(8,128)(2,1)S(1)} all-to-all(bf16[8,8,3072]{2,1,0:T(8,128)(2,1)S(1)} %bitcast.72), channel_id=1, replica_groups=mesh['zh'=2,'core'=2,'xh'=2,'xl'=2,'yh'=2,'yl'=2,'zc'=2,'zf'=2] {'xh','z..., dimensions={0} | all-to-all | bytes 786432 | tf_op jit(solution)/shard_map/all_to_all | solution.py:282
  203.4 13.0 %collective-permute-start.20 = (bf16[8,3200]{1,0:T(8,128)(2,1)S(1)}, bf16[8,3200]{1,0:T(8,128)(2,1)S(1)}, u32[]{:S(2)}, u32[]{:S(2)}) collective-permute-start(bf16[8,3200]{1,0:T(8,128)(2,1)S(1)} %shard_map.109), channel_id=1, source_target_pairs={{0,64},{2,66},{64,130},{66,128},{128,192},{130,194},{192,0},{194,2... | collective-permute-start | bytes 153608 | tf_op jit(solution)/shard_map/ppermute | solution.py:35
  216.4 1.6 collective-permute-done.20
  218.1 14.5 %all_to_all.69 = bf16[8,8,3072]{2,1,0:T(8,128)(2,1)S(1)} all-to-all(bf16[8,8,3072]{2,1,0:T(8,128)(2,1)S(1)} %broadcast_in_dim.38), channel_id=1, replica_groups=mesh['zh'=2,'core'=2,'xh'=2,'xl'=2,'yh'=2,'yl'=2,'zc'=2,'zf'=2] {'xh','z..., dimensions={0} | all-to-all | bytes 786432 | tf_op jit(solution)/shard_map/all_to_all | solution.py:45
  232.7 4.9 %shard_map.110 = bf16[64,3072]{1,0:T(8,128)(2,1)S(1)} custom-call(bf16[64,3072]{1,0:T(8,128)(2,1)S(1)} %bitcast.73, f32[3,3072]{1,0:T(4,128)S(1)} %reshape.75.mod_ref, bf16[1280,3072]{1,0:T(8,128)(2,1)S(1)} %get-tuple-element.80.up, bf16[1280,3072]{1,0:T(8,128)(2,1)S(1)} %get-tuple-element.81.down, bf16[256,3072]{1,0:T(8,128)(2,1)S(1)} %get-tuple-element.84.up_end, ...), custom_call_target="tpu_custom_call" | custom-call | flops 1207959552 | bytes 19660800 | tf_op jit(solution)/shard_map/pallas_call | solution.py:79
  237.6 15.6 %all_to_all.70.parts_ref = bf16[8,8,3072]{2,1,0:T(8,128)(2,1)S(1)} all-to-all(bf16[8,8,3072]{2,1,0:T(8,128)(2,1)S(1)} %bitcast.74), channel_id=1, replica_groups=mesh['zh'=2,'core'=2,'xh'=2,'xl'=2,'yh'=2,'yl'=2,'zc'=2,'zf'=2] {'xh','z..., dimensions={0} | all-to-all | bytes 786432 | tf_op jit(solution)/shard_map/all_to_all | solution.py:282
  253.3 3.2 %collective-permute-start.21 = (bf16[8,3200]{1,0:T(8,128)(2,1)S(1)}, bf16[8,3200]{1,0:T(8,128)(2,1)S(1)}, u32[]{:S(2)}, u32[]{:S(2)}) collective-permute-start(bf16[8,3200]{1,0:T(8,128)(2,1)S(1)} %shard_map.111), channel_id=1, source_target_pairs={{0,64},{2,66},{64,130},{66,128},{128,192},{130,194},{1,65},{3,67},... | collective-permute-start | bytes 153608 | tf_op jit(solution)/shard_map/ppermute | solution.py:35
  256.6 2.6 collective-permute-done.21
  259.2 16.2 %all_to_all.71 = bf16[8,8,3072]{2,1,0:T(8,128)(2,1)S(1)} all-to-all(bf16[8,8,3072]{2,1,0:T(8,128)(2,1)S(1)} %broadcast_in_dim.39), channel_id=1, replica_groups=mesh['zh'=2,'core'=2,'xh'=2,'xl'=2,'yh'=2,'yl'=2,'zc'=2,'zf'=2] {'xh','z..., dimensions={0} | all-to-all | bytes 786432 | tf_op jit(solution)/shard_map/all_to_all | solution.py:45
  275.4 4.9 %shard_map.112 = bf16[64,3072]{1,0:T(8,128)(2,1)S(1)} custom-call(bf16[64,3072]{1,0:T(8,128)(2,1)S(1)} %bitcast.68, f32[3,3072]{1,0:T(4,128)S(1)} %reshape.75.mod_ref, bf16[1280,3072]{1,0:T(8,128)(2,1)S(1)} %get-tuple-element.80.up, bf16[1280,3072]{1,0:T(8,128)(2,1)S(1)} %get-tuple-element.81.down, bf16[256,3072]{1,0:T(8,128)(2,1)S(1)} %get-tuple-element.84.up_end, ...), custom_call_target="tpu_custom_call" | custom-call | flops 1207959552 | bytes 19660800 | tf_op jit(solution)/shard_map/pallas_call | solution.py:79
  280.3 14.1 %all_to_all.72.parts_ref = bf16[8,8,3072]{2,1,0:T(8,128)(2,1)S(1)} all-to-all(bf16[8,8,3072]{2,1,0:T(8,128)(2,1)S(1)} %bitcast.69), channel_id=1, replica_groups=mesh['zh'=2,'core'=2,'xh'=2,'xl'=2,'yh'=2,'yl'=2,'zc'=2,'zf'=2] {'xh','z..., dimensions={0} | all-to-all | bytes 786432 | tf_op jit(solution)/shard_map/all_to_all | solution.py:282
  294.5 4.8 %collective-permute-start.24 = (bf16[8,3200]{1,0:T(8,128)(2,1)S(1)}, bf16[8,3200]{1,0:T(8,128)(2,1)S(1)}, u32[]{:S(2)}, u32[]{:S(2)}) collective-permute-start(bf16[8,3200]{1,0:T(8,128)(2,1)S(1)} %shard_map.113), channel_id=1, source_target_pairs={{0,64},{2,66},{64,128},{66,130},{128,194},{130,192},{1,65},{3,67},... | collective-permute-start | bytes 153608 | tf_op jit(solution)/shard_map/ppermute | solution.py:35
  299.3 1.3 collective-permute-start.23
  (96 shorter events, 21.2 us)
Async XLA Ops:
  0.6 62.4 %copy-start = (bf16[1,144,3584]{2,1,0:T(8,128)(2,1)S(1)}, bf16[1,144,3584]{2,1,0:T(8,128)(2,1)}, u32[]{:S(2)}) copy-start(bf16[1,144,3584]{2,1,0:T(8,128)(2,1)} %param.15) | copy-start | bytes 3096580
  0.6 1.7 copy-start.1
  2.4 0.8 copy-start.6
  3.3 18.1 %copy-start.8 = (s32[1,8]{1,0:T(1,128)S(1)}, s32[1,8]{1,0:T(1,128)}, u32[]{:S(2)}) copy-start(s32[1,8]{1,0:T(1,128)} %param.12) | copy-start | bytes 100
  3.3 18.2 %copy-start.7 = (bf16[1,8,3072]{2,1,0:T(8,128)(2,1)S(1)}, bf16[1,8,3072]{2,1,0:T(8,128)(2,1)}, u32[]{:S(2)}) copy-start(bf16[1,8,3072]{2,1,0:T(8,128)(2,1)} %param.11) | copy-start | bytes 147460
  4.9 40.6 %collective-permute-start = (bf16[192,3072]{1,0:T(8,128)(2,1)}, bf16[192,3072]{1,0:T(8,128)(2,1)S(1)}, u32[]{:S(2)}, u32[]{:S(2)}) collective-permute-start(bf16[192,3072]{1,0:T(8,128)(2,1)} %get-tuple-element.57.refs_0_), channel_id=1, source_target_pairs={{4,0},{8,4},{12,8},{0,12},{5,1},{9,5},{13,9},{1,13},{6,2},{10,6},{... | collective-permute-start | bytes 3538952 | tf_op jit(solution)/shard_map/ppermute | solution.py:28
  8.5 37.0 %collective-permute-start.1 = (bf16[192,3072]{1,0:T(8,128)(2,1)}, bf16[192,3072]{1,0:T(8,128)(2,1)S(1)}, u32[]{:S(2)}, u32[]{:S(2)}) collective-permute-start(bf16[192,3072]{1,0:T(8,128)(2,1)} %get-tuple-element.56.refs_1_), channel_id=1, source_target_pairs={{12,0},{0,4},{4,8},{8,12},{13,1},{1,5},{5,9},{9,13},{14,2},{2,6},{... | collective-permute-start | bytes 3538952 | tf_op jit(solution)/shard_map/ppermute | solution.py:28
  8.5 37.0 %collective-permute-start.2 = (bf16[192,3072]{1,0:T(8,128)(2,1)}, bf16[192,3072]{1,0:T(8,128)(2,1)}, u32[]{:S(2)}, u32[]{:S(2)}) collective-permute-start(bf16[192,3072]{1,0:T(8,128)(2,1)} %get-tuple-element.57.refs_0_), channel_id=1, source_target_pairs={{16,0},{32,16},{48,32},{0,48},{17,1},{33,17},{49,33},{1,49},{18,2}... | collective-permute-start | bytes 3538952 | tf_op jit(solution)/shard_map/ppermute | solution.py:28
  11.0 34.5 %collective-permute-start.3 = (bf16[192,3072]{1,0:T(8,128)(2,1)}, bf16[192,3072]{1,0:T(8,128)(2,1)}, u32[]{:S(2)}, u32[]{:S(2)}) collective-permute-start(bf16[192,3072]{1,0:T(8,128)(2,1)} %get-tuple-element.56.refs_1_), channel_id=1, source_target_pairs={{48,0},{0,16},{16,32},{32,48},{49,1},{1,17},{17,33},{33,49},{50,2}... | collective-permute-start | bytes 3538952 | tf_op jit(solution)/shard_map/ppermute | solution.py:28
  11.7 19.4 %all-to-all-start = ((f32[16,28,128]{2,1,0:T(8,128)}), f32[16,28,128]{2,1,0:T(8,128)}, u32[]{:S(2)}, u32[]{:S(2)}) async-start(f32[16,28,128]{2,1,0:T(8,128)} %broadcast_in_dim.28), calls=%async_computation | async-start | bytes 524288 | tf_op jit(solution)/shard_map/all_to_all | solution.py:45
  46.3 14.5 %all-to-all-start.2 = ((f32[16,28,128]{2,1,0:T(8,128)}), f32[16,28,128]{2,1,0:T(8,128)}, u32[]{:S(2)}, u32[]{:S(2)}) async-start(f32[16,28,128]{2,1,0:T(8,128)} %broadcast_in_dim.31), calls=%async_computation.2 | async-start | bytes 524288 | tf_op jit(solution)/shard_map/all_to_all | solution.py:45
  53.4 31.4 %collective-permute-start.4 = (bf16[192,3072]{1,0:T(8,128)(2,1)}, bf16[192,3072]{1,0:T(8,128)(2,1)}, u32[]{:S(2)}, u32[]{:S(2)}) collective-permute-start(bf16[192,3072]{1,0:T(8,128)(2,1)} %get-tuple-element.56.refs_1_), channel_id=1, source_target_pairs={{4,0},{8,4},{12,8},{0,12},{5,1},{9,5},{13,9},{1,13},{6,2},{10,6},{... | collective-permute-start | bytes 3538952 | tf_op jit(solution)/shard_map/ppermute | solution.py:28
  55.9 28.9 %collective-permute-start.5 = (bf16[192,3072]{1,0:T(8,128)(2,1)}, bf16[192,3072]{1,0:T(8,128)(2,1)}, u32[]{:S(2)}, u32[]{:S(2)}) collective-permute-start(bf16[192,3072]{1,0:T(8,128)(2,1)} %get-tuple-element.57.refs_0_), channel_id=1, source_target_pairs={{12,0},{0,4},{4,8},{8,12},{13,1},{1,5},{5,9},{9,13},{14,2},{2,6},{... | collective-permute-start | bytes 3538952 | tf_op jit(solution)/shard_map/ppermute | solution.py:28
  55.9 28.9 %collective-permute-start.6 = (bf16[192,3072]{1,0:T(8,128)(2,1)S(1)}, bf16[192,3072]{1,0:T(8,128)(2,1)}, u32[]{:S(2)}, u32[]{:S(2)}) collective-permute-start(bf16[192,3072]{1,0:T(8,128)(2,1)S(1)} %collective-permute-done.refs_4_), channel_id=1, source_target_pairs={{16,0},{32,16},{48,32},{0,48},{17,1},{33,17},{49,33},{1,49},{18,2}... | collective-permute-start | bytes 3538952 | tf_op jit(solution)/shard_map/ppermute | solution.py:28
  58.3 26.5 %collective-permute-start.7 = (bf16[192,3072]{1,0:T(8,128)(2,1)S(1)}, bf16[192,3072]{1,0:T(8,128)(2,1)}, u32[]{:S(2)}, u32[]{:S(2)}) collective-permute-start(bf16[192,3072]{1,0:T(8,128)(2,1)S(1)} %collective-permute-done.1.refs_5_), channel_id=1, source_target_pairs={{48,0},{0,16},{16,32},{32,48},{49,1},{1,17},{17,33},{33,49},{50,2}... | collective-permute-start | bytes 3538952 | tf_op jit(solution)/shard_map/ppermute | solution.py:28
  64.1 10.6 %all-to-all-start.3 = ((f32[4,2,128]{2,1,0:T(2,128)}), f32[4,2,128]{2,1,0:T(2,128)S(1)}, u32[]{:S(2)}, u32[]{:S(2)}) async-start(f32[4,2,128]{2,1,0:T(2,128)} %broadcast_in_dim.33), calls=%async_computation.3 | async-start | bytes 8192 | tf_op jit(solution)/shard_map/all_to_all | solution.py:45
  70.1 4.5 %copy-start.5 = (bf16[1,8,3072]{2,1,0:T(8,128)(2,1)S(1)}, bf16[1,8,3072]{2,1,0:T(8,128)(2,1)}, u32[]{:S(2)}) copy-start(bf16[1,8,3072]{2,1,0:T(8,128)(2,1)} %param.9) | copy-start | bytes 147460
  75.3 9.4 %all-to-all-start.4 = ((bf16[4,8,3072]{2,1,0:T(8,128)(2,1)}), bf16[4,8,3072]{2,1,0:T(8,128)(2,1)}, u32[]{:S(2)}, u32[]{:S(2)}) async-start(bf16[4,8,3072]{2,1,0:T(8,128)(2,1)} %broadcast_in_dim.34), calls=%async_computation.4 | async-start | bytes 393216 | tf_op jit(solution)/shard_map/all_to_all | solution.py:45
  79.3 7.7 %copy-start.9 = (s32[1,8]{1,0:T(1,128)S(1)}, s32[1,8]{1,0:T(1,128)}, u32[]{:S(2)}) copy-start(s32[1,8]{1,0:T(1,128)} %param.10) | copy-start | bytes 100
  84.8 11.2 %collective-permute-start.9 = (bf16[96,3072]{1,0:T(8,128)(2,1)}, bf16[96,3072]{1,0:T(8,128)(2,1)}, u32[]{:S(2)}, u32[]{:S(2)}) collective-permute-start(bf16[96,3072]{1,0:T(8,128)(2,1)} %get-tuple-element.59), channel_id=1, source_target_pairs={{4,0},{8,4},{12,8},{0,12},{5,1},{9,5},{13,9},{1,13},{6,2},{10,6},{... | collective-permute-start | bytes 1769480 | tf_op jit(solution)/shard_map/ppermute | solution.py:28
  86.1 22.5 %collective-permute-start.10 = (bf16[96,3072]{1,0:T(8,128)(2,1)}, bf16[96,3072]{1,0:T(8,128)(2,1)}, u32[]{:S(2)}, u32[]{:S(2)}) collective-permute-start(bf16[96,3072]{1,0:T(8,128)(2,1)} %get-tuple-element.60), channel_id=1, source_target_pairs={{4,0},{8,4},{12,8},{0,12},{5,1},{9,5},{13,9},{1,13},{6,2},{10,6},{... | collective-permute-start | bytes 1769480 | tf_op jit(solution)/shard_map/ppermute | solution.py:28
  87.0 39.1 %collective-permute-start.13 = (bf16[192,3072]{1,0:T(8,128)(2,1)}, bf16[192,3072]{1,0:T(8,128)(2,1)}, u32[]{:S(2)}, u32[]{:S(2)}) collective-permute-start(bf16[192,3072]{1,0:T(8,128)(2,1)} %collective-permute-done.5.refs_7_), channel_id=1, source_target_pairs={{16,0},{32,16},{48,32},{0,48},{17,1},{33,17},{49,33},{1,49},{18,2}... | collective-permute-start | bytes 3538952 | tf_op jit(solution)/shard_map/ppermute | solution.py:28
  87.8 38.3 %collective-permute-start.14 = (bf16[192,3072]{1,0:T(8,128)(2,1)}, bf16[192,3072]{1,0:T(8,128)(2,1)}, u32[]{:S(2)}, u32[]{:S(2)}) collective-permute-start(bf16[192,3072]{1,0:T(8,128)(2,1)} %collective-permute-done.4.refs_6_), channel_id=1, source_target_pairs={{48,0},{0,16},{16,32},{32,48},{49,1},{1,17},{17,33},{33,49},{50,2}... | collective-permute-start | bytes 3538952 | tf_op jit(solution)/shard_map/ppermute | solution.py:28
  88.5 40.5 %collective-permute-start.8 = (bf16[4,8,3072]{2,1,0:T(8,128)(2,1)}, bf16[4,8,3072]{2,1,0:T(8,128)(2,1)}, u32[]{:S(2)}, u32[]{:S(2)}) collective-permute-start(bf16[4,8,3072]{2,1,0:T(8,128)(2,1)} %all-to-all-done.4), channel_id=1, source_target_pairs={{0,32},{32,0},{1,33},{33,1},{2,34},{34,2},{3,35},{35,3},{4,36},{36... | collective-permute-start | bytes 589832 | tf_op jit(solution)/shard_map/ppermute | solution.py:201
  89.9 27.0 %all-to-all-start.5 = ((f32[16,4,2,128]{3,2,1,0:T(2,128)}), f32[16,4,2,128]{3,2,1,0:T(2,128)}, u32[]{:S(2)}, u32[]{:S(2)}) async-start(f32[16,4,2,128]{3,2,1,0:T(2,128)} %broadcast_in_dim.36), calls=%async_computation.5 | async-start | bytes 131072 | tf_op jit(solution)/shard_map/all_to_all | solution.py:45
  96.0 23.3 %collective-permute-start.11 = (bf16[96,3072]{1,0:T(8,128)(2,1)}, bf16[96,3072]{1,0:T(8,128)(2,1)}, u32[]{:S(2)}, u32[]{:S(2)}) collective-permute-start(bf16[96,3072]{1,0:T(8,128)(2,1)} %get-tuple-element.61), channel_id=1, source_target_pairs={{12,0},{0,4},{4,8},{8,12},{13,1},{1,5},{5,9},{9,13},{14,2},{2,6},{... | collective-permute-start | bytes 1769480 | tf_op jit(solution)/shard_map/ppermute | solution.py:28
  108.7 17.5 %collective-permute-start.12 = (bf16[96,3072]{1,0:T(8,128)(2,1)}, bf16[96,3072]{1,0:T(8,128)(2,1)}, u32[]{:S(2)}, u32[]{:S(2)}) collective-permute-start(bf16[96,3072]{1,0:T(8,128)(2,1)} %get-tuple-element.62), channel_id=1, source_target_pairs={{12,0},{0,4},{4,8},{8,12},{13,1},{1,5},{5,9},{9,13},{14,2},{2,6},{... | collective-permute-start | bytes 1769480 | tf_op jit(solution)/shard_map/ppermute | solution.py:28
  126.1 10.8 %collective-permute-start.15 = (bf16[96,3072]{1,0:T(8,128)(2,1)}, bf16[96,3072]{1,0:T(8,128)(2,1)S(1)}, u32[]{:S(2)}, u32[]{:S(2)}) collective-permute-start(bf16[96,3072]{1,0:T(8,128)(2,1)} %collective-permute-done.9.refs_12_), channel_id=1, source_target_pairs={{16,0},{32,16},{48,32},{0,48},{17,1},{33,17},{49,33},{1,49},{18,2}... | collective-permute-start | bytes 1769480 | tf_op jit(solution)/shard_map/ppermute | solution.py:28
  127.0 11.3 %collective-permute-start.16 = (bf16[96,3072]{1,0:T(8,128)(2,1)}, bf16[96,3072]{1,0:T(8,128)(2,1)S(1)}, u32[]{:S(2)}, u32[]{:S(2)}) collective-permute-start(bf16[96,3072]{1,0:T(8,128)(2,1)} %collective-permute-done.11.refs_14_.refs_0_), channel_id=1, source_target_pairs={{48,0},{0,16},{16,32},{32,48},{49,1},{1,17},{17,33},{33,49},{50,2}... | collective-permute-start | bytes 1769480 | tf_op jit(solution)/shard_map/ppermute | solution.py:28
  127.6 10.7 %collective-permute-start.17 = (bf16[96,3072]{1,0:T(8,128)(2,1)}, bf16[96,3072]{1,0:T(8,128)(2,1)S(1)}, u32[]{:S(2)}, u32[]{:S(2)}) collective-permute-start(bf16[96,3072]{1,0:T(8,128)(2,1)} %slice.87), channel_id=1, source_target_pairs={{4,0},{8,4},{12,8},{0,12},{5,1},{9,5},{13,9},{1,13},{6,2},{10,6},{... | collective-permute-start | bytes 1769480 | tf_op jit(solution)/shard_map/ppermute | solution.py:28
  128.3 10.4 %collective-permute-start.18 = (bf16[96,3072]{1,0:T(8,128)(2,1)}, bf16[96,3072]{1,0:T(8,128)(2,1)S(1)}, u32[]{:S(2)}, u32[]{:S(2)}) collective-permute-start(bf16[96,3072]{1,0:T(8,128)(2,1)} %slice.88), channel_id=1, source_target_pairs={{12,0},{0,4},{4,8},{8,12},{13,1},{1,5},{5,9},{9,13},{14,2},{2,6},{... | collective-permute-start | bytes 1769480 | tf_op jit(solution)/shard_map/ppermute | solution.py:28
  144.9 28.3 %copy-start.3 = (bf16[8,3200]{1,0:T(8,128)(2,1)S(1)}, bf16[8,3200]{1,0:T(8,128)(2,1)}, u32[]{:S(2)}) copy-start(bf16[8,3200]{1,0:T(8,128)(2,1)} %get-tuple-element.90) | copy-start | bytes 153604
  166.4 6.7 %collective-permute-start.19 = (bf16[8,3200]{1,0:T(8,128)(2,1)S(1)}, bf16[8,3200]{1,0:T(8,128)(2,1)S(1)}, u32[]{:S(2)}, u32[]{:S(2)}) collective-permute-start(bf16[8,3200]{1,0:T(8,128)(2,1)S(1)} %shard_map.107), channel_id=1, source_target_pairs={{0,64},{2,66},{64,130},{66,128},{128,192},{130,194},{192,0},{194,2... | collective-permute-start | bytes 153608 | tf_op jit(solution)/shard_map/ppermute | solution.py:35
  190.7 27.4 %copy-start.2 = (bf16[8,3200]{1,0:T(8,128)(2,1)S(1)}, bf16[8,3200]{1,0:T(8,128)(2,1)}, u32[]{:S(2)}) copy-start(bf16[8,3200]{1,0:T(8,128)(2,1)} %get-tuple-element.89) | copy-start | bytes 153604
  203.4 14.6 %collective-permute-start.20 = (bf16[8,3200]{1,0:T(8,128)(2,1)S(1)}, bf16[8,3200]{1,0:T(8,128)(2,1)S(1)}, u32[]{:S(2)}, u32[]{:S(2)}) collective-permute-start(bf16[8,3200]{1,0:T(8,128)(2,1)S(1)} %shard_map.109), channel_id=1, source_target_pairs={{0,64},{2,66},{64,130},{66,128},{128,192},{130,194},{192,0},{194,2... | collective-permute-start | bytes 153608 | tf_op jit(solution)/shard_map/ppermute | solution.py:35
  253.3 5.8 %collective-permute-start.21 = (bf16[8,3200]{1,0:T(8,128)(2,1)S(1)}, bf16[8,3200]{1,0:T(8,128)(2,1)S(1)}, u32[]{:S(2)}, u32[]{:S(2)}) collective-permute-start(bf16[8,3200]{1,0:T(8,128)(2,1)S(1)} %shard_map.111), channel_id=1, source_target_pairs={{0,64},{2,66},{64,130},{66,128},{128,192},{130,194},{1,65},{3,67},... | collective-permute-start | bytes 153608 | tf_op jit(solution)/shard_map/ppermute | solution.py:35
  280.3 20.9 %copy-start.4 = (bf16[8,3200]{1,0:T(8,128)(2,1)S(1)}, bf16[8,3200]{1,0:T(8,128)(2,1)}, u32[]{:S(2)}) copy-start(bf16[8,3200]{1,0:T(8,128)(2,1)} %get-tuple-element.93) | copy-start | bytes 153604
  294.5 6.8 %collective-permute-start.24 = (bf16[8,3200]{1,0:T(8,128)(2,1)S(1)}, bf16[8,3200]{1,0:T(8,128)(2,1)S(1)}, u32[]{:S(2)}, u32[]{:S(2)}) collective-permute-start(bf16[8,3200]{1,0:T(8,128)(2,1)S(1)} %shard_map.113), channel_id=1, source_target_pairs={{0,64},{2,66},{64,128},{66,130},{128,194},{130,192},{1,65},{3,67},... | collective-permute-start | bytes 153608 | tf_op jit(solution)/shard_map/ppermute | solution.py:35
  299.3 3.1 %collective-permute-start.23 = (bf16[8,3200]{1,0:T(8,128)(2,1)S(1)}, bf16[8,3200]{1,0:T(8,128)(2,1)S(1)}, u32[]{:S(2)}, u32[]{:S(2)}) collective-permute-start(bf16[8,3200]{1,0:T(8,128)(2,1)S(1)} %broadcast_select_fusion), channel_id=1, source_target_pairs={{0,64},{2,66},{192,194},{194,192},{1,65},{3,67},{193,195},{195,193... | collective-permute-start | bytes 153608 | tf_op jit(solution)/shard_map/ppermute | solution.py:35
  300.6 1.8 collective-permute-start.22

commit v5 on v4

--- a/solution.py
+++ b/solution.py
@@ -195,9 +195,12 @@
     line, mine, halves, yp_second, ym_first, xa_yp, xb_ym = together(
         (line, mine, halves, yp_second, ym_first, xa_yp, xb_ym)
     )
-    y2 = [from_neighbour(half, "y", 1 if i < 2 else -1) for i, half in enumerate(halves)]
+    y2 = [from_neighbour(halves[0], "y", 1), None, from_neighbour(halves[2], "y", -1), None]
     xa_ym = from_neighbour(ym_first, "x", 1)
     xb_yp = from_neighbour(yp_second, "x", -1)
+    halves, y2[0], y2[2] = together((halves, y2[0], y2[2]))
+    y2[1] = from_neighbour(halves[1], "y", 1)
+    y2[3] = from_neighbour(halves[3], "y", -1)
     theirs = lax.ppermute(mine, "xh", [(0, 1), (1, 0)])
     modes = exchange(line, PLANE)
     modes = modes.reshape(-1, rows * LANES)[:, :columns].reshape(3, -1)

time: 304 us -> 299 us (0.984)
  waiting for transfers between devices: 53.6 us -> 45.6 us
  starting transfers between devices: 77.4 us -> 81.7 us
    ppermute x18, waiting for transfers between devices: 24 us -> 5.58 us  [from_neighbour(): return lax.ppermute(block, (axis + 'h', axis + 'l'), route)]
    all_to_all x5, waiting for transfers between devices: 22.4 us -> 33.1 us  [exchange(): return lax.all_to_all(copies, axes, 0, 0)]
  transfers between devices with their start and end apart: 30 -> 30, of which waited for: 15 -> 14; matrix products, arithmetic and copies ran while one was open for 6% -> 6% of each run, Pallas kernels for 2% -> 2%
where the time goes in v5:
time: 299 us; the launch traced here: 297 us
  blocking collectives  118 us (39%)
  starting transfers between devices  81.7 us (27%)
  waiting for transfers between devices  45.6 us (15%)
  Pallas kernels  26.4 us (9%)
  local copies, waits for them, and re-layouts  15.7 us (5%)
  other arithmetic  6.59 us (2%)
    all_to_all x4, blocking collectives, per_device(): lax.all_to_all(partial.reshape(GROUP_SIZE, tokens, breadth), GROUP, 0, 0)  61.9 us
    all_to_all x4, blocking collectives, exchange(): return lax.all_to_all(copies, axes, 0, 0)  56.4 us
    all_to_all x5, waiting for transfers between devices, exchange(): return lax.all_to_all(copies, axes, 0, 0)  33.1 us
    all_to_all x5, starting transfers between devices, exchange(): return lax.all_to_all(copies, axes, 0, 0)  31.8 us
    ppermute x6, starting transfers between devices, between_sections(): return lax.ppermute(block, SECTION + ('zc',), route)  29.8 us
    pallas_call x4, Pallas kernels, layer(): pl.pallas_call(layer_kernel, out_shape=jax.ShapeDtypeStruct((rows, breadt...  19.8 us
    ppermute x18, starting transfers between devices, from_neighbour(): return lax.ppermute(block, (axis + 'h', axis + 'l'), route)  18.5 us
    ppermute x6, waiting for transfers between devices, between_sections(): return lax.ppermute(block, SECTION + ('zc',), route)  6.9 us
  transfers between devices with their start and end apart: 30, of which 14 were waited for; matrix products, arithmetic and copies ran while one was open for 6% of the time, Pallas kernels for 2%

profile of v5, /device:TPU:1, one launch (start us, length us, event | category | flops | bytes accessed | tf_op | source)
XLA Modules:
  0.0 297.2 jit_solution(17162723489958573867)
XLA Ops:
  0.7 1.5 slice_bitcast_fusion
  3.3 1.6 pad_maximum_fusion
  4.9 3.6 %collective-permute-start = (bf16[192,3072]{1,0:T(8,128)(2,1)}, bf16[192,3072]{1,0:T(8,128)(2,1)S(1)}, u32[]{:S(2)}, u32[]{:S(2)}) collective-permute-start(bf16[192,3072]{1,0:T(8,128)(2,1)} %get-tuple-element.61.refs_0_), channel_id=1, source_target_pairs={{4,0},{8,4},{12,8},{0,12},{5,1},{9,5},{13,9},{1,13},{6,2},{10,6},{... | collective-permute-start | bytes 3538952 | tf_op jit(solution)/shard_map/ppermute | solution.py:28
  8.5 2.5 collective-permute-start.2
  11.7 9.7 %all-to-all-start = ((f32[16,28,128]{2,1,0:T(8,128)}), f32[16,28,128]{2,1,0:T(8,128)}, u32[]{:S(2)}, u32[]{:S(2)}) async-start(f32[16,28,128]{2,1,0:T(8,128)} %broadcast_in_dim.28), calls=%async_computation | async-start | bytes 524288 | tf_op jit(solution)/shard_map/all_to_all | solution.py:45
  21.5 9.6 %all-to-all-done = f32[16,28,128]{2,1,0:T(8,128)} async-done(((f32[16,28,128]{2,1,0:T(8,128)}), f32[16,28,128]{2,1,0:T(8,128)}, u32[]{:S(2)}, u32[]{:S(2)}) %all-to-all-start) | async-done | bytes 229408 | tf_op jit(solution)/shard_map/all_to_all | solution.py:45
  32.1 13.4 %all_to_all.65 = bf16[4,8,3200]{2,1,0:T(8,128)(2,1)} all-to-all(bf16[4,8,3200]{2,1,0:T(8,128)(2,1)S(1)} %broadcast_in_dim.30), channel_id=1, replica_groups=mesh['zh'=2,'core'=2,'xh'=2,'xl'=2,'yh'=2,'yl'=2,'zc'=2,'zf'=2] {'zh','c..., dimensions={0} | all-to-all | bytes 409600 | tf_op jit(solution)/shard_map/all_to_all | solution.py:45
  46.3 7.1 %all-to-all-start.2 = ((f32[16,28,128]{2,1,0:T(8,128)}), f32[16,28,128]{2,1,0:T(8,128)}, u32[]{:S(2)}, u32[]{:S(2)}) async-start(f32[16,28,128]{2,1,0:T(8,128)} %broadcast_in_dim.31), calls=%async_computation.2 | async-start | bytes 524288 | tf_op jit(solution)/shard_map/all_to_all | solution.py:45
  53.4 2.5 collective-permute-start.4
  55.9 2.4 collective-permute-start.6
  58.3 2.5 all-to-all-done.2
  64.1 6.0 %all-to-all-start.3 = ((f32[4,2,128]{2,1,0:T(2,128)}), f32[4,2,128]{2,1,0:T(2,128)S(1)}, u32[]{:S(2)}, u32[]{:S(2)}) async-start(f32[4,2,128]{2,1,0:T(2,128)} %broadcast_in_dim.33), calls=%async_computation.3 | async-start | bytes 8192 | tf_op jit(solution)/shard_map/all_to_all | solution.py:45
  71.2 3.4 %all-to-all-done.3 = f32[4,2,128]{2,1,0:T(2,128)S(1)} async-done(((f32[4,2,128]{2,1,0:T(2,128)}), f32[4,2,128]{2,1,0:T(2,128)S(1)}, u32[]{:S(2)}, u32[]{:S(2)}) %all-to-all-start.3) | async-done | bytes 4128 | tf_op jit(solution)/shard_map/all_to_all | solution.py:45
  75.3 4.0 %all-to-all-start.4 = ((bf16[4,8,3072]{2,1,0:T(8,128)(2,1)}), bf16[4,8,3072]{2,1,0:T(8,128)(2,1)}, u32[]{:S(2)}, u32[]{:S(2)}) async-start(bf16[4,8,3072]{2,1,0:T(8,128)(2,1)} %broadcast_in_dim.34), calls=%async_computation.4 | async-start | bytes 393216 | tf_op jit(solution)/shard_map/all_to_all | solution.py:45
  80.5 4.3 %all-to-all-done.4 = bf16[4,8,3072]{2,1,0:T(8,128)(2,1)} async-done(((bf16[4,8,3072]{2,1,0:T(8,128)(2,1)}), bf16[4,8,3072]{2,1,0:T(8,128)(2,1)}, u32[]{:S(2)}, u32[]{:S(2)}) %all-to-all-start.4) | async-done | bytes 196640 | tf_op jit(solution)/shard_map/all_to_all | solution.py:45
  84.8 1.3 collective-permute-start.9
  86.4 1.3 collective-permute-start.13
  87.9 1.8 collective-permute-start.8
  90.3 5.0 %all-to-all-start.5 = ((f32[16,4,2,128]{3,2,1,0:T(2,128)}), f32[16,4,2,128]{3,2,1,0:T(2,128)}, u32[]{:S(2)}, u32[]{:S(2)}) async-start(f32[16,4,2,128]{3,2,1,0:T(2,128)} %broadcast_in_dim.36), calls=%async_computation.5 | async-start | bytes 131072 | tf_op jit(solution)/shard_map/all_to_all | solution.py:45
  96.0 1.3 collective-permute-done.10.refs_14_.refs_0_
  98.8 1.5 slice_bitcast_fusion.4
  100.3 1.9 slice.87
  102.3 1.9 slice.88
  104.2 13.3 %all-to-all-done.5 = f32[16,4,2,128]{3,2,1,0:T(2,128)} async-done(((f32[16,4,2,128]{3,2,1,0:T(2,128)}), f32[16,4,2,128]{3,2,1,0:T(2,128)}, u32[]{:S(2)}, u32[]{:S(2)}) %all-to-all-start.5) | async-done | bytes 65568 | tf_op jit(solution)/shard_map/all_to_all | solution.py:45
  117.5 1.5 copy.19
  120.2 1.2 collective-permute-start.16
  124.1 5.1 %shard_map.104 = (bf16[1280,3072]{1,0:T(8,128)(2,1)S(1)}, bf16[1280,3072]{1,0:T(8,128)(2,1)S(1)}) custom-call(bf16[192,3072]{1,0:T(8,128)(2,1)} %get-tuple-element.61.refs_0_, bf16[192,3072]{1,0:T(8,128)(2,1)} %get-tuple-element.60.refs_1_, bf16[192,3072]{1,0:T(8,128)(2,1)} %collective-permute-done.2.refs_2_, ...), custom_call_target="tpu_custom_call" | custom-call | bytes 31457280 | tf_op jit(solution)/shard_map/pallas_call | solution.py:118
  130.7 2.0 collective-permute-done.18.refs_5_
  132.8 1.2 shard_map.105
  133.9 4.9 %shard_map.106 = bf16[64,3072]{1,0:T(8,128)(2,1)S(1)} custom-call(bf16[64,3072]{1,0:T(8,128)(2,1)S(1)} %bitcast.67, f32[3,3072]{1,0:T(4,128)S(1)} %reshape.75.mod_ref, bf16[1280,3072]{1,0:T(8,128)(2,1)S(1)} %get-tuple-element.88.up, bf16[1280,3072]{1,0:T(8,128)(2,1)S(1)} %get-tuple-element.89.down, bf16[256,3072]{1,0:T(8,128)(2,1)S(1)} %get-tuple-element.92.up_end, ...), custom_call_target="tpu_custom_call" | custom-call | flops 1207959552 | bytes 19660800 | tf_op jit(solution)/shard_map/pallas_call | solution.py:79
  138.9 20.2 %all_to_all.66.parts_ref = bf16[8,8,3072]{2,1,0:T(8,128)(2,1)S(1)} all-to-all(bf16[8,8,3072]{2,1,0:T(8,128)(2,1)S(1)} %bitcast.70), channel_id=1, replica_groups=mesh['zh'=2,'core'=2,'xh'=2,'xl'=2,'yh'=2,'yl'=2,'zc'=2,'zf'=2] {'xh','z..., dimensions={0} | all-to-all | bytes 786432 | tf_op jit(solution)/shard_map/all_to_all | solution.py:285
  159.2 5.8 %collective-permute-start.19 = (bf16[8,3200]{1,0:T(8,128)(2,1)S(1)}, bf16[8,3200]{1,0:T(8,128)(2,1)S(1)}, u32[]{:S(2)}, u32[]{:S(2)}) collective-permute-start(bf16[8,3200]{1,0:T(8,128)(2,1)S(1)} %shard_map.107), channel_id=1, source_target_pairs={{0,64},{2,66},{64,130},{66,128},{128,192},{130,194},{192,0},{194,2... | collective-permute-start | bytes 153608 | tf_op jit(solution)/shard_map/ppermute | solution.py:35
  165.0 2.6 collective-permute-done.19
  167.7 12.5 %all_to_all.67 = bf16[8,8,3072]{2,1,0:T(8,128)(2,1)S(1)} all-to-all(bf16[8,8,3072]{2,1,0:T(8,128)(2,1)S(1)} %broadcast_in_dim.37), channel_id=1, replica_groups=mesh['zh'=2,'core'=2,'xh'=2,'xl'=2,'yh'=2,'yl'=2,'zc'=2,'zf'=2] {'xh','z..., dimensions={0} | all-to-all | bytes 786432 | tf_op jit(solution)/shard_map/all_to_all | solution.py:45
  180.2 4.9 %shard_map.108 = bf16[64,3072]{1,0:T(8,128)(2,1)S(1)} custom-call(bf16[64,3072]{1,0:T(8,128)(2,1)S(1)} %bitcast.71, f32[3,3072]{1,0:T(4,128)S(1)} %reshape.75.mod_ref, bf16[1280,3072]{1,0:T(8,128)(2,1)S(1)} %get-tuple-element.88.up, bf16[1280,3072]{1,0:T(8,128)(2,1)S(1)} %get-tuple-element.89.down, bf16[256,3072]{1,0:T(8,128)(2,1)S(1)} %get-tuple-element.92.up_end, ...), custom_call_target="tpu_custom_call" | custom-call | flops 1207959552 | bytes 19660800 | tf_op jit(solution)/shard_map/pallas_call | solution.py:79
  185.2 12.7 %all_to_all.68.parts_ref = bf16[8,8,3072]{2,1,0:T(8,128)(2,1)S(1)} all-to-all(bf16[8,8,3072]{2,1,0:T(8,128)(2,1)S(1)} %bitcast.72), channel_id=1, replica_groups=mesh['zh'=2,'core'=2,'xh'=2,'xl'=2,'yh'=2,'yl'=2,'zc'=2,'zf'=2] {'xh','z..., dimensions={0} | all-to-all | bytes 786432 | tf_op jit(solution)/shard_map/all_to_all | solution.py:285
  197.9 12.7 %collective-permute-start.20 = (bf16[8,3200]{1,0:T(8,128)(2,1)S(1)}, bf16[8,3200]{1,0:T(8,128)(2,1)S(1)}, u32[]{:S(2)}, u32[]{:S(2)}) collective-permute-start(bf16[8,3200]{1,0:T(8,128)(2,1)S(1)} %shard_map.109), channel_id=1, source_target_pairs={{0,64},{2,66},{64,130},{66,128},{128,192},{130,194},{192,0},{194,2... | collective-permute-start | bytes 153608 | tf_op jit(solution)/shard_map/ppermute | solution.py:35
  210.6 1.6 collective-permute-done.20
  212.3 14.3 %all_to_all.69 = bf16[8,8,3072]{2,1,0:T(8,128)(2,1)S(1)} all-to-all(bf16[8,8,3072]{2,1,0:T(8,128)(2,1)S(1)} %broadcast_in_dim.38), channel_id=1, replica_groups=mesh['zh'=2,'core'=2,'xh'=2,'xl'=2,'yh'=2,'yl'=2,'zc'=2,'zf'=2] {'xh','z..., dimensions={0} | all-to-all | bytes 786432 | tf_op jit(solution)/shard_map/all_to_all | solution.py:45
  226.6 4.9 %shard_map.110 = bf16[64,3072]{1,0:T(8,128)(2,1)S(1)} custom-call(bf16[64,3072]{1,0:T(8,128)(2,1)S(1)} %bitcast.73, f32[3,3072]{1,0:T(4,128)S(1)} %reshape.75.mod_ref, bf16[1280,3072]{1,0:T(8,128)(2,1)S(1)} %get-tuple-element.88.up, bf16[1280,3072]{1,0:T(8,128)(2,1)S(1)} %get-tuple-element.89.down, bf16[256,3072]{1,0:T(8,128)(2,1)S(1)} %get-tuple-element.92.up_end, ...), custom_call_target="tpu_custom_call" | custom-call | flops 1207959552 | bytes 19660800 | tf_op jit(solution)/shard_map/pallas_call | solution.py:79
  231.5 15.0 %all_to_all.70.parts_ref = bf16[8,8,3072]{2,1,0:T(8,128)(2,1)S(1)} all-to-all(bf16[8,8,3072]{2,1,0:T(8,128)(2,1)S(1)} %bitcast.74), channel_id=1, replica_groups=mesh['zh'=2,'core'=2,'xh'=2,'xl'=2,'yh'=2,'yl'=2,'zc'=2,'zf'=2] {'xh','z..., dimensions={0} | all-to-all | bytes 786432 | tf_op jit(solution)/shard_map/all_to_all | solution.py:285
  246.6 4.1 %collective-permute-start.21 = (bf16[8,3200]{1,0:T(8,128)(2,1)S(1)}, bf16[8,3200]{1,0:T(8,128)(2,1)S(1)}, u32[]{:S(2)}, u32[]{:S(2)}) collective-permute-start(bf16[8,3200]{1,0:T(8,128)(2,1)S(1)} %shard_map.111), channel_id=1, source_target_pairs={{0,64},{2,66},{64,130},{66,128},{128,192},{130,194},{1,65},{3,67},... | collective-permute-start | bytes 153608 | tf_op jit(solution)/shard_map/ppermute | solution.py:35
  250.7 2.2 collective-permute-done.21
  253.0 16.2 %all_to_all.71 = bf16[8,8,3072]{2,1,0:T(8,128)(2,1)S(1)} all-to-all(bf16[8,8,3072]{2,1,0:T(8,128)(2,1)S(1)} %broadcast_in_dim.39), channel_id=1, replica_groups=mesh['zh'=2,'core'=2,'xh'=2,'xl'=2,'yh'=2,'yl'=2,'zc'=2,'zf'=2] {'xh','z..., dimensions={0} | all-to-all | bytes 786432 | tf_op jit(solution)/shard_map/all_to_all | solution.py:45
  269.2 4.9 %shard_map.112 = bf16[64,3072]{1,0:T(8,128)(2,1)S(1)} custom-call(bf16[64,3072]{1,0:T(8,128)(2,1)S(1)} %bitcast.68, f32[3,3072]{1,0:T(4,128)S(1)} %reshape.75.mod_ref, bf16[1280,3072]{1,0:T(8,128)(2,1)S(1)} %get-tuple-element.88.up, bf16[1280,3072]{1,0:T(8,128)(2,1)S(1)} %get-tuple-element.89.down, bf16[256,3072]{1,0:T(8,128)(2,1)S(1)} %get-tuple-element.92.up_end, ...), custom_call_target="tpu_custom_call" | custom-call | flops 1207959552 | bytes 19660800 | tf_op jit(solution)/shard_map/pallas_call | solution.py:79
  274.1 14.1 %all_to_all.72.parts_ref = bf16[8,8,3072]{2,1,0:T(8,128)(2,1)S(1)} all-to-all(bf16[8,8,3072]{2,1,0:T(8,128)(2,1)S(1)} %bitcast.69), channel_id=1, replica_groups=mesh['zh'=2,'core'=2,'xh'=2,'xl'=2,'yh'=2,'yl'=2,'zc'=2,'zf'=2] {'xh','z..., dimensions={0} | all-to-all | bytes 786432 | tf_op jit(solution)/shard_map/all_to_all | solution.py:285
  288.3 5.2 %collective-permute-start.24 = (bf16[8,3200]{1,0:T(8,128)(2,1)S(1)}, bf16[8,3200]{1,0:T(8,128)(2,1)S(1)}, u32[]{:S(2)}, u32[]{:S(2)}) collective-permute-start(bf16[8,3200]{1,0:T(8,128)(2,1)S(1)} %shard_map.113), channel_id=1, source_target_pairs={{0,64},{2,66},{64,128},{66,130},{128,194},{130,192},{1,65},{3,67},... | collective-permute-start | bytes 153608 | tf_op jit(solution)/shard_map/ppermute | solution.py:35
  293.5 1.3 collective-permute-start.23
  (96 shorter events, 20.2 us)
Async XLA Ops:
  0.6 62.4 %copy-start = (bf16[1,144,3584]{2,1,0:T(8,128)(2,1)S(1)}, bf16[1,144,3584]{2,1,0:T(8,128)(2,1)}, u32[]{:S(2)}) copy-start(bf16[1,144,3584]{2,1,0:T(8,128)(2,1)} %param.15) | copy-start | bytes 3096580
  0.6 1.7 copy-start.1
  2.4 0.8 copy-start.6
  3.3 18.1 %copy-start.8 = (s32[1,8]{1,0:T(1,128)S(1)}, s32[1,8]{1,0:T(1,128)}, u32[]{:S(2)}) copy-start(s32[1,8]{1,0:T(1,128)} %param.12) | copy-start | bytes 100
  3.3 18.2 %copy-start.7 = (bf16[1,8,3072]{2,1,0:T(8,128)(2,1)S(1)}, bf16[1,8,3072]{2,1,0:T(8,128)(2,1)}, u32[]{:S(2)}) copy-start(bf16[1,8,3072]{2,1,0:T(8,128)(2,1)} %param.11) | copy-start | bytes 147460
  4.9 40.6 %collective-permute-start = (bf16[192,3072]{1,0:T(8,128)(2,1)}, bf16[192,3072]{1,0:T(8,128)(2,1)S(1)}, u32[]{:S(2)}, u32[]{:S(2)}) collective-permute-start(bf16[192,3072]{1,0:T(8,128)(2,1)} %get-tuple-element.61.refs_0_), channel_id=1, source_target_pairs={{4,0},{8,4},{12,8},{0,12},{5,1},{9,5},{13,9},{1,13},{6,2},{10,6},{... | collective-permute-start | bytes 3538952 | tf_op jit(solution)/shard_map/ppermute | solution.py:28
  8.5 37.0 %collective-permute-start.1 = (bf16[192,3072]{1,0:T(8,128)(2,1)}, bf16[192,3072]{1,0:T(8,128)(2,1)S(1)}, u32[]{:S(2)}, u32[]{:S(2)}) collective-permute-start(bf16[192,3072]{1,0:T(8,128)(2,1)} %get-tuple-element.60.refs_1_), channel_id=1, source_target_pairs={{12,0},{0,4},{4,8},{8,12},{13,1},{1,5},{5,9},{9,13},{14,2},{2,6},{... | collective-permute-start | bytes 3538952 | tf_op jit(solution)/shard_map/ppermute | solution.py:28
  8.5 37.0 %collective-permute-start.2 = (bf16[192,3072]{1,0:T(8,128)(2,1)}, bf16[192,3072]{1,0:T(8,128)(2,1)}, u32[]{:S(2)}, u32[]{:S(2)}) collective-permute-start(bf16[192,3072]{1,0:T(8,128)(2,1)} %get-tuple-element.61.refs_0_), channel_id=1, source_target_pairs={{16,0},{32,16},{48,32},{0,48},{17,1},{33,17},{49,33},{1,49},{18,2}... | collective-permute-start | bytes 3538952 | tf_op jit(solution)/shard_map/ppermute | solution.py:28
  11.0 34.5 %collective-permute-start.3 = (bf16[192,3072]{1,0:T(8,128)(2,1)}, bf16[192,3072]{1,0:T(8,128)(2,1)}, u32[]{:S(2)}, u32[]{:S(2)}) collective-permute-start(bf16[192,3072]{1,0:T(8,128)(2,1)} %get-tuple-element.60.refs_1_), channel_id=1, source_target_pairs={{48,0},{0,16},{16,32},{32,48},{49,1},{1,17},{17,33},{33,49},{50,2}... | collective-permute-start | bytes 3538952 | tf_op jit(solution)/shard_map/ppermute | solution.py:28
  11.7 19.4 %all-to-all-start = ((f32[16,28,128]{2,1,0:T(8,128)}), f32[16,28,128]{2,1,0:T(8,128)}, u32[]{:S(2)}, u32[]{:S(2)}) async-start(f32[16,28,128]{2,1,0:T(8,128)} %broadcast_in_dim.28), calls=%async_computation | async-start | bytes 524288 | tf_op jit(solution)/shard_map/all_to_all | solution.py:45
  46.3 14.5 %all-to-all-start.2 = ((f32[16,28,128]{2,1,0:T(8,128)}), f32[16,28,128]{2,1,0:T(8,128)}, u32[]{:S(2)}, u32[]{:S(2)}) async-start(f32[16,28,128]{2,1,0:T(8,128)} %broadcast_in_dim.31), calls=%async_computation.2 | async-start | bytes 524288 | tf_op jit(solution)/shard_map/all_to_all | solution.py:45
  53.4 31.4 %collective-permute-start.4 = (bf16[192,3072]{1,0:T(8,128)(2,1)}, bf16[192,3072]{1,0:T(8,128)(2,1)}, u32[]{:S(2)}, u32[]{:S(2)}) collective-permute-start(bf16[192,3072]{1,0:T(8,128)(2,1)} %get-tuple-element.60.refs_1_), channel_id=1, source_target_pairs={{4,0},{8,4},{12,8},{0,12},{5,1},{9,5},{13,9},{1,13},{6,2},{10,6},{... | collective-permute-start | bytes 3538952 | tf_op jit(solution)/shard_map/ppermute | solution.py:28
  55.9 28.9 %collective-permute-start.5 = (bf16[192,3072]{1,0:T(8,128)(2,1)}, bf16[192,3072]{1,0:T(8,128)(2,1)}, u32[]{:S(2)}, u32[]{:S(2)}) collective-permute-start(bf16[192,3072]{1,0:T(8,128)(2,1)} %get-tuple-element.61.refs_0_), channel_id=1, source_target_pairs={{12,0},{0,4},{4,8},{8,12},{13,1},{1,5},{5,9},{9,13},{14,2},{2,6},{... | collective-permute-start | bytes 3538952 | tf_op jit(solution)/shard_map/ppermute | solution.py:28
  55.9 28.9 %collective-permute-start.6 = (bf16[192,3072]{1,0:T(8,128)(2,1)S(1)}, bf16[192,3072]{1,0:T(8,128)(2,1)}, u32[]{:S(2)}, u32[]{:S(2)}) collective-permute-start(bf16[192,3072]{1,0:T(8,128)(2,1)S(1)} %collective-permute-done.refs_4_), channel_id=1, source_target_pairs={{16,0},{32,16},{48,32},{0,48},{17,1},{33,17},{49,33},{1,49},{18,2}... | collective-permute-start | bytes 3538952 | tf_op jit(solution)/shard_map/ppermute | solution.py:28
  58.3 26.5 %collective-permute-start.7 = (bf16[192,3072]{1,0:T(8,128)(2,1)S(1)}, bf16[192,3072]{1,0:T(8,128)(2,1)}, u32[]{:S(2)}, u32[]{:S(2)}) collective-permute-start(bf16[192,3072]{1,0:T(8,128)(2,1)S(1)} %collective-permute-done.1.refs_5_), channel_id=1, source_target_pairs={{48,0},{0,16},{16,32},{32,48},{49,1},{1,17},{17,33},{33,49},{50,2}... | collective-permute-start | bytes 3538952 | tf_op jit(solution)/shard_map/ppermute | solution.py:28
  64.1 10.6 %all-to-all-start.3 = ((f32[4,2,128]{2,1,0:T(2,128)}), f32[4,2,128]{2,1,0:T(2,128)S(1)}, u32[]{:S(2)}, u32[]{:S(2)}) async-start(f32[4,2,128]{2,1,0:T(2,128)} %broadcast_in_dim.33), calls=%async_computation.3 | async-start | bytes 8192 | tf_op jit(solution)/shard_map/all_to_all | solution.py:45
  70.1 4.5 %copy-start.5 = (bf16[1,8,3072]{2,1,0:T(8,128)(2,1)S(1)}, bf16[1,8,3072]{2,1,0:T(8,128)(2,1)}, u32[]{:S(2)}) copy-start(bf16[1,8,3072]{2,1,0:T(8,128)(2,1)} %param.9) | copy-start | bytes 147460
  75.3 9.4 %all-to-all-start.4 = ((bf16[4,8,3072]{2,1,0:T(8,128)(2,1)}), bf16[4,8,3072]{2,1,0:T(8,128)(2,1)}, u32[]{:S(2)}, u32[]{:S(2)}) async-start(bf16[4,8,3072]{2,1,0:T(8,128)(2,1)} %broadcast_in_dim.34), calls=%async_computation.4 | async-start | bytes 393216 | tf_op jit(solution)/shard_map/all_to_all | solution.py:45
  79.3 7.0 %copy-start.9 = (s32[1,8]{1,0:T(1,128)S(1)}, s32[1,8]{1,0:T(1,128)}, u32[]{:S(2)}) copy-start(s32[1,8]{1,0:T(1,128)} %param.10) | copy-start | bytes 100
  84.8 11.2 %collective-permute-start.9 = (bf16[96,3072]{1,0:T(8,128)(2,1)}, bf16[96,3072]{1,0:T(8,128)(2,1)}, u32[]{:S(2)}, u32[]{:S(2)}) collective-permute-start(bf16[96,3072]{1,0:T(8,128)(2,1)} %get-tuple-element.63), channel_id=1, source_target_pairs={{4,0},{8,4},{12,8},{0,12},{5,1},{9,5},{13,9},{1,13},{6,2},{10,6},{... | collective-permute-start | bytes 1769480 | tf_op jit(solution)/shard_map/ppermute | solution.py:28
  86.1 11.2 %collective-permute-start.10 = (bf16[96,3072]{1,0:T(8,128)(2,1)}, bf16[96,3072]{1,0:T(8,128)(2,1)}, u32[]{:S(2)}, u32[]{:S(2)}) collective-permute-start(bf16[96,3072]{1,0:T(8,128)(2,1)} %get-tuple-element.65), channel_id=1, source_target_pairs={{12,0},{0,4},{4,8},{8,12},{13,1},{1,5},{5,9},{9,13},{14,2},{2,6},{... | collective-permute-start | bytes 1769480 | tf_op jit(solution)/shard_map/ppermute | solution.py:28
  86.4 33.6 %collective-permute-start.13 = (bf16[192,3072]{1,0:T(8,128)(2,1)}, bf16[192,3072]{1,0:T(8,128)(2,1)}, u32[]{:S(2)}, u32[]{:S(2)}) collective-permute-start(bf16[192,3072]{1,0:T(8,128)(2,1)} %collective-permute-done.5.refs_7_), channel_id=1, source_target_pairs={{16,0},{32,16},{48,32},{0,48},{17,1},{33,17},{49,33},{1,49},{18,2}... | collective-permute-start | bytes 3538952 | tf_op jit(solution)/shard_map/ppermute | solution.py:28
  87.7 32.2 %collective-permute-start.14 = (bf16[192,3072]{1,0:T(8,128)(2,1)}, bf16[192,3072]{1,0:T(8,128)(2,1)}, u32[]{:S(2)}, u32[]{:S(2)}) collective-permute-start(bf16[192,3072]{1,0:T(8,128)(2,1)} %collective-permute-done.4.refs_6_), channel_id=1, source_target_pairs={{48,0},{0,16},{16,32},{32,48},{49,1},{1,17},{17,33},{33,49},{50,2}... | collective-permute-start | bytes 3538952 | tf_op jit(solution)/shard_map/ppermute | solution.py:28
  87.9 35.0 %collective-permute-start.8 = (bf16[4,8,3072]{2,1,0:T(8,128)(2,1)}, bf16[4,8,3072]{2,1,0:T(8,128)(2,1)}, u32[]{:S(2)}, u32[]{:S(2)}) collective-permute-start(bf16[4,8,3072]{2,1,0:T(8,128)(2,1)} %all-to-all-done.4), channel_id=1, source_target_pairs={{0,32},{32,0},{1,33},{33,1},{2,34},{34,2},{3,35},{35,3},{4,36},{36... | collective-permute-start | bytes 589832 | tf_op jit(solution)/shard_map/ppermute | solution.py:204
  90.3 27.1 %all-to-all-start.5 = ((f32[16,4,2,128]{3,2,1,0:T(2,128)}), f32[16,4,2,128]{3,2,1,0:T(2,128)}, u32[]{:S(2)}, u32[]{:S(2)}) async-start(f32[16,4,2,128]{3,2,1,0:T(2,128)} %broadcast_in_dim.36), calls=%async_computation.5 | async-start | bytes 131072 | tf_op jit(solution)/shard_map/all_to_all | solution.py:45
  97.3 22.6 %collective-permute-start.11 = (bf16[96,3072]{1,0:T(8,128)(2,1)}, bf16[96,3072]{1,0:T(8,128)(2,1)}, u32[]{:S(2)}, u32[]{:S(2)}) collective-permute-start(bf16[96,3072]{1,0:T(8,128)(2,1)} %get-tuple-element.68), channel_id=1, source_target_pairs={{4,0},{8,4},{12,8},{0,12},{5,1},{9,5},{13,9},{1,13},{6,2},{10,6},{... | collective-permute-start | bytes 1769480 | tf_op jit(solution)/shard_map/ppermute | solution.py:28
  98.1 21.8 %collective-permute-start.12 = (bf16[96,3072]{1,0:T(8,128)(2,1)}, bf16[96,3072]{1,0:T(8,128)(2,1)}, u32[]{:S(2)}, u32[]{:S(2)}) collective-permute-start(bf16[96,3072]{1,0:T(8,128)(2,1)} %get-tuple-element.70), channel_id=1, source_target_pairs={{12,0},{0,4},{4,8},{8,12},{13,1},{1,5},{5,9},{9,13},{14,2},{2,6},{... | collective-permute-start | bytes 1769480 | tf_op jit(solution)/shard_map/ppermute | solution.py:28
  119.9 9.3 %collective-permute-start.15 = (bf16[96,3072]{1,0:T(8,128)(2,1)}, bf16[96,3072]{1,0:T(8,128)(2,1)S(1)}, u32[]{:S(2)}, u32[]{:S(2)}) collective-permute-start(bf16[96,3072]{1,0:T(8,128)(2,1)} %collective-permute-done.9.refs_12_), channel_id=1, source_target_pairs={{16,0},{32,16},{48,32},{0,48},{17,1},{33,17},{49,33},{1,49},{18,2}... | collective-permute-start | bytes 1769480 | tf_op jit(solution)/shard_map/ppermute | solution.py:28
  120.2 10.2 %collective-permute-start.16 = (bf16[96,3072]{1,0:T(8,128)(2,1)}, bf16[96,3072]{1,0:T(8,128)(2,1)S(1)}, u32[]{:S(2)}, u32[]{:S(2)}) collective-permute-start(bf16[96,3072]{1,0:T(8,128)(2,1)} %collective-permute-done.10.refs_14_.refs_0_), channel_id=1, source_target_pairs={{48,0},{0,16},{16,32},{32,48},{49,1},{1,17},{17,33},{33,49},{50,2}... | collective-permute-start | bytes 1769480 | tf_op jit(solution)/shard_map/ppermute | solution.py:28
  121.5 9.2 %collective-permute-start.17 = (bf16[96,3072]{1,0:T(8,128)(2,1)}, bf16[96,3072]{1,0:T(8,128)(2,1)S(1)}, u32[]{:S(2)}, u32[]{:S(2)}) collective-permute-start(bf16[96,3072]{1,0:T(8,128)(2,1)} %slice.87), channel_id=1, source_target_pairs={{4,0},{8,4},{12,8},{0,12},{5,1},{9,5},{13,9},{1,13},{6,2},{10,6},{... | collective-permute-start | bytes 1769480 | tf_op jit(solution)/shard_map/ppermute | solution.py:28
  122.3 10.4 %collective-permute-start.18 = (bf16[96,3072]{1,0:T(8,128)(2,1)}, bf16[96,3072]{1,0:T(8,128)(2,1)S(1)}, u32[]{:S(2)}, u32[]{:S(2)}) collective-permute-start(bf16[96,3072]{1,0:T(8,128)(2,1)} %slice.88), channel_id=1, source_target_pairs={{12,0},{0,4},{4,8},{8,12},{13,1},{1,5},{5,9},{9,13},{14,2},{2,6},{... | collective-permute-start | bytes 1769480 | tf_op jit(solution)/shard_map/ppermute | solution.py:28
  138.9 28.7 %copy-start.3 = (bf16[8,3200]{1,0:T(8,128)(2,1)S(1)}, bf16[8,3200]{1,0:T(8,128)(2,1)}, u32[]{:S(2)}) copy-start(bf16[8,3200]{1,0:T(8,128)(2,1)} %get-tuple-element.98) | copy-start | bytes 153604
  159.2 8.5 %collective-permute-start.19 = (bf16[8,3200]{1,0:T(8,128)(2,1)S(1)}, bf16[8,3200]{1,0:T(8,128)(2,1)S(1)}, u32[]{:S(2)}, u32[]{:S(2)}) collective-permute-start(bf16[8,3200]{1,0:T(8,128)(2,1)S(1)} %shard_map.107), channel_id=1, source_target_pairs={{0,64},{2,66},{64,130},{66,128},{128,192},{130,194},{192,0},{194,2... | collective-permute-start | bytes 153608 | tf_op jit(solution)/shard_map/ppermute | solution.py:35
  185.1 27.1 %copy-start.2 = (bf16[8,3200]{1,0:T(8,128)(2,1)S(1)}, bf16[8,3200]{1,0:T(8,128)(2,1)}, u32[]{:S(2)}) copy-start(bf16[8,3200]{1,0:T(8,128)(2,1)} %get-tuple-element.97) | copy-start | bytes 153604
  197.9 14.3 %collective-permute-start.20 = (bf16[8,3200]{1,0:T(8,128)(2,1)S(1)}, bf16[8,3200]{1,0:T(8,128)(2,1)S(1)}, u32[]{:S(2)}, u32[]{:S(2)}) collective-permute-start(bf16[8,3200]{1,0:T(8,128)(2,1)S(1)} %shard_map.109), channel_id=1, source_target_pairs={{0,64},{2,66},{64,130},{66,128},{128,192},{130,194},{192,0},{194,2... | collective-permute-start | bytes 153608 | tf_op jit(solution)/shard_map/ppermute | solution.py:35
  246.6 6.3 %collective-permute-start.21 = (bf16[8,3200]{1,0:T(8,128)(2,1)S(1)}, bf16[8,3200]{1,0:T(8,128)(2,1)S(1)}, u32[]{:S(2)}, u32[]{:S(2)}) collective-permute-start(bf16[8,3200]{1,0:T(8,128)(2,1)S(1)} %shard_map.111), channel_id=1, source_target_pairs={{0,64},{2,66},{64,130},{66,128},{128,192},{130,194},{1,65},{3,67},... | collective-permute-start | bytes 153608 | tf_op jit(solution)/shard_map/ppermute | solution.py:35
  274.1 21.3 %copy-start.4 = (bf16[8,3200]{1,0:T(8,128)(2,1)S(1)}, bf16[8,3200]{1,0:T(8,128)(2,1)}, u32[]{:S(2)}) copy-start(bf16[8,3200]{1,0:T(8,128)(2,1)} %get-tuple-element.101) | copy-start | bytes 153604
  288.3 7.2 %collective-permute-start.24 = (bf16[8,3200]{1,0:T(8,128)(2,1)S(1)}, bf16[8,3200]{1,0:T(8,128)(2,1)S(1)}, u32[]{:S(2)}, u32[]{:S(2)}) collective-permute-start(bf16[8,3200]{1,0:T(8,128)(2,1)S(1)} %shard_map.113), channel_id=1, source_target_pairs={{0,64},{2,66},{64,128},{66,130},{128,194},{130,192},{1,65},{3,67},... | collective-permute-start | bytes 153608 | tf_op jit(solution)/shard_map/ppermute | solution.py:35
  293.5 3.1 %collective-permute-start.23 = (bf16[8,3200]{1,0:T(8,128)(2,1)S(1)}, bf16[8,3200]{1,0:T(8,128)(2,1)S(1)}, u32[]{:S(2)}, u32[]{:S(2)}) collective-permute-start(bf16[8,3200]{1,0:T(8,128)(2,1)S(1)} %broadcast_select_fusion), channel_id=1, source_target_pairs={{0,64},{2,66},{192,194},{194,192},{1,65},{3,67},{193,195},{195,193... | collective-permute-start | bytes 153608 | tf_op jit(solution)/shard_map/ppermute | solution.py:35
  294.8 1.8 collective-permute-start.22

commit v6 on v5

--- a/solution.py
+++ b/solution.py
@@ -203,13 +203,13 @@
     y2[3] = from_neighbour(halves[3], "y", -1)
     theirs = lax.ppermute(mine, "xh", [(0, 1), (1, 0)])
     modes = exchange(line, PLANE)
-    modes = modes.reshape(-1, rows * LANES)[:, :columns].reshape(3, -1)
     xa_yp_down = xa_yp[middle:]
     xb_ym_down = xb_ym[middle:]
 
     y2, xa_ym, xb_yp, xa_yp_down, xb_ym_down, modes = together(
         (y2, xa_ym, xb_yp, xa_yp_down, xb_ym_down, modes)
     )
+    modes = modes.reshape(-1, rows * LANES)[:, :columns].reshape(3, -1)
     xa_y2_up = from_neighbour(y2[0], "x", 1)
     xb_y2_up = from_neighbour(y2[2], "x", -1)
     xa_y2_down = from_neighbour(xa_yp_down, "y", 1)

time: 299 us -> 297 us (level)
  transfers between devices with their start and end apart: 30 -> 30, of which waited for: 14 -> 12; matrix products, arithmetic and copies ran while one was open for 6% -> 6% of each run, Pallas kernels for 2% -> 2%
where the time goes in v6:
time: 297 us; the launch traced here: 296 us
  blocking collectives  118 us (40%)
  starting transfers between devices  81.7 us (28%)
  waiting for transfers between devices  43.4 us (15%)
  Pallas kernels  27.2 us (9%)
  local copies, waits for them, and re-layouts  14.8 us (5%)
  other arithmetic  7.33 us (2%)
    all_to_all x4, blocking collectives, per_device(): lax.all_to_all(partial.reshape(GROUP_SIZE, tokens, breadth), GROUP, 0, 0)  62 us
    all_to_all x4, blocking collectives, exchange(): return lax.all_to_all(copies, axes, 0, 0)  56.3 us
    all_to_all x5, waiting for transfers between devices, exchange(): return lax.all_to_all(copies, axes, 0, 0)  33 us
    all_to_all x5, starting transfers between devices, exchange(): return lax.all_to_all(copies, axes, 0, 0)  31.7 us
    ppermute x6, starting transfers between devices, between_sections(): return lax.ppermute(block, SECTION + ('zc',), route)  29.8 us
    pallas_call x4, Pallas kernels, layer(): pl.pallas_call(layer_kernel, out_shape=jax.ShapeDtypeStruct((rows, breadt...  19.8 us
    ppermute x18, starting transfers between devices, from_neighbour(): return lax.ppermute(block, (axis + 'h', axis + 'l'), route)  18.5 us
    pallas_call x2, Pallas kernels, place(): pl.pallas_call(functools.partial(place_kernel, plan), out_shape=[jax.Shap...  7.04 us
  transfers between devices with their start and end apart: 30, of which 12 were waited for; matrix products, arithmetic and copies ran while one was open for 6% of the time, Pallas kernels for 2%

profile of v6, /device:TPU:1, one launch (start us, length us, event | category | flops | bytes accessed | tf_op | source)
XLA Modules:
  0.0 295.6 jit_solution(15313167185184818229)
XLA Ops:
  0.7 1.5 slice_bitcast_fusion
  3.3 1.6 pad_maximum_fusion
  4.9 3.6 %collective-permute-start = (bf16[192,3072]{1,0:T(8,128)(2,1)}, bf16[192,3072]{1,0:T(8,128)(2,1)S(1)}, u32[]{:S(2)}, u32[]{:S(2)}) collective-permute-start(bf16[192,3072]{1,0:T(8,128)(2,1)} %get-tuple-element.61.refs_0_), channel_id=1, source_target_pairs={{4,0},{8,4},{12,8},{0,12},{5,1},{9,5},{13,9},{1,13},{6,2},{10,6},{... | collective-permute-start | bytes 3538952 | tf_op jit(solution)/shard_map/ppermute | solution.py:28
  8.5 2.5 collective-permute-start.2
  11.7 9.7 %all-to-all-start = ((f32[16,28,128]{2,1,0:T(8,128)}), f32[16,28,128]{2,1,0:T(8,128)}, u32[]{:S(2)}, u32[]{:S(2)}) async-start(f32[16,28,128]{2,1,0:T(8,128)} %broadcast_in_dim.28), calls=%async_computation | async-start | bytes 524288 | tf_op jit(solution)/shard_map/all_to_all | solution.py:45
  21.5 9.6 %all-to-all-done = f32[16,28,128]{2,1,0:T(8,128)} async-done(((f32[16,28,128]{2,1,0:T(8,128)}), f32[16,28,128]{2,1,0:T(8,128)}, u32[]{:S(2)}, u32[]{:S(2)}) %all-to-all-start) | async-done | bytes 229408 | tf_op jit(solution)/shard_map/all_to_all | solution.py:45
  32.1 13.4 %all_to_all.65 = bf16[4,8,3200]{2,1,0:T(8,128)(2,1)} all-to-all(bf16[4,8,3200]{2,1,0:T(8,128)(2,1)S(1)} %broadcast_in_dim.30), channel_id=1, replica_groups=mesh['zh'=2,'core'=2,'xh'=2,'xl'=2,'yh'=2,'yl'=2,'zc'=2,'zf'=2] {'zh','c..., dimensions={0} | all-to-all | bytes 409600 | tf_op jit(solution)/shard_map/all_to_all | solution.py:45
  46.3 7.1 %all-to-all-start.2 = ((f32[16,28,128]{2,1,0:T(8,128)}), f32[16,28,128]{2,1,0:T(8,128)}, u32[]{:S(2)}, u32[]{:S(2)}) async-start(f32[16,28,128]{2,1,0:T(8,128)} %broadcast_in_dim.31), calls=%async_computation.2 | async-start | bytes 524288 | tf_op jit(solution)/shard_map/all_to_all | solution.py:45
  53.3 2.5 collective-permute-start.4
  55.9 2.4 collective-permute-start.6
  58.3 2.5 all-to-all-done.2
  64.0 6.0 %all-to-all-start.3 = ((f32[4,2,128]{2,1,0:T(2,128)}), f32[4,2,128]{2,1,0:T(2,128)S(1)}, u32[]{:S(2)}, u32[]{:S(2)}) async-start(f32[4,2,128]{2,1,0:T(2,128)} %broadcast_in_dim.33), calls=%async_computation.3 | async-start | bytes 8192 | tf_op jit(solution)/shard_map/all_to_all | solution.py:45
  70.1 1.1 fusion.14
  71.2 3.4 %all-to-all-done.3 = f32[4,2,128]{2,1,0:T(2,128)S(1)} async-done(((f32[4,2,128]{2,1,0:T(2,128)}), f32[4,2,128]{2,1,0:T(2,128)S(1)}, u32[]{:S(2)}, u32[]{:S(2)}) %all-to-all-start.3) | async-done | bytes 4128 | tf_op jit(solution)/shard_map/all_to_all | solution.py:45
  75.3 4.0 %all-to-all-start.4 = ((bf16[4,8,3072]{2,1,0:T(8,128)(2,1)}), bf16[4,8,3072]{2,1,0:T(8,128)(2,1)}, u32[]{:S(2)}, u32[]{:S(2)}) async-start(bf16[4,8,3072]{2,1,0:T(8,128)(2,1)} %broadcast_in_dim.34), calls=%async_computation.4 | async-start | bytes 393216 | tf_op jit(solution)/shard_map/all_to_all | solution.py:45
  80.4 4.4 %all-to-all-done.4 = bf16[4,8,3072]{2,1,0:T(8,128)(2,1)} async-done(((bf16[4,8,3072]{2,1,0:T(8,128)(2,1)}), bf16[4,8,3072]{2,1,0:T(8,128)(2,1)}, u32[]{:S(2)}, u32[]{:S(2)}) %all-to-all-start.4) | async-done | bytes 196640 | tf_op jit(solution)/shard_map/all_to_all | solution.py:45
  84.8 1.3 collective-permute-start.9
  86.4 1.3 collective-permute-start.13
  87.9 1.7 collective-permute-start.8
  90.3 4.9 %all-to-all-start.5 = ((f32[16,4,2,128]{3,2,1,0:T(2,128)}), f32[16,4,2,128]{3,2,1,0:T(2,128)S(1)}, u32[]{:S(2)}, u32[]{:S(2)}) async-start(f32[16,4,2,128]{3,2,1,0:T(2,128)} %broadcast_in_dim.36), calls=%async_computation.5 | async-start | bytes 131072 | tf_op jit(solution)/shard_map/all_to_all | solution.py:45
  96.0 1.3 collective-permute-done.10.refs_14_.refs_0_
  98.8 1.6 slice_bitcast_fusion.4
  100.3 1.9 slice.87
  102.2 1.9 slice.88
  104.2 13.2 %all-to-all-done.5 = f32[16,4,2,128]{3,2,1,0:T(2,128)S(1)} async-done(((f32[16,4,2,128]{3,2,1,0:T(2,128)}), f32[16,4,2,128]{3,2,1,0:T(2,128)S(1)}, u32[]{:S(2)}, u32[]{:S(2)}) %all-to-all-start.5) | async-done | bytes 65568 | tf_op jit(solution)/shard_map/all_to_all | solution.py:45
  117.7 1.2 collective-permute-start.16
  123.8 5.1 %shard_map.104 = (bf16[1280,3072]{1,0:T(8,128)(2,1)S(1)}, bf16[1280,3072]{1,0:T(8,128)(2,1)S(1)}) custom-call(bf16[192,3072]{1,0:T(8,128)(2,1)} %get-tuple-element.61.refs_0_, bf16[192,3072]{1,0:T(8,128)(2,1)} %get-tuple-element.60.refs_1_, bf16[192,3072]{1,0:T(8,128)(2,1)} %collective-permute-done.2.refs_2_, ...), custom_call_target="tpu_custom_call" | custom-call | bytes 31457280 | tf_op jit(solution)/shard_map/pallas_call | solution.py:118
  129.0 1.4 collective-permute-done.18.refs_5_
  130.4 1.9 shard_map.105
  132.3 4.9 %shard_map.106 = bf16[64,3072]{1,0:T(8,128)(2,1)S(1)} custom-call(bf16[64,3072]{1,0:T(8,128)(2,1)S(1)} %bitcast.67, f32[3,3072]{1,0:T(4,128)S(1)} %reshape.75.mod_ref, bf16[1280,3072]{1,0:T(8,128)(2,1)S(1)} %get-tuple-element.88.up, bf16[1280,3072]{1,0:T(8,128)(2,1)S(1)} %get-tuple-element.89.down, bf16[256,3072]{1,0:T(8,128)(2,1)S(1)} %get-tuple-element.92.up_end, ...), custom_call_target="tpu_custom_call" | custom-call | flops 1207959552 | bytes 19660800 | tf_op jit(solution)/shard_map/pallas_call | solution.py:79
  137.2 20.1 %all_to_all.66.parts_ref = bf16[8,8,3072]{2,1,0:T(8,128)(2,1)S(1)} all-to-all(bf16[8,8,3072]{2,1,0:T(8,128)(2,1)S(1)} %bitcast.70), channel_id=1, replica_groups=mesh['zh'=2,'core'=2,'xh'=2,'xl'=2,'yh'=2,'yl'=2,'zc'=2,'zf'=2] {'xh','z..., dimensions={0} | all-to-all | bytes 786432 | tf_op jit(solution)/shard_map/all_to_all | solution.py:285
  157.4 5.8 %collective-permute-start.19 = (bf16[8,3200]{1,0:T(8,128)(2,1)S(1)}, bf16[8,3200]{1,0:T(8,128)(2,1)S(1)}, u32[]{:S(2)}, u32[]{:S(2)}) collective-permute-start(bf16[8,3200]{1,0:T(8,128)(2,1)S(1)} %shard_map.107), channel_id=1, source_target_pairs={{0,64},{2,66},{64,130},{66,128},{128,192},{130,194},{192,0},{194,2... | collective-permute-start | bytes 153608 | tf_op jit(solution)/shard_map/ppermute | solution.py:35
  163.3 2.6 collective-permute-done.19
  165.9 12.5 %all_to_all.67 = bf16[8,8,3072]{2,1,0:T(8,128)(2,1)S(1)} all-to-all(bf16[8,8,3072]{2,1,0:T(8,128)(2,1)S(1)} %broadcast_in_dim.37), channel_id=1, replica_groups=mesh['zh'=2,'core'=2,'xh'=2,'xl'=2,'yh'=2,'yl'=2,'zc'=2,'zf'=2] {'xh','z..., dimensions={0} | all-to-all | bytes 786432 | tf_op jit(solution)/shard_map/all_to_all | solution.py:45
  178.5 4.9 %shard_map.108 = bf16[64,3072]{1,0:T(8,128)(2,1)S(1)} custom-call(bf16[64,3072]{1,0:T(8,128)(2,1)S(1)} %bitcast.71, f32[3,3072]{1,0:T(4,128)S(1)} %reshape.75.mod_ref, bf16[1280,3072]{1,0:T(8,128)(2,1)S(1)} %get-tuple-element.88.up, bf16[1280,3072]{1,0:T(8,128)(2,1)S(1)} %get-tuple-element.89.down, bf16[256,3072]{1,0:T(8,128)(2,1)S(1)} %get-tuple-element.92.up_end, ...), custom_call_target="tpu_custom_call" | custom-call | flops 1207959552 | bytes 19660800 | tf_op jit(solution)/shard_map/pallas_call | solution.py:79
  183.4 12.7 %all_to_all.68.parts_ref = bf16[8,8,3072]{2,1,0:T(8,128)(2,1)S(1)} all-to-all(bf16[8,8,3072]{2,1,0:T(8,128)(2,1)S(1)} %bitcast.72), channel_id=1, replica_groups=mesh['zh'=2,'core'=2,'xh'=2,'xl'=2,'yh'=2,'yl'=2,'zc'=2,'zf'=2] {'xh','z..., dimensions={0} | all-to-all | bytes 786432 | tf_op jit(solution)/shard_map/all_to_all | solution.py:285
  196.2 12.7 %collective-permute-start.20 = (bf16[8,3200]{1,0:T(8,128)(2,1)S(1)}, bf16[8,3200]{1,0:T(8,128)(2,1)S(1)}, u32[]{:S(2)}, u32[]{:S(2)}) collective-permute-start(bf16[8,3200]{1,0:T(8,128)(2,1)S(1)} %shard_map.109), channel_id=1, source_target_pairs={{0,64},{2,66},{64,130},{66,128},{128,192},{130,194},{192,0},{194,2... | collective-permute-start | bytes 153608 | tf_op jit(solution)/shard_map/ppermute | solution.py:35
  208.9 1.6 collective-permute-done.20
  210.6 14.2 %all_to_all.69 = bf16[8,8,3072]{2,1,0:T(8,128)(2,1)S(1)} all-to-all(bf16[8,8,3072]{2,1,0:T(8,128)(2,1)S(1)} %broadcast_in_dim.38), channel_id=1, replica_groups=mesh['zh'=2,'core'=2,'xh'=2,'xl'=2,'yh'=2,'yl'=2,'zc'=2,'zf'=2] {'xh','z..., dimensions={0} | all-to-all | bytes 786432 | tf_op jit(solution)/shard_map/all_to_all | solution.py:45
  224.8 4.9 %shard_map.110 = bf16[64,3072]{1,0:T(8,128)(2,1)S(1)} custom-call(bf16[64,3072]{1,0:T(8,128)(2,1)S(1)} %bitcast.73, f32[3,3072]{1,0:T(4,128)S(1)} %reshape.75.mod_ref, bf16[1280,3072]{1,0:T(8,128)(2,1)S(1)} %get-tuple-element.88.up, bf16[1280,3072]{1,0:T(8,128)(2,1)S(1)} %get-tuple-element.89.down, bf16[256,3072]{1,0:T(8,128)(2,1)S(1)} %get-tuple-element.92.up_end, ...), custom_call_target="tpu_custom_call" | custom-call | flops 1207959552 | bytes 19660800 | tf_op jit(solution)/shard_map/pallas_call | solution.py:79
  229.8 15.2 %all_to_all.70.parts_ref = bf16[8,8,3072]{2,1,0:T(8,128)(2,1)S(1)} all-to-all(bf16[8,8,3072]{2,1,0:T(8,128)(2,1)S(1)} %bitcast.74), channel_id=1, replica_groups=mesh['zh'=2,'core'=2,'xh'=2,'xl'=2,'yh'=2,'yl'=2,'zc'=2,'zf'=2] {'xh','z..., dimensions={0} | all-to-all | bytes 786432 | tf_op jit(solution)/shard_map/all_to_all | solution.py:285
  245.0 4.1 %collective-permute-start.21 = (bf16[8,3200]{1,0:T(8,128)(2,1)S(1)}, bf16[8,3200]{1,0:T(8,128)(2,1)S(1)}, u32[]{:S(2)}, u32[]{:S(2)}) collective-permute-start(bf16[8,3200]{1,0:T(8,128)(2,1)S(1)} %shard_map.111), channel_id=1, source_target_pairs={{0,64},{2,66},{64,130},{66,128},{128,192},{130,194},{1,65},{3,67},... | collective-permute-start | bytes 153608 | tf_op jit(solution)/shard_map/ppermute | solution.py:35
  249.1 2.2 collective-permute-done.21
  251.4 16.2 %all_to_all.71 = bf16[8,8,3072]{2,1,0:T(8,128)(2,1)S(1)} all-to-all(bf16[8,8,3072]{2,1,0:T(8,128)(2,1)S(1)} %broadcast_in_dim.39), channel_id=1, replica_groups=mesh['zh'=2,'core'=2,'xh'=2,'xl'=2,'yh'=2,'yl'=2,'zc'=2,'zf'=2] {'xh','z..., dimensions={0} | all-to-all | bytes 786432 | tf_op jit(solution)/shard_map/all_to_all | solution.py:45
  267.5 4.9 %shard_map.112 = bf16[64,3072]{1,0:T(8,128)(2,1)S(1)} custom-call(bf16[64,3072]{1,0:T(8,128)(2,1)S(1)} %bitcast.68, f32[3,3072]{1,0:T(4,128)S(1)} %reshape.75.mod_ref, bf16[1280,3072]{1,0:T(8,128)(2,1)S(1)} %get-tuple-element.88.up, bf16[1280,3072]{1,0:T(8,128)(2,1)S(1)} %get-tuple-element.89.down, bf16[256,3072]{1,0:T(8,128)(2,1)S(1)} %get-tuple-element.92.up_end, ...), custom_call_target="tpu_custom_call" | custom-call | flops 1207959552 | bytes 19660800 | tf_op jit(solution)/shard_map/pallas_call | solution.py:79
  272.5 14.1 %all_to_all.72.parts_ref = bf16[8,8,3072]{2,1,0:T(8,128)(2,1)S(1)} all-to-all(bf16[8,8,3072]{2,1,0:T(8,128)(2,1)S(1)} %bitcast.69), channel_id=1, replica_groups=mesh['zh'=2,'core'=2,'xh'=2,'xl'=2,'yh'=2,'yl'=2,'zc'=2,'zf'=2] {'xh','z..., dimensions={0} | all-to-all | bytes 786432 | tf_op jit(solution)/shard_map/all_to_all | solution.py:285
  286.7 5.2 %collective-permute-start.24 = (bf16[8,3200]{1,0:T(8,128)(2,1)S(1)}, bf16[8,3200]{1,0:T(8,128)(2,1)S(1)}, u32[]{:S(2)}, u32[]{:S(2)}) collective-permute-start(bf16[8,3200]{1,0:T(8,128)(2,1)S(1)} %shard_map.113), channel_id=1, source_target_pairs={{0,64},{2,66},{64,128},{66,130},{128,194},{130,192},{1,65},{3,67},... | collective-permute-start | bytes 153608 | tf_op jit(solution)/shard_map/ppermute | solution.py:35
  291.9 1.3 collective-permute-start.23
  (100 shorter events, 19.1 us)
Async XLA Ops:
  0.6 62.4 %copy-start = (bf16[1,144,3584]{2,1,0:T(8,128)(2,1)S(1)}, bf16[1,144,3584]{2,1,0:T(8,128)(2,1)}, u32[]{:S(2)}) copy-start(bf16[1,144,3584]{2,1,0:T(8,128)(2,1)} %param.15) | copy-start | bytes 3096580
  0.6 1.7 copy-start.2
  2.4 0.8 copy-start.8
  3.3 18.1 %copy-start.10 = (s32[1,8]{1,0:T(1,128)S(1)}, s32[1,8]{1,0:T(1,128)}, u32[]{:S(2)}) copy-start(s32[1,8]{1,0:T(1,128)} %param.12) | copy-start | bytes 100
  3.3 18.2 %copy-start.9 = (bf16[1,8,3072]{2,1,0:T(8,128)(2,1)S(1)}, bf16[1,8,3072]{2,1,0:T(8,128)(2,1)}, u32[]{:S(2)}) copy-start(bf16[1,8,3072]{2,1,0:T(8,128)(2,1)} %param.11) | copy-start | bytes 147460
  4.9 40.6 %collective-permute-start = (bf16[192,3072]{1,0:T(8,128)(2,1)}, bf16[192,3072]{1,0:T(8,128)(2,1)S(1)}, u32[]{:S(2)}, u32[]{:S(2)}) collective-permute-start(bf16[192,3072]{1,0:T(8,128)(2,1)} %get-tuple-element.61.refs_0_), channel_id=1, source_target_pairs={{4,0},{8,4},{12,8},{0,12},{5,1},{9,5},{13,9},{1,13},{6,2},{10,6},{... | collective-permute-start | bytes 3538952 | tf_op jit(solution)/shard_map/ppermute | solution.py:28
  8.5 37.0 %collective-permute-start.1 = (bf16[192,3072]{1,0:T(8,128)(2,1)}, bf16[192,3072]{1,0:T(8,128)(2,1)S(1)}, u32[]{:S(2)}, u32[]{:S(2)}) collective-permute-start(bf16[192,3072]{1,0:T(8,128)(2,1)} %get-tuple-element.60.refs_1_), channel_id=1, source_target_pairs={{12,0},{0,4},{4,8},{8,12},{13,1},{1,5},{5,9},{9,13},{14,2},{2,6},{... | collective-permute-start | bytes 3538952 | tf_op jit(solution)/shard_map/ppermute | solution.py:28
  8.5 37.0 %collective-permute-start.2 = (bf16[192,3072]{1,0:T(8,128)(2,1)}, bf16[192,3072]{1,0:T(8,128)(2,1)}, u32[]{:S(2)}, u32[]{:S(2)}) collective-permute-start(bf16[192,3072]{1,0:T(8,128)(2,1)} %get-tuple-element.61.refs_0_), channel_id=1, source_target_pairs={{16,0},{32,16},{48,32},{0,48},{17,1},{33,17},{49,33},{1,49},{18,2}... | collective-permute-start | bytes 3538952 | tf_op jit(solution)/shard_map/ppermute | solution.py:28
  11.0 34.5 %collective-permute-start.3 = (bf16[192,3072]{1,0:T(8,128)(2,1)}, bf16[192,3072]{1,0:T(8,128)(2,1)}, u32[]{:S(2)}, u32[]{:S(2)}) collective-permute-start(bf16[192,3072]{1,0:T(8,128)(2,1)} %get-tuple-element.60.refs_1_), channel_id=1, source_target_pairs={{48,0},{0,16},{16,32},{32,48},{49,1},{1,17},{17,33},{33,49},{50,2}... | collective-permute-start | bytes 3538952 | tf_op jit(solution)/shard_map/ppermute | solution.py:28
  11.7 19.4 %all-to-all-start = ((f32[16,28,128]{2,1,0:T(8,128)}), f32[16,28,128]{2,1,0:T(8,128)}, u32[]{:S(2)}, u32[]{:S(2)}) async-start(f32[16,28,128]{2,1,0:T(8,128)} %broadcast_in_dim.28), calls=%async_computation | async-start | bytes 524288 | tf_op jit(solution)/shard_map/all_to_all | solution.py:45
  46.3 14.5 %all-to-all-start.2 = ((f32[16,28,128]{2,1,0:T(8,128)}), f32[16,28,128]{2,1,0:T(8,128)}, u32[]{:S(2)}, u32[]{:S(2)}) async-start(f32[16,28,128]{2,1,0:T(8,128)} %broadcast_in_dim.31), calls=%async_computation.2 | async-start | bytes 524288 | tf_op jit(solution)/shard_map/all_to_all | solution.py:45
  53.3 31.4 %collective-permute-start.4 = (bf16[192,3072]{1,0:T(8,128)(2,1)}, bf16[192,3072]{1,0:T(8,128)(2,1)}, u32[]{:S(2)}, u32[]{:S(2)}) collective-permute-start(bf16[192,3072]{1,0:T(8,128)(2,1)} %get-tuple-element.60.refs_1_), channel_id=1, source_target_pairs={{4,0},{8,4},{12,8},{0,12},{5,1},{9,5},{13,9},{1,13},{6,2},{10,6},{... | collective-permute-start | bytes 3538952 | tf_op jit(solution)/shard_map/ppermute | solution.py:28
  55.9 28.9 %collective-permute-start.5 = (bf16[192,3072]{1,0:T(8,128)(2,1)}, bf16[192,3072]{1,0:T(8,128)(2,1)}, u32[]{:S(2)}, u32[]{:S(2)}) collective-permute-start(bf16[192,3072]{1,0:T(8,128)(2,1)} %get-tuple-element.61.refs_0_), channel_id=1, source_target_pairs={{12,0},{0,4},{4,8},{8,12},{13,1},{1,5},{5,9},{9,13},{14,2},{2,6},{... | collective-permute-start | bytes 3538952 | tf_op jit(solution)/shard_map/ppermute | solution.py:28
  55.9 28.9 %collective-permute-start.6 = (bf16[192,3072]{1,0:T(8,128)(2,1)S(1)}, bf16[192,3072]{1,0:T(8,128)(2,1)}, u32[]{:S(2)}, u32[]{:S(2)}) collective-permute-start(bf16[192,3072]{1,0:T(8,128)(2,1)S(1)} %collective-permute-done.refs_4_), channel_id=1, source_target_pairs={{16,0},{32,16},{48,32},{0,48},{17,1},{33,17},{49,33},{1,49},{18,2}... | collective-permute-start | bytes 3538952 | tf_op jit(solution)/shard_map/ppermute | solution.py:28
  58.3 26.5 %collective-permute-start.7 = (bf16[192,3072]{1,0:T(8,128)(2,1)S(1)}, bf16[192,3072]{1,0:T(8,128)(2,1)}, u32[]{:S(2)}, u32[]{:S(2)}) collective-permute-start(bf16[192,3072]{1,0:T(8,128)(2,1)S(1)} %collective-permute-done.1.refs_5_), channel_id=1, source_target_pairs={{48,0},{0,16},{16,32},{32,48},{49,1},{1,17},{17,33},{33,49},{50,2}... | collective-permute-start | bytes 3538952 | tf_op jit(solution)/shard_map/ppermute | solution.py:28
  64.0 10.6 %all-to-all-start.3 = ((f32[4,2,128]{2,1,0:T(2,128)}), f32[4,2,128]{2,1,0:T(2,128)S(1)}, u32[]{:S(2)}, u32[]{:S(2)}) async-start(f32[4,2,128]{2,1,0:T(2,128)} %broadcast_in_dim.33), calls=%async_computation.3 | async-start | bytes 8192 | tf_op jit(solution)/shard_map/all_to_all | solution.py:45
  70.1 4.5 %copy-start.7 = (bf16[1,8,3072]{2,1,0:T(8,128)(2,1)S(1)}, bf16[1,8,3072]{2,1,0:T(8,128)(2,1)}, u32[]{:S(2)}) copy-start(bf16[1,8,3072]{2,1,0:T(8,128)(2,1)} %param.9) | copy-start | bytes 147460
  75.3 9.5 %all-to-all-start.4 = ((bf16[4,8,3072]{2,1,0:T(8,128)(2,1)}), bf16[4,8,3072]{2,1,0:T(8,128)(2,1)}, u32[]{:S(2)}, u32[]{:S(2)}) async-start(bf16[4,8,3072]{2,1,0:T(8,128)(2,1)} %broadcast_in_dim.34), calls=%async_computation.4 | async-start | bytes 393216 | tf_op jit(solution)/shard_map/all_to_all | solution.py:45
  79.3 7.0 %copy-start.11 = (s32[1,8]{1,0:T(1,128)S(1)}, s32[1,8]{1,0:T(1,128)}, u32[]{:S(2)}) copy-start(s32[1,8]{1,0:T(1,128)} %param.10) | copy-start | bytes 100
  84.8 11.2 %collective-permute-start.9 = (bf16[96,3072]{1,0:T(8,128)(2,1)}, bf16[96,3072]{1,0:T(8,128)(2,1)}, u32[]{:S(2)}, u32[]{:S(2)}) collective-permute-start(bf16[96,3072]{1,0:T(8,128)(2,1)} %get-tuple-element.63), channel_id=1, source_target_pairs={{4,0},{8,4},{12,8},{0,12},{5,1},{9,5},{13,9},{1,13},{6,2},{10,6},{... | collective-permute-start | bytes 1769480 | tf_op jit(solution)/shard_map/ppermute | solution.py:28
  86.1 11.2 %collective-permute-start.10 = (bf16[96,3072]{1,0:T(8,128)(2,1)}, bf16[96,3072]{1,0:T(8,128)(2,1)}, u32[]{:S(2)}, u32[]{:S(2)}) collective-permute-start(bf16[96,3072]{1,0:T(8,128)(2,1)} %get-tuple-element.65), channel_id=1, source_target_pairs={{12,0},{0,4},{4,8},{8,12},{13,1},{1,5},{5,9},{9,13},{14,2},{2,6},{... | collective-permute-start | bytes 1769480 | tf_op jit(solution)/shard_map/ppermute | solution.py:28
  86.4 31.0 %collective-permute-start.13 = (bf16[192,3072]{1,0:T(8,128)(2,1)}, bf16[192,3072]{1,0:T(8,128)(2,1)}, u32[]{:S(2)}, u32[]{:S(2)}) collective-permute-start(bf16[192,3072]{1,0:T(8,128)(2,1)} %collective-permute-done.5.refs_7_), channel_id=1, source_target_pairs={{16,0},{32,16},{48,32},{0,48},{17,1},{33,17},{49,33},{1,49},{18,2}... | collective-permute-start | bytes 3538952 | tf_op jit(solution)/shard_map/ppermute | solution.py:28
  87.7 29.7 %collective-permute-start.14 = (bf16[192,3072]{1,0:T(8,128)(2,1)}, bf16[192,3072]{1,0:T(8,128)(2,1)}, u32[]{:S(2)}, u32[]{:S(2)}) collective-permute-start(bf16[192,3072]{1,0:T(8,128)(2,1)} %collective-permute-done.4.refs_6_), channel_id=1, source_target_pairs={{48,0},{0,16},{16,32},{32,48},{49,1},{1,17},{17,33},{33,49},{50,2}... | collective-permute-start | bytes 3538952 | tf_op jit(solution)/shard_map/ppermute | solution.py:28
  87.9 32.5 %collective-permute-start.8 = (bf16[4,8,3072]{2,1,0:T(8,128)(2,1)}, bf16[4,8,3072]{2,1,0:T(8,128)(2,1)}, u32[]{:S(2)}, u32[]{:S(2)}) collective-permute-start(bf16[4,8,3072]{2,1,0:T(8,128)(2,1)} %all-to-all-done.4), channel_id=1, source_target_pairs={{0,32},{32,0},{1,33},{33,1},{2,34},{34,2},{3,35},{35,3},{4,36},{36... | collective-permute-start | bytes 589832 | tf_op jit(solution)/shard_map/ppermute | solution.py:204
  90.3 27.0 %all-to-all-start.5 = ((f32[16,4,2,128]{3,2,1,0:T(2,128)}), f32[16,4,2,128]{3,2,1,0:T(2,128)S(1)}, u32[]{:S(2)}, u32[]{:S(2)}) async-start(f32[16,4,2,128]{3,2,1,0:T(2,128)} %broadcast_in_dim.36), calls=%async_computation.5 | async-start | bytes 131072 | tf_op jit(solution)/shard_map/all_to_all | solution.py:45
  97.3 20.0 %collective-permute-start.11 = (bf16[96,3072]{1,0:T(8,128)(2,1)}, bf16[96,3072]{1,0:T(8,128)(2,1)}, u32[]{:S(2)}, u32[]{:S(2)}) collective-permute-start(bf16[96,3072]{1,0:T(8,128)(2,1)} %get-tuple-element.68), channel_id=1, source_target_pairs={{4,0},{8,4},{12,8},{0,12},{5,1},{9,5},{13,9},{1,13},{6,2},{10,6},{... | collective-permute-start | bytes 1769480 | tf_op jit(solution)/shard_map/ppermute | solution.py:28
  98.1 19.3 %collective-permute-start.12 = (bf16[96,3072]{1,0:T(8,128)(2,1)}, bf16[96,3072]{1,0:T(8,128)(2,1)}, u32[]{:S(2)}, u32[]{:S(2)}) collective-permute-start(bf16[96,3072]{1,0:T(8,128)(2,1)} %get-tuple-element.70), channel_id=1, source_target_pairs={{12,0},{0,4},{4,8},{8,12},{13,1},{1,5},{5,9},{9,13},{14,2},{2,6},{... | collective-permute-start | bytes 1769480 | tf_op jit(solution)/shard_map/ppermute | solution.py:28
  117.4 11.6 %collective-permute-start.15 = (bf16[96,3072]{1,0:T(8,128)(2,1)}, bf16[96,3072]{1,0:T(8,128)(2,1)}, u32[]{:S(2)}, u32[]{:S(2)}) collective-permute-start(bf16[96,3072]{1,0:T(8,128)(2,1)} %collective-permute-done.9.refs_12_), channel_id=1, source_target_pairs={{16,0},{32,16},{48,32},{0,48},{17,1},{33,17},{49,33},{1,49},{18,2}... | collective-permute-start | bytes 1769480 | tf_op jit(solution)/shard_map/ppermute | solution.py:28
  117.7 11.3 %collective-permute-start.16 = (bf16[96,3072]{1,0:T(8,128)(2,1)}, bf16[96,3072]{1,0:T(8,128)(2,1)}, u32[]{:S(2)}, u32[]{:S(2)}) collective-permute-start(bf16[96,3072]{1,0:T(8,128)(2,1)} %collective-permute-done.10.refs_14_.refs_0_), channel_id=1, source_target_pairs={{48,0},{0,16},{16,32},{32,48},{49,1},{1,17},{17,33},{33,49},{50,2}... | collective-permute-start | bytes 1769480 | tf_op jit(solution)/shard_map/ppermute | solution.py:28
  118.9 10.1 %collective-permute-start.17 = (bf16[96,3072]{1,0:T(8,128)(2,1)}, bf16[96,3072]{1,0:T(8,128)(2,1)}, u32[]{:S(2)}, u32[]{:S(2)}) collective-permute-start(bf16[96,3072]{1,0:T(8,128)(2,1)} %slice.87), channel_id=1, source_target_pairs={{4,0},{8,4},{12,8},{0,12},{5,1},{9,5},{13,9},{1,13},{6,2},{10,6},{... | collective-permute-start | bytes 1769480 | tf_op jit(solution)/shard_map/ppermute | solution.py:28
  119.7 10.6 %collective-permute-start.18 = (bf16[96,3072]{1,0:T(8,128)(2,1)}, bf16[96,3072]{1,0:T(8,128)(2,1)}, u32[]{:S(2)}, u32[]{:S(2)}) collective-permute-start(bf16[96,3072]{1,0:T(8,128)(2,1)} %slice.88), channel_id=1, source_target_pairs={{12,0},{0,4},{4,8},{8,12},{13,1},{1,5},{5,9},{9,13},{14,2},{2,6},{... | collective-permute-start | bytes 1769480 | tf_op jit(solution)/shard_map/ppermute | solution.py:28
  129.0 3.3 %copy-start.1 = (bf16[2,4,8,3072]{3,2,1,0:T(8,128)(2,1)S(1)}, bf16[2,4,8,3072]{3,2,1,0:T(8,128)(2,1)}, u32[]{:S(2)}) copy-start(bf16[2,4,8,3072]{3,2,1,0:T(8,128)(2,1)} %pad_maximum_fusion.2) | copy-start | bytes 1179652
  137.2 28.6 %copy-start.5 = (bf16[8,3200]{1,0:T(8,128)(2,1)S(1)}, bf16[8,3200]{1,0:T(8,128)(2,1)}, u32[]{:S(2)}) copy-start(bf16[8,3200]{1,0:T(8,128)(2,1)} %get-tuple-element.98) | copy-start | bytes 153604
  157.4 8.5 %collective-permute-start.19 = (bf16[8,3200]{1,0:T(8,128)(2,1)S(1)}, bf16[8,3200]{1,0:T(8,128)(2,1)S(1)}, u32[]{:S(2)}, u32[]{:S(2)}) collective-permute-start(bf16[8,3200]{1,0:T(8,128)(2,1)S(1)} %shard_map.107), channel_id=1, source_target_pairs={{0,64},{2,66},{64,130},{66,128},{128,192},{130,194},{192,0},{194,2... | collective-permute-start | bytes 153608 | tf_op jit(solution)/shard_map/ppermute | solution.py:35
  183.4 27.1 %copy-start.4 = (bf16[8,3200]{1,0:T(8,128)(2,1)S(1)}, bf16[8,3200]{1,0:T(8,128)(2,1)}, u32[]{:S(2)}) copy-start(bf16[8,3200]{1,0:T(8,128)(2,1)} %get-tuple-element.97) | copy-start | bytes 153604
  196.2 14.3 %collective-permute-start.20 = (bf16[8,3200]{1,0:T(8,128)(2,1)S(1)}, bf16[8,3200]{1,0:T(8,128)(2,1)S(1)}, u32[]{:S(2)}, u32[]{:S(2)}) collective-permute-start(bf16[8,3200]{1,0:T(8,128)(2,1)S(1)} %shard_map.109), channel_id=1, source_target_pairs={{0,64},{2,66},{64,130},{66,128},{128,192},{130,194},{192,0},{194,2... | collective-permute-start | bytes 153608 | tf_op jit(solution)/shard_map/ppermute | solution.py:35
  229.7 21.6 %copy-start.3 = (bf16[8,3200]{1,0:T(8,128)(2,1)S(1)}, bf16[8,3200]{1,0:T(8,128)(2,1)}, u32[]{:S(2)}) copy-start(bf16[8,3200]{1,0:T(8,128)(2,1)} %get-tuple-element.99) | copy-start | bytes 153604
  245.0 6.3 %collective-permute-start.21 = (bf16[8,3200]{1,0:T(8,128)(2,1)S(1)}, bf16[8,3200]{1,0:T(8,128)(2,1)S(1)}, u32[]{:S(2)}, u32[]{:S(2)}) collective-permute-start(bf16[8,3200]{1,0:T(8,128)(2,1)S(1)} %shard_map.111), channel_id=1, source_target_pairs={{0,64},{2,66},{64,130},{66,128},{128,192},{130,194},{1,65},{3,67},... | collective-permute-start | bytes 153608 | tf_op jit(solution)/shard_map/ppermute | solution.py:35
  272.5 21.3 %copy-start.6 = (bf16[8,3200]{1,0:T(8,128)(2,1)S(1)}, bf16[8,3200]{1,0:T(8,128)(2,1)}, u32[]{:S(2)}) copy-start(bf16[8,3200]{1,0:T(8,128)(2,1)} %get-tuple-element.101) | copy-start | bytes 153604
  286.7 7.2 %collective-permute-start.24 = (bf16[8,3200]{1,0:T(8,128)(2,1)S(1)}, bf16[8,3200]{1,0:T(8,128)(2,1)S(1)}, u32[]{:S(2)}, u32[]{:S(2)}) collective-permute-start(bf16[8,3200]{1,0:T(8,128)(2,1)S(1)} %shard_map.113), channel_id=1, source_target_pairs={{0,64},{2,66},{64,128},{66,130},{128,194},{130,192},{1,65},{3,67},... | collective-permute-start | bytes 153608 | tf_op jit(solution)/shard_map/ppermute | solution.py:35
  291.9 3.1 %collective-permute-start.23 = (bf16[8,3200]{1,0:T(8,128)(2,1)S(1)}, bf16[8,3200]{1,0:T(8,128)(2,1)S(1)}, u32[]{:S(2)}, u32[]{:S(2)}) collective-permute-start(bf16[8,3200]{1,0:T(8,128)(2,1)S(1)} %broadcast_select_fusion), channel_id=1, source_target_pairs={{0,64},{2,66},{192,194},{194,192},{1,65},{3,67},{193,195},{195,193... | collective-permute-start | bytes 153608 | tf_op jit(solution)/shard_map/ppermute | solution.py:35
  293.2 1.8 collective-permute-start.22

commit v7 on v6

--- a/solution.py
+++ b/solution.py
@@ -201,14 +201,10 @@
     halves, y2[0], y2[2] = together((halves, y2[0], y2[2]))
     y2[1] = from_neighbour(halves[1], "y", 1)
     y2[3] = from_neighbour(halves[3], "y", -1)
-    theirs = lax.ppermute(mine, "xh", [(0, 1), (1, 0)])
     modes = exchange(line, PLANE)
     xa_yp_down = xa_yp[middle:]
     xb_ym_down = xb_ym[middle:]
 
-    y2, xa_ym, xb_yp, xa_yp_down, xb_ym_down, modes = together(
-        (y2, xa_ym, xb_yp, xa_yp_down, xb_ym_down, modes)
-    )
     modes = modes.reshape(-1, rows * LANES)[:, :columns].reshape(3, -1)
     xa_y2_up = from_neighbour(y2[0], "x", 1)
     xb_y2_up = from_neighbour(y2[2], "x", -1)
@@ -227,7 +223,8 @@
     ]
     plan += [(count + which, 0, middle, which, count * middle) for which in (0, 1)]
     plan += [(count + 2 + which, 0, cut, which, main - cut) for which in (0, 1)]
-    up_rows, down_rows = place(plan, whole + y2, main)
+    up_rows, down_rows = place(plan, after(whole + y2, modes), main)
+    theirs = lax.ppermute(after(mine, xa_ym, xb_yp), "xh", [(0, 1), (1, 0)])
     upper = lax.axis_index("xh") == 1
     gathered = jnp.stack([jnp.where(upper, theirs, mine), jnp.where(upper, mine, theirs)])
     plan = [(which, cut, middle - cut, which, 0) for which in (0, 1)]

time: 297 us -> 296 us (level)
  waiting for transfers between devices: 43.4 us -> 39.8 us
    all_to_all x5, waiting for transfers between devices: 33 us -> 19.8 us  [exchange(): return lax.all_to_all(copies, axes, 0, 0)]
    ppermute x18, waiting for transfers between devices: 3.49 us -> 13 us  [from_neighbour(): return lax.ppermute(block, (axis + 'h', axis + 'l'), route)]
  transfers between devices with their start and end apart: 30 -> 30, of which waited for: 12 -> 12; matrix products, arithmetic and copies ran while one was open for 6% -> 5% of each run, Pallas kernels for 2% -> 2%
where the time goes in v7:
time: 296 us; the launch traced here: 295 us
  blocking collectives  120 us (41%)
  starting transfers between devices  83.4 us (28%)
  waiting for transfers between devices  39.8 us (13%)
  Pallas kernels  27.2 us (9%)
  local copies, waits for them, and re-layouts  14.8 us (5%)
  other arithmetic  6.59 us (2%)
    all_to_all x4, blocking collectives, per_device(): lax.all_to_all(partial.reshape(GROUP_SIZE, tokens, breadth), GROUP, 0, 0)  63.6 us
    all_to_all x4, blocking collectives, exchange(): return lax.all_to_all(copies, axes, 0, 0)  56.6 us
    all_to_all x5, starting transfers between devices, exchange(): return lax.all_to_all(copies, axes, 0, 0)  31.9 us
    ppermute x6, starting transfers between devices, between_sections(): return lax.ppermute(block, SECTION + ('zc',), route)  29.8 us
    ppermute x18, starting transfers between devices, from_neighbour(): return lax.ppermute(block, (axis + 'h', axis + 'l'), route)  20 us
    all_to_all x5, waiting for transfers between devices, exchange(): return lax.all_to_all(copies, axes, 0, 0)  19.8 us
    pallas_call x4, Pallas kernels, layer(): pl.pallas_call(layer_kernel, out_shape=jax.ShapeDtypeStruct((rows, breadt...  19.8 us
    ppermute x18, waiting for transfers between devices, from_neighbour(): return lax.ppermute(block, (axis + 'h', axis + 'l'), route)  13 us
  transfers between devices with their start and end apart: 30, of which 12 were waited for; matrix products, arithmetic and copies ran while one was open for 5% of the time, Pallas kernels for 2%

profile of v7, /device:TPU:1, one launch (start us, length us, event | category | flops | bytes accessed | tf_op | source)
XLA Modules:
  0.0 294.9 jit_solution(2526858569869001778)
XLA Ops:
  0.7 1.5 slice_bitcast_fusion
  3.3 1.6 pad_maximum_fusion
  4.9 3.6 %collective-permute-start = (bf16[192,3072]{1,0:T(8,128)(2,1)}, bf16[192,3072]{1,0:T(8,128)(2,1)S(1)}, u32[]{:S(2)}, u32[]{:S(2)}) collective-permute-start(bf16[192,3072]{1,0:T(8,128)(2,1)} %get-tuple-element.90.refs_0_), channel_id=1, source_target_pairs={{4,0},{8,4},{12,8},{0,12},{5,1},{9,5},{13,9},{1,13},{6,2},{10,6},{... | collective-permute-start | bytes 3538952 | tf_op jit(solution)/shard_map/ppermute | solution.py:28
  8.5 2.5 collective-permute-start.2
  11.7 9.7 %all-to-all-start = ((f32[16,28,128]{2,1,0:T(8,128)}), f32[16,28,128]{2,1,0:T(8,128)}, u32[]{:S(2)}, u32[]{:S(2)}) async-start(f32[16,28,128]{2,1,0:T(8,128)} %broadcast_in_dim.28), calls=%async_computation | async-start | bytes 524288 | tf_op jit(solution)/shard_map/all_to_all | solution.py:45
  21.5 9.6 %all-to-all-done = f32[16,28,128]{2,1,0:T(8,128)} async-done(((f32[16,28,128]{2,1,0:T(8,128)}), f32[16,28,128]{2,1,0:T(8,128)}, u32[]{:S(2)}, u32[]{:S(2)}) %all-to-all-start) | async-done | bytes 229408 | tf_op jit(solution)/shard_map/all_to_all | solution.py:45
  32.1 13.4 %all_to_all.65 = bf16[4,8,3200]{2,1,0:T(8,128)(2,1)} all-to-all(bf16[4,8,3200]{2,1,0:T(8,128)(2,1)S(1)} %broadcast_in_dim.30), channel_id=1, replica_groups=mesh['zh'=2,'core'=2,'xh'=2,'xl'=2,'yh'=2,'yl'=2,'zc'=2,'zf'=2] {'zh','c..., dimensions={0} | all-to-all | bytes 409600 | tf_op jit(solution)/shard_map/all_to_all | solution.py:45
  46.3 7.1 %all-to-all-start.2 = ((f32[16,28,128]{2,1,0:T(8,128)}), f32[16,28,128]{2,1,0:T(8,128)}, u32[]{:S(2)}, u32[]{:S(2)}) async-start(f32[16,28,128]{2,1,0:T(8,128)} %broadcast_in_dim.31), calls=%async_computation.2 | async-start | bytes 524288 | tf_op jit(solution)/shard_map/all_to_all | solution.py:45
  53.3 2.5 collective-permute-start.4
  55.9 2.4 collective-permute-start.6
  58.3 2.5 all-to-all-done.2
  64.0 6.0 %all-to-all-start.3 = ((f32[4,2,128]{2,1,0:T(2,128)}), f32[4,2,128]{2,1,0:T(2,128)S(1)}, u32[]{:S(2)}, u32[]{:S(2)}) async-start(f32[4,2,128]{2,1,0:T(2,128)} %broadcast_in_dim.33), calls=%async_computation.3 | async-start | bytes 8192 | tf_op jit(solution)/shard_map/all_to_all | solution.py:45
  71.2 3.4 %all-to-all-done.3 = f32[4,2,128]{2,1,0:T(2,128)S(1)} async-done(((f32[4,2,128]{2,1,0:T(2,128)}), f32[4,2,128]{2,1,0:T(2,128)S(1)}, u32[]{:S(2)}, u32[]{:S(2)}) %all-to-all-start.3) | async-done | bytes 4128 | tf_op jit(solution)/shard_map/all_to_all | solution.py:45
  75.3 4.0 %all-to-all-start.4 = ((bf16[4,8,3072]{2,1,0:T(8,128)(2,1)}), bf16[4,8,3072]{2,1,0:T(8,128)(2,1)}, u32[]{:S(2)}, u32[]{:S(2)}) async-start(bf16[4,8,3072]{2,1,0:T(8,128)(2,1)} %broadcast_in_dim.34), calls=%async_computation.4 | async-start | bytes 393216 | tf_op jit(solution)/shard_map/all_to_all | solution.py:45
  80.5 4.3 %all-to-all-done.4 = bf16[4,8,3072]{2,1,0:T(8,128)(2,1)} async-done(((bf16[4,8,3072]{2,1,0:T(8,128)(2,1)}), bf16[4,8,3072]{2,1,0:T(8,128)(2,1)}, u32[]{:S(2)}, u32[]{:S(2)}) %all-to-all-start.4) | async-done | bytes 196640 | tf_op jit(solution)/shard_map/all_to_all | solution.py:45
  84.8 1.3 collective-permute-start.11
  86.3 1.3 collective-permute-start.8
  87.8 8.2 %collective-permute-done.11.refs_12_ = bf16[96,3072]{1,0:T(8,128)(2,1)} collective-permute-done((bf16[96,3072]{1,0:T(8,128)(2,1)}, bf16[96,3072]{1,0:T(8,128)(2,1)}, u32[]{:S(2)}, u32[]{:S(2)}) %collective-permute-start.11) | collective-permute-done | bytes 589856 | tf_op jit(solution)/shard_map/ppermute | solution.py:28
  96.0 1.3 collective-permute-done.12.refs_14_.refs_0_
  99.5 5.1 %all-to-all-start.5 = ((f32[16,4,2,128]{3,2,1,0:T(2,128)}), f32[16,4,2,128]{3,2,1,0:T(2,128)}, u32[]{:S(2)}, u32[]{:S(2)}) async-start(f32[16,4,2,128]{3,2,1,0:T(2,128)} %broadcast_in_dim.36), calls=%async_computation.5 | async-start | bytes 131072 | tf_op jit(solution)/shard_map/all_to_all | solution.py:45
  104.6 2.0 slice.93
  106.6 2.5 collective-permute-start.17
  109.1 1.9 slice.94
  111.5 2.0 collective-permute-start.15
  113.5 1.8 collective-permute-start.10
  115.9 1.5 copy.19
  118.4 5.1 %shard_map.104 = (bf16[1280,3072]{1,0:T(8,128)(2,1)S(1)}, bf16[1280,3072]{1,0:T(8,128)(2,1)S(1)}) custom-call(bf16[192,3072]{1,0:T(8,128)(2,1)} %get-tuple-element.90.refs_0_, bf16[192,3072]{1,0:T(8,128)(2,1)} %get-tuple-element.91.refs_1_, bf16[192,3072]{1,0:T(8,128)(2,1)} %collective-permute-done.2.refs_2_, ...), custom_call_target="tpu_custom_call" | custom-call | bytes 31457280 | tf_op jit(solution)/shard_map/pallas_call | solution.py:118
  123.6 3.0 %collective-permute-done.16.refs_3_ = bf16[96,3072]{1,0:T(8,128)(2,1)} collective-permute-done((bf16[96,3072]{1,0:T(8,128)(2,1)}, bf16[96,3072]{1,0:T(8,128)(2,1)}, u32[]{:S(2)}, u32[]{:S(2)}) %collective-permute-start.16) | collective-permute-done | bytes 589856 | tf_op jit(solution)/shard_map/ppermute | solution.py:28
  126.6 1.9 shard_map.105
  129.6 4.9 %shard_map.106 = bf16[64,3072]{1,0:T(8,128)(2,1)S(1)} custom-call(bf16[64,3072]{1,0:T(8,128)(2,1)S(1)} %bitcast.69, f32[3,3072]{1,0:T(4,128)S(1)} %reshape.75.mod_ref, bf16[1280,3072]{1,0:T(8,128)(2,1)S(1)} %get-tuple-element.106.up, bf16[1280,3072]{1,0:T(8,128)(2,1)S(1)} %get-tuple-element.107.down, bf16[256,3072]{1,0:T(8,128)(2,1)S(1)} %get-tuple-element.108.up_end, ...), custom_call_target="tpu_custom_call" | custom-call | flops 1207959552 | bytes 19660800 | tf_op jit(solution)/shard_map/pallas_call | solution.py:79
  134.5 21.5 %all_to_all.66.parts_ref = bf16[8,8,3072]{2,1,0:T(8,128)(2,1)S(1)} all-to-all(bf16[8,8,3072]{2,1,0:T(8,128)(2,1)S(1)} %bitcast.70), channel_id=1, replica_groups=mesh['zh'=2,'core'=2,'xh'=2,'xl'=2,'yh'=2,'yl'=2,'zc'=2,'zf'=2] {'xh','z..., dimensions={0} | all-to-all | bytes 786432 | tf_op jit(solution)/shard_map/all_to_all | solution.py:282
  156.1 6.5 %collective-permute-start.19 = (bf16[8,3200]{1,0:T(8,128)(2,1)S(1)}, bf16[8,3200]{1,0:T(8,128)(2,1)S(1)}, u32[]{:S(2)}, u32[]{:S(2)}) collective-permute-start(bf16[8,3200]{1,0:T(8,128)(2,1)S(1)} %shard_map.107), channel_id=1, source_target_pairs={{0,64},{2,66},{64,130},{66,128},{128,192},{130,194},{192,0},{194,2... | collective-permute-start | bytes 153608 | tf_op jit(solution)/shard_map/ppermute | solution.py:35
  162.6 2.5 collective-permute-done.19
  165.1 12.5 %all_to_all.67 = bf16[8,8,3072]{2,1,0:T(8,128)(2,1)S(1)} all-to-all(bf16[8,8,3072]{2,1,0:T(8,128)(2,1)S(1)} %broadcast_in_dim.37), channel_id=1, replica_groups=mesh['zh'=2,'core'=2,'xh'=2,'xl'=2,'yh'=2,'yl'=2,'zc'=2,'zf'=2] {'xh','z..., dimensions={0} | all-to-all | bytes 786432 | tf_op jit(solution)/shard_map/all_to_all | solution.py:45
  177.7 4.9 %shard_map.108 = bf16[64,3072]{1,0:T(8,128)(2,1)S(1)} custom-call(bf16[64,3072]{1,0:T(8,128)(2,1)S(1)} %bitcast.71, f32[3,3072]{1,0:T(4,128)S(1)} %reshape.75.mod_ref, bf16[1280,3072]{1,0:T(8,128)(2,1)S(1)} %get-tuple-element.106.up, bf16[1280,3072]{1,0:T(8,128)(2,1)S(1)} %get-tuple-element.107.down, bf16[256,3072]{1,0:T(8,128)(2,1)S(1)} %get-tuple-element.108.up_end, ...), custom_call_target="tpu_custom_call" | custom-call | flops 1207959552 | bytes 19660800 | tf_op jit(solution)/shard_map/pallas_call | solution.py:79
  182.6 12.7 %all_to_all.68.parts_ref = bf16[8,8,3072]{2,1,0:T(8,128)(2,1)S(1)} all-to-all(bf16[8,8,3072]{2,1,0:T(8,128)(2,1)S(1)} %bitcast.72), channel_id=1, replica_groups=mesh['zh'=2,'core'=2,'xh'=2,'xl'=2,'yh'=2,'yl'=2,'zc'=2,'zf'=2] {'xh','z..., dimensions={0} | all-to-all | bytes 786432 | tf_op jit(solution)/shard_map/all_to_all | solution.py:282
  195.4 12.9 %collective-permute-start.20 = (bf16[8,3200]{1,0:T(8,128)(2,1)S(1)}, bf16[8,3200]{1,0:T(8,128)(2,1)S(1)}, u32[]{:S(2)}, u32[]{:S(2)}) collective-permute-start(bf16[8,3200]{1,0:T(8,128)(2,1)S(1)} %shard_map.109), channel_id=1, source_target_pairs={{0,64},{2,66},{64,130},{66,128},{128,192},{130,194},{192,0},{194,2... | collective-permute-start | bytes 153608 | tf_op jit(solution)/shard_map/ppermute | solution.py:35
  208.3 1.6 collective-permute-done.20
  210.0 14.5 %all_to_all.69 = bf16[8,8,3072]{2,1,0:T(8,128)(2,1)S(1)} all-to-all(bf16[8,8,3072]{2,1,0:T(8,128)(2,1)S(1)} %broadcast_in_dim.38), channel_id=1, replica_groups=mesh['zh'=2,'core'=2,'xh'=2,'xl'=2,'yh'=2,'yl'=2,'zc'=2,'zf'=2] {'xh','z..., dimensions={0} | all-to-all | bytes 786432 | tf_op jit(solution)/shard_map/all_to_all | solution.py:45
  224.4 4.9 %shard_map.110 = bf16[64,3072]{1,0:T(8,128)(2,1)S(1)} custom-call(bf16[64,3072]{1,0:T(8,128)(2,1)S(1)} %bitcast.73, f32[3,3072]{1,0:T(4,128)S(1)} %reshape.75.mod_ref, bf16[1280,3072]{1,0:T(8,128)(2,1)S(1)} %get-tuple-element.106.up, bf16[1280,3072]{1,0:T(8,128)(2,1)S(1)} %get-tuple-element.107.down, bf16[256,3072]{1,0:T(8,128)(2,1)S(1)} %get-tuple-element.108.up_end, ...), custom_call_target="tpu_custom_call" | custom-call | flops 1207959552 | bytes 19660800 | tf_op jit(solution)/shard_map/pallas_call | solution.py:79
  229.4 15.4 %all_to_all.70.parts_ref = bf16[8,8,3072]{2,1,0:T(8,128)(2,1)S(1)} all-to-all(bf16[8,8,3072]{2,1,0:T(8,128)(2,1)S(1)} %bitcast.74), channel_id=1, replica_groups=mesh['zh'=2,'core'=2,'xh'=2,'xl'=2,'yh'=2,'yl'=2,'zc'=2,'zf'=2] {'xh','z..., dimensions={0} | all-to-all | bytes 786432 | tf_op jit(solution)/shard_map/all_to_all | solution.py:282
  244.9 3.5 %collective-permute-start.21 = (bf16[8,3200]{1,0:T(8,128)(2,1)S(1)}, bf16[8,3200]{1,0:T(8,128)(2,1)S(1)}, u32[]{:S(2)}, u32[]{:S(2)}) collective-permute-start(bf16[8,3200]{1,0:T(8,128)(2,1)S(1)} %shard_map.111), channel_id=1, source_target_pairs={{0,64},{2,66},{64,130},{66,128},{128,192},{130,194},{1,65},{3,67},... | collective-permute-start | bytes 153608 | tf_op jit(solution)/shard_map/ppermute | solution.py:35
  248.4 2.4 collective-permute-done.21
  250.9 16.2 %all_to_all.71 = bf16[8,8,3072]{2,1,0:T(8,128)(2,1)S(1)} all-to-all(bf16[8,8,3072]{2,1,0:T(8,128)(2,1)S(1)} %broadcast_in_dim.39), channel_id=1, replica_groups=mesh['zh'=2,'core'=2,'xh'=2,'xl'=2,'yh'=2,'yl'=2,'zc'=2,'zf'=2] {'xh','z..., dimensions={0} | all-to-all | bytes 786432 | tf_op jit(solution)/shard_map/all_to_all | solution.py:45
  267.1 4.9 %shard_map.112 = bf16[64,3072]{1,0:T(8,128)(2,1)S(1)} custom-call(bf16[64,3072]{1,0:T(8,128)(2,1)S(1)} %bitcast.67, f32[3,3072]{1,0:T(4,128)S(1)} %reshape.75.mod_ref, bf16[1280,3072]{1,0:T(8,128)(2,1)S(1)} %get-tuple-element.106.up, bf16[1280,3072]{1,0:T(8,128)(2,1)S(1)} %get-tuple-element.107.down, bf16[256,3072]{1,0:T(8,128)(2,1)S(1)} %get-tuple-element.108.up_end, ...), custom_call_target="tpu_custom_call" | custom-call | flops 1207959552 | bytes 19660800 | tf_op jit(solution)/shard_map/pallas_call | solution.py:79
  272.0 14.1 %all_to_all.72.parts_ref = bf16[8,8,3072]{2,1,0:T(8,128)(2,1)S(1)} all-to-all(bf16[8,8,3072]{2,1,0:T(8,128)(2,1)S(1)} %bitcast.68), channel_id=1, replica_groups=mesh['zh'=2,'core'=2,'xh'=2,'xl'=2,'yh'=2,'yl'=2,'zc'=2,'zf'=2] {'xh','z..., dimensions={0} | all-to-all | bytes 786432 | tf_op jit(solution)/shard_map/all_to_all | solution.py:282
  286.2 4.9 %collective-permute-start.24 = (bf16[8,3200]{1,0:T(8,128)(2,1)S(1)}, bf16[8,3200]{1,0:T(8,128)(2,1)S(1)}, u32[]{:S(2)}, u32[]{:S(2)}) collective-permute-start(bf16[8,3200]{1,0:T(8,128)(2,1)S(1)} %shard_map.113), channel_id=1, source_target_pairs={{0,64},{2,66},{64,128},{66,130},{128,194},{130,192},{1,65},{3,67},... | collective-permute-start | bytes 153608 | tf_op jit(solution)/shard_map/ppermute | solution.py:35
  291.1 1.3 collective-permute-start.23
  (98 shorter events, 17.4 us)
Async XLA Ops:
  0.6 62.4 %copy-start = (bf16[1,144,3584]{2,1,0:T(8,128)(2,1)S(1)}, bf16[1,144,3584]{2,1,0:T(8,128)(2,1)}, u32[]{:S(2)}) copy-start(bf16[1,144,3584]{2,1,0:T(8,128)(2,1)} %param.15) | copy-start | bytes 3096580
  0.6 1.7 copy-start.1
  2.4 0.8 copy-start.7
  3.3 18.1 %copy-start.9 = (s32[1,8]{1,0:T(1,128)S(1)}, s32[1,8]{1,0:T(1,128)}, u32[]{:S(2)}) copy-start(s32[1,8]{1,0:T(1,128)} %param.12) | copy-start | bytes 100
  3.3 18.2 %copy-start.8 = (bf16[1,8,3072]{2,1,0:T(8,128)(2,1)S(1)}, bf16[1,8,3072]{2,1,0:T(8,128)(2,1)}, u32[]{:S(2)}) copy-start(bf16[1,8,3072]{2,1,0:T(8,128)(2,1)} %param.11) | copy-start | bytes 147460
  4.9 40.6 %collective-permute-start = (bf16[192,3072]{1,0:T(8,128)(2,1)}, bf16[192,3072]{1,0:T(8,128)(2,1)S(1)}, u32[]{:S(2)}, u32[]{:S(2)}) collective-permute-start(bf16[192,3072]{1,0:T(8,128)(2,1)} %get-tuple-element.90.refs_0_), channel_id=1, source_target_pairs={{4,0},{8,4},{12,8},{0,12},{5,1},{9,5},{13,9},{1,13},{6,2},{10,6},{... | collective-permute-start | bytes 3538952 | tf_op jit(solution)/shard_map/ppermute | solution.py:28
  8.5 37.0 %collective-permute-start.1 = (bf16[192,3072]{1,0:T(8,128)(2,1)}, bf16[192,3072]{1,0:T(8,128)(2,1)S(1)}, u32[]{:S(2)}, u32[]{:S(2)}) collective-permute-start(bf16[192,3072]{1,0:T(8,128)(2,1)} %get-tuple-element.91.refs_1_), channel_id=1, source_target_pairs={{12,0},{0,4},{4,8},{8,12},{13,1},{1,5},{5,9},{9,13},{14,2},{2,6},{... | collective-permute-start | bytes 3538952 | tf_op jit(solution)/shard_map/ppermute | solution.py:28
  8.5 37.0 %collective-permute-start.2 = (bf16[192,3072]{1,0:T(8,128)(2,1)}, bf16[192,3072]{1,0:T(8,128)(2,1)}, u32[]{:S(2)}, u32[]{:S(2)}) collective-permute-start(bf16[192,3072]{1,0:T(8,128)(2,1)} %get-tuple-element.90.refs_0_), channel_id=1, source_target_pairs={{16,0},{32,16},{48,32},{0,48},{17,1},{33,17},{49,33},{1,49},{18,2}... | collective-permute-start | bytes 3538952 | tf_op jit(solution)/shard_map/ppermute | solution.py:28
  11.0 34.5 %collective-permute-start.3 = (bf16[192,3072]{1,0:T(8,128)(2,1)}, bf16[192,3072]{1,0:T(8,128)(2,1)}, u32[]{:S(2)}, u32[]{:S(2)}) collective-permute-start(bf16[192,3072]{1,0:T(8,128)(2,1)} %get-tuple-element.91.refs_1_), channel_id=1, source_target_pairs={{48,0},{0,16},{16,32},{32,48},{49,1},{1,17},{17,33},{33,49},{50,2}... | collective-permute-start | bytes 3538952 | tf_op jit(solution)/shard_map/ppermute | solution.py:28
  11.7 19.4 %all-to-all-start = ((f32[16,28,128]{2,1,0:T(8,128)}), f32[16,28,128]{2,1,0:T(8,128)}, u32[]{:S(2)}, u32[]{:S(2)}) async-start(f32[16,28,128]{2,1,0:T(8,128)} %broadcast_in_dim.28), calls=%async_computation | async-start | bytes 524288 | tf_op jit(solution)/shard_map/all_to_all | solution.py:45
  46.3 14.5 %all-to-all-start.2 = ((f32[16,28,128]{2,1,0:T(8,128)}), f32[16,28,128]{2,1,0:T(8,128)}, u32[]{:S(2)}, u32[]{:S(2)}) async-start(f32[16,28,128]{2,1,0:T(8,128)} %broadcast_in_dim.31), calls=%async_computation.2 | async-start | bytes 524288 | tf_op jit(solution)/shard_map/all_to_all | solution.py:45
  53.3 31.5 %collective-permute-start.4 = (bf16[192,3072]{1,0:T(8,128)(2,1)}, bf16[192,3072]{1,0:T(8,128)(2,1)}, u32[]{:S(2)}, u32[]{:S(2)}) collective-permute-start(bf16[192,3072]{1,0:T(8,128)(2,1)} %get-tuple-element.91.refs_1_), channel_id=1, source_target_pairs={{4,0},{8,4},{12,8},{0,12},{5,1},{9,5},{13,9},{1,13},{6,2},{10,6},{... | collective-permute-start | bytes 3538952 | tf_op jit(solution)/shard_map/ppermute | solution.py:28
  55.9 28.9 %collective-permute-start.5 = (bf16[192,3072]{1,0:T(8,128)(2,1)}, bf16[192,3072]{1,0:T(8,128)(2,1)}, u32[]{:S(2)}, u32[]{:S(2)}) collective-permute-start(bf16[192,3072]{1,0:T(8,128)(2,1)} %get-tuple-element.90.refs_0_), channel_id=1, source_target_pairs={{12,0},{0,4},{4,8},{8,12},{13,1},{1,5},{5,9},{9,13},{14,2},{2,6},{... | collective-permute-start | bytes 3538952 | tf_op jit(solution)/shard_map/ppermute | solution.py:28
  55.9 28.9 %collective-permute-start.6 = (bf16[192,3072]{1,0:T(8,128)(2,1)S(1)}, bf16[192,3072]{1,0:T(8,128)(2,1)}, u32[]{:S(2)}, u32[]{:S(2)}) collective-permute-start(bf16[192,3072]{1,0:T(8,128)(2,1)S(1)} %collective-permute-done.refs_4_), channel_id=1, source_target_pairs={{16,0},{32,16},{48,32},{0,48},{17,1},{33,17},{49,33},{1,49},{18,2}... | collective-permute-start | bytes 3538952 | tf_op jit(solution)/shard_map/ppermute | solution.py:28
  58.3 26.5 %collective-permute-start.7 = (bf16[192,3072]{1,0:T(8,128)(2,1)S(1)}, bf16[192,3072]{1,0:T(8,128)(2,1)}, u32[]{:S(2)}, u32[]{:S(2)}) collective-permute-start(bf16[192,3072]{1,0:T(8,128)(2,1)S(1)} %collective-permute-done.1.refs_5_), channel_id=1, source_target_pairs={{48,0},{0,16},{16,32},{32,48},{49,1},{1,17},{17,33},{33,49},{50,2}... | collective-permute-start | bytes 3538952 | tf_op jit(solution)/shard_map/ppermute | solution.py:28
  64.0 10.6 %all-to-all-start.3 = ((f32[4,2,128]{2,1,0:T(2,128)}), f32[4,2,128]{2,1,0:T(2,128)S(1)}, u32[]{:S(2)}, u32[]{:S(2)}) async-start(f32[4,2,128]{2,1,0:T(2,128)} %broadcast_in_dim.33), calls=%async_computation.3 | async-start | bytes 8192 | tf_op jit(solution)/shard_map/all_to_all | solution.py:45
  70.1 4.5 %copy-start.6 = (bf16[1,8,3072]{2,1,0:T(8,128)(2,1)S(1)}, bf16[1,8,3072]{2,1,0:T(8,128)(2,1)}, u32[]{:S(2)}) copy-start(bf16[1,8,3072]{2,1,0:T(8,128)(2,1)} %param.9) | copy-start | bytes 147460
  75.3 9.4 %all-to-all-start.4 = ((bf16[4,8,3072]{2,1,0:T(8,128)(2,1)}), bf16[4,8,3072]{2,1,0:T(8,128)(2,1)}, u32[]{:S(2)}, u32[]{:S(2)}) async-start(bf16[4,8,3072]{2,1,0:T(8,128)(2,1)} %broadcast_in_dim.34), calls=%async_computation.4 | async-start | bytes 393216 | tf_op jit(solution)/shard_map/all_to_all | solution.py:45
  79.3 19.4 %copy-start.10 = (s32[1,8]{1,0:T(1,128)S(1)}, s32[1,8]{1,0:T(1,128)}, u32[]{:S(2)}) copy-start(s32[1,8]{1,0:T(1,128)} %param.10) | copy-start | bytes 100
  84.8 11.2 %collective-permute-start.11 = (bf16[96,3072]{1,0:T(8,128)(2,1)}, bf16[96,3072]{1,0:T(8,128)(2,1)}, u32[]{:S(2)}, u32[]{:S(2)}) collective-permute-start(bf16[96,3072]{1,0:T(8,128)(2,1)} %get-tuple-element.82), channel_id=1, source_target_pairs={{4,0},{8,4},{12,8},{0,12},{5,1},{9,5},{13,9},{1,13},{6,2},{10,6},{... | collective-permute-start | bytes 1769480 | tf_op jit(solution)/shard_map/ppermute | solution.py:28
  86.1 11.2 %collective-permute-start.12 = (bf16[96,3072]{1,0:T(8,128)(2,1)}, bf16[96,3072]{1,0:T(8,128)(2,1)}, u32[]{:S(2)}, u32[]{:S(2)}) collective-permute-start(bf16[96,3072]{1,0:T(8,128)(2,1)} %get-tuple-element.84), channel_id=1, source_target_pairs={{12,0},{0,4},{4,8},{8,12},{13,1},{1,5},{5,9},{9,13},{14,2},{2,6},{... | collective-permute-start | bytes 1769480 | tf_op jit(solution)/shard_map/ppermute | solution.py:28
  86.3 24.7 %collective-permute-start.8 = (bf16[192,3072]{1,0:T(8,128)(2,1)}, bf16[192,3072]{1,0:T(8,128)(2,1)}, u32[]{:S(2)}, u32[]{:S(2)}) collective-permute-start(bf16[192,3072]{1,0:T(8,128)(2,1)} %collective-permute-done.5.refs_7_), channel_id=1, source_target_pairs={{16,0},{32,16},{48,32},{0,48},{17,1},{33,17},{49,33},{1,49},{18,2}... | collective-permute-start | bytes 3538952 | tf_op jit(solution)/shard_map/ppermute | solution.py:28
  87.7 23.8 %collective-permute-start.9 = (bf16[192,3072]{1,0:T(8,128)(2,1)}, bf16[192,3072]{1,0:T(8,128)(2,1)}, u32[]{:S(2)}, u32[]{:S(2)}) collective-permute-start(bf16[192,3072]{1,0:T(8,128)(2,1)} %collective-permute-done.4.refs_6_), channel_id=1, source_target_pairs={{48,0},{0,16},{16,32},{32,48},{49,1},{1,17},{17,33},{33,49},{50,2}... | collective-permute-start | bytes 3538952 | tf_op jit(solution)/shard_map/ppermute | solution.py:28
  97.3 16.2 %collective-permute-start.13 = (bf16[96,3072]{1,0:T(8,128)(2,1)}, bf16[96,3072]{1,0:T(8,128)(2,1)}, u32[]{:S(2)}, u32[]{:S(2)}) collective-permute-start(bf16[96,3072]{1,0:T(8,128)(2,1)} %get-tuple-element.87), channel_id=1, source_target_pairs={{4,0},{8,4},{12,8},{0,12},{5,1},{9,5},{13,9},{1,13},{6,2},{10,6},{... | collective-permute-start | bytes 1769480 | tf_op jit(solution)/shard_map/ppermute | solution.py:28
  97.7 15.8 %collective-permute-start.14 = (bf16[96,3072]{1,0:T(8,128)(2,1)}, bf16[96,3072]{1,0:T(8,128)(2,1)}, u32[]{:S(2)}, u32[]{:S(2)}) collective-permute-start(bf16[96,3072]{1,0:T(8,128)(2,1)} %get-tuple-element.89), channel_id=1, source_target_pairs={{12,0},{0,4},{4,8},{8,12},{13,1},{1,5},{5,9},{9,13},{14,2},{2,6},{... | collective-permute-start | bytes 1769480 | tf_op jit(solution)/shard_map/ppermute | solution.py:28
  99.5 16.4 %all-to-all-start.5 = ((f32[16,4,2,128]{3,2,1,0:T(2,128)}), f32[16,4,2,128]{3,2,1,0:T(2,128)}, u32[]{:S(2)}, u32[]{:S(2)}) async-start(f32[16,4,2,128]{3,2,1,0:T(2,128)} %broadcast_in_dim.36), calls=%async_computation.5 | async-start | bytes 131072 | tf_op jit(solution)/shard_map/all_to_all | solution.py:45
  104.6 10.7 %copy-start.2 = (bf16[4,8,3200]{2,1,0:T(8,128)(2,1)S(1)}, bf16[4,8,3200]{2,1,0:T(8,128)(2,1)}, u32[]{:S(2)}) copy-start(bf16[4,8,3200]{2,1,0:T(8,128)(2,1)} %all_to_all.65) | copy-start | bytes 614404
  106.6 17.0 %collective-permute-start.17 = (bf16[96,3072]{1,0:T(8,128)(2,1)}, bf16[96,3072]{1,0:T(8,128)(2,1)}, u32[]{:S(2)}, u32[]{:S(2)}) collective-permute-start(bf16[96,3072]{1,0:T(8,128)(2,1)} %slice.93), channel_id=1, source_target_pairs={{4,0},{8,4},{12,8},{0,12},{5,1},{9,5},{13,9},{1,13},{6,2},{10,6},{... | collective-permute-start | bytes 1769480 | tf_op jit(solution)/shard_map/ppermute | solution.py:28
  111.0 12.5 %collective-permute-start.18 = (bf16[96,3072]{1,0:T(8,128)(2,1)}, bf16[96,3072]{1,0:T(8,128)(2,1)}, u32[]{:S(2)}, u32[]{:S(2)}) collective-permute-start(bf16[96,3072]{1,0:T(8,128)(2,1)} %slice.94), channel_id=1, source_target_pairs={{12,0},{0,4},{4,8},{8,12},{13,1},{1,5},{5,9},{9,13},{14,2},{2,6},{... | collective-permute-start | bytes 1769480 | tf_op jit(solution)/shard_map/ppermute | solution.py:28
  111.5 12.1 %collective-permute-start.15 = (bf16[96,3072]{1,0:T(8,128)(2,1)}, bf16[96,3072]{1,0:T(8,128)(2,1)}, u32[]{:S(2)}, u32[]{:S(2)}) collective-permute-start(bf16[96,3072]{1,0:T(8,128)(2,1)} %collective-permute-done.11.refs_12_), channel_id=1, source_target_pairs={{16,0},{32,16},{48,32},{0,48},{17,1},{33,17},{49,33},{1,49},{18,2}... | collective-permute-start | bytes 1769480 | tf_op jit(solution)/shard_map/ppermute | solution.py:28
  113.5 13.1 %collective-permute-start.16 = (bf16[96,3072]{1,0:T(8,128)(2,1)}, bf16[96,3072]{1,0:T(8,128)(2,1)}, u32[]{:S(2)}, u32[]{:S(2)}) collective-permute-start(bf16[96,3072]{1,0:T(8,128)(2,1)} %collective-permute-done.12.refs_14_.refs_0_), channel_id=1, source_target_pairs={{48,0},{0,16},{16,32},{32,48},{49,1},{1,17},{17,33},{33,49},{50,2}... | collective-permute-start | bytes 1769480 | tf_op jit(solution)/shard_map/ppermute | solution.py:28
  113.5 15.0 %collective-permute-start.10 = (bf16[4,8,3072]{2,1,0:T(8,128)(2,1)}, bf16[4,8,3072]{2,1,0:T(8,128)(2,1)}, u32[]{:S(2)}, u32[]{:S(2)}) collective-permute-start(bf16[4,8,3072]{2,1,0:T(8,128)(2,1)} %all-to-all-done.4), channel_id=1, source_target_pairs={{0,32},{32,0},{1,33},{33,1},{2,34},{34,2},{3,35},{35,3},{4,36},{36... | collective-permute-start | bytes 589832 | tf_op jit(solution)/shard_map/ppermute | solution.py:227
  134.5 30.6 %copy-start.4 = (bf16[8,3200]{1,0:T(8,128)(2,1)S(1)}, bf16[8,3200]{1,0:T(8,128)(2,1)}, u32[]{:S(2)}) copy-start(bf16[8,3200]{1,0:T(8,128)(2,1)} %get-tuple-element.114) | copy-start | bytes 153604
  156.1 9.0 %collective-permute-start.19 = (bf16[8,3200]{1,0:T(8,128)(2,1)S(1)}, bf16[8,3200]{1,0:T(8,128)(2,1)S(1)}, u32[]{:S(2)}, u32[]{:S(2)}) collective-permute-start(bf16[8,3200]{1,0:T(8,128)(2,1)S(1)} %shard_map.107), channel_id=1, source_target_pairs={{0,64},{2,66},{64,130},{66,128},{128,192},{130,194},{192,0},{194,2... | collective-permute-start | bytes 153608 | tf_op jit(solution)/shard_map/ppermute | solution.py:35
  182.6 27.3 %copy-start.3 = (bf16[8,3200]{1,0:T(8,128)(2,1)S(1)}, bf16[8,3200]{1,0:T(8,128)(2,1)}, u32[]{:S(2)}) copy-start(bf16[8,3200]{1,0:T(8,128)(2,1)} %get-tuple-element.113) | copy-start | bytes 153604
  195.4 14.5 %collective-permute-start.20 = (bf16[8,3200]{1,0:T(8,128)(2,1)S(1)}, bf16[8,3200]{1,0:T(8,128)(2,1)S(1)}, u32[]{:S(2)}, u32[]{:S(2)}) collective-permute-start(bf16[8,3200]{1,0:T(8,128)(2,1)S(1)} %shard_map.109), channel_id=1, source_target_pairs={{0,64},{2,66},{64,130},{66,128},{128,192},{130,194},{192,0},{194,2... | collective-permute-start | bytes 153608 | tf_op jit(solution)/shard_map/ppermute | solution.py:35
  244.9 5.9 %collective-permute-start.21 = (bf16[8,3200]{1,0:T(8,128)(2,1)S(1)}, bf16[8,3200]{1,0:T(8,128)(2,1)S(1)}, u32[]{:S(2)}, u32[]{:S(2)}) collective-permute-start(bf16[8,3200]{1,0:T(8,128)(2,1)S(1)} %shard_map.111), channel_id=1, source_target_pairs={{0,64},{2,66},{64,130},{66,128},{128,192},{130,194},{1,65},{3,67},... | collective-permute-start | bytes 153608 | tf_op jit(solution)/shard_map/ppermute | solution.py:35
  272.0 21.1 %copy-start.5 = (bf16[8,3200]{1,0:T(8,128)(2,1)S(1)}, bf16[8,3200]{1,0:T(8,128)(2,1)}, u32[]{:S(2)}) copy-start(bf16[8,3200]{1,0:T(8,128)(2,1)} %get-tuple-element.117) | copy-start | bytes 153604
  286.2 6.9 %collective-permute-start.24 = (bf16[8,3200]{1,0:T(8,128)(2,1)S(1)}, bf16[8,3200]{1,0:T(8,128)(2,1)S(1)}, u32[]{:S(2)}, u32[]{:S(2)}) collective-permute-start(bf16[8,3200]{1,0:T(8,128)(2,1)S(1)} %shard_map.113), channel_id=1, source_target_pairs={{0,64},{2,66},{64,128},{66,130},{128,194},{130,192},{1,65},{3,67},... | collective-permute-start | bytes 153608 | tf_op jit(solution)/shard_map/ppermute | solution.py:35
  291.1 3.1 %collective-permute-start.23 = (bf16[8,3200]{1,0:T(8,128)(2,1)S(1)}, bf16[8,3200]{1,0:T(8,128)(2,1)S(1)}, u32[]{:S(2)}, u32[]{:S(2)}) collective-permute-start(bf16[8,3200]{1,0:T(8,128)(2,1)S(1)} %broadcast_select_fusion), channel_id=1, source_target_pairs={{0,64},{2,66},{192,194},{194,192},{1,65},{3,67},{193,195},{195,193... | collective-permute-start | bytes 153608 | tf_op jit(solution)/shard_map/ppermute | solution.py:35
  292.4 1.8 collective-permute-start.22

commit v8 on v7

--- a/solution.py
+++ b/solution.py
@@ -269,10 +269,10 @@
         travelling_inputs[0],
         arriving,
     )
-    is_third = section_id == 2
+    is_even = section_id % 2 == 0
     entering = [entering[section] for section in range(SECTIONS)]
-    gathered, waiting, gate, entering, is_first, is_third = lax.optimization_barrier(
-        (gathered, waiting, mod[2:], entering, is_first, is_third)
+    gathered, waiting, gate, entering, is_first, is_even = lax.optimization_barrier(
+        (gathered, waiting, mod[2:], entering, is_first, is_even)
     )
     moves = []
     for tick in range(SECTIONS):
@@ -281,19 +281,21 @@
         partial = layer(gathered.reshape(GROUP_SIZE * tokens, breadth), mod, *weights)
         parts = lax.all_to_all(partial.reshape(GROUP_SIZE, tokens, breadth), GROUP, 0, 0)
         if tick == last:
-            third = between_sections(after(produced, parts), [(last, 2, 1)])
+            produced, held = after((produced, moves[0]), parts)
+            third = jnp.where(is_first, held, produced)
+            third = between_sections(third, [(last, 2, 1), (0, 0, 1)])
         produced = close(parts, waiting, gate)
         if tick < last:
             edges = [(0, 1, 0), (1, 2, 1), (2, 3, 0)]
             if tick < 2:
-                edges.append((last, 0, 0))
+                edges.append((last, 0, 1))
         else:
             edges = [(0, 1, 0), (1, 2, 0), (2, 3, 1)]
         moves.append(between_sections(produced, edges))
         waiting = jnp.where(is_first, entering[tick], moves[tick])
     sent = jnp.where(is_first, moves[1], produced)
-    second = between_sections(sent, [(0, 1, 0), (last, last, 1)])
-    done = jnp.where(is_first, moves[0], jnp.where(is_third, third, second))
+    second = between_sections(sent, [(0, 1, 1), (last, last, 1)])
+    done = jnp.where(is_even, third, second)
     return done[None, :, :breadth], waiting[None, :, :breadth]
 
 

time: 296 us -> 301 us (1.017)
  blocking collectives: 120 us -> 124 us
  starting transfers between devices: 83.4 us -> 80.2 us
    all_to_all x4, blocking collectives: 56.6 us -> 60.1 us  [exchange(): return lax.all_to_all(copies, axes, 0, 0)]
    ppermute x6, starting transfers between devices: 29.8 us -> 26.6 us  [between_sections(): return lax.ppermute(block, SECTION + ('zc',), route)]
where the time goes in v8:
time: 301 us; the launch traced here: 298 us
  blocking collectives  124 us (41%)
  starting transfers between devices  80.2 us (27%)
  waiting for transfers between devices  41.6 us (14%)
  Pallas kernels  27.2 us (9%)
  local copies, waits for them, and re-layouts  14.8 us (5%)
  other arithmetic  6.6 us (2%)
    all_to_all x4, blocking collectives, per_device(): lax.all_to_all(partial.reshape(GROUP_SIZE, tokens, breadth), GROUP, 0, 0)  64.3 us
    all_to_all x4, blocking collectives, exchange(): return lax.all_to_all(copies, axes, 0, 0)  60.1 us
    all_to_all x5, starting transfers between devices, exchange(): return lax.all_to_all(copies, axes, 0, 0)  31.9 us
    ppermute x6, starting transfers between devices, between_sections(): return lax.ppermute(block, SECTION + ('zc',), route)  26.6 us
    ppermute x18, starting transfers between devices, from_neighbour(): return lax.ppermute(block, (axis + 'h', axis + 'l'), route)  20 us
    all_to_all x5, waiting for transfers between devices, exchange(): return lax.all_to_all(copies, axes, 0, 0)  19.8 us
    pallas_call x4, Pallas kernels, layer(): pl.pallas_call(layer_kernel, out_shape=jax.ShapeDtypeStruct((rows, breadt...  19.8 us
    ppermute x18, waiting for transfers between devices, from_neighbour(): return lax.ppermute(block, (axis + 'h', axis + 'l'), route)  13 us
  transfers between devices with their start and end apart: 30, of which 12 were waited for; matrix products, arithmetic and copies ran while one was open for 5% of the time, Pallas kernels for 2%

profile of v8, /device:TPU:1, one launch (start us, length us, event | category | flops | bytes accessed | tf_op | source)
XLA Modules:
  0.0 297.7 jit_solution(6889840342224509659)
XLA Ops:
  0.7 1.5 slice_bitcast_fusion
  3.3 1.6 pad_maximum_fusion
  4.9 3.6 %collective-permute-start = (bf16[192,3072]{1,0:T(8,128)(2,1)}, bf16[192,3072]{1,0:T(8,128)(2,1)S(1)}, u32[]{:S(2)}, u32[]{:S(2)}) collective-permute-start(bf16[192,3072]{1,0:T(8,128)(2,1)} %get-tuple-element.94.refs_0_), channel_id=1, source_target_pairs={{4,0},{8,4},{12,8},{0,12},{5,1},{9,5},{13,9},{1,13},{6,2},{10,6},{... | collective-permute-start | bytes 3538952 | tf_op jit(solution)/shard_map/ppermute | solution.py:28
  8.5 2.5 collective-permute-start.2
  11.7 9.7 %all-to-all-start = ((f32[16,28,128]{2,1,0:T(8,128)}), f32[16,28,128]{2,1,0:T(8,128)}, u32[]{:S(2)}, u32[]{:S(2)}) async-start(f32[16,28,128]{2,1,0:T(8,128)} %broadcast_in_dim.28), calls=%async_computation | async-start | bytes 524288 | tf_op jit(solution)/shard_map/all_to_all | solution.py:45
  21.5 9.6 %all-to-all-done = f32[16,28,128]{2,1,0:T(8,128)} async-done(((f32[16,28,128]{2,1,0:T(8,128)}), f32[16,28,128]{2,1,0:T(8,128)}, u32[]{:S(2)}, u32[]{:S(2)}) %all-to-all-start) | async-done | bytes 229408 | tf_op jit(solution)/shard_map/all_to_all | solution.py:45
  32.1 13.4 %all_to_all.65 = bf16[4,8,3200]{2,1,0:T(8,128)(2,1)} all-to-all(bf16[4,8,3200]{2,1,0:T(8,128)(2,1)S(1)} %broadcast_in_dim.30), channel_id=1, replica_groups=mesh['zh'=2,'core'=2,'xh'=2,'xl'=2,'yh'=2,'yl'=2,'zc'=2,'zf'=2] {'zh','c..., dimensions={0} | all-to-all | bytes 409600 | tf_op jit(solution)/shard_map/all_to_all | solution.py:45
  46.3 7.1 %all-to-all-start.2 = ((f32[16,28,128]{2,1,0:T(8,128)}), f32[16,28,128]{2,1,0:T(8,128)}, u32[]{:S(2)}, u32[]{:S(2)}) async-start(f32[16,28,128]{2,1,0:T(8,128)} %broadcast_in_dim.31), calls=%async_computation.2 | async-start | bytes 524288 | tf_op jit(solution)/shard_map/all_to_all | solution.py:45
  53.3 2.5 collective-permute-start.4
  55.9 2.4 collective-permute-start.6
  58.3 2.5 all-to-all-done.2
  64.0 6.0 %all-to-all-start.3 = ((f32[4,2,128]{2,1,0:T(2,128)}), f32[4,2,128]{2,1,0:T(2,128)S(1)}, u32[]{:S(2)}, u32[]{:S(2)}) async-start(f32[4,2,128]{2,1,0:T(2,128)} %broadcast_in_dim.33), calls=%async_computation.3 | async-start | bytes 8192 | tf_op jit(solution)/shard_map/all_to_all | solution.py:45
  71.2 3.4 %all-to-all-done.3 = f32[4,2,128]{2,1,0:T(2,128)S(1)} async-done(((f32[4,2,128]{2,1,0:T(2,128)}), f32[4,2,128]{2,1,0:T(2,128)S(1)}, u32[]{:S(2)}, u32[]{:S(2)}) %all-to-all-start.3) | async-done | bytes 4128 | tf_op jit(solution)/shard_map/all_to_all | solution.py:45
  75.3 4.0 %all-to-all-start.4 = ((bf16[4,8,3072]{2,1,0:T(8,128)(2,1)}), bf16[4,8,3072]{2,1,0:T(8,128)(2,1)}, u32[]{:S(2)}, u32[]{:S(2)}) async-start(bf16[4,8,3072]{2,1,0:T(8,128)(2,1)} %broadcast_in_dim.34), calls=%async_computation.4 | async-start | bytes 393216 | tf_op jit(solution)/shard_map/all_to_all | solution.py:45
  80.5 4.3 %all-to-all-done.4 = bf16[4,8,3072]{2,1,0:T(8,128)(2,1)} async-done(((bf16[4,8,3072]{2,1,0:T(8,128)(2,1)}), bf16[4,8,3072]{2,1,0:T(8,128)(2,1)}, u32[]{:S(2)}, u32[]{:S(2)}) %all-to-all-start.4) | async-done | bytes 196640 | tf_op jit(solution)/shard_map/all_to_all | solution.py:45
  84.8 1.3 collective-permute-start.11
  86.3 1.3 collective-permute-start.8
  87.8 8.2 %collective-permute-done.11.refs_12_ = bf16[96,3072]{1,0:T(8,128)(2,1)} collective-permute-done((bf16[96,3072]{1,0:T(8,128)(2,1)}, bf16[96,3072]{1,0:T(8,128)(2,1)}, u32[]{:S(2)}, u32[]{:S(2)}) %collective-permute-start.11) | collective-permute-done | bytes 589856 | tf_op jit(solution)/shard_map/ppermute | solution.py:28
  96.0 1.3 collective-permute-done.12.refs_14_.refs_0_
  99.5 5.1 %all-to-all-start.5 = ((f32[16,4,2,128]{3,2,1,0:T(2,128)}), f32[16,4,2,128]{3,2,1,0:T(2,128)}, u32[]{:S(2)}, u32[]{:S(2)}) async-start(f32[16,4,2,128]{3,2,1,0:T(2,128)} %broadcast_in_dim.36), calls=%async_computation.5 | async-start | bytes 131072 | tf_op jit(solution)/shard_map/all_to_all | solution.py:45
  104.6 2.0 slice.93
  106.6 2.5 collective-permute-start.17
  109.1 1.9 slice.94
  111.5 2.0 collective-permute-start.15
  113.5 1.8 collective-permute-start.10
  115.9 1.5 copy.19
  118.4 5.1 %shard_map.104 = (bf16[1280,3072]{1,0:T(8,128)(2,1)S(1)}, bf16[1280,3072]{1,0:T(8,128)(2,1)S(1)}) custom-call(bf16[192,3072]{1,0:T(8,128)(2,1)} %get-tuple-element.94.refs_0_, bf16[192,3072]{1,0:T(8,128)(2,1)} %get-tuple-element.95.refs_1_, bf16[192,3072]{1,0:T(8,128)(2,1)} %collective-permute-done.2.refs_2_, ...), custom_call_target="tpu_custom_call" | custom-call | bytes 31457280 | tf_op jit(solution)/shard_map/pallas_call | solution.py:118
  123.6 3.0 %collective-permute-done.16.refs_3_ = bf16[96,3072]{1,0:T(8,128)(2,1)} collective-permute-done((bf16[96,3072]{1,0:T(8,128)(2,1)}, bf16[96,3072]{1,0:T(8,128)(2,1)}, u32[]{:S(2)}, u32[]{:S(2)}) %collective-permute-start.16) | collective-permute-done | bytes 589856 | tf_op jit(solution)/shard_map/ppermute | solution.py:28
  126.6 1.9 shard_map.105
  129.6 4.9 %shard_map.106 = bf16[64,3072]{1,0:T(8,128)(2,1)S(1)} custom-call(bf16[64,3072]{1,0:T(8,128)(2,1)S(1)} %bitcast.69, f32[3,3072]{1,0:T(4,128)S(1)} %reshape.75.mod_ref, bf16[1280,3072]{1,0:T(8,128)(2,1)S(1)} %get-tuple-element.110.up, bf16[1280,3072]{1,0:T(8,128)(2,1)S(1)} %get-tuple-element.111.down, bf16[256,3072]{1,0:T(8,128)(2,1)S(1)} %get-tuple-element.112.up_end, ...), custom_call_target="tpu_custom_call" | custom-call | flops 1207959552 | bytes 19660800 | tf_op jit(solution)/shard_map/pallas_call | solution.py:79
  134.5 21.5 %all_to_all.66.parts_ref = bf16[8,8,3072]{2,1,0:T(8,128)(2,1)S(1)} all-to-all(bf16[8,8,3072]{2,1,0:T(8,128)(2,1)S(1)} %bitcast.70), channel_id=1, replica_groups=mesh['zh'=2,'core'=2,'xh'=2,'xl'=2,'yh'=2,'yl'=2,'zc'=2,'zf'=2] {'xh','z..., dimensions={0} | all-to-all | bytes 786432 | tf_op jit(solution)/shard_map/all_to_all | solution.py:282
  156.1 6.5 %collective-permute-start.19 = (bf16[8,3200]{1,0:T(8,128)(2,1)S(1)}, bf16[8,3200]{1,0:T(8,128)(2,1)S(1)}, u32[]{:S(2)}, u32[]{:S(2)}) collective-permute-start(bf16[8,3200]{1,0:T(8,128)(2,1)S(1)} %shard_map.107), channel_id=1, source_target_pairs={{0,64},{2,66},{64,130},{66,128},{128,192},{130,194},{192,2},{194,0... | collective-permute-start | bytes 153608 | tf_op jit(solution)/shard_map/ppermute | solution.py:35
  162.6 2.5 collective-permute-done.19
  165.1 12.6 %all_to_all.67 = bf16[8,8,3072]{2,1,0:T(8,128)(2,1)S(1)} all-to-all(bf16[8,8,3072]{2,1,0:T(8,128)(2,1)S(1)} %broadcast_in_dim.37), channel_id=1, replica_groups=mesh['zh'=2,'core'=2,'xh'=2,'xl'=2,'yh'=2,'yl'=2,'zc'=2,'zf'=2] {'xh','z..., dimensions={0} | all-to-all | bytes 786432 | tf_op jit(solution)/shard_map/all_to_all | solution.py:45
  177.8 4.9 %shard_map.108 = bf16[64,3072]{1,0:T(8,128)(2,1)S(1)} custom-call(bf16[64,3072]{1,0:T(8,128)(2,1)S(1)} %bitcast.71, f32[3,3072]{1,0:T(4,128)S(1)} %reshape.75.mod_ref, bf16[1280,3072]{1,0:T(8,128)(2,1)S(1)} %get-tuple-element.110.up, bf16[1280,3072]{1,0:T(8,128)(2,1)S(1)} %get-tuple-element.111.down, bf16[256,3072]{1,0:T(8,128)(2,1)S(1)} %get-tuple-element.112.up_end, ...), custom_call_target="tpu_custom_call" | custom-call | flops 1207959552 | bytes 19660800 | tf_op jit(solution)/shard_map/pallas_call | solution.py:79
  182.7 12.7 %all_to_all.68.parts_ref = bf16[8,8,3072]{2,1,0:T(8,128)(2,1)S(1)} all-to-all(bf16[8,8,3072]{2,1,0:T(8,128)(2,1)S(1)} %bitcast.72), channel_id=1, replica_groups=mesh['zh'=2,'core'=2,'xh'=2,'xl'=2,'yh'=2,'yl'=2,'zc'=2,'zf'=2] {'xh','z..., dimensions={0} | all-to-all | bytes 786432 | tf_op jit(solution)/shard_map/all_to_all | solution.py:282
  195.5 11.1 %collective-permute-start.20 = (bf16[8,3200]{1,0:T(8,128)(2,1)S(1)}, bf16[8,3200]{1,0:T(8,128)(2,1)S(1)}, u32[]{:S(2)}, u32[]{:S(2)}) collective-permute-start(bf16[8,3200]{1,0:T(8,128)(2,1)S(1)} %shard_map.109), channel_id=1, source_target_pairs={{0,64},{2,66},{64,130},{66,128},{128,192},{130,194},{192,2},{194,0... | collective-permute-start | bytes 153608 | tf_op jit(solution)/shard_map/ppermute | solution.py:35
  207.8 17.8 %all_to_all.69 = bf16[8,8,3072]{2,1,0:T(8,128)(2,1)S(1)} all-to-all(bf16[8,8,3072]{2,1,0:T(8,128)(2,1)S(1)} %broadcast_in_dim.38), channel_id=1, replica_groups=mesh['zh'=2,'core'=2,'xh'=2,'xl'=2,'yh'=2,'yl'=2,'zc'=2,'zf'=2] {'xh','z..., dimensions={0} | all-to-all | bytes 786432 | tf_op jit(solution)/shard_map/all_to_all | solution.py:45
  225.7 4.9 %shard_map.110 = bf16[64,3072]{1,0:T(8,128)(2,1)S(1)} custom-call(bf16[64,3072]{1,0:T(8,128)(2,1)S(1)} %bitcast.73, f32[3,3072]{1,0:T(4,128)S(1)} %reshape.75.mod_ref, bf16[1280,3072]{1,0:T(8,128)(2,1)S(1)} %get-tuple-element.110.up, bf16[1280,3072]{1,0:T(8,128)(2,1)S(1)} %get-tuple-element.111.down, bf16[256,3072]{1,0:T(8,128)(2,1)S(1)} %get-tuple-element.112.up_end, ...), custom_call_target="tpu_custom_call" | custom-call | flops 1207959552 | bytes 19660800 | tf_op jit(solution)/shard_map/pallas_call | solution.py:79
  230.6 16.1 %all_to_all.70.parts_ref = bf16[8,8,3072]{2,1,0:T(8,128)(2,1)S(1)} all-to-all(bf16[8,8,3072]{2,1,0:T(8,128)(2,1)S(1)} %bitcast.74), channel_id=1, replica_groups=mesh['zh'=2,'core'=2,'xh'=2,'xl'=2,'yh'=2,'yl'=2,'zc'=2,'zf'=2] {'xh','z..., dimensions={0} | all-to-all | bytes 786432 | tf_op jit(solution)/shard_map/all_to_all | solution.py:282
  246.8 1.9 collective-permute-start.21
  248.7 1.4 collective-permute-done.21
  250.2 16.3 %all_to_all.71 = bf16[8,8,3072]{2,1,0:T(8,128)(2,1)S(1)} all-to-all(bf16[8,8,3072]{2,1,0:T(8,128)(2,1)S(1)} %broadcast_in_dim.39), channel_id=1, replica_groups=mesh['zh'=2,'core'=2,'xh'=2,'xl'=2,'yh'=2,'yl'=2,'zc'=2,'zf'=2] {'xh','z..., dimensions={0} | all-to-all | bytes 786432 | tf_op jit(solution)/shard_map/all_to_all | solution.py:45
  266.5 4.9 %shard_map.112 = bf16[64,3072]{1,0:T(8,128)(2,1)S(1)} custom-call(bf16[64,3072]{1,0:T(8,128)(2,1)S(1)} %bitcast.67, f32[3,3072]{1,0:T(4,128)S(1)} %reshape.75.mod_ref, bf16[1280,3072]{1,0:T(8,128)(2,1)S(1)} %get-tuple-element.110.up, bf16[1280,3072]{1,0:T(8,128)(2,1)S(1)} %get-tuple-element.111.down, bf16[256,3072]{1,0:T(8,128)(2,1)S(1)} %get-tuple-element.112.up_end, ...), custom_call_target="tpu_custom_call" | custom-call | flops 1207959552 | bytes 19660800 | tf_op jit(solution)/shard_map/pallas_call | solution.py:79
  271.4 14.1 %all_to_all.72.parts_ref = bf16[8,8,3072]{2,1,0:T(8,128)(2,1)S(1)} all-to-all(bf16[8,8,3072]{2,1,0:T(8,128)(2,1)S(1)} %bitcast.68), channel_id=1, replica_groups=mesh['zh'=2,'core'=2,'xh'=2,'xl'=2,'yh'=2,'yl'=2,'zc'=2,'zf'=2] {'xh','z..., dimensions={0} | all-to-all | bytes 786432 | tf_op jit(solution)/shard_map/all_to_all | solution.py:282
  285.6 5.1 %collective-permute-start.24 = (bf16[8,3200]{1,0:T(8,128)(2,1)S(1)}, bf16[8,3200]{1,0:T(8,128)(2,1)S(1)}, u32[]{:S(2)}, u32[]{:S(2)}) collective-permute-start(bf16[8,3200]{1,0:T(8,128)(2,1)S(1)} %shard_map.113), channel_id=1, source_target_pairs={{0,64},{2,66},{64,128},{66,130},{128,194},{130,192},{1,65},{3,67},... | collective-permute-start | bytes 153608 | tf_op jit(solution)/shard_map/ppermute | solution.py:35
  290.8 1.3 collective-permute-start.23
  293.4 3.7 %collective-permute-done.23 = bf16[8,3200]{1,0:T(8,128)(2,1)S(1)} collective-permute-done((bf16[8,3200]{1,0:T(8,128)(2,1)S(1)}, bf16[8,3200]{1,0:T(8,128)(2,1)S(1)}, u32[]{:S(2)}, u32[]{:S(2)}) %collective-permute-start.23) | collective-permute-done | bytes 51232 | tf_op jit(solution)/shard_map/ppermute | solution.py:35
  (99 shorter events, 18.1 us)
Async XLA Ops:
  0.6 62.4 %copy-start = (bf16[1,144,3584]{2,1,0:T(8,128)(2,1)S(1)}, bf16[1,144,3584]{2,1,0:T(8,128)(2,1)}, u32[]{:S(2)}) copy-start(bf16[1,144,3584]{2,1,0:T(8,128)(2,1)} %param.15) | copy-start | bytes 3096580
  0.6 1.7 copy-start.1
  2.4 0.8 copy-start.7
  3.3 18.1 %copy-start.9 = (s32[1,8]{1,0:T(1,128)S(1)}, s32[1,8]{1,0:T(1,128)}, u32[]{:S(2)}) copy-start(s32[1,8]{1,0:T(1,128)} %param.12) | copy-start | bytes 100
  3.3 18.2 %copy-start.8 = (bf16[1,8,3072]{2,1,0:T(8,128)(2,1)S(1)}, bf16[1,8,3072]{2,1,0:T(8,128)(2,1)}, u32[]{:S(2)}) copy-start(bf16[1,8,3072]{2,1,0:T(8,128)(2,1)} %param.11) | copy-start | bytes 147460
  4.9 40.6 %collective-permute-start = (bf16[192,3072]{1,0:T(8,128)(2,1)}, bf16[192,3072]{1,0:T(8,128)(2,1)S(1)}, u32[]{:S(2)}, u32[]{:S(2)}) collective-permute-start(bf16[192,3072]{1,0:T(8,128)(2,1)} %get-tuple-element.94.refs_0_), channel_id=1, source_target_pairs={{4,0},{8,4},{12,8},{0,12},{5,1},{9,5},{13,9},{1,13},{6,2},{10,6},{... | collective-permute-start | bytes 3538952 | tf_op jit(solution)/shard_map/ppermute | solution.py:28
  8.5 37.0 %collective-permute-start.1 = (bf16[192,3072]{1,0:T(8,128)(2,1)}, bf16[192,3072]{1,0:T(8,128)(2,1)S(1)}, u32[]{:S(2)}, u32[]{:S(2)}) collective-permute-start(bf16[192,3072]{1,0:T(8,128)(2,1)} %get-tuple-element.95.refs_1_), channel_id=1, source_target_pairs={{12,0},{0,4},{4,8},{8,12},{13,1},{1,5},{5,9},{9,13},{14,2},{2,6},{... | collective-permute-start | bytes 3538952 | tf_op jit(solution)/shard_map/ppermute | solution.py:28
  8.5 37.0 %collective-permute-start.2 = (bf16[192,3072]{1,0:T(8,128)(2,1)}, bf16[192,3072]{1,0:T(8,128)(2,1)}, u32[]{:S(2)}, u32[]{:S(2)}) collective-permute-start(bf16[192,3072]{1,0:T(8,128)(2,1)} %get-tuple-element.94.refs_0_), channel_id=1, source_target_pairs={{16,0},{32,16},{48,32},{0,48},{17,1},{33,17},{49,33},{1,49},{18,2}... | collective-permute-start | bytes 3538952 | tf_op jit(solution)/shard_map/ppermute | solution.py:28
  11.0 34.5 %collective-permute-start.3 = (bf16[192,3072]{1,0:T(8,128)(2,1)}, bf16[192,3072]{1,0:T(8,128)(2,1)}, u32[]{:S(2)}, u32[]{:S(2)}) collective-permute-start(bf16[192,3072]{1,0:T(8,128)(2,1)} %get-tuple-element.95.refs_1_), channel_id=1, source_target_pairs={{48,0},{0,16},{16,32},{32,48},{49,1},{1,17},{17,33},{33,49},{50,2}... | collective-permute-start | bytes 3538952 | tf_op jit(solution)/shard_map/ppermute | solution.py:28
  11.7 19.4 %all-to-all-start = ((f32[16,28,128]{2,1,0:T(8,128)}), f32[16,28,128]{2,1,0:T(8,128)}, u32[]{:S(2)}, u32[]{:S(2)}) async-start(f32[16,28,128]{2,1,0:T(8,128)} %broadcast_in_dim.28), calls=%async_computation | async-start | bytes 524288 | tf_op jit(solution)/shard_map/all_to_all | solution.py:45
  46.3 14.5 %all-to-all-start.2 = ((f32[16,28,128]{2,1,0:T(8,128)}), f32[16,28,128]{2,1,0:T(8,128)}, u32[]{:S(2)}, u32[]{:S(2)}) async-start(f32[16,28,128]{2,1,0:T(8,128)} %broadcast_in_dim.31), calls=%async_computation.2 | async-start | bytes 524288 | tf_op jit(solution)/shard_map/all_to_all | solution.py:45
  53.3 31.5 %collective-permute-start.4 = (bf16[192,3072]{1,0:T(8,128)(2,1)}, bf16[192,3072]{1,0:T(8,128)(2,1)}, u32[]{:S(2)}, u32[]{:S(2)}) collective-permute-start(bf16[192,3072]{1,0:T(8,128)(2,1)} %get-tuple-element.95.refs_1_), channel_id=1, source_target_pairs={{4,0},{8,4},{12,8},{0,12},{5,1},{9,5},{13,9},{1,13},{6,2},{10,6},{... | collective-permute-start | bytes 3538952 | tf_op jit(solution)/shard_map/ppermute | solution.py:28
  55.9 28.9 %collective-permute-start.5 = (bf16[192,3072]{1,0:T(8,128)(2,1)}, bf16[192,3072]{1,0:T(8,128)(2,1)}, u32[]{:S(2)}, u32[]{:S(2)}) collective-permute-start(bf16[192,3072]{1,0:T(8,128)(2,1)} %get-tuple-element.94.refs_0_), channel_id=1, source_target_pairs={{12,0},{0,4},{4,8},{8,12},{13,1},{1,5},{5,9},{9,13},{14,2},{2,6},{... | collective-permute-start | bytes 3538952 | tf_op jit(solution)/shard_map/ppermute | solution.py:28
  55.9 28.9 %collective-permute-start.6 = (bf16[192,3072]{1,0:T(8,128)(2,1)S(1)}, bf16[192,3072]{1,0:T(8,128)(2,1)}, u32[]{:S(2)}, u32[]{:S(2)}) collective-permute-start(bf16[192,3072]{1,0:T(8,128)(2,1)S(1)} %collective-permute-done.refs_4_), channel_id=1, source_target_pairs={{16,0},{32,16},{48,32},{0,48},{17,1},{33,17},{49,33},{1,49},{18,2}... | collective-permute-start | bytes 3538952 | tf_op jit(solution)/shard_map/ppermute | solution.py:28
  58.3 26.5 %collective-permute-start.7 = (bf16[192,3072]{1,0:T(8,128)(2,1)S(1)}, bf16[192,3072]{1,0:T(8,128)(2,1)}, u32[]{:S(2)}, u32[]{:S(2)}) collective-permute-start(bf16[192,3072]{1,0:T(8,128)(2,1)S(1)} %collective-permute-done.1.refs_5_), channel_id=1, source_target_pairs={{48,0},{0,16},{16,32},{32,48},{49,1},{1,17},{17,33},{33,49},{50,2}... | collective-permute-start | bytes 3538952 | tf_op jit(solution)/shard_map/ppermute | solution.py:28
  64.0 10.6 %all-to-all-start.3 = ((f32[4,2,128]{2,1,0:T(2,128)}), f32[4,2,128]{2,1,0:T(2,128)S(1)}, u32[]{:S(2)}, u32[]{:S(2)}) async-start(f32[4,2,128]{2,1,0:T(2,128)} %broadcast_in_dim.33), calls=%async_computation.3 | async-start | bytes 8192 | tf_op jit(solution)/shard_map/all_to_all | solution.py:45
  70.1 4.5 %copy-start.6 = (bf16[1,8,3072]{2,1,0:T(8,128)(2,1)S(1)}, bf16[1,8,3072]{2,1,0:T(8,128)(2,1)}, u32[]{:S(2)}) copy-start(bf16[1,8,3072]{2,1,0:T(8,128)(2,1)} %param.9) | copy-start | bytes 147460
  75.3 9.4 %all-to-all-start.4 = ((bf16[4,8,3072]{2,1,0:T(8,128)(2,1)}), bf16[4,8,3072]{2,1,0:T(8,128)(2,1)}, u32[]{:S(2)}, u32[]{:S(2)}) async-start(bf16[4,8,3072]{2,1,0:T(8,128)(2,1)} %broadcast_in_dim.34), calls=%async_computation.4 | async-start | bytes 393216 | tf_op jit(solution)/shard_map/all_to_all | solution.py:45
  79.3 19.4 %copy-start.10 = (s32[1,8]{1,0:T(1,128)S(1)}, s32[1,8]{1,0:T(1,128)}, u32[]{:S(2)}) copy-start(s32[1,8]{1,0:T(1,128)} %param.10) | copy-start | bytes 100
  84.8 11.2 %collective-permute-start.11 = (bf16[96,3072]{1,0:T(8,128)(2,1)}, bf16[96,3072]{1,0:T(8,128)(2,1)}, u32[]{:S(2)}, u32[]{:S(2)}) collective-permute-start(bf16[96,3072]{1,0:T(8,128)(2,1)} %get-tuple-element.86), channel_id=1, source_target_pairs={{4,0},{8,4},{12,8},{0,12},{5,1},{9,5},{13,9},{1,13},{6,2},{10,6},{... | collective-permute-start | bytes 1769480 | tf_op jit(solution)/shard_map/ppermute | solution.py:28
  86.1 11.2 %collective-permute-start.12 = (bf16[96,3072]{1,0:T(8,128)(2,1)}, bf16[96,3072]{1,0:T(8,128)(2,1)}, u32[]{:S(2)}, u32[]{:S(2)}) collective-permute-start(bf16[96,3072]{1,0:T(8,128)(2,1)} %get-tuple-element.88), channel_id=1, source_target_pairs={{12,0},{0,4},{4,8},{8,12},{13,1},{1,5},{5,9},{9,13},{14,2},{2,6},{... | collective-permute-start | bytes 1769480 | tf_op jit(solution)/shard_map/ppermute | solution.py:28
  86.3 24.7 %collective-permute-start.8 = (bf16[192,3072]{1,0:T(8,128)(2,1)}, bf16[192,3072]{1,0:T(8,128)(2,1)}, u32[]{:S(2)}, u32[]{:S(2)}) collective-permute-start(bf16[192,3072]{1,0:T(8,128)(2,1)} %collective-permute-done.5.refs_7_), channel_id=1, source_target_pairs={{16,0},{32,16},{48,32},{0,48},{17,1},{33,17},{49,33},{1,49},{18,2}... | collective-permute-start | bytes 3538952 | tf_op jit(solution)/shard_map/ppermute | solution.py:28
  87.7 23.8 %collective-permute-start.9 = (bf16[192,3072]{1,0:T(8,128)(2,1)}, bf16[192,3072]{1,0:T(8,128)(2,1)}, u32[]{:S(2)}, u32[]{:S(2)}) collective-permute-start(bf16[192,3072]{1,0:T(8,128)(2,1)} %collective-permute-done.4.refs_6_), channel_id=1, source_target_pairs={{48,0},{0,16},{16,32},{32,48},{49,1},{1,17},{17,33},{33,49},{50,2}... | collective-permute-start | bytes 3538952 | tf_op jit(solution)/shard_map/ppermute | solution.py:28
  97.3 16.2 %collective-permute-start.13 = (bf16[96,3072]{1,0:T(8,128)(2,1)}, bf16[96,3072]{1,0:T(8,128)(2,1)}, u32[]{:S(2)}, u32[]{:S(2)}) collective-permute-start(bf16[96,3072]{1,0:T(8,128)(2,1)} %get-tuple-element.91), channel_id=1, source_target_pairs={{4,0},{8,4},{12,8},{0,12},{5,1},{9,5},{13,9},{1,13},{6,2},{10,6},{... | collective-permute-start | bytes 1769480 | tf_op jit(solution)/shard_map/ppermute | solution.py:28
  97.7 15.8 %collective-permute-start.14 = (bf16[96,3072]{1,0:T(8,128)(2,1)}, bf16[96,3072]{1,0:T(8,128)(2,1)}, u32[]{:S(2)}, u32[]{:S(2)}) collective-permute-start(bf16[96,3072]{1,0:T(8,128)(2,1)} %get-tuple-element.93), channel_id=1, source_target_pairs={{12,0},{0,4},{4,8},{8,12},{13,1},{1,5},{5,9},{9,13},{14,2},{2,6},{... | collective-permute-start | bytes 1769480 | tf_op jit(solution)/shard_map/ppermute | solution.py:28
  99.5 16.4 %all-to-all-start.5 = ((f32[16,4,2,128]{3,2,1,0:T(2,128)}), f32[16,4,2,128]{3,2,1,0:T(2,128)}, u32[]{:S(2)}, u32[]{:S(2)}) async-start(f32[16,4,2,128]{3,2,1,0:T(2,128)} %broadcast_in_dim.36), calls=%async_computation.5 | async-start | bytes 131072 | tf_op jit(solution)/shard_map/all_to_all | solution.py:45
  104.6 10.7 %copy-start.2 = (bf16[4,8,3200]{2,1,0:T(8,128)(2,1)S(1)}, bf16[4,8,3200]{2,1,0:T(8,128)(2,1)}, u32[]{:S(2)}) copy-start(bf16[4,8,3200]{2,1,0:T(8,128)(2,1)} %all_to_all.65) | copy-start | bytes 614404
  106.6 17.0 %collective-permute-start.17 = (bf16[96,3072]{1,0:T(8,128)(2,1)}, bf16[96,3072]{1,0:T(8,128)(2,1)}, u32[]{:S(2)}, u32[]{:S(2)}) collective-permute-start(bf16[96,3072]{1,0:T(8,128)(2,1)} %slice.93), channel_id=1, source_target_pairs={{4,0},{8,4},{12,8},{0,12},{5,1},{9,5},{13,9},{1,13},{6,2},{10,6},{... | collective-permute-start | bytes 1769480 | tf_op jit(solution)/shard_map/ppermute | solution.py:28
  111.0 12.5 %collective-permute-start.18 = (bf16[96,3072]{1,0:T(8,128)(2,1)}, bf16[96,3072]{1,0:T(8,128)(2,1)}, u32[]{:S(2)}, u32[]{:S(2)}) collective-permute-start(bf16[96,3072]{1,0:T(8,128)(2,1)} %slice.94), channel_id=1, source_target_pairs={{12,0},{0,4},{4,8},{8,12},{13,1},{1,5},{5,9},{9,13},{14,2},{2,6},{... | collective-permute-start | bytes 1769480 | tf_op jit(solution)/shard_map/ppermute | solution.py:28
  111.5 12.1 %collective-permute-start.15 = (bf16[96,3072]{1,0:T(8,128)(2,1)}, bf16[96,3072]{1,0:T(8,128)(2,1)}, u32[]{:S(2)}, u32[]{:S(2)}) collective-permute-start(bf16[96,3072]{1,0:T(8,128)(2,1)} %collective-permute-done.11.refs_12_), channel_id=1, source_target_pairs={{16,0},{32,16},{48,32},{0,48},{17,1},{33,17},{49,33},{1,49},{18,2}... | collective-permute-start | bytes 1769480 | tf_op jit(solution)/shard_map/ppermute | solution.py:28
  113.5 13.1 %collective-permute-start.16 = (bf16[96,3072]{1,0:T(8,128)(2,1)}, bf16[96,3072]{1,0:T(8,128)(2,1)}, u32[]{:S(2)}, u32[]{:S(2)}) collective-permute-start(bf16[96,3072]{1,0:T(8,128)(2,1)} %collective-permute-done.12.refs_14_.refs_0_), channel_id=1, source_target_pairs={{48,0},{0,16},{16,32},{32,48},{49,1},{1,17},{17,33},{33,49},{50,2}... | collective-permute-start | bytes 1769480 | tf_op jit(solution)/shard_map/ppermute | solution.py:28
  113.5 15.0 %collective-permute-start.10 = (bf16[4,8,3072]{2,1,0:T(8,128)(2,1)}, bf16[4,8,3072]{2,1,0:T(8,128)(2,1)}, u32[]{:S(2)}, u32[]{:S(2)}) collective-permute-start(bf16[4,8,3072]{2,1,0:T(8,128)(2,1)} %all-to-all-done.4), channel_id=1, source_target_pairs={{0,32},{32,0},{1,33},{33,1},{2,34},{34,2},{3,35},{35,3},{4,36},{36... | collective-permute-start | bytes 589832 | tf_op jit(solution)/shard_map/ppermute | solution.py:227
  134.5 30.6 %copy-start.4 = (bf16[8,3200]{1,0:T(8,128)(2,1)S(1)}, bf16[8,3200]{1,0:T(8,128)(2,1)}, u32[]{:S(2)}) copy-start(bf16[8,3200]{1,0:T(8,128)(2,1)} %get-tuple-element.80) | copy-start | bytes 153604
  156.1 9.0 %collective-permute-start.19 = (bf16[8,3200]{1,0:T(8,128)(2,1)S(1)}, bf16[8,3200]{1,0:T(8,128)(2,1)S(1)}, u32[]{:S(2)}, u32[]{:S(2)}) collective-permute-start(bf16[8,3200]{1,0:T(8,128)(2,1)S(1)} %shard_map.107), channel_id=1, source_target_pairs={{0,64},{2,66},{64,130},{66,128},{128,192},{130,194},{192,2},{194,0... | collective-permute-start | bytes 153608 | tf_op jit(solution)/shard_map/ppermute | solution.py:35
  182.7 25.1 %copy-start.3 = (bf16[8,3200]{1,0:T(8,128)(2,1)S(1)}, bf16[8,3200]{1,0:T(8,128)(2,1)}, u32[]{:S(2)}) copy-start(bf16[8,3200]{1,0:T(8,128)(2,1)} %get-tuple-element.79) | copy-start | bytes 153604
  195.5 12.3 %collective-permute-start.20 = (bf16[8,3200]{1,0:T(8,128)(2,1)S(1)}, bf16[8,3200]{1,0:T(8,128)(2,1)S(1)}, u32[]{:S(2)}, u32[]{:S(2)}) collective-permute-start(bf16[8,3200]{1,0:T(8,128)(2,1)S(1)} %shard_map.109), channel_id=1, source_target_pairs={{0,64},{2,66},{64,130},{66,128},{128,192},{130,194},{192,2},{194,0... | collective-permute-start | bytes 153608 | tf_op jit(solution)/shard_map/ppermute | solution.py:35
  246.8 3.3 %collective-permute-start.21 = (bf16[8,3200]{1,0:T(8,128)(2,1)S(1)}, bf16[8,3200]{1,0:T(8,128)(2,1)S(1)}, u32[]{:S(2)}, u32[]{:S(2)}) collective-permute-start(bf16[8,3200]{1,0:T(8,128)(2,1)S(1)} %shard_map.111), channel_id=1, source_target_pairs={{0,64},{2,66},{64,130},{66,128},{128,192},{130,194},{1,65},{3,67},... | collective-permute-start | bytes 153608 | tf_op jit(solution)/shard_map/ppermute | solution.py:35
  271.4 21.4 %copy-start.5 = (bf16[8,3200]{1,0:T(8,128)(2,1)S(1)}, bf16[8,3200]{1,0:T(8,128)(2,1)}, u32[]{:S(2)}) copy-start(bf16[8,3200]{1,0:T(8,128)(2,1)} %get-tuple-element.119) | copy-start | bytes 153604
  285.6 7.1 %collective-permute-start.24 = (bf16[8,3200]{1,0:T(8,128)(2,1)S(1)}, bf16[8,3200]{1,0:T(8,128)(2,1)S(1)}, u32[]{:S(2)}, u32[]{:S(2)}) collective-permute-start(bf16[8,3200]{1,0:T(8,128)(2,1)S(1)} %shard_map.113), channel_id=1, source_target_pairs={{0,64},{2,66},{64,128},{66,130},{128,194},{130,192},{1,65},{3,67},... | collective-permute-start | bytes 153608 | tf_op jit(solution)/shard_map/ppermute | solution.py:35
  290.8 6.3 %collective-permute-start.23 = (bf16[8,3200]{1,0:T(8,128)(2,1)S(1)}, bf16[8,3200]{1,0:T(8,128)(2,1)S(1)}, u32[]{:S(2)}, u32[]{:S(2)}) collective-permute-start(bf16[8,3200]{1,0:T(8,128)(2,1)S(1)} %broadcast_select_fusion), channel_id=1, source_target_pairs={{0,66},{2,64},{192,194},{194,192},{1,67},{3,65},{193,195},{195,193... | collective-permute-start | bytes 153608 | tf_op jit(solution)/shard_map/ppermute | solution.py:35
  292.1 5.0 %collective-permute-start.22 = (bf16[8,3200]{1,0:T(8,128)(2,1)S(1)}, bf16[8,3200]{1,0:T(8,128)(2,1)S(1)}, u32[]{:S(2)}, u32[]{:S(2)}) collective-permute-start(bf16[8,3200]{1,0:T(8,128)(2,1)S(1)} %broadcast_select_fusion.1), channel_id=1, source_target_pairs={{192,130},{194,128},{0,2},{2,0},{193,131},{195,129},{1,3},{3,1},{1... | collective-permute-start | bytes 153608 | tf_op jit(solution)/shard_map/ppermute | solution.py:35

commit v9 on v7

--- a/solution.py
+++ b/solution.py
@@ -171,10 +171,9 @@
     xa = from_neighbour(first, "x", 1)
     xb = from_neighbour(second, "x", -1)
     partial = jnp.sum(exchange(partial, SECTION + LINE), axis=0)
-    entering = exchange(after(arriving, partial), SECTION)
-
-    first, second, yp_first, ym_second, xa, xb, partial, entering = together(
-        (first, second, yp_first, ym_second, xa, xb, partial, entering)
+
+    first, second, yp_first, ym_second, xa, xb, partial = together(
+        (first, second, yp_first, ym_second, xa, xb, partial)
     )
     pooled = jnp.sum(exchange(partial, PLANE), axis=0)
     yp_second = from_neighbour(second, "y", 1)
@@ -201,7 +200,8 @@
     halves, y2[0], y2[2] = together((halves, y2[0], y2[2]))
     y2[1] = from_neighbour(halves[1], "y", 1)
     y2[3] = from_neighbour(halves[3], "y", -1)
-    modes = exchange(line, PLANE)
+    entering = exchange(after(arriving, line), SECTION)
+    modes = exchange(after(line, entering), PLANE)
     xa_yp_down = xa_yp[middle:]
     xb_ym_down = xb_ym[middle:]
 

time: 296 us -> 303 us (1.024)
  waiting for transfers between devices: 39.8 us -> 43.3 us
    ppermute x18, waiting for transfers between devices: 13 us -> 22.6 us  [from_neighbour(): return lax.ppermute(block, (axis + 'h', axis + 'l'), route)]
    all_to_all x5, waiting for transfers between devices: 19.8 us -> 13.6 us  [exchange(): return lax.all_to_all(copies, axes, 0, 0)]
    all_to_all x4, blocking collectives: 56.6 us -> 62.4 us  [exchange(): return lax.all_to_all(copies, axes, 0, 0)]
    all_to_all x4, blocking collectives: 63.6 us -> 58.6 us  [per_device(): lax.all_to_all(partial.reshape(GROUP_SIZE, tokens, breadth), GROUP, 0, 0)]
    all_to_all x5, starting transfers between devices: 31.9 us -> 34.9 us  [exchange(): return lax.all_to_all(copies, axes, 0, 0)]
  transfers between devices with their start and end apart: 30 -> 30, of which waited for: 12 -> 17; matrix products, arithmetic and copies ran while one was open for 5% -> 5% of each run, Pallas kernels for 2% -> 2%
where the time goes in v9:
time: 303 us; the launch traced here: 301 us
  blocking collectives  121 us (40%)
  starting transfers between devices  84.5 us (28%)
  waiting for transfers between devices  43.3 us (14%)
  Pallas kernels  27.2 us (9%)
  local copies, waits for them, and re-layouts  15.6 us (5%)
  other arithmetic  6.59 us (2%)
    all_to_all x4, blocking collectives, exchange(): return lax.all_to_all(copies, axes, 0, 0)  62.4 us
    all_to_all x4, blocking collectives, per_device(): lax.all_to_all(partial.reshape(GROUP_SIZE, tokens, breadth), GROUP, 0, 0)  58.6 us
    all_to_all x5, starting transfers between devices, exchange(): return lax.all_to_all(copies, axes, 0, 0)  34.9 us
    ppermute x6, starting transfers between devices, between_sections(): return lax.ppermute(block, SECTION + ('zc',), route)  27.3 us
    ppermute x18, waiting for transfers between devices, from_neighbour(): return lax.ppermute(block, (axis + 'h', axis + 'l'), route)  22.6 us
    ppermute x18, starting transfers between devices, from_neighbour(): return lax.ppermute(block, (axis + 'h', axis + 'l'), route)  20.6 us
    pallas_call x4, Pallas kernels, layer(): pl.pallas_call(layer_kernel, out_shape=jax.ShapeDtypeStruct((rows, breadt...  19.8 us
    all_to_all x5, waiting for transfers between devices, exchange(): return lax.all_to_all(copies, axes, 0, 0)  13.6 us
  transfers between devices with their start and end apart: 30, of which 17 were waited for; matrix products, arithmetic and copies ran while one was open for 5% of the time, Pallas kernels for 2%

profile of v9, /device:TPU:1, one launch (start us, length us, event | category | flops | bytes accessed | tf_op | source)
XLA Modules:
  0.0 301.1 jit_solution(2530365757956381941)
XLA Ops:
  3.3 1.6 pad_maximum_fusion
  4.9 3.6 %collective-permute-start = (bf16[192,3072]{1,0:T(8,128)(2,1)}, bf16[192,3072]{1,0:T(8,128)(2,1)S(1)}, u32[]{:S(2)}, u32[]{:S(2)}) collective-permute-start(bf16[192,3072]{1,0:T(8,128)(2,1)} %get-tuple-element.90.refs_0_), channel_id=1, source_target_pairs={{4,0},{8,4},{12,8},{0,12},{5,1},{9,5},{13,9},{1,13},{6,2},{10,6},{... | collective-permute-start | bytes 3538952 | tf_op jit(solution)/shard_map/ppermute | solution.py:28
  8.5 2.5 collective-permute-start.2
  11.0 19.2 %all_to_all.65 = f32[16,28,128]{2,1,0:T(8,128)} all-to-all(f32[16,28,128]{2,1,0:T(8,128)S(1)} %broadcast_in_dim.28), channel_id=1, replica_groups=mesh['zh'=2,'core'=2,'xh'=2,'xl'=2,'yh'=2,'yl'=2,'zc'=2,'zf'=2] {'zh','c..., dimensions={0} | all-to-all | bytes 458752 | tf_op jit(solution)/shard_map/all_to_all | solution.py:45
  31.2 2.3 collective-permute-done.refs_4_
  33.4 3.1 %collective-permute-done.1.refs_5_ = bf16[192,3072]{1,0:T(8,128)(2,1)S(1)} collective-permute-done((bf16[192,3072]{1,0:T(8,128)(2,1)}, bf16[192,3072]{1,0:T(8,128)(2,1)S(1)}, u32[]{:S(2)}, u32[]{:S(2)}) %collective-permute-start.1) | collective-permute-done | bytes 1179680 | tf_op jit(solution)/shard_map/ppermute | solution.py:28
  36.5 2.2 collective-permute-done.3.refs_3_
  39.5 4.2 %all-to-all-start.1 = ((f32[16,28,128]{2,1,0:T(8,128)}), f32[16,28,128]{2,1,0:T(8,128)}, u32[]{:S(2)}, u32[]{:S(2)}) async-start(f32[16,28,128]{2,1,0:T(8,128)} %broadcast_in_dim.29), calls=%async_computation.1 | async-start | bytes 524288 | tf_op jit(solution)/shard_map/all_to_all | solution.py:45
  43.7 2.5 collective-permute-start.4
  46.1 2.4 collective-permute-start.6
  48.5 2.5 all-to-all-done.1
  54.3 5.6 %all-to-all-start.2 = ((f32[4,2,128]{2,1,0:T(2,128)}), f32[4,2,128]{2,1,0:T(2,128)S(1)}, u32[]{:S(2)}, u32[]{:S(2)}) async-start(f32[4,2,128]{2,1,0:T(2,128)} %broadcast_in_dim.31), calls=%async_computation.2 | async-start | bytes 8192 | tf_op jit(solution)/shard_map/all_to_all | solution.py:45
  61.1 3.4 %all-to-all-done.2 = f32[4,2,128]{2,1,0:T(2,128)S(1)} async-done(((f32[4,2,128]{2,1,0:T(2,128)}), f32[4,2,128]{2,1,0:T(2,128)S(1)}, u32[]{:S(2)}, u32[]{:S(2)}) %all-to-all-start.2) | async-done | bytes 4128 | tf_op jit(solution)/shard_map/all_to_all | solution.py:45
  65.2 4.0 %all-to-all-start.3 = ((bf16[4,8,3072]{2,1,0:T(8,128)(2,1)}), bf16[4,8,3072]{2,1,0:T(8,128)(2,1)}, u32[]{:S(2)}, u32[]{:S(2)}) async-start(bf16[4,8,3072]{2,1,0:T(8,128)(2,1)} %broadcast_in_dim.32), calls=%async_computation.3 | async-start | bytes 393216 | tf_op jit(solution)/shard_map/all_to_all | solution.py:45
  70.3 4.3 %all-to-all-done.3 = bf16[4,8,3072]{2,1,0:T(8,128)(2,1)} async-done(((bf16[4,8,3072]{2,1,0:T(8,128)(2,1)}), bf16[4,8,3072]{2,1,0:T(8,128)(2,1)}, u32[]{:S(2)}, u32[]{:S(2)}) %all-to-all-start.3) | async-done | bytes 196640 | tf_op jit(solution)/shard_map/all_to_all | solution.py:45
  75.5 1.8 collective-permute-start.8
  78.8 7.8 %collective-permute-done.11.refs_12_ = bf16[96,3072]{1,0:T(8,128)(2,1)} collective-permute-done((bf16[96,3072]{1,0:T(8,128)(2,1)}, bf16[96,3072]{1,0:T(8,128)(2,1)}, u32[]{:S(2)}, u32[]{:S(2)}) %collective-permute-start.11) | collective-permute-done | bytes 589856 | tf_op jit(solution)/shard_map/ppermute | solution.py:28
  86.7 1.8 collective-permute-done.12.refs_14_.refs_0_
  90.7 17.0 %all-to-all-start.4 = ((bf16[4,8,3200]{2,1,0:T(8,128)(2,1)}), bf16[4,8,3200]{2,1,0:T(8,128)(2,1)}, u32[]{:S(2)}, u32[]{:S(2)}) async-start(bf16[4,8,3200]{2,1,0:T(8,128)(2,1)} %broadcast_in_dim.35), calls=%async_computation.4 | async-start | bytes 409600 | tf_op jit(solution)/shard_map/all_to_all | solution.py:45
  107.7 1.9 slice.93
  110.8 1.9 slice.94
  112.8 3.4 %all-to-all-done.4 = bf16[4,8,3200]{2,1,0:T(8,128)(2,1)} async-done(((bf16[4,8,3200]{2,1,0:T(8,128)(2,1)}), bf16[4,8,3200]{2,1,0:T(8,128)(2,1)}, u32[]{:S(2)}, u32[]{:S(2)}) %all-to-all-start.4) | async-done | bytes 204832 | tf_op jit(solution)/shard_map/all_to_all | solution.py:45
  116.8 4.2 %all-to-all-start.5 = ((f32[16,4,2,128]{3,2,1,0:T(2,128)}), f32[16,4,2,128]{3,2,1,0:T(2,128)}, u32[]{:S(2)}, u32[]{:S(2)}) async-start(f32[16,4,2,128]{3,2,1,0:T(2,128)} %broadcast_in_dim.36), calls=%async_computation.5 | async-start | bytes 131072 | tf_op jit(solution)/shard_map/all_to_all | solution.py:45
  122.3 2.5 collective-permute-start.15
  124.8 1.7 collective-permute-start.10
  126.5 1.5 slice_bitcast_fusion.4
  130.5 5.1 %shard_map.104 = (bf16[1280,3072]{1,0:T(8,128)(2,1)S(1)}, bf16[1280,3072]{1,0:T(8,128)(2,1)S(1)}) custom-call(bf16[192,3072]{1,0:T(8,128)(2,1)} %get-tuple-element.90.refs_0_, bf16[192,3072]{1,0:T(8,128)(2,1)} %get-tuple-element.91.refs_1_, bf16[192,3072]{1,0:T(8,128)(2,1)} %collective-permute-done.2.refs_2_, ...), custom_call_target="tpu_custom_call" | custom-call | bytes 31457280 | tf_op jit(solution)/shard_map/pallas_call | solution.py:118
  135.6 1.5 collective-permute-done.18.refs_5_
  137.1 3.0 collective-permute-done.16.refs_3_
  140.1 1.9 shard_map.105
  143.2 4.9 %shard_map.106 = bf16[64,3072]{1,0:T(8,128)(2,1)S(1)} custom-call(bf16[64,3072]{1,0:T(8,128)(2,1)S(1)} %bitcast.69, f32[3,3072]{1,0:T(4,128)S(1)} %reshape.75.mod_ref, bf16[1280,3072]{1,0:T(8,128)(2,1)S(1)} %get-tuple-element.106.up, bf16[1280,3072]{1,0:T(8,128)(2,1)S(1)} %get-tuple-element.107.down, bf16[256,3072]{1,0:T(8,128)(2,1)S(1)} %get-tuple-element.108.up_end, ...), custom_call_target="tpu_custom_call" | custom-call | flops 1207959552 | bytes 19660800 | tf_op jit(solution)/shard_map/pallas_call | solution.py:79
  148.2 16.4 %all_to_all.66.parts_ref = bf16[8,8,3072]{2,1,0:T(8,128)(2,1)S(1)} all-to-all(bf16[8,8,3072]{2,1,0:T(8,128)(2,1)S(1)} %bitcast.70), channel_id=1, replica_groups=mesh['zh'=2,'core'=2,'xh'=2,'xl'=2,'yh'=2,'yl'=2,'zc'=2,'zf'=2] {'xh','z..., dimensions={0} | all-to-all | bytes 786432 | tf_op jit(solution)/shard_map/all_to_all | solution.py:282
  164.6 4.2 %collective-permute-start.19 = (bf16[8,3200]{1,0:T(8,128)(2,1)S(1)}, bf16[8,3200]{1,0:T(8,128)(2,1)S(1)}, u32[]{:S(2)}, u32[]{:S(2)}) collective-permute-start(bf16[8,3200]{1,0:T(8,128)(2,1)S(1)} %shard_map.107), channel_id=1, source_target_pairs={{0,64},{2,66},{64,130},{66,128},{128,192},{130,194},{192,0},{194,2... | collective-permute-start | bytes 153608 | tf_op jit(solution)/shard_map/ppermute | solution.py:35
  168.8 2.4 collective-permute-done.19
  171.3 12.5 %all_to_all.67 = bf16[8,8,3072]{2,1,0:T(8,128)(2,1)S(1)} all-to-all(bf16[8,8,3072]{2,1,0:T(8,128)(2,1)S(1)} %broadcast_in_dim.37), channel_id=1, replica_groups=mesh['zh'=2,'core'=2,'xh'=2,'xl'=2,'yh'=2,'yl'=2,'zc'=2,'zf'=2] {'xh','z..., dimensions={0} | all-to-all | bytes 786432 | tf_op jit(solution)/shard_map/all_to_all | solution.py:45
  183.8 4.9 %shard_map.108 = bf16[64,3072]{1,0:T(8,128)(2,1)S(1)} custom-call(bf16[64,3072]{1,0:T(8,128)(2,1)S(1)} %bitcast.71, f32[3,3072]{1,0:T(4,128)S(1)} %reshape.75.mod_ref, bf16[1280,3072]{1,0:T(8,128)(2,1)S(1)} %get-tuple-element.106.up, bf16[1280,3072]{1,0:T(8,128)(2,1)S(1)} %get-tuple-element.107.down, bf16[256,3072]{1,0:T(8,128)(2,1)S(1)} %get-tuple-element.108.up_end, ...), custom_call_target="tpu_custom_call" | custom-call | flops 1207959552 | bytes 19660800 | tf_op jit(solution)/shard_map/pallas_call | solution.py:79
  188.8 12.7 %all_to_all.68.parts_ref = bf16[8,8,3072]{2,1,0:T(8,128)(2,1)S(1)} all-to-all(bf16[8,8,3072]{2,1,0:T(8,128)(2,1)S(1)} %bitcast.72), channel_id=1, replica_groups=mesh['zh'=2,'core'=2,'xh'=2,'xl'=2,'yh'=2,'yl'=2,'zc'=2,'zf'=2] {'xh','z..., dimensions={0} | all-to-all | bytes 786432 | tf_op jit(solution)/shard_map/all_to_all | solution.py:282
  201.5 13.0 %collective-permute-start.20 = (bf16[8,3200]{1,0:T(8,128)(2,1)S(1)}, bf16[8,3200]{1,0:T(8,128)(2,1)S(1)}, u32[]{:S(2)}, u32[]{:S(2)}) collective-permute-start(bf16[8,3200]{1,0:T(8,128)(2,1)S(1)} %shard_map.109), channel_id=1, source_target_pairs={{0,64},{2,66},{64,130},{66,128},{128,192},{130,194},{192,0},{194,2... | collective-permute-start | bytes 153608 | tf_op jit(solution)/shard_map/ppermute | solution.py:35
  214.5 1.6 collective-permute-done.20
  216.2 14.5 %all_to_all.69 = bf16[8,8,3072]{2,1,0:T(8,128)(2,1)S(1)} all-to-all(bf16[8,8,3072]{2,1,0:T(8,128)(2,1)S(1)} %broadcast_in_dim.38), channel_id=1, replica_groups=mesh['zh'=2,'core'=2,'xh'=2,'xl'=2,'yh'=2,'yl'=2,'zc'=2,'zf'=2] {'xh','z..., dimensions={0} | all-to-all | bytes 786432 | tf_op jit(solution)/shard_map/all_to_all | solution.py:45
  230.7 4.9 %shard_map.110 = bf16[64,3072]{1,0:T(8,128)(2,1)S(1)} custom-call(bf16[64,3072]{1,0:T(8,128)(2,1)S(1)} %bitcast.73, f32[3,3072]{1,0:T(4,128)S(1)} %reshape.75.mod_ref, bf16[1280,3072]{1,0:T(8,128)(2,1)S(1)} %get-tuple-element.106.up, bf16[1280,3072]{1,0:T(8,128)(2,1)S(1)} %get-tuple-element.107.down, bf16[256,3072]{1,0:T(8,128)(2,1)S(1)} %get-tuple-element.108.up_end, ...), custom_call_target="tpu_custom_call" | custom-call | flops 1207959552 | bytes 19660800 | tf_op jit(solution)/shard_map/pallas_call | solution.py:79
  235.7 15.5 %all_to_all.70.parts_ref = bf16[8,8,3072]{2,1,0:T(8,128)(2,1)S(1)} all-to-all(bf16[8,8,3072]{2,1,0:T(8,128)(2,1)S(1)} %bitcast.74), channel_id=1, replica_groups=mesh['zh'=2,'core'=2,'xh'=2,'xl'=2,'yh'=2,'yl'=2,'zc'=2,'zf'=2] {'xh','z..., dimensions={0} | all-to-all | bytes 786432 | tf_op jit(solution)/shard_map/all_to_all | solution.py:282
  251.3 3.4 %collective-permute-start.21 = (bf16[8,3200]{1,0:T(8,128)(2,1)S(1)}, bf16[8,3200]{1,0:T(8,128)(2,1)S(1)}, u32[]{:S(2)}, u32[]{:S(2)}) collective-permute-start(bf16[8,3200]{1,0:T(8,128)(2,1)S(1)} %shard_map.111), channel_id=1, source_target_pairs={{0,64},{2,66},{64,130},{66,128},{128,192},{130,194},{1,65},{3,67},... | collective-permute-start | bytes 153608 | tf_op jit(solution)/shard_map/ppermute | solution.py:35
  254.6 2.5 collective-permute-done.21
  257.2 16.2 %all_to_all.71 = bf16[8,8,3072]{2,1,0:T(8,128)(2,1)S(1)} all-to-all(bf16[8,8,3072]{2,1,0:T(8,128)(2,1)S(1)} %broadcast_in_dim.39), channel_id=1, replica_groups=mesh['zh'=2,'core'=2,'xh'=2,'xl'=2,'yh'=2,'yl'=2,'zc'=2,'zf'=2] {'xh','z..., dimensions={0} | all-to-all | bytes 786432 | tf_op jit(solution)/shard_map/all_to_all | solution.py:45
  273.4 4.9 %shard_map.112 = bf16[64,3072]{1,0:T(8,128)(2,1)S(1)} custom-call(bf16[64,3072]{1,0:T(8,128)(2,1)S(1)} %bitcast.67, f32[3,3072]{1,0:T(4,128)S(1)} %reshape.75.mod_ref, bf16[1280,3072]{1,0:T(8,128)(2,1)S(1)} %get-tuple-element.106.up, bf16[1280,3072]{1,0:T(8,128)(2,1)S(1)} %get-tuple-element.107.down, bf16[256,3072]{1,0:T(8,128)(2,1)S(1)} %get-tuple-element.108.up_end, ...), custom_call_target="tpu_custom_call" | custom-call | flops 1207959552 | bytes 19660800 | tf_op jit(solution)/shard_map/pallas_call | solution.py:79
  278.3 14.1 %all_to_all.72.parts_ref = bf16[8,8,3072]{2,1,0:T(8,128)(2,1)S(1)} all-to-all(bf16[8,8,3072]{2,1,0:T(8,128)(2,1)S(1)} %bitcast.68), channel_id=1, replica_groups=mesh['zh'=2,'core'=2,'xh'=2,'xl'=2,'yh'=2,'yl'=2,'zc'=2,'zf'=2] {'xh','z..., dimensions={0} | all-to-all | bytes 786432 | tf_op jit(solution)/shard_map/all_to_all | solution.py:282
  292.5 4.8 %collective-permute-start.24 = (bf16[8,3200]{1,0:T(8,128)(2,1)S(1)}, bf16[8,3200]{1,0:T(8,128)(2,1)S(1)}, u32[]{:S(2)}, u32[]{:S(2)}) collective-permute-start(bf16[8,3200]{1,0:T(8,128)(2,1)S(1)} %shard_map.113), channel_id=1, source_target_pairs={{0,64},{2,66},{64,128},{66,130},{128,194},{130,192},{1,65},{3,67},... | collective-permute-start | bytes 153608 | tf_op jit(solution)/shard_map/ppermute | solution.py:35
  (96 shorter events, 24.9 us)
Async XLA Ops:
  0.6 52.7 %copy-start = (bf16[1,144,3584]{2,1,0:T(8,128)(2,1)S(1)}, bf16[1,144,3584]{2,1,0:T(8,128)(2,1)}, u32[]{:S(2)}) copy-start(bf16[1,144,3584]{2,1,0:T(8,128)(2,1)} %param.15) | copy-start | bytes 3096580
  0.6 1.7 copy-start.1
  2.4 0.8 copy-start.6
  4.9 28.5 %collective-permute-start = (bf16[192,3072]{1,0:T(8,128)(2,1)}, bf16[192,3072]{1,0:T(8,128)(2,1)S(1)}, u32[]{:S(2)}, u32[]{:S(2)}) collective-permute-start(bf16[192,3072]{1,0:T(8,128)(2,1)} %get-tuple-element.90.refs_0_), channel_id=1, source_target_pairs={{4,0},{8,4},{12,8},{0,12},{5,1},{9,5},{13,9},{1,13},{6,2},{10,6},{... | collective-permute-start | bytes 3538952 | tf_op jit(solution)/shard_map/ppermute | solution.py:28
  8.5 28.0 %collective-permute-start.1 = (bf16[192,3072]{1,0:T(8,128)(2,1)}, bf16[192,3072]{1,0:T(8,128)(2,1)S(1)}, u32[]{:S(2)}, u32[]{:S(2)}) collective-permute-start(bf16[192,3072]{1,0:T(8,128)(2,1)} %get-tuple-element.91.refs_1_), channel_id=1, source_target_pairs={{12,0},{0,4},{4,8},{8,12},{13,1},{1,5},{5,9},{9,13},{14,2},{2,6},{... | collective-permute-start | bytes 3538952 | tf_op jit(solution)/shard_map/ppermute | solution.py:28
  8.5 28.0 %collective-permute-start.2 = (bf16[192,3072]{1,0:T(8,128)(2,1)}, bf16[192,3072]{1,0:T(8,128)(2,1)}, u32[]{:S(2)}, u32[]{:S(2)}) collective-permute-start(bf16[192,3072]{1,0:T(8,128)(2,1)} %get-tuple-element.90.refs_0_), channel_id=1, source_target_pairs={{16,0},{32,16},{48,32},{0,48},{17,1},{33,17},{49,33},{1,49},{18,2}... | collective-permute-start | bytes 3538952 | tf_op jit(solution)/shard_map/ppermute | solution.py:28
  11.0 27.7 %collective-permute-start.3 = (bf16[192,3072]{1,0:T(8,128)(2,1)}, bf16[192,3072]{1,0:T(8,128)(2,1)}, u32[]{:S(2)}, u32[]{:S(2)}) collective-permute-start(bf16[192,3072]{1,0:T(8,128)(2,1)} %get-tuple-element.91.refs_1_), channel_id=1, source_target_pairs={{48,0},{0,16},{16,32},{32,48},{49,1},{1,17},{17,33},{33,49},{50,2}... | collective-permute-start | bytes 3538952 | tf_op jit(solution)/shard_map/ppermute | solution.py:28
  39.5 11.6 %all-to-all-start.1 = ((f32[16,28,128]{2,1,0:T(8,128)}), f32[16,28,128]{2,1,0:T(8,128)}, u32[]{:S(2)}, u32[]{:S(2)}) async-start(f32[16,28,128]{2,1,0:T(8,128)} %broadcast_in_dim.29), calls=%async_computation.1 | async-start | bytes 524288 | tf_op jit(solution)/shard_map/all_to_all | solution.py:45
  43.7 31.0 %collective-permute-start.4 = (bf16[192,3072]{1,0:T(8,128)(2,1)}, bf16[192,3072]{1,0:T(8,128)(2,1)}, u32[]{:S(2)}, u32[]{:S(2)}) collective-permute-start(bf16[192,3072]{1,0:T(8,128)(2,1)} %get-tuple-element.91.refs_1_), channel_id=1, source_target_pairs={{4,0},{8,4},{12,8},{0,12},{5,1},{9,5},{13,9},{1,13},{6,2},{10,6},{... | collective-permute-start | bytes 3538952 | tf_op jit(solution)/shard_map/ppermute | solution.py:28
  46.1 29.4 %collective-permute-start.5 = (bf16[192,3072]{1,0:T(8,128)(2,1)}, bf16[192,3072]{1,0:T(8,128)(2,1)}, u32[]{:S(2)}, u32[]{:S(2)}) collective-permute-start(bf16[192,3072]{1,0:T(8,128)(2,1)} %get-tuple-element.90.refs_0_), channel_id=1, source_target_pairs={{12,0},{0,4},{4,8},{8,12},{13,1},{1,5},{5,9},{9,13},{14,2},{2,6},{... | collective-permute-start | bytes 3538952 | tf_op jit(solution)/shard_map/ppermute | solution.py:28
  46.1 29.4 %collective-permute-start.6 = (bf16[192,3072]{1,0:T(8,128)(2,1)S(1)}, bf16[192,3072]{1,0:T(8,128)(2,1)}, u32[]{:S(2)}, u32[]{:S(2)}) collective-permute-start(bf16[192,3072]{1,0:T(8,128)(2,1)S(1)} %collective-permute-done.refs_4_), channel_id=1, source_target_pairs={{16,0},{32,16},{48,32},{0,48},{17,1},{33,17},{49,33},{1,49},{18,2}... | collective-permute-start | bytes 3538952 | tf_op jit(solution)/shard_map/ppermute | solution.py:28
  48.5 26.9 %collective-permute-start.7 = (bf16[192,3072]{1,0:T(8,128)(2,1)S(1)}, bf16[192,3072]{1,0:T(8,128)(2,1)}, u32[]{:S(2)}, u32[]{:S(2)}) collective-permute-start(bf16[192,3072]{1,0:T(8,128)(2,1)S(1)} %collective-permute-done.1.refs_5_), channel_id=1, source_target_pairs={{48,0},{0,16},{16,32},{32,48},{49,1},{1,17},{17,33},{33,49},{50,2}... | collective-permute-start | bytes 3538952 | tf_op jit(solution)/shard_map/ppermute | solution.py:28
  54.3 10.2 %all-to-all-start.2 = ((f32[4,2,128]{2,1,0:T(2,128)}), f32[4,2,128]{2,1,0:T(2,128)S(1)}, u32[]{:S(2)}, u32[]{:S(2)}) async-start(f32[4,2,128]{2,1,0:T(2,128)} %broadcast_in_dim.31), calls=%async_computation.2 | async-start | bytes 8192 | tf_op jit(solution)/shard_map/all_to_all | solution.py:45
  60.0 4.5 %copy-start.5 = (bf16[1,8,3072]{2,1,0:T(8,128)(2,1)S(1)}, bf16[1,8,3072]{2,1,0:T(8,128)(2,1)}, u32[]{:S(2)}) copy-start(bf16[1,8,3072]{2,1,0:T(8,128)(2,1)} %param.9) | copy-start | bytes 147460
  65.2 9.5 %all-to-all-start.3 = ((bf16[4,8,3072]{2,1,0:T(8,128)(2,1)}), bf16[4,8,3072]{2,1,0:T(8,128)(2,1)}, u32[]{:S(2)}, u32[]{:S(2)}) async-start(bf16[4,8,3072]{2,1,0:T(8,128)(2,1)} %broadcast_in_dim.32), calls=%async_computation.3 | async-start | bytes 393216 | tf_op jit(solution)/shard_map/all_to_all | solution.py:45
  69.2 9.5 %copy-start.8 = (s32[1,8]{1,0:T(1,128)S(1)}, s32[1,8]{1,0:T(1,128)}, u32[]{:S(2)}) copy-start(s32[1,8]{1,0:T(1,128)} %param.12) | copy-start | bytes 100
  69.2 9.6 %copy-start.7 = (bf16[1,8,3072]{2,1,0:T(8,128)(2,1)S(1)}, bf16[1,8,3072]{2,1,0:T(8,128)(2,1)}, u32[]{:S(2)}) copy-start(bf16[1,8,3072]{2,1,0:T(8,128)(2,1)} %param.11) | copy-start | bytes 147460
  69.2 20.8 %copy-start.9 = (s32[1,8]{1,0:T(1,128)S(1)}, s32[1,8]{1,0:T(1,128)}, u32[]{:S(2)}) copy-start(s32[1,8]{1,0:T(1,128)} %param.10) | copy-start | bytes 100
  75.5 45.5 %collective-permute-start.8 = (bf16[192,3072]{1,0:T(8,128)(2,1)}, bf16[192,3072]{1,0:T(8,128)(2,1)}, u32[]{:S(2)}, u32[]{:S(2)}) collective-permute-start(bf16[192,3072]{1,0:T(8,128)(2,1)} %collective-permute-done.5.refs_7_), channel_id=1, source_target_pairs={{16,0},{32,16},{48,32},{0,48},{17,1},{33,17},{49,33},{1,49},{18,2}... | collective-permute-start | bytes 3538952 | tf_op jit(solution)/shard_map/ppermute | solution.py:28
  77.3 45.0 %collective-permute-start.9 = (bf16[192,3072]{1,0:T(8,128)(2,1)}, bf16[192,3072]{1,0:T(8,128)(2,1)}, u32[]{:S(2)}, u32[]{:S(2)}) collective-permute-start(bf16[192,3072]{1,0:T(8,128)(2,1)} %collective-permute-done.4.refs_6_), channel_id=1, source_target_pairs={{48,0},{0,16},{16,32},{32,48},{49,1},{1,17},{17,33},{33,49},{50,2}... | collective-permute-start | bytes 3538952 | tf_op jit(solution)/shard_map/ppermute | solution.py:28
  77.3 9.4 %collective-permute-start.11 = (bf16[96,3072]{1,0:T(8,128)(2,1)}, bf16[96,3072]{1,0:T(8,128)(2,1)}, u32[]{:S(2)}, u32[]{:S(2)}) collective-permute-start(bf16[96,3072]{1,0:T(8,128)(2,1)} %get-tuple-element.82), channel_id=1, source_target_pairs={{4,0},{8,4},{12,8},{0,12},{5,1},{9,5},{13,9},{1,13},{6,2},{10,6},{... | collective-permute-start | bytes 1769480 | tf_op jit(solution)/shard_map/ppermute | solution.py:28
  77.9 10.6 %collective-permute-start.12 = (bf16[96,3072]{1,0:T(8,128)(2,1)}, bf16[96,3072]{1,0:T(8,128)(2,1)}, u32[]{:S(2)}, u32[]{:S(2)}) collective-permute-start(bf16[96,3072]{1,0:T(8,128)(2,1)} %get-tuple-element.84), channel_id=1, source_target_pairs={{12,0},{0,4},{4,8},{8,12},{13,1},{1,5},{5,9},{9,13},{14,2},{2,6},{... | collective-permute-start | bytes 1769480 | tf_op jit(solution)/shard_map/ppermute | solution.py:28
  88.5 36.2 %collective-permute-start.13 = (bf16[96,3072]{1,0:T(8,128)(2,1)}, bf16[96,3072]{1,0:T(8,128)(2,1)}, u32[]{:S(2)}, u32[]{:S(2)}) collective-permute-start(bf16[96,3072]{1,0:T(8,128)(2,1)} %get-tuple-element.87), channel_id=1, source_target_pairs={{4,0},{8,4},{12,8},{0,12},{5,1},{9,5},{13,9},{1,13},{6,2},{10,6},{... | collective-permute-start | bytes 1769480 | tf_op jit(solution)/shard_map/ppermute | solution.py:28
  88.5 36.2 %collective-permute-start.14 = (bf16[96,3072]{1,0:T(8,128)(2,1)}, bf16[96,3072]{1,0:T(8,128)(2,1)}, u32[]{:S(2)}, u32[]{:S(2)}) collective-permute-start(bf16[96,3072]{1,0:T(8,128)(2,1)} %get-tuple-element.89), channel_id=1, source_target_pairs={{12,0},{0,4},{4,8},{8,12},{13,1},{1,5},{5,9},{9,13},{14,2},{2,6},{... | collective-permute-start | bytes 1769480 | tf_op jit(solution)/shard_map/ppermute | solution.py:28
  90.7 25.5 %all-to-all-start.4 = ((bf16[4,8,3200]{2,1,0:T(8,128)(2,1)}), bf16[4,8,3200]{2,1,0:T(8,128)(2,1)}, u32[]{:S(2)}, u32[]{:S(2)}) async-start(bf16[4,8,3200]{2,1,0:T(8,128)(2,1)} %broadcast_in_dim.35), calls=%async_computation.4 | async-start | bytes 409600 | tf_op jit(solution)/shard_map/all_to_all | solution.py:45
  109.6 26.0 %collective-permute-start.17 = (bf16[96,3072]{1,0:T(8,128)(2,1)}, bf16[96,3072]{1,0:T(8,128)(2,1)}, u32[]{:S(2)}, u32[]{:S(2)}) collective-permute-start(bf16[96,3072]{1,0:T(8,128)(2,1)} %slice.93), channel_id=1, source_target_pairs={{4,0},{8,4},{12,8},{0,12},{5,1},{9,5},{13,9},{1,13},{6,2},{10,6},{... | collective-permute-start | bytes 1769480 | tf_op jit(solution)/shard_map/ppermute | solution.py:28
  116.8 11.2 %all-to-all-start.5 = ((f32[16,4,2,128]{3,2,1,0:T(2,128)}), f32[16,4,2,128]{3,2,1,0:T(2,128)}, u32[]{:S(2)}, u32[]{:S(2)}) async-start(f32[16,4,2,128]{3,2,1,0:T(2,128)} %broadcast_in_dim.36), calls=%async_computation.5 | async-start | bytes 131072 | tf_op jit(solution)/shard_map/all_to_all | solution.py:45
  121.0 16.1 %collective-permute-start.18 = (bf16[96,3072]{1,0:T(8,128)(2,1)}, bf16[96,3072]{1,0:T(8,128)(2,1)}, u32[]{:S(2)}, u32[]{:S(2)}) collective-permute-start(bf16[96,3072]{1,0:T(8,128)(2,1)} %slice.94), channel_id=1, source_target_pairs={{12,0},{0,4},{4,8},{8,12},{13,1},{1,5},{5,9},{9,13},{14,2},{2,6},{... | collective-permute-start | bytes 1769480 | tf_op jit(solution)/shard_map/ppermute | solution.py:28
  122.3 14.9 %collective-permute-start.15 = (bf16[96,3072]{1,0:T(8,128)(2,1)}, bf16[96,3072]{1,0:T(8,128)(2,1)}, u32[]{:S(2)}, u32[]{:S(2)}) collective-permute-start(bf16[96,3072]{1,0:T(8,128)(2,1)} %collective-permute-done.11.refs_12_), channel_id=1, source_target_pairs={{16,0},{32,16},{48,32},{0,48},{17,1},{33,17},{49,33},{1,49},{18,2}... | collective-permute-start | bytes 1769480 | tf_op jit(solution)/shard_map/ppermute | solution.py:28
  124.7 15.4 %collective-permute-start.16 = (bf16[96,3072]{1,0:T(8,128)(2,1)}, bf16[96,3072]{1,0:T(8,128)(2,1)}, u32[]{:S(2)}, u32[]{:S(2)}) collective-permute-start(bf16[96,3072]{1,0:T(8,128)(2,1)} %collective-permute-done.12.refs_14_.refs_0_), channel_id=1, source_target_pairs={{48,0},{0,16},{16,32},{32,48},{49,1},{1,17},{17,33},{33,49},{50,2}... | collective-permute-start | bytes 1769480 | tf_op jit(solution)/shard_map/ppermute | solution.py:28
  124.8 17.4 %collective-permute-start.10 = (bf16[4,8,3072]{2,1,0:T(8,128)(2,1)}, bf16[4,8,3072]{2,1,0:T(8,128)(2,1)}, u32[]{:S(2)}, u32[]{:S(2)}) collective-permute-start(bf16[4,8,3072]{2,1,0:T(8,128)(2,1)} %all-to-all-done.3), channel_id=1, source_target_pairs={{0,32},{32,0},{1,33},{33,1},{2,34},{34,2},{3,35},{35,3},{4,36},{36... | collective-permute-start | bytes 589832 | tf_op jit(solution)/shard_map/ppermute | solution.py:227
  148.2 23.1 %copy-start.3 = (bf16[8,3200]{1,0:T(8,128)(2,1)S(1)}, bf16[8,3200]{1,0:T(8,128)(2,1)}, u32[]{:S(2)}) copy-start(bf16[8,3200]{1,0:T(8,128)(2,1)} %get-tuple-element.114) | copy-start | bytes 153604
  164.6 6.6 %collective-permute-start.19 = (bf16[8,3200]{1,0:T(8,128)(2,1)S(1)}, bf16[8,3200]{1,0:T(8,128)(2,1)S(1)}, u32[]{:S(2)}, u32[]{:S(2)}) collective-permute-start(bf16[8,3200]{1,0:T(8,128)(2,1)S(1)} %shard_map.107), channel_id=1, source_target_pairs={{0,64},{2,66},{64,130},{66,128},{128,192},{130,194},{192,0},{194,2... | collective-permute-start | bytes 153608 | tf_op jit(solution)/shard_map/ppermute | solution.py:35
  188.8 27.4 %copy-start.2 = (bf16[8,3200]{1,0:T(8,128)(2,1)S(1)}, bf16[8,3200]{1,0:T(8,128)(2,1)}, u32[]{:S(2)}) copy-start(bf16[8,3200]{1,0:T(8,128)(2,1)} %get-tuple-element.113) | copy-start | bytes 153604
  201.5 14.6 %collective-permute-start.20 = (bf16[8,3200]{1,0:T(8,128)(2,1)S(1)}, bf16[8,3200]{1,0:T(8,128)(2,1)S(1)}, u32[]{:S(2)}, u32[]{:S(2)}) collective-permute-start(bf16[8,3200]{1,0:T(8,128)(2,1)S(1)} %shard_map.109), channel_id=1, source_target_pairs={{0,64},{2,66},{64,130},{66,128},{128,192},{130,194},{192,0},{194,2... | collective-permute-start | bytes 153608 | tf_op jit(solution)/shard_map/ppermute | solution.py:35
  251.3 5.9 %collective-permute-start.21 = (bf16[8,3200]{1,0:T(8,128)(2,1)S(1)}, bf16[8,3200]{1,0:T(8,128)(2,1)S(1)}, u32[]{:S(2)}, u32[]{:S(2)}) collective-permute-start(bf16[8,3200]{1,0:T(8,128)(2,1)S(1)} %shard_map.111), channel_id=1, source_target_pairs={{0,64},{2,66},{64,130},{66,128},{128,192},{130,194},{1,65},{3,67},... | collective-permute-start | bytes 153608 | tf_op jit(solution)/shard_map/ppermute | solution.py:35
  278.3 21.0 %copy-start.4 = (bf16[8,3200]{1,0:T(8,128)(2,1)S(1)}, bf16[8,3200]{1,0:T(8,128)(2,1)}, u32[]{:S(2)}) copy-start(bf16[8,3200]{1,0:T(8,128)(2,1)} %get-tuple-element.117) | copy-start | bytes 153604
  292.5 6.8 %collective-permute-start.24 = (bf16[8,3200]{1,0:T(8,128)(2,1)S(1)}, bf16[8,3200]{1,0:T(8,128)(2,1)S(1)}, u32[]{:S(2)}, u32[]{:S(2)}) collective-permute-start(bf16[8,3200]{1,0:T(8,128)(2,1)S(1)} %shard_map.113), channel_id=1, source_target_pairs={{0,64},{2,66},{64,128},{66,130},{128,194},{130,192},{1,65},{3,67},... | collective-permute-start | bytes 153608 | tf_op jit(solution)/shard_map/ppermute | solution.py:35
  297.4 3.1 %collective-permute-start.23 = (bf16[8,3200]{1,0:T(8,128)(2,1)S(1)}, bf16[8,3200]{1,0:T(8,128)(2,1)S(1)}, u32[]{:S(2)}, u32[]{:S(2)}) collective-permute-start(bf16[8,3200]{1,0:T(8,128)(2,1)S(1)} %broadcast_select_fusion), channel_id=1, source_target_pairs={{0,64},{2,66},{192,194},{194,192},{1,65},{3,67},{193,195},{195,193... | collective-permute-start | bytes 153608 | tf_op jit(solution)/shard_map/ppermute | solution.py:35
  298.7 1.8 collective-permute-start.22
